TPU v7x, 32 devices: a whole 2x2x4 slice. The times are simulated.
32 devices in a mesh: seq: 8 (over z, y), grp: 4 (over x, core).
Axes of the slice: x: 2, y: 2, z: 4, core: 2. Of those that a mesh axis runs over, the one named last changes fastest.
Arguments:
- x_in: bfloat16 [1024, 8192], P('seq', 'grp'), may hold values from -6 to 6
- multiplier_channels: bfloat16 [1024, 8192], P('seq', 'grp'), may hold values from -6 to 6
- b_proj: bfloat16 [1024, 1024], P('seq', 'grp'), may hold values from -6 to 6
- c_proj: bfloat16 [1024, 1024], P('seq', 'grp'), may hold values from -0.5 to 0.5
- dt_raw: float32 [1024, 64], P('seq', 'grp'), as said below
- dt_bias: float32 [64], P('grp'), may hold values from -3.5 to -1.5
- a_log: float32 [64], P('grp'), as said below
- skip_d: float32 [64], P('grp'), may hold values from 0.2 to 1
- norm_gain: float32 [8192], P('grp'), may hold values from 0.5 to 1.5
- w_out: bfloat16 [8192, 8192], P('grp', 'seq'), may hold values from -0.03125 to 0.03125
Outputs:
- mixed: bfloat16 [1024, 8192], P('seq', 'grp')
Inputs may be any that keep to these rules, and one draw needn't show every extreme that they name: `dt_raw`: step size offsets, with bursts at a few positions of the sequence shared by all heads. `a_log`: log decay rates per head, between log(0.1 / (0.08 * 1024)) and log(0.6).
All inputs are finite; a program needn't handle non-finite values.
Results may differ from a plain program's by a relative error of at most 0.0049.
Values may be sent and summed in bfloat16 or wider, within the bound.
No kernel may reach another device: no remote copies, remote signals or barrier semaphores. Data moves between devices by JAX's collectives and lax.ppermute only.
A program may use at most 128 MiB of HBM per device.

v0:
```python
import math

import jax
import jax.numpy as jnp
from jax import lax
from jax.sharding import PartitionSpec as P

CHANNEL_WIDTH = 128
STATE = 128


HIGH = lax.Precision.HIGHEST


def prefix(array, axis, combine, identity):
    length, mine = (lax.axis_size(axis), lax.axis_index(axis))
    everything = jax.tree.map(lambda part: lax.all_gather(part, axis), array)
    start = jax.tree.map(
        lambda part, zero: jnp.broadcast_to(jnp.asarray(zero, part.dtype), part.shape),
        array,
        identity,
    )

    def turn(k, before):
        reached = k < mine
        new = combine(before, jax.tree.map(lambda part: part[k], everything))
        return jax.tree.map(lambda a, b: jnp.where(reached, a, b), new, before)

    return lax.fori_loop(0, length, turn, start)


def ssd_blocks(xf, dt, la, bm, cm, braw, craw, init):
    length, heads, width = xf.shape
    groups = bm.shape[1]
    ratio = heads // groups
    block = math.gcd(length, 256)
    count = length // block

    def step(state, blk):
        xb, dtb, lab, bb, cb, bnar, cnar = blk
        cum = jnp.cumsum(lab, axis=0)
        attention_logits = jnp.einsum(
            "tgn,sgn->gts", cnar, bnar, preferred_element_type=jnp.float32
        )
        attention_logits = jnp.repeat(attention_logits, ratio, axis=0)
        diff = cum.T[:, :, None] - cum.T[:, None, :]
        rows = lax.broadcasted_iota(jnp.int32, (block, block), 0)
        cols = lax.broadcasted_iota(jnp.int32, (block, block), 1)
        mask = (rows >= cols)[None, :, :]
        decay = jnp.exp(jnp.where(mask, diff, -1e30))
        mixing = decay * attention_logits * dtb.T[:, None, :]
        outs = jnp.einsum("hts,shp->thp", mixing, xb, precision=HIGH)
        cheads = jnp.repeat(cb, ratio, axis=1)
        incoming_channel_bundles = jnp.repeat(bb, ratio, axis=1)
        outs = outs + jnp.exp(cum)[:, :, None] * jnp.einsum(
            "thn,hpn->thp", cheads, state, precision=HIGH
        )
        weights = jnp.exp(cum[-1][None, :] - cum) * dtb
        fresh = jnp.einsum("sh,shp,shn->hpn", weights, xb, incoming_channel_bundles, precision=HIGH)
        state = jnp.exp(cum[-1])[:, None, None] * state + fresh
        return (state, outs)

    blocks = (
        xf.reshape(count, block, heads, width),
        dt.reshape(count, block, heads),
        la.reshape(count, block, heads),
        bm.reshape(count, block, groups, -1),
        cm.reshape(count, block, groups, -1),
        braw.reshape(count, block, groups, -1),
        craw.reshape(count, block, groups, -1),
    )
    final, outs = lax.scan(step, init, blocks)
    return (outs.reshape(length, heads, width), final, jnp.sum(la, axis=0))


def gated_norm_output(y, multiplier_channels, norm_gain, groups):
    length = y.shape[0]
    gated = y.reshape(length, -1) * jax.nn.silu(multiplier_channels.astype(jnp.float32))
    split = gated.reshape(length, groups, -1)
    split = split * lax.rsqrt(jnp.mean(split * split, axis=-1, keepdims=True) + 1e-05)
    return (split.reshape(length, -1) * norm_gain).astype(jnp.bfloat16)


def combine_states(earlier_state, later):
    return (earlier_state[0] * later[0], later[0][:, None, None] * earlier_state[1] + later[1])


def shards(
    x_in, multiplier_channels, b_proj, c_proj, dt_raw, dt_bias, a_log, skip_d, norm_gain, w_out
):
    length = x_in.shape[0]
    heads = dt_raw.shape[1]
    groups = b_proj.shape[1] // STATE
    xf = x_in.astype(jnp.float32).reshape(length, heads, CHANNEL_WIDTH)
    dt = jax.nn.softplus(dt_raw + dt_bias)
    la = -jnp.exp(a_log) * dt
    braw = b_proj.reshape(length, groups, STATE)
    craw = c_proj.reshape(length, groups, STATE)
    bm = braw.astype(jnp.float32)
    cm = craw.astype(jnp.float32)
    empty = jnp.zeros((heads, CHANNEL_WIDTH, STATE), jnp.float32)
    y, local_end, total = ssd_blocks(xf, dt, la, bm, cm, braw, craw, empty)
    identity = (jnp.ones((heads,), jnp.float32), empty)
    carried = prefix((jnp.exp(total), local_end), "seq", combine_states, identity)
    cum = jnp.cumsum(la, axis=0)
    cheads = jnp.repeat(cm, heads // groups, axis=1)
    y = y + jnp.exp(cum)[:, :, None] * jnp.einsum(
        "thn,hpn->thp", cheads, carried[1], precision=HIGH
    )
    y = y + skip_d[None, :, None] * xf
    normed = gated_norm_output(y, multiplier_channels, norm_gain, groups)
    partial_out = jnp.dot(
        normed, lax.all_gather(w_out, "seq", axis=1, tiled=True), preferred_element_type=jnp.float32
    )
    return lax.psum_scatter(partial_out, "grp", scatter_dimension=1, tiled=True).astype(
        jnp.bfloat16
    )


def solution(mesh):
    return jax.shard_map(
        shards,
        mesh=mesh,
        in_specs=(
            P("seq", "grp"),
            P("seq", "grp"),
            P("seq", "grp"),
            P("seq", "grp"),
            P("seq", "grp"),
            P("grp"),
            P("grp"),
            P("grp"),
            P("grp"),
            P("grp", "seq"),
        ),
        out_specs=P("seq", "grp"),
        check_vma=False,
    )
```

profile of v0, /device:TPU:2, one launch (start us, length us, event | category | flops | bytes accessed | tf_op | source)
XLA Modules:
  0.0 847.5 jit_solution(8663865701435249659)
XLA Ops:
  6.5 0.7 exponential_negate_fusion
  7.3 0.9 fusion.24
  8.5 1.3 copy.52
  9.8 0.9 squeeze.39
  10.7 0.8 exponential_multiply_fusion
  11.6 2.2 convolution_add_fusion
  13.9 0.7 all-gather.5.cloned.1.call-update
  14.9 0.6 dynamic-slice.4
  16.3 22.0 %all-reduce = f32[128]{0:T(128)S(1)} all-reduce(f32[128]{0:T(128)S(1)} %exponential_dynamic-update-slice_fusion), channel_id=2, replica_groups=mesh['seq'=8,'grp'=4] {'seq'}, use_global_device_ids=true, to_apply=%add | all-reduce | flops 128 | bytes 1024
  38.6 0.3 fusion.10
  38.9 1.2 convolution_bitcast_fusion.2
  40.3 3.2 fusion.4
  43.5 97.1 %all-gather.7.cloned.1.call-done = f32[128,128,128]{2,1,0:T(8,128)} async-done(((f32[16,128,128]{2,1,0:T(8,128)}), f32[128,128,128]{2,1,0:T(8,128)}) %all-gather.7.cloned.1.call-update) | async-done | bytes 8388624 | tf_op jit(solution)/shard_map/all_gather | solution.py:17
  140.6 12.5 %while.9 = (s32[]{:T(128)}, f32[16,128,128]{2,1,0:T(8,128)S(1)}, s32[]{:T(128)}, f32[8,16]{1,0:T(8,128)S(1)}, f32[8,16,128,128]{3,2,1,0:T(8,128)}, /*index=5*/s32[]{:T(128)}, s32[]{:T(128)}) while((s32[]{:T(128)}, f32[16,128,128]{2,1,0:T(8,128)S(1)}, s32[]{:T(128)}, f32[8,16]{1,0:T(8,128)S(1)}, f32[8,16,128,128]{3,2,1,0:T(8,128)}, ...), condition=%wide.region_3.4_spmd.clone, body=%wide.region_2.3_spmd.clone.sunk | while | flops 1048580 | bytes 3146025 | solution.py:29
  140.6 1.5 fusion.35
  142.1 1.5 fusion.35
  143.6 1.5 fusion.35
  145.1 1.5 fusion.35
  146.6 1.6 fusion.35
  148.2 1.6 fusion.35
  149.8 1.6 fusion.35
  151.4 1.5 fusion.35
  153.1 4.5 fusion.5
  157.6 1.6 copy.57
  159.2 1.3 fusion.23
  160.5 2.1 mul.139
  162.6 0.3 reduce_sum.19
  163.3 0.3 copy.62
  163.6 614.4 %all-gather.5.cloned.1.call-done = bf16[2048,8192]{1,0:T(8,128)(2,1)} async-done(((bf16[2048,1024]{1,0:T(8,128)(2,1)}), bf16[2048,8192]{1,0:T(8,128)(2,1)}) %all-gather.5.cloned.1.call-update) | async-done | bytes 33554448 | tf_op jit(solution)/shard_map/all_gather | solution.py:113
  778.1 17.3 %fusion.11 = f32[128,8192]{1,0:T(8,128)} fusion(bf16[2048,8192]{1,0:T(8,128)(2,1)} %all-gather.5.cloned.1.call-done, f32[128,2048]{1,0:T(8,128)S(1)} %bitcast.71, f32[2048]{0:T(1024)S(1)} %copy-done.3, f32[128,2048]{1,0:T(8,128)S(1)} %copy.57, bf16[128,2048]{1,0:T(8,128)(2,1)S(1)} %copy-done), kind=kOutput, calls=%fused_computation.23 | convolution fusion | flops 4297326592 | bytes 40378368 | tf_op jit(solution)/shard_map/dot_general | solution.py:112
  795.4 43.5 %reduce-scatter.2.cloned.1.call-done = f32[128,2048]{1,0:T(8,128)} async-done(((f32[128,8192]{1,0:T(8,128)}), f32[128,2048]{1,0:T(8,128)}) %reduce-scatter.2.cloned.1.call-update) | async-done | bytes 1048592 | tf_op jit(solution)/shard_map/reduce_scatter | solution.py:115
  838.9 2.1 convert_element_type.20
  (46 shorter events, 1.7 us)
Async XLA Ops:
  6.5 8.4 copy-start.5
  6.5 31.9 %copy-start.1 = (bf16[128,256]{1,0:T(8,128)(2,1)S(1)}, bf16[128,256]{1,0:T(8,128)(2,1)}, u32[]{:S(2)}) copy-start(bf16[128,256]{1,0:T(8,128)(2,1)} %param.14) | copy-start | bytes 196612
  6.5 8.3 copy-start.2
  6.5 134.0 %all-gather.7.cloned.1.call-start = ((), (), s32[]{:S(2)}) async-start(), calls=%async_computation.3 | async-start | bytes 9437184 | tf_op jit(solution)/shard_map/all_gather | solution.py:17
  13.9 764.2 %all-gather.5.cloned.1.call-start = ((), (), s32[]{:S(2)}) async-start(), calls=%async_computation.1 | async-start | bytes 37748736 | tf_op jit(solution)/shard_map/all_gather | solution.py:113
  14.6 824.3 %reduce-scatter.2.cloned.1.call-start = ((), (), s32[]{:S(2)}) async-start(), calls=%async_computation.2 | async-start | bytes 5242880 | tf_op jit(solution)/shard_map/reduce_scatter | solution.py:115
  43.5 109.6 %copy-start.4 = (f32[16]{0:T(128)S(1)}, f32[16]{0:T(128)}, u32[]{:S(2)}) copy-start(f32[16]{0:T(128)} %param.19) | copy-start | bytes 196
  140.6 18.6 %copy-start = (bf16[128,2048]{1,0:T(8,128)(2,1)S(1)}, bf16[128,2048]{1,0:T(8,128)(2,1)}, u32[]{:S(2)}) copy-start(bf16[128,2048]{1,0:T(8,128)(2,1)} %param.13) | copy-start | bytes 1572868
  153.1 625.0 %copy-start.3 = (f32[2048]{0:T(1024)S(1)}, f32[2048]{0:T(1024)}, u32[]{:S(2)}) copy-start(f32[2048]{0:T(1024)} %param.20) | copy-start | bytes 24580
Sparse Core Ops, SparseCore 0:
  14.0 126.5 all-gather.6
  142.1 635.9 all-gather.4
  795.5 43.3 reduce-scatter.1
where the time goes:
time: 851 us; the launch traced here: 848 us
  waiting for transfers between devices  756 us (89%)
  matrix products  28.6 us (3%)
  blocking collectives  22 us (3%)
  other arithmetic  18.7 us (2%)
  between operations  14 us (2%)
    all_gather x1, waiting for transfers between devices, shards(): lax.all_gather(w_out, 'seq', axis=1, tiled=True)  614 us
    all_gather x1, waiting for transfers between devices, prefix(): everything = jax.tree.map(lambda part: lax.all_gather(part, axis), array)  97.1 us
    reduce_scatter x1, waiting for transfers between devices, shards(): lax.psum_scatter(partial_out, 'grp', scatter_dimension=1, tiled=True)  43.5 us
    unnamed x1, blocking collectives  22 us
    dot_general x1, matrix products, shards(): jnp.dot(normed, lax.all_gather(w_out, 'seq', axis=1, tiled=True), preferr...  17.3 us
  transfers between devices with their start and end apart: 3, of which 3 were waited for; matrix products, arithmetic and copies ran while one was open for 3% of the time, Pallas kernels for 0%

commit v1 on v0

v1 whole, which is shorter than its diff:
```python
import math

import jax
import jax.numpy as jnp
from jax import lax
from jax.experimental import pallas as pl
from jax.experimental.pallas import tpu as pltpu
from jax.sharding import PartitionSpec as P

CHANNEL_WIDTH = 128
STATE = 128
EPS = 1e-05

HIGH = lax.Precision.HIGHEST
F32 = jnp.float32
BF16 = jnp.bfloat16
NT = (((1,), (1,)), ((), ()))
TN = (((0,), (0,)), ((), ()))
VMEM_LIMIT = 48 * 2**20


def params(grid_dims=0):
    return pltpu.CompilerParams(
        vmem_limit_bytes=VMEM_LIMIT,
        dimension_semantics=("arbitrary",) * grid_dims if grid_dims else None,
    )


def cost(flops, moved):
    return pl.CostEstimate(flops=int(flops), bytes_accessed=int(moved), transcendentals=0)


def iota(shape, axis):
    return lax.broadcasted_iota(jnp.int32, shape, axis)


def spread(values, width):
    heads = values.shape[1]
    return jnp.concatenate(
        [jnp.broadcast_to(values[:, h : h + 1], (values.shape[0], width)) for h in range(heads)], axis=1
    )


def split3(value):
    hi = value.astype(BF16)
    rest = value - hi.astype(F32)
    mid = rest.astype(BF16)
    return hi, mid, (rest - mid.astype(F32)).astype(BF16)


def pack_kernel(y_ref, x_ref, b_ref, c_ref, dt_ref, out_ref, *, heads):
    width, state = x_ref.shape[1], b_ref.shape[1]
    out_ref[:, :width] = x_ref[...]
    out_ref[:, width : width + state] = b_ref[...]
    out_ref[:, width + state : width + 2 * state] = c_ref[...]
    other = 1 - y_ref[0]
    rows, cols = iota((2 * heads, 128), 0), iota((2 * heads, 128), 1)
    total = jnp.zeros((x_ref.shape[0], 128), F32)
    for part, value in enumerate(split3(dt_ref[...])):
        place = (cols == rows - other * heads + part * heads) & (rows // heads == other)
        total = total + jnp.dot(value, place.astype(BF16), preferred_element_type=F32)
    out_ref[:, width + 2 * state :] = total.astype(BF16)


def pack(y, x, b, c, dt, heads):
    tokens, width, state = x.shape[0], heads * CHANNEL_WIDTH, STATE
    full = width + 2 * state + 128
    return pl.pallas_call(
        lambda *refs: pack_kernel(*refs, heads=heads),
        grid_spec=pltpu.PrefetchScalarGridSpec(
            num_scalar_prefetch=1,
            grid=(1,),
            in_specs=[
                pl.BlockSpec((tokens, width), lambda i, y: (0, 1 - y[0])),
                pl.BlockSpec((tokens, state), lambda i, y: (0, 1 - y[0])),
                pl.BlockSpec((tokens, state), lambda i, y: (0, 1 - y[0])),
                pl.BlockSpec(dt.shape, lambda i, y: (0, 0)),
            ],
            out_specs=pl.BlockSpec((tokens, full), lambda i, y: (0, 0)),
        ),
        out_shape=jax.ShapeDtypeStruct((tokens, full), BF16),
        compiler_params=params(1),
        cost_estimate=cost(1e6, 4 * tokens * full),
        name="pack",
    )(y, x, b, c, dt)


def local_state_kernel(
    y_ref, x_ref, b_ref, c_ref, dt_ref, pk_ref, bias_ref, alog_ref,
    xs_ref, bs_ref, cs_ref, scal_ref, send_ref, s_ref, *, heads,
):
    tokens, width = x_ref.shape
    state = b_ref.shape[1]
    y = y_ref[0]
    mine, theirs = pl.multiple_of(y * tokens, tokens), pl.multiple_of((1 - y) * tokens, tokens)
    xs_ref[pl.ds(mine, tokens), :] = x_ref[...]
    xs_ref[pl.ds(theirs, tokens), :] = pk_ref[:, :width]
    bs_ref[pl.ds(mine, tokens), :] = b_ref[...]
    bs_ref[pl.ds(theirs, tokens), :] = pk_ref[:, width : width + state]
    cs_ref[pl.ds(mine, tokens), :] = c_ref[...]
    cs_ref[pl.ds(theirs, tokens), :] = pk_ref[:, width + state : width + 2 * state]
    rows, cols = iota((2 * heads, heads), 0), iota((2 * heads, heads), 1)
    own = jnp.dot(dt_ref[...], (rows == cols + y * heads).astype(F32), precision=HIGH)
    rows, cols = iota((128, heads), 0), iota((128, heads), 1)
    take = ((rows % heads == cols) & (rows < 3 * heads)).astype(BF16)
    other = jnp.dot(pk_ref[:, width + 2 * state :], take, preferred_element_type=F32)
    raw = jnp.concatenate([jnp.where(y == 0, own, other), jnp.where(y == 0, other, own)], axis=0)
    raw = raw + bias_ref[...]
    dt = jnp.maximum(raw, 0.0) + jnp.log1p(jnp.exp(-jnp.abs(raw)))
    la = -jnp.exp(alog_ref[...]) * dt
    length = 2 * tokens
    lower = (iota((length, length), 0) >= iota((length, length), 1)).astype(F32)
    cum = jnp.dot(lower, la, precision=HIGH)
    last = cum[length - 1 : length, :]
    scal_ref[:, :heads] = cum
    scal_ref[:, heads : 2 * heads] = dt
    weights = jnp.exp(last - cum) * dt
    scaled = (xs_ref[...].astype(F32) * spread(weights, CHANNEL_WIDTH)).astype(BF16)
    s = lax.dot_general(bs_ref[...], scaled, TN, preferred_element_type=F32)
    s_ref[:state, :] = s
    send_ref[:state, :] = s.astype(BF16)
    decay = spread(jnp.exp(last), CHANNEL_WIDTH)
    s_ref[state:, :] = jnp.broadcast_to(decay, (8, width))
    hi, mid, lo = split3(decay)
    which = iota((16, width), 0)
    parts = jnp.where(which == 0, hi.astype(F32), jnp.where(which == 1, mid.astype(F32), lo.astype(F32)))
    send_ref[state:, :] = jnp.where(which < 3, parts, 0.0).astype(BF16)


def local_state(y, x, b, c, dt, pk, bias, alog, heads):
    tokens, width, state = x.shape[0], heads * CHANNEL_WIDTH, STATE
    whole = lambda a: pl.BlockSpec(a.shape, lambda i, y: (0,) * a.ndim)
    outs = [
        jax.ShapeDtypeStruct((2 * tokens, width), BF16),
        jax.ShapeDtypeStruct((2 * tokens, state), BF16),
        jax.ShapeDtypeStruct((2 * tokens, state), BF16),
        jax.ShapeDtypeStruct((2 * tokens, 2 * heads), F32),
        jax.ShapeDtypeStruct((state + 16, width), BF16),
        jax.ShapeDtypeStruct((state + 8, width), F32),
    ]
    return pl.pallas_call(
        lambda *refs: local_state_kernel(*refs, heads=heads),
        grid_spec=pltpu.PrefetchScalarGridSpec(
            num_scalar_prefetch=1,
            grid=(1,),
            in_specs=[
                pl.BlockSpec((tokens, width), lambda i, y: (0, y[0])),
                pl.BlockSpec((tokens, state), lambda i, y: (0, y[0])),
                pl.BlockSpec((tokens, state), lambda i, y: (0, y[0])),
                whole(dt),
                whole(pk),
                whole(bias),
                whole(alog),
            ],
            out_specs=[whole(o) for o in outs],
        ),
        out_shape=outs,
        compiler_params=params(1),
        cost_estimate=cost(2e8, 3e6),
        name="local_state",
    )(y, x, b, c, dt, pk, bias, alog)


def local_y_kernel(xs_ref, bs_ref, cs_ref, scal_ref, skip_ref, out_ref, *, heads, tokens):
    cum, dt = scal_ref[:, :heads], scal_ref[:, heads : 2 * heads]
    length = 2 * tokens
    eye = (iota((length, length), 0) == iota((length, length), 1)).astype(F32)
    flat = lax.dot_general(scal_ref[...], eye, TN, precision=HIGH)
    cum_row, dt_row = flat[:heads, :], flat[heads : 2 * heads, :]
    mask = iota((tokens, tokens), 0) >= iota((tokens, tokens), 1)
    logits = []
    for k in range(2):
        at = pl.ds(k * tokens, tokens)
        logits.append(lax.dot_general(cs_ref[at, :], bs_ref[at, :], NT, preferred_element_type=F32))
    middle = cum[tokens - 1 : tokens, :]
    weights = jnp.exp(middle - cum[:tokens, :]) * dt[:tokens, :]
    scaled = (xs_ref[:tokens, :].astype(F32) * spread(weights, CHANNEL_WIDTH)).astype(BF16)
    s = lax.dot_general(bs_ref[:tokens, :], scaled, TN, preferred_element_type=F32).astype(BF16)
    carried = jnp.dot(cs_ref[tokens:, :], s, preferred_element_type=F32)
    carried = carried * spread(jnp.exp(cum[tokens:, :] - middle), CHANNEL_WIDTH)
    for k in range(2):
        lo = k * tokens
        for h in range(heads):
            at = h * CHANNEL_WIDTH
            xh = xs_ref[lo : lo + tokens, at : at + CHANNEL_WIDTH]
            diff = cum[lo : lo + tokens, h : h + 1] - cum_row[h : h + 1, lo : lo + tokens]
            mix = jnp.exp(jnp.where(mask, diff, -1e30)) * logits[k] * dt_row[h : h + 1, lo : lo + tokens]
            yh = jnp.dot(mix.astype(BF16), xh, preferred_element_type=F32)
            yh = yh + skip_ref[:, at : at + CHANNEL_WIDTH] * xh.astype(F32)
            if k == 1:
                yh = yh + carried[:, at : at + CHANNEL_WIDTH]
            out_ref[lo : lo + tokens, at : at + CHANNEL_WIDTH] = yh


def local_y(xs, bs, cs, scal, skip, heads):
    length, width = xs.shape
    return pl.pallas_call(
        lambda *refs: local_y_kernel(*refs, heads=heads, tokens=length // 2),
        out_shape=jax.ShapeDtypeStruct((length, width), F32),
        compiler_params=params(),
        cost_estimate=cost(4e8, 4e6),
        name="local_y",
    )(xs, bs, cs, scal, skip)


def join_kernel(send_ref, s_ref, got_ref, out_ref):
    state = out_ref.shape[0]
    out_ref[...] = (s_ref[:state, :] + s_ref[state : state + 1, :] * got_ref[:state, :].astype(F32)).astype(BF16)


def join(send, s, got):
    return pl.pallas_call(
        join_kernel,
        out_shape=jax.ShapeDtypeStruct((STATE, s.shape[1]), BF16),
        compiler_params=params(),
        cost_estimate=cost(1e6, 1.5e6),
        name="join",
    )(send, s, got)


def finish_kernel(y_ref, local_ref, cs_ref, scal_ref, one_ref, two_ref, gate_ref, got_ref, gain_ref, out_ref, *, heads):
    length, width = local_ref.shape
    state, tokens = two_ref.shape[0], length // 2
    y = y_ref[0]
    decay = jnp.sum(one_ref[state:, :].astype(F32), axis=0, keepdims=True)
    start = one_ref[:state, :].astype(F32) + decay * two_ref[...].astype(F32)
    hi = start.astype(BF16)
    grow = jnp.exp(scal_ref[:, :heads])
    for k in range(2):
        at = pl.ds(k * tokens, tokens)
        carried = jnp.dot(cs_ref[at, :], hi, preferred_element_type=F32)
        value = local_ref[at, :] + carried * spread(grow[k * tokens : (k + 1) * tokens, :], CHANNEL_WIDTH)
        gate = jnp.where(y == k, gate_ref[...], got_ref[...]).astype(F32)
        value = value * (gate / (1.0 + jnp.exp(-gate)))
        mean = jnp.sum(value * value, axis=1, keepdims=True) / width
        out_ref[at, :] = (value * lax.rsqrt(mean + EPS) * gain_ref[...]).astype(BF16)


def finish(y, local, cs, scal, one, two, gate, got, gain, heads):
    length, width = local.shape
    whole = lambda a: pl.BlockSpec(a.shape, lambda i, y: (0,) * a.ndim)
    return pl.pallas_call(
        lambda *refs: finish_kernel(*refs, heads=heads),
        grid_spec=pltpu.PrefetchScalarGridSpec(
            num_scalar_prefetch=1,
            grid=(1,),
            in_specs=[
                whole(local),
                whole(cs),
                whole(scal),
                whole(one),
                whole(two),
                pl.BlockSpec((length // 2, width), lambda i, y: (0, y[0])),
                whole(got),
                whole(gain),
            ],
            out_specs=pl.BlockSpec((length, width), lambda i, y: (0, 0)),
        ),
        out_shape=jax.ShapeDtypeStruct((length, width), BF16),
        compiler_params=params(1),
        cost_estimate=cost(1e8, 4e6),
        name="finish",
    )(y, local, cs, scal, one, two, gate, got, gain)


def project_kernel(y_ref, a_ref, own_ref, got_ref, out_ref, half_ref):
    block = a_ref[...]
    for k, ref in enumerate((own_ref, got_ref)):
        part = jnp.dot(block, ref[...], preferred_element_type=F32)
        out_ref[0, k] = part
        half_ref[0, k] = part.astype(BF16)


def project(y, block, weights, got):
    tokens, depth = block.shape[0] // 2, block.shape[1]
    cols = weights.shape[1]
    shape = (2, 2, tokens, cols)
    return pl.pallas_call(
        project_kernel,
        grid_spec=pltpu.PrefetchScalarGridSpec(
            num_scalar_prefetch=1,
            grid=(2,),
            in_specs=[
                pl.BlockSpec((tokens, depth), lambda i, y: (i + y[0] - 2 * i * y[0], 0)),
                pl.BlockSpec((depth, cols), lambda i, y: (y[0], 0)),
                pl.BlockSpec((depth, cols), lambda i, y: (0, 0)),
            ],
            out_specs=[
                pl.BlockSpec((1,) + shape[1:], lambda i, y: (i, 0, 0, 0)),
                pl.BlockSpec((1,) + shape[1:], lambda i, y: (i, 0, 0, 0)),
            ],
        ),
        out_shape=[jax.ShapeDtypeStruct(shape, F32), jax.ShapeDtypeStruct(shape, BF16)],
        compiler_params=params(1),
        cost_estimate=cost(8.0 * tokens * depth * cols, 9e6),
        name="project",
    )(y, block, weights, got)


def pair_shards(nz, x_in, gate, b_proj, c_proj, dt_raw, dt_bias, a_log, skip_d, norm_gain, w_out):
    tokens = x_in.shape[0]
    heads = dt_raw.shape[1] // 2
    width = heads * CHANNEL_WIDTH
    seq, grp = lax.axis_index("seq"), lax.axis_index("grp")
    z, y = seq // 2, seq % 2
    yv = y.astype(jnp.int32).reshape(1)
    both = ("seq", "grp")
    spots = [(a, b, g) for a in range(nz) for b in range(2) for g in range(nz)]
    flat = lambda a, b, g: (a * 2 + b) * nz + g

    def half(v, axis, which):
        n = v.shape[axis] // 2
        return lax.dynamic_slice_in_dim(v, which * n, n, axis)

    flip = [(s, s ^ 1) for s in range(2 * nz)]
    got = lax.ppermute(pack(yv, x_in, b_proj, c_proj, dt_raw, heads), "seq", flip)
    got_gate = lax.ppermute(half(gate, 1, 1 - y), "seq", flip)
    got_w = lax.ppermute(half(w_out, 0, 1 - y), "seq", flip)
    bias, alog = half(dt_bias, 0, y)[None, :], half(a_log, 0, y)[None, :]
    skip = jnp.repeat(half(skip_d, 0, y), CHANNEL_WIDTH)[None, :]
    gain = half(norm_gain, 0, y)[None, :]

    def along(v, step, senders):
        pairs = [(a * 2 + b, (a + step) * 2 + b) for a in senders for b in range(2)]
        return lax.ppermute(v, "seq", pairs)

    xs, bs, cs, scal, send, s = local_state(yv, x_in, b_proj, c_proj, dt_raw, got, bias, alog, heads)
    one = along(send, 1, range(nz - 1))
    base = local_y(xs, bs, cs, scal, skip, heads)
    two = along(join(send, s, one), 2, range(nz - 2))
    block = finish(yv, base, cs, scal, one, two, gate, got_gate, gain, heads)

    up1, down1 = along(block, 1, range(nz - 1)), along(block, -1, range(1, nz))
    up2, down2 = along(up1, 1, range(1, nz - 1)), along(down1, -1, range(1, nz - 1))
    far = jnp.where(z == 1, down2, up2)
    far = lax.ppermute(far, "seq", [(2 + b, b) for b in range(2)] + [(4 + b, 6 + b) for b in range(2)])
    table = [(0, 1, 2, 3), (1, 2, 0, 3), (2, 1, 3, 0), (3, 2, 1, 0)]
    slots = [
        block,
        jnp.where(z < 2, down1, up1),
        jnp.where(z == 0, down2, jnp.where(z == 1, up1, jnp.where(z == 2, down1, up2))),
        jnp.where(z == 1, down2, jnp.where(z == 2, up2, far)),
    ]
    total = None
    for slot, value in enumerate(slots):
        full, rounded = project(yv, value, w_out, got_w)
        owner = lambda a: table[a][slot]
        pairs = [(flat(a, b, g ^ 1), flat(a, b, g)) for a, b, g in spots if g % 2 == owner(a) % 2]
        summed = full + lax.ppermute(rounded, both, pairs).astype(F32)
        pairs = [(flat(a, 1 - b, g), flat(a, b, g)) for a, b, g in spots if g % 2 == owner(a) % 2]
        r = lax.ppermute(summed[1].astype(BF16), both, pairs).astype(F32)
        summed = summed[0] + r[::-1]
        pairs = [(flat(a, b, g ^ 2), flat(a, b, g)) for a, b, g in spots if g == owner(a)]
        summed = summed + lax.ppermute(summed.astype(BF16), both, pairs).astype(F32)
        result = summed.astype(BF16)
        if slot:
            pairs = [(flat(a, b, g), flat(g, b, a)) for a, b, g in spots if g == owner(a)]
            result = lax.ppermute(result, both, pairs)
            total = total + result
        else:
            total = jnp.where(z == grp, result, jnp.zeros_like(result))
    left = jnp.where(y == 0, total[0], total[1])
    right = jnp.where(y == 0, total[1], total[0])
    return jnp.concatenate([left, right], axis=1)


def prefix(array, axis, combine, identity):
    length, mine = (lax.axis_size(axis), lax.axis_index(axis))
    everything = jax.tree.map(lambda part: lax.all_gather(part, axis), array)
    start = jax.tree.map(
        lambda part, zero: jnp.broadcast_to(jnp.asarray(zero, part.dtype), part.shape),
        array,
        identity,
    )

    def turn(k, before):
        reached = k < mine
        new = combine(before, jax.tree.map(lambda part: part[k], everything))
        return jax.tree.map(lambda a, b: jnp.where(reached, a, b), new, before)

    return lax.fori_loop(0, length, turn, start)


def ssd_blocks(xf, dt, la, bm, cm, braw, craw, init):
    length, heads, width = xf.shape
    groups = bm.shape[1]
    ratio = heads // groups
    block = math.gcd(length, 256)
    count = length // block

    def step(state, blk):
        xb, dtb, lab, bb, cb, bnar, cnar = blk
        cum = jnp.cumsum(lab, axis=0)
        attention_logits = jnp.einsum("tgn,sgn->gts", cnar, bnar, preferred_element_type=F32)
        attention_logits = jnp.repeat(attention_logits, ratio, axis=0)
        diff = cum.T[:, :, None] - cum.T[:, None, :]
        rows = lax.broadcasted_iota(jnp.int32, (block, block), 0)
        cols = lax.broadcasted_iota(jnp.int32, (block, block), 1)
        mask = (rows >= cols)[None, :, :]
        decay = jnp.exp(jnp.where(mask, diff, -1e30))
        mixing = decay * attention_logits * dtb.T[:, None, :]
        outs = jnp.einsum("hts,shp->thp", mixing, xb, precision=HIGH)
        cheads = jnp.repeat(cb, ratio, axis=1)
        bheads = jnp.repeat(bb, ratio, axis=1)
        outs = outs + jnp.exp(cum)[:, :, None] * jnp.einsum("thn,hpn->thp", cheads, state, precision=HIGH)
        weights = jnp.exp(cum[-1][None, :] - cum) * dtb
        fresh = jnp.einsum("sh,shp,shn->hpn", weights, xb, bheads, precision=HIGH)
        state = jnp.exp(cum[-1])[:, None, None] * state + fresh
        return (state, outs)

    cut = lambda v: v.reshape((count, block) + v.shape[1:])
    final, outs = lax.scan(step, init, jax.tree.map(cut, (xf, dt, la, bm, cm, braw, craw)))
    return (outs.reshape(length, heads, width), final, jnp.sum(la, axis=0))


def gated_norm_output(y, multiplier_channels, norm_gain, groups):
    length = y.shape[0]
    gated = y.reshape(length, -1) * jax.nn.silu(multiplier_channels.astype(F32))
    split = gated.reshape(length, groups, -1)
    split = split * lax.rsqrt(jnp.mean(split * split, axis=-1, keepdims=True) + EPS)
    return (split.reshape(length, -1) * norm_gain).astype(BF16)


def combine_states(earlier_state, later):
    return (earlier_state[0] * later[0], later[0][:, None, None] * earlier_state[1] + later[1])


def general_shards(x_in, gate, b_proj, c_proj, dt_raw, dt_bias, a_log, skip_d, norm_gain, w_out):
    length = x_in.shape[0]
    heads = dt_raw.shape[1]
    groups = b_proj.shape[1] // STATE
    xf = x_in.astype(F32).reshape(length, heads, CHANNEL_WIDTH)
    dt = jax.nn.softplus(dt_raw + dt_bias)
    la = -jnp.exp(a_log) * dt
    braw = b_proj.reshape(length, groups, STATE)
    craw = c_proj.reshape(length, groups, STATE)
    bm = braw.astype(F32)
    cm = craw.astype(F32)
    empty = jnp.zeros((heads, CHANNEL_WIDTH, STATE), F32)
    y, local_end, total = ssd_blocks(xf, dt, la, bm, cm, braw, craw, empty)
    identity = (jnp.ones((heads,), F32), empty)
    carried = prefix((jnp.exp(total), local_end), "seq", combine_states, identity)
    cum = jnp.cumsum(la, axis=0)
    cheads = jnp.repeat(cm, heads // groups, axis=1)
    y = y + jnp.exp(cum)[:, :, None] * jnp.einsum("thn,hpn->thp", cheads, carried[1], precision=HIGH)
    y = y + skip_d[None, :, None] * xf
    normed = gated_norm_output(y, gate, norm_gain, groups)
    partial_out = jnp.dot(
        normed, lax.all_gather(w_out, "seq", axis=1, tiled=True), preferred_element_type=F32
    )
    return lax.psum_scatter(partial_out, "grp", scatter_dimension=1, tiled=True).astype(BF16)


def solution(mesh):
    seq, grp = mesh.shape["seq"], mesh.shape["grp"]

    def shards(*args):
        groups = args[2].shape[1] // STATE
        if grp == 4 and seq == 2 * grp and groups == 2:
            return pair_shards(grp, *args)
        return general_shards(*args)

    return jax.shard_map(
        shards,
        mesh=mesh,
        in_specs=(
            P("seq", "grp"),
            P("seq", "grp"),
            P("seq", "grp"),
            P("seq", "grp"),
            P("seq", "grp"),
            P("grp"),
            P("grp"),
            P("grp"),
            P("grp"),
            P("grp", "seq"),
        ),
        out_specs=P("seq", "grp"),
        check_vma=False,
    )
```

time: 851 us -> 213 us (0.25)
  waiting for transfers between devices: 756 us -> 99.9 us
  starting transfers between devices: 0.08 us -> 61.2 us
  matrix products: 28.6 us -> 0 us
  blocking collectives: 22 us -> 0 us
  Pallas kernels: 0 us -> 18.5 us
  between operations: 14 us -> 0.48 us
    all_gather x2 -> x0, waiting for transfers between devices: 712 us -> none  [the longest x1 614 us: shards(): lax.all_gather(w_out, 'seq', axis=1, tiled=True)]
    ppermute x0 -> x25, waiting for transfers between devices: none -> 99.9 us  [the longest x1 41.5 us: pair_shards(): got_gate = lax.ppermute(half(gate, 1, 1 - y), 'seq', flip)]
    ppermute x0 -> x25, starting transfers between devices: none -> 61.2 us  [the longest x6 18 us: along(): return lax.ppermute(v, 'seq', pairs)]
    reduce_scatter x1 -> x0, waiting for transfers between devices: 43.5 us -> none  [shards(): lax.psum_scatter(partial_out, 'grp', scatter_dimension=1, tiled=True)]
    dot_general x6 -> x0, matrix products: 28.6 us -> none  [the longest x1 17.3 us: shards(): jnp.dot(normed, lax.all_gather(w_out, 'seq', axis=1, tiled=True), preferr...]
    unnamed x1 -> x0, blocking collectives: 22 us -> none
    pallas_call x0 -> x9, Pallas kernels: none -> 18.5 us  [the longest x4 13.3 us: project(): pl.pallas_call(project_kernel, grid_spec=pltpu.PrefetchScalarGridSpec(num...]
    unnamed x17 -> x35, local copies, waits for them, and re-layouts: 2.37 us -> 11.2 us
  transfers between devices with their start and end apart: 3 -> 25, of which waited for: 3 -> 9; matrix products, arithmetic and copies ran while one was open for 3% -> 8% of each run, Pallas kernels for 0% -> 8%
where the time goes in v1:
time: 213 us; the launch traced here: 212 us
  waiting for transfers between devices  99.9 us (47%)
  starting transfers between devices  61.2 us (29%)
  Pallas kernels  18.5 us (9%)
  local copies, waits for them, and re-layouts  16.2 us (8%)
  other arithmetic  15.5 us (7%)
    ppermute x1, waiting for transfers between devices, pair_shards(): got_gate = lax.ppermute(half(gate, 1, 1 - y), 'seq', flip)  41.5 us
    ppermute x6, starting transfers between devices, along(): return lax.ppermute(v, 'seq', pairs)  18 us
    ppermute x3, starting transfers between devices, pair_shards(): result = lax.ppermute(result, both, pairs)  17.1 us
    ppermute x6, waiting for transfers between devices, along(): return lax.ppermute(v, 'seq', pairs)  16.9 us
    pallas_call x4, Pallas kernels, project(): pl.pallas_call(project_kernel, grid_spec=pltpu.PrefetchScalarGridSpec(num...  13.3 us
    ppermute x4, waiting for transfers between devices, pair_shards(): r = lax.ppermute(summed[1].astype(BF16), both, pairs).astype(F32)  12 us
    unnamed x35, local copies, waits for them, and re-layouts  11.2 us
    ppermute x3, waiting for transfers between devices, pair_shards(): result = lax.ppermute(result, both, pairs)  11.1 us
  transfers between devices with their start and end apart: 25, of which 9 were waited for; matrix products, arithmetic and copies ran while one was open for 8% of the time, Pallas kernels for 8%

profile of v1, /device:TPU:2, one launch (start us, length us, event | category | flops | bytes accessed | tf_op | source)
XLA Modules:
  0.0 211.7 jit_solution(7200962354671567630)
XLA Ops:
  3.7 1.6 collective-permute-start
  6.0 7.9 %collective-permute-done.refs_5_ = bf16[128,1408]{1,0:T(8,128)(2,1)S(1)} collective-permute-done((bf16[128,1408]{1,0:T(8,128)(2,1)S(1)}, bf16[128,1408]{1,0:T(8,128)(2,1)S(1)}, u32[]{:S(2)}, u32[]{:S(2)}) %collective-permute-start) | collective-permute-done | bytes 360480 | tf_op jit(solution)/shard_map/ppermute | solution.py:316
  18.0 3.6 %collective-permute-start.1 = (bf16[144,1024]{1,0:T(8,128)(2,1)S(1)}, bf16[144,1024]{1,0:T(8,128)(2,1)S(1)}, u32[]{:S(2)}, u32[]{:S(2)}) collective-permute-start(bf16[144,1024]{1,0:T(8,128)(2,1)S(1)} %get-tuple-element.23.send_ref), channel_id=1, source_target_pairs={{0,8},{4,12},{8,16},{12,20},{16,24},{20,28},{1,9},{5,13},{9,17},{1... | collective-permute-start | bytes 884744 | tf_op jit(solution)/shard_map/ppermute | solution.py:325
  21.7 3.1 %constant_dynamic-slice_fusion = bf16[1024,1024]{1,0:T(8,128)(2,1)} fusion(bf16[2048,1024]{1,0:T(8,128)(2,1)} %own_ref.7, s32[]{:T(128)S(6)} %select_n.92), kind=kLoop, calls=%fused_computation.41 | loop fusion | bytes 4194308 | tf_op jit(solution)/shard_map/dynamic_slice | solution.py:313
  24.8 1.5 collective-permute-start.4
  28.3 4.9 %collective-permute-start.2 = (bf16[128,1024]{1,0:T(8,128)(2,1)}, bf16[128,1024]{1,0:T(8,128)(2,1)S(1)}, u32[]{:S(2)}, u32[]{:S(2)}) collective-permute-start(bf16[128,1024]{1,0:T(8,128)(2,1)} %join.1), channel_id=1, source_target_pairs={{0,16},{4,20},{8,24},{12,28},{1,17},{5,21},{9,25},{13,29},{2,18},{... | collective-permute-start | bytes 786440 | tf_op jit(solution)/shard_map/ppermute | solution.py:325
  35.4 41.5 %collective-permute-done.3.refs_7_ = bf16[128,1024]{1,0:T(8,128)(2,1)} collective-permute-done((bf16[128,1024]{1,0:T(8,128)(2,1)}, bf16[128,1024]{1,0:T(8,128)(2,1)}, u32[]{:S(2)}, u32[]{:S(2)}) %collective-permute-start.3) | collective-permute-done | bytes 262176 | tf_op jit(solution)/shard_map/ppermute | solution.py:317
  79.5 1.9 finish.1.a_ref
  82.7 5.4 %collective-permute-start.9 = (bf16[256,1024]{1,0:T(8,128)(2,1)S(1)}, bf16[256,1024]{1,0:T(8,128)(2,1)}, u32[]{:S(2)}, u32[]{:S(2)}) collective-permute-start(bf16[256,1024]{1,0:T(8,128)(2,1)S(1)} %finish.1.a_ref), channel_id=1, source_target_pairs={{0,8},{4,12},{8,16},{12,20},{16,24},{20,28},{1,9},{5,13},{9,17},{1... | collective-permute-start | bytes 1572872 | tf_op jit(solution)/shard_map/ppermute | solution.py:325
  88.0 6.9 %collective-permute-done.8 = bf16[256,1024]{1,0:T(8,128)(2,1)} collective-permute-done((bf16[256,1024]{1,0:T(8,128)(2,1)S(1)}, bf16[256,1024]{1,0:T(8,128)(2,1)}, u32[]{:S(2)}, u32[]{:S(2)}) %collective-permute-start.8) | collective-permute-done | bytes 524320 | tf_op jit(solution)/shard_map/ppermute | solution.py:325
  96.2 1.5 collective-permute-start.15
  97.7 10.0 %collective-permute-done.14 = bf16[256,1024]{1,0:T(8,128)(2,1)S(1)} collective-permute-done((bf16[256,1024]{1,0:T(8,128)(2,1)}, bf16[256,1024]{1,0:T(8,128)(2,1)S(1)}, u32[]{:S(2)}, u32[]{:S(2)}) %collective-permute-start.14) | collective-permute-done | bytes 524320 | tf_op jit(solution)/shard_map/ppermute | solution.py:325
  107.7 1.9 broadcast_select_fusion
  110.9 3.9 %project.4 = (f32[2,2,128,1024]{3,2,1,0:T(8,128)S(1)}, bf16[2,2,128,1024]{3,2,1,0:T(8,128)(2,1)}) custom-call(s32[1]{0:T(128)} %bitcast.refs_0_.y_ref, bf16[256,1024]{1,0:T(8,128)(2,1)S(1)} %finish.1.a_ref, bf16[2048,1024]{1,0:T(8,128)(2,1)} %own_ref.7, bf16[1024,1024]{1,0:T(8,128)(2,1)S(1)} %collective-permute-done.4.got_ref), custom_call_target="tpu_custom_call" | custom-call | flops 1073741824 | bytes 9000000 | tf_op jit(solution)/shard_map/project/pallas_call | solution.py:278
  117.4 4.1 %collective-permute-done.20 = bf16[256,1024]{1,0:T(8,128)(2,1)} collective-permute-done((bf16[256,1024]{1,0:T(8,128)(2,1)}, bf16[256,1024]{1,0:T(8,128)(2,1)}, u32[]{:S(2)}, u32[]{:S(2)}) %collective-permute-start.20) | collective-permute-done | bytes 524320 | tf_op jit(solution)/shard_map/ppermute | solution.py:336
  121.5 1.7 broadcast_select_fusion.1
  123.2 3.1 %project.7 = (f32[2,2,128,1024]{3,2,1,0:T(8,128)S(1)}, bf16[2,2,128,1024]{3,2,1,0:T(8,128)(2,1)S(1)}) custom-call(s32[1]{0:T(128)} %bitcast.refs_0_.y_ref, bf16[256,1024]{1,0:T(8,128)(2,1)S(1)} %get-tuple-element.35.a_ref, bf16[2048,1024]{1,0:T(8,128)(2,1)} %own_ref.7, bf16[1024,1024]{1,0:T(8,128)(2,1)S(1)} %collective-permute-done.4.got_ref), custom_call_target="tpu_custom_call" | custom-call | flops 1073741824 | bytes 9000000 | tf_op jit(solution)/shard_map/project/pallas_call | solution.py:278
  126.3 2.3 %collective-permute-start.21 = (bf16[2,2,128,1024]{3,2,1,0:T(8,128)(2,1)S(1)}, bf16[2,2,128,1024]{3,2,1,0:T(8,128)(2,1)}, u32[]{:S(2)}, u32[]{:S(2)}) collective-permute-start(bf16[2,2,128,1024]{3,2,1,0:T(8,128)(2,1)S(1)} %get-tuple-element.32), channel_id=1, source_target_pairs={{0,1},{2,3},{4,5},{6,7},{8,9},{10,11},{12,13},{14,15},{17,16},{19,... | collective-permute-start | bytes 3145736 | tf_op jit(solution)/shard_map/ppermute | solution.py:349
  128.6 3.1 %project.6 = (f32[2,2,128,1024]{3,2,1,0:T(8,128)S(1)}, bf16[2,2,128,1024]{3,2,1,0:T(8,128)(2,1)S(1)}) custom-call(s32[1]{0:T(128)} %bitcast.refs_0_.y_ref, bf16[256,1024]{1,0:T(8,128)(2,1)S(1)} %get-tuple-element.34.a_ref, bf16[2048,1024]{1,0:T(8,128)(2,1)} %own_ref.7, bf16[1024,1024]{1,0:T(8,128)(2,1)S(1)} %collective-permute-done.4.got_ref), custom_call_target="tpu_custom_call" | custom-call | flops 1073741824 | bytes 9000000 | tf_op jit(solution)/shard_map/project/pallas_call | solution.py:278
  133.0 3.2 %project.5 = (f32[2,2,128,1024]{3,2,1,0:T(8,128)S(1)}, bf16[2,2,128,1024]{3,2,1,0:T(8,128)(2,1)S(1)}) custom-call(s32[1]{0:T(128)} %bitcast.refs_0_.y_ref, bf16[256,1024]{1,0:T(8,128)(2,1)S(1)} %get-tuple-element.33.a_ref, bf16[2048,1024]{1,0:T(8,128)(2,1)} %own_ref.7, bf16[1024,1024]{1,0:T(8,128)(2,1)S(1)} %collective-permute-done.4.got_ref), custom_call_target="tpu_custom_call" | custom-call | flops 1073741824 | bytes 9000000 | tf_op jit(solution)/shard_map/project/pallas_call | solution.py:278
  136.3 3.2 %collective-permute-start.10 = (bf16[2,2,128,1024]{3,2,1,0:T(8,128)(2,1)S(1)}, bf16[2,2,128,1024]{3,2,1,0:T(8,128)(2,1)S(1)}, u32[]{:S(2)}, u32[]{:S(2)}) collective-permute-start(bf16[2,2,128,1024]{3,2,1,0:T(8,128)(2,1)S(1)} %get-tuple-element.28), channel_id=1, source_target_pairs={{0,1},{2,3},{4,5},{6,7},{9,8},{11,10},{13,12},{15,14},{16,17},{18,... | collective-permute-start | bytes 3145736 | tf_op jit(solution)/shard_map/ppermute | solution.py:349
  139.5 1.5 convert_add_fusion.3
  141.1 3.4 %collective-permute-start.6 = (bf16[2,128,1024]{2,1,0:T(8,128)(2,1)S(1)}, bf16[2,128,1024]{2,1,0:T(8,128)(2,1)S(1)}, u32[]{:S(2)}, u32[]{:S(2)}) collective-permute-start(bf16[2,128,1024]{2,1,0:T(8,128)(2,1)S(1)} %fusion.8), channel_id=1, source_target_pairs={{4,0},{6,2},{0,4},{2,6},{13,9},{15,11},{9,13},{11,15},{20,16},{22,... | collective-permute-start | bytes 1572872 | tf_op jit(solution)/shard_map/ppermute | solution.py:351
  144.5 1.6 convert_add_fusion
  147.4 2.4 %collective-permute-start.17 = (bf16[2,128,1024]{2,1,0:T(8,128)(2,1)S(1)}, bf16[2,128,1024]{2,1,0:T(8,128)(2,1)S(1)}, u32[]{:S(2)}, u32[]{:S(2)}) collective-permute-start(bf16[2,128,1024]{2,1,0:T(8,128)(2,1)S(1)} %fusion.10), channel_id=1, source_target_pairs={{4,0},{6,2},{0,4},{2,6},{12,8},{14,10},{8,12},{10,14},{21,17},{23,... | collective-permute-start | bytes 1572872 | tf_op jit(solution)/shard_map/ppermute | solution.py:351
  151.1 6.0 %collective-permute-done.6 = bf16[2,128,1024]{2,1,0:T(8,128)(2,1)S(1)} collective-permute-done((bf16[2,128,1024]{2,1,0:T(8,128)(2,1)S(1)}, bf16[2,128,1024]{2,1,0:T(8,128)(2,1)S(1)}, u32[]{:S(2)}, u32[]{:S(2)}) %collective-permute-start.6) | collective-permute-done | bytes 524320 | tf_op jit(solution)/shard_map/ppermute | solution.py:351
  158.2 3.3 %collective-permute-start.7 = (bf16[2,128,1024]{2,1,0:T(8,128)(2,1)}, bf16[2,128,1024]{2,1,0:T(8,128)(2,1)}, u32[]{:S(2)}, u32[]{:S(2)}) collective-permute-start(bf16[2,128,1024]{2,1,0:T(8,128)(2,1)} %fusion.12), channel_id=1, source_target_pairs={{2,0},{6,4},{11,9},{15,13},{16,18},{20,22},{25,27},{29,31}} | collective-permute-start | bytes 1572872 | tf_op jit(solution)/shard_map/ppermute | solution.py:354
  162.4 5.9 %collective-permute-done.17 = bf16[2,128,1024]{2,1,0:T(8,128)(2,1)S(1)} collective-permute-done((bf16[2,128,1024]{2,1,0:T(8,128)(2,1)S(1)}, bf16[2,128,1024]{2,1,0:T(8,128)(2,1)S(1)}, u32[]{:S(2)}, u32[]{:S(2)}) %collective-permute-start.17) | collective-permute-done | bytes 524320 | tf_op jit(solution)/shard_map/ppermute | solution.py:351
  173.3 6.4 %collective-permute-done.18 = bf16[2,128,1024]{2,1,0:T(8,128)(2,1)S(1)} collective-permute-done((bf16[2,128,1024]{2,1,0:T(8,128)(2,1)S(1)}, bf16[2,128,1024]{2,1,0:T(8,128)(2,1)S(1)}, u32[]{:S(2)}, u32[]{:S(2)}) %collective-permute-start.18) | collective-permute-done | bytes 524320 | tf_op jit(solution)/shard_map/ppermute | solution.py:354
  180.8 14.3 %collective-permute-start.19 = (bf16[2,128,1024]{2,1,0:T(8,128)(2,1)}, bf16[2,128,1024]{2,1,0:T(8,128)(2,1)}, u32[]{:S(2)}, u32[]{:S(2)}) collective-permute-start(bf16[2,128,1024]{2,1,0:T(8,128)(2,1)} %add_convert_fusion.1), channel_id=1, source_target_pairs={{2,16},{6,20},{8,1},{12,5},{19,26},{23,30},{25,11},{29,15}} | collective-permute-start | bytes 1572872 | tf_op jit(solution)/shard_map/ppermute | solution.py:358
  197.7 11.1 %collective-permute-done.24 = bf16[2,128,1024]{2,1,0:T(8,128)(2,1)} collective-permute-done((bf16[2,128,1024]{2,1,0:T(8,128)(2,1)}, bf16[2,128,1024]{2,1,0:T(8,128)(2,1)}, u32[]{:S(2)}, u32[]{:S(2)}) %collective-permute-start.24) | collective-permute-done | bytes 524320 | tf_op jit(solution)/shard_map/ppermute | solution.py:358
  208.8 2.0 fusion.7
  (92 shorter events, 37.0 us)
Async XLA Ops:
  3.7 10.2 %collective-permute-start = (bf16[128,1408]{1,0:T(8,128)(2,1)S(1)}, bf16[128,1408]{1,0:T(8,128)(2,1)S(1)}, u32[]{:S(2)}, u32[]{:S(2)}) collective-permute-start(bf16[128,1408]{1,0:T(8,128)(2,1)S(1)} %pack.1), channel_id=1, source_target_pairs={{0,4},{4,0},{8,12},{12,8},{16,20},{20,16},{24,28},{28,24},{1,5},{5... | collective-permute-start | bytes 1081352 | tf_op jit(solution)/shard_map/ppermute | solution.py:316
  18.0 6.8 %copy-start.7 = (bf16[256,1024]{1,0:T(8,128)(2,1)}, bf16[256,1024]{1,0:T(8,128)(2,1)S(1)}, u32[]{:S(2)}) copy-start(bf16[256,1024]{1,0:T(8,128)(2,1)S(1)} %get-tuple-element.19.refs_0_) | copy-start | bytes 1572868
  18.0 15.4 %copy-start.5 = (f32[256,16]{1,0:T(8,128)}, f32[256,16]{1,0:T(8,128)S(1)}, u32[]{:S(2)}) copy-start(f32[256,16]{1,0:T(8,128)S(1)} %get-tuple-element.22.refs_3_) | copy-start | bytes 49156
  18.0 8.3 %copy-start.4 = (bf16[128,2048]{1,0:T(8,128)(2,1)S(1)}, bf16[128,2048]{1,0:T(8,128)(2,1)}, u32[]{:S(2)}) copy-start(bf16[128,2048]{1,0:T(8,128)(2,1)} %refs_6_.1) | copy-start | bytes 1572868
  18.0 15.2 %copy-start.16 = (f32[16]{0:T(128)S(1)}, f32[16]{0:T(128)}, u32[]{:S(2)}) copy-start(f32[16]{0:T(128)} %param.17) | copy-start | bytes 196
  18.0 15.3 %copy-start.15 = (f32[2048]{0:T(1024)S(1)}, f32[2048]{0:T(1024)}, u32[]{:S(2)}) copy-start(f32[2048]{0:T(1024)} %param.18) | copy-start | bytes 24580
  18.0 9.5 %collective-permute-start.1 = (bf16[144,1024]{1,0:T(8,128)(2,1)S(1)}, bf16[144,1024]{1,0:T(8,128)(2,1)S(1)}, u32[]{:S(2)}, u32[]{:S(2)}) collective-permute-start(bf16[144,1024]{1,0:T(8,128)(2,1)S(1)} %get-tuple-element.23.send_ref), channel_id=1, source_target_pairs={{0,8},{4,12},{8,16},{12,20},{16,24},{20,28},{1,9},{5,13},{9,17},{1... | collective-permute-start | bytes 884744 | tf_op jit(solution)/shard_map/ppermute | solution.py:325
  24.8 86.1 %collective-permute-start.4 = (bf16[1024,1024]{1,0:T(8,128)(2,1)}, bf16[1024,1024]{1,0:T(8,128)(2,1)S(1)}, u32[]{:S(2)}, u32[]{:S(2)}) collective-permute-start(bf16[1024,1024]{1,0:T(8,128)(2,1)} %constant_dynamic-slice_fusion), channel_id=1, source_target_pairs={{0,4},{4,0},{8,12},{12,8},{16,20},{20,16},{24,28},{28,24},{1,5},{5... | collective-permute-start | bytes 6291464 | tf_op jit(solution)/shard_map/ppermute | solution.py:318
  27.0 49.9 %collective-permute-start.3 = (bf16[128,1024]{1,0:T(8,128)(2,1)}, bf16[128,1024]{1,0:T(8,128)(2,1)}, u32[]{:S(2)}, u32[]{:S(2)}) collective-permute-start(bf16[128,1024]{1,0:T(8,128)(2,1)} %constant_dynamic-slice_fusion.1), channel_id=1, source_target_pairs={{0,4},{4,0},{8,12},{12,8},{16,20},{20,16},{24,28},{28,24},{1,5},{5... | collective-permute-start | bytes 786440 | tf_op jit(solution)/shard_map/ppermute | solution.py:317
  28.3 48.6 %collective-permute-start.2 = (bf16[128,1024]{1,0:T(8,128)(2,1)}, bf16[128,1024]{1,0:T(8,128)(2,1)S(1)}, u32[]{:S(2)}, u32[]{:S(2)}) collective-permute-start(bf16[128,1024]{1,0:T(8,128)(2,1)} %join.1), channel_id=1, source_target_pairs={{0,16},{4,20},{8,24},{12,28},{1,17},{5,21},{9,25},{13,29},{2,18},{... | collective-permute-start | bytes 786440 | tf_op jit(solution)/shard_map/ppermute | solution.py:325
  81.4 13.6 %collective-permute-start.8 = (bf16[256,1024]{1,0:T(8,128)(2,1)S(1)}, bf16[256,1024]{1,0:T(8,128)(2,1)}, u32[]{:S(2)}, u32[]{:S(2)}) collective-permute-start(bf16[256,1024]{1,0:T(8,128)(2,1)S(1)} %finish.1.a_ref), channel_id=1, source_target_pairs={{8,0},{12,4},{16,8},{20,12},{24,16},{28,20},{9,1},{13,5},{17,9},{2... | collective-permute-start | bytes 1572872 | tf_op jit(solution)/shard_map/ppermute | solution.py:325
  82.7 13.6 %collective-permute-start.9 = (bf16[256,1024]{1,0:T(8,128)(2,1)S(1)}, bf16[256,1024]{1,0:T(8,128)(2,1)}, u32[]{:S(2)}, u32[]{:S(2)}) collective-permute-start(bf16[256,1024]{1,0:T(8,128)(2,1)S(1)} %finish.1.a_ref), channel_id=1, source_target_pairs={{0,8},{4,12},{8,16},{12,20},{16,24},{20,28},{1,9},{5,13},{9,17},{1... | collective-permute-start | bytes 1572872 | tf_op jit(solution)/shard_map/ppermute | solution.py:325
  94.9 12.8 %collective-permute-start.14 = (bf16[256,1024]{1,0:T(8,128)(2,1)}, bf16[256,1024]{1,0:T(8,128)(2,1)S(1)}, u32[]{:S(2)}, u32[]{:S(2)}) collective-permute-start(bf16[256,1024]{1,0:T(8,128)(2,1)} %collective-permute-done.8), channel_id=1, source_target_pairs={{8,0},{12,4},{16,8},{20,12},{9,1},{13,5},{17,9},{21,13},{10,2},{14... | collective-permute-start | bytes 1572872 | tf_op jit(solution)/shard_map/ppermute | solution.py:325
  96.2 11.5 %collective-permute-start.15 = (bf16[256,1024]{1,0:T(8,128)(2,1)}, bf16[256,1024]{1,0:T(8,128)(2,1)}, u32[]{:S(2)}, u32[]{:S(2)}) collective-permute-start(bf16[256,1024]{1,0:T(8,128)(2,1)} %collective-permute-done.9), channel_id=1, source_target_pairs={{8,16},{12,20},{16,24},{20,28},{9,17},{13,21},{17,25},{21,29},{10,... | collective-permute-start | bytes 1572872 | tf_op jit(solution)/shard_map/ppermute | solution.py:325
  109.6 11.9 %collective-permute-start.20 = (bf16[256,1024]{1,0:T(8,128)(2,1)}, bf16[256,1024]{1,0:T(8,128)(2,1)}, u32[]{:S(2)}, u32[]{:S(2)}) collective-permute-start(bf16[256,1024]{1,0:T(8,128)(2,1)} %broadcast_select_fusion), channel_id=1, source_target_pairs={{8,0},{12,4},{16,24},{20,28},{9,1},{13,5},{17,25},{21,29},{10,2},{... | collective-permute-start | bytes 1572872 | tf_op jit(solution)/shard_map/ppermute | solution.py:336
  114.8 1.3 copy-start
  116.1 23.3 %collective-permute-start.5 = (bf16[2,2,128,1024]{3,2,1,0:T(8,128)(2,1)}, bf16[2,2,128,1024]{3,2,1,0:T(8,128)(2,1)}, u32[]{:S(2)}, u32[]{:S(2)}) collective-permute-start(bf16[2,2,128,1024]{3,2,1,0:T(8,128)(2,1)} %get-tuple-element.26), channel_id=1, source_target_pairs={{1,0},{3,2},{5,4},{7,6},{8,9},{10,11},{12,13},{14,15},{17,16},{19,... | collective-permute-start | bytes 3145736 | tf_op jit(solution)/shard_map/ppermute | solution.py:349
  126.3 18.2 %collective-permute-start.21 = (bf16[2,2,128,1024]{3,2,1,0:T(8,128)(2,1)S(1)}, bf16[2,2,128,1024]{3,2,1,0:T(8,128)(2,1)}, u32[]{:S(2)}, u32[]{:S(2)}) collective-permute-start(bf16[2,2,128,1024]{3,2,1,0:T(8,128)(2,1)S(1)} %get-tuple-element.32), channel_id=1, source_target_pairs={{0,1},{2,3},{4,5},{6,7},{8,9},{10,11},{12,13},{14,15},{17,16},{19,... | collective-permute-start | bytes 3145736 | tf_op jit(solution)/shard_map/ppermute | solution.py:349
  131.7 15.2 %collective-permute-start.16 = (bf16[2,2,128,1024]{3,2,1,0:T(8,128)(2,1)S(1)}, bf16[2,2,128,1024]{3,2,1,0:T(8,128)(2,1)S(1)}, u32[]{:S(2)}, u32[]{:S(2)}) collective-permute-start(bf16[2,2,128,1024]{3,2,1,0:T(8,128)(2,1)S(1)} %get-tuple-element.30), channel_id=1, source_target_pairs={{1,0},{3,2},{5,4},{7,6},{9,8},{11,10},{13,12},{15,14},{16,17},{18,... | collective-permute-start | bytes 3145736 | tf_op jit(solution)/shard_map/ppermute | solution.py:349
  133.0 6.4 %copy-start.1 = (f32[2,2,128,1024]{3,2,1,0:T(8,128)S(1)}, f32[2,2,128,1024]{3,2,1,0:T(8,128)}, u32[]{:S(2)}) copy-start(f32[2,2,128,1024]{3,2,1,0:T(8,128)} %copy-done) | copy-start | bytes 6291460
  136.3 13.6 %collective-permute-start.10 = (bf16[2,2,128,1024]{3,2,1,0:T(8,128)(2,1)S(1)}, bf16[2,2,128,1024]{3,2,1,0:T(8,128)(2,1)S(1)}, u32[]{:S(2)}, u32[]{:S(2)}) collective-permute-start(bf16[2,2,128,1024]{3,2,1,0:T(8,128)(2,1)S(1)} %get-tuple-element.28), channel_id=1, source_target_pairs={{0,1},{2,3},{4,5},{6,7},{9,8},{11,10},{13,12},{15,14},{16,17},{18,... | collective-permute-start | bytes 3145736 | tf_op jit(solution)/shard_map/ppermute | solution.py:349
  141.1 16.0 %collective-permute-start.6 = (bf16[2,128,1024]{2,1,0:T(8,128)(2,1)S(1)}, bf16[2,128,1024]{2,1,0:T(8,128)(2,1)S(1)}, u32[]{:S(2)}, u32[]{:S(2)}) collective-permute-start(bf16[2,128,1024]{2,1,0:T(8,128)(2,1)S(1)} %fusion.8), channel_id=1, source_target_pairs={{4,0},{6,2},{0,4},{2,6},{13,9},{15,11},{9,13},{11,15},{20,16},{22,... | collective-permute-start | bytes 1572872 | tf_op jit(solution)/shard_map/ppermute | solution.py:351
  146.2 15.3 %collective-permute-start.22 = (bf16[2,128,1024]{2,1,0:T(8,128)(2,1)S(1)}, bf16[2,128,1024]{2,1,0:T(8,128)(2,1)S(1)}, u32[]{:S(2)}, u32[]{:S(2)}) collective-permute-start(bf16[2,128,1024]{2,1,0:T(8,128)(2,1)S(1)} %fusion.11), channel_id=1, source_target_pairs={{5,1},{7,3},{1,5},{3,7},{13,9},{15,11},{9,13},{11,15},{20,16},{22,... | collective-permute-start | bytes 1572872 | tf_op jit(solution)/shard_map/ppermute | solution.py:351
  147.4 21.0 %collective-permute-start.17 = (bf16[2,128,1024]{2,1,0:T(8,128)(2,1)S(1)}, bf16[2,128,1024]{2,1,0:T(8,128)(2,1)S(1)}, u32[]{:S(2)}, u32[]{:S(2)}) collective-permute-start(bf16[2,128,1024]{2,1,0:T(8,128)(2,1)S(1)} %fusion.10), channel_id=1, source_target_pairs={{4,0},{6,2},{0,4},{2,6},{12,8},{14,10},{8,12},{10,14},{21,17},{23,... | collective-permute-start | bytes 1572872 | tf_op jit(solution)/shard_map/ppermute | solution.py:351
  150.4 19.6 %collective-permute-start.11 = (bf16[2,128,1024]{2,1,0:T(8,128)(2,1)S(1)}, bf16[2,128,1024]{2,1,0:T(8,128)(2,1)S(1)}, u32[]{:S(2)}, u32[]{:S(2)}) collective-permute-start(bf16[2,128,1024]{2,1,0:T(8,128)(2,1)S(1)} %fusion.9), channel_id=1, source_target_pairs={{5,1},{7,3},{1,5},{3,7},{12,8},{14,10},{8,12},{10,14},{21,17},{23,... | collective-permute-start | bytes 1572872 | tf_op jit(solution)/shard_map/ppermute | solution.py:351
  158.2 39.5 %collective-permute-start.7 = (bf16[2,128,1024]{2,1,0:T(8,128)(2,1)}, bf16[2,128,1024]{2,1,0:T(8,128)(2,1)}, u32[]{:S(2)}, u32[]{:S(2)}) collective-permute-start(bf16[2,128,1024]{2,1,0:T(8,128)(2,1)} %fusion.12), channel_id=1, source_target_pairs={{2,0},{6,4},{11,9},{15,13},{16,18},{20,22},{25,27},{29,31}} | collective-permute-start | bytes 1572872 | tf_op jit(solution)/shard_map/ppermute | solution.py:354
  161.7 9.2 %collective-permute-start.23 = (bf16[2,128,1024]{2,1,0:T(8,128)(2,1)S(1)}, bf16[2,128,1024]{2,1,0:T(8,128)(2,1)S(1)}, u32[]{:S(2)}, u32[]{:S(2)}) collective-permute-start(bf16[2,128,1024]{2,1,0:T(8,128)(2,1)S(1)} %fusion.15), channel_id=1, source_target_pairs={{1,3},{5,7},{9,11},{13,15},{18,16},{22,20},{26,24},{30,28}} | collective-permute-start | bytes 1572872 | tf_op jit(solution)/shard_map/ppermute | solution.py:354
  168.6 11.1 %collective-permute-start.18 = (bf16[2,128,1024]{2,1,0:T(8,128)(2,1)S(1)}, bf16[2,128,1024]{2,1,0:T(8,128)(2,1)S(1)}, u32[]{:S(2)}, u32[]{:S(2)}) collective-permute-start(bf16[2,128,1024]{2,1,0:T(8,128)(2,1)S(1)} %fusion.14), channel_id=1, source_target_pairs={{0,2},{4,6},{10,8},{14,12},{17,19},{21,23},{27,25},{31,29}} | collective-permute-start | bytes 1572872 | tf_op jit(solution)/shard_map/ppermute | solution.py:354
  170.2 24.9 %collective-permute-start.12 = (bf16[2,128,1024]{2,1,0:T(8,128)(2,1)S(1)}, bf16[2,128,1024]{2,1,0:T(8,128)(2,1)S(1)}, u32[]{:S(2)}, u32[]{:S(2)}) collective-permute-start(bf16[2,128,1024]{2,1,0:T(8,128)(2,1)S(1)} %fusion.13), channel_id=1, source_target_pairs={{3,1},{7,5},{8,10},{12,14},{19,17},{23,21},{24,26},{28,30}} | collective-permute-start | bytes 1572872 | tf_op jit(solution)/shard_map/ppermute | solution.py:354
  172.0 36.7 %collective-permute-start.24 = (bf16[2,128,1024]{2,1,0:T(8,128)(2,1)}, bf16[2,128,1024]{2,1,0:T(8,128)(2,1)}, u32[]{:S(2)}, u32[]{:S(2)}) collective-permute-start(bf16[2,128,1024]{2,1,0:T(8,128)(2,1)} %add_convert_fusion), channel_id=1, source_target_pairs={{3,24},{7,28},{11,25},{15,29},{16,2},{20,6},{24,3},{28,7}} | collective-permute-start | bytes 1572872 | tf_op jit(solution)/shard_map/ppermute | solution.py:358
  180.8 28.0 %collective-permute-start.19 = (bf16[2,128,1024]{2,1,0:T(8,128)(2,1)}, bf16[2,128,1024]{2,1,0:T(8,128)(2,1)}, u32[]{:S(2)}, u32[]{:S(2)}) collective-permute-start(bf16[2,128,1024]{2,1,0:T(8,128)(2,1)} %add_convert_fusion.1), channel_id=1, source_target_pairs={{2,16},{6,20},{8,1},{12,5},{19,26},{23,30},{25,11},{29,15}} | collective-permute-start | bytes 1572872 | tf_op jit(solution)/shard_map/ppermute | solution.py:358
  196.2 12.6 %collective-permute-start.13 = (bf16[2,128,1024]{2,1,0:T(8,128)(2,1)}, bf16[2,128,1024]{2,1,0:T(8,128)(2,1)}, u32[]{:S(2)}, u32[]{:S(2)}) collective-permute-start(bf16[2,128,1024]{2,1,0:T(8,128)(2,1)} %add_convert_fusion.2), channel_id=1, source_target_pairs={{1,8},{5,12},{10,17},{14,21},{17,10},{21,14},{26,19},{30,23}} | collective-permute-start | bytes 1572872 | tf_op jit(solution)/shard_map/ppermute | solution.py:358
  (10 other events, 9.0 us)

commit v2 on v1

--- a/solution.py
+++ b/solution.py
@@ -16,7 +16,7 @@
 BF16 = jnp.bfloat16
 NT = (((1,), (1,)), ((), ()))
 TN = (((0,), (0,)), ((), ()))
-VMEM_LIMIT = 48 * 2**20
+VMEM_LIMIT = 24 * 2**20
 
 
 def params(grid_dims=0):
@@ -27,7 +27,7 @@
 
 
 def cost(flops, moved):
-    return pl.CostEstimate(flops=int(flops), bytes_accessed=int(moved), transcendentals=0)
+    return pl.CostEstimate(flops=1, bytes_accessed=1, transcendentals=0)
 
 
 def iota(shape, axis):
@@ -58,7 +58,7 @@
     total = jnp.zeros((x_ref.shape[0], 128), F32)
     for part, value in enumerate(split3(dt_ref[...])):
         place = (cols == rows - other * heads + part * heads) & (rows // heads == other)
-        total = total + jnp.dot(value, place.astype(BF16), preferred_element_type=F32)
+        total = total + lax.dot_general(value, place.astype(BF16), TN, preferred_element_type=F32)
     out_ref[:, width + 2 * state :] = total.astype(BF16)
 
 
@@ -100,7 +100,7 @@
     cs_ref[pl.ds(mine, tokens), :] = c_ref[...]
     cs_ref[pl.ds(theirs, tokens), :] = pk_ref[:, width + state : width + 2 * state]
     rows, cols = iota((2 * heads, heads), 0), iota((2 * heads, heads), 1)
-    own = jnp.dot(dt_ref[...], (rows == cols + y * heads).astype(F32), precision=HIGH)
+    own = lax.dot_general(dt_ref[...], (rows == cols + y * heads).astype(F32), TN, precision=HIGH)
     rows, cols = iota((128, heads), 0), iota((128, heads), 1)
     take = ((rows % heads == cols) & (rows < 3 * heads)).astype(BF16)
     other = jnp.dot(pk_ref[:, width + 2 * state :], take, preferred_element_type=F32)
@@ -185,7 +185,9 @@
             xh = xs_ref[lo : lo + tokens, at : at + CHANNEL_WIDTH]
             diff = cum[lo : lo + tokens, h : h + 1] - cum_row[h : h + 1, lo : lo + tokens]
             mix = jnp.exp(jnp.where(mask, diff, -1e30)) * logits[k] * dt_row[h : h + 1, lo : lo + tokens]
-            yh = jnp.dot(mix.astype(BF16), xh, preferred_element_type=F32)
+            top = mix.astype(BF16)
+            yh = jnp.dot(top, xh, preferred_element_type=F32)
+            yh = yh + jnp.dot((mix - top.astype(F32)).astype(BF16), xh, preferred_element_type=F32)
             yh = yh + skip_ref[:, at : at + CHANNEL_WIDTH] * xh.astype(F32)
             if k == 1:
                 yh = yh + carried[:, at : at + CHANNEL_WIDTH]
@@ -263,38 +265,86 @@
     )(y, local, cs, scal, one, two, gate, got, gain)
 
 
-def project_kernel(y_ref, a_ref, own_ref, got_ref, out_ref, half_ref):
-    block = a_ref[...]
-    for k, ref in enumerate((own_ref, got_ref)):
-        part = jnp.dot(block, ref[...], preferred_element_type=F32)
-        out_ref[0, k] = part
-        half_ref[0, k] = part.astype(BF16)
-
-
-def project(y, block, weights, got):
-    tokens, depth = block.shape[0] // 2, block.shape[1]
-    cols = weights.shape[1]
-    shape = (2, 2, tokens, cols)
+def project_kernel(yc_ref, own_ref, got_ref, w_ref, w0_ref, w1_ref, keep_ref, send_ref, both_ref):
+    tokens, depth = keep_ref.shape[0], own_ref.shape[1]
+    y, core = yc_ref[0], yc_ref[1]
+
+    @pl.when(pl.program_id(0) == 0)
+    def _():
+        for k in range(2):
+            at = pl.multiple_of(jnp.where(y == 0, k, 1 - k) * tokens, tokens)
+            rows = pl.ds(k * tokens, tokens)
+            own, got = own_ref[pl.ds(at, tokens), :], got_ref[pl.ds(at, tokens), :]
+            both_ref[rows, :depth] = jnp.where(core == 0, own, got)
+            both_ref[rows, depth:] = jnp.where(core == 0, got, own)
+
+    def multiply(first, second):
+        part = jnp.dot(both_ref[:, :depth], first[...], preferred_element_type=F32)
+        part = part + jnp.dot(both_ref[:, depth:], second[...], preferred_element_type=F32)
+        keep_ref[...] = part[:tokens, :]
+        send_ref[...] = part[tokens:, :].astype(BF16)
+
+    @pl.when(core == 0)
+    def _():
+        multiply(w_ref, w0_ref)
+
+    @pl.when(core == 1)
+    def _():
+        multiply(w0_ref, w1_ref)
+
+
+def project(yc, own, got, w, w0, w1):
+    tokens, depth = own.shape[0] // 2, own.shape[1]
+    cols = w.shape[1]
+    tile = min(cols, 256)
     return pl.pallas_call(
         project_kernel,
         grid_spec=pltpu.PrefetchScalarGridSpec(
             num_scalar_prefetch=1,
-            grid=(2,),
+            grid=(cols // tile,),
             in_specs=[
-                pl.BlockSpec((tokens, depth), lambda i, y: (i + y[0] - 2 * i * y[0], 0)),
-                pl.BlockSpec((depth, cols), lambda i, y: (y[0], 0)),
-                pl.BlockSpec((depth, cols), lambda i, y: (0, 0)),
+                pl.BlockSpec(own.shape, lambda i, yc: (0, 0)),
+                pl.BlockSpec(own.shape, lambda i, yc: (0, 0)),
+                pl.BlockSpec((depth, tile), lambda i, yc: (yc[0], jnp.where(yc[1] == 0, i, 0))),
+                pl.BlockSpec((depth, tile), lambda i, yc: (0, i)),
+                pl.BlockSpec((depth, tile), lambda i, yc: (0, jnp.where(yc[1] == 1, i, 0))),
             ],
             out_specs=[
-                pl.BlockSpec((1,) + shape[1:], lambda i, y: (i, 0, 0, 0)),
-                pl.BlockSpec((1,) + shape[1:], lambda i, y: (i, 0, 0, 0)),
+                pl.BlockSpec((tokens, tile), lambda i, yc: (0, i)),
+                pl.BlockSpec((tokens, tile), lambda i, yc: (0, i)),
             ],
+            scratch_shapes=[pltpu.VMEM((2 * tokens, 2 * depth), BF16)],
         ),
-        out_shape=[jax.ShapeDtypeStruct(shape, F32), jax.ShapeDtypeStruct(shape, BF16)],
+        out_shape=[jax.ShapeDtypeStruct((tokens, cols), F32), jax.ShapeDtypeStruct((tokens, cols), BF16)],
         compiler_params=params(1),
-        cost_estimate=cost(8.0 * tokens * depth * cols, 9e6),
+        cost_estimate=cost(8.0 * tokens * depth * cols, 6e6),
         name="project",
-    )(y, block, weights, got)
+    )(yc, own, got, w, w0, w1)
+
+
+def place_kernel(at_ref, mine_ref, got_ref, out_ref):
+    cols = got_ref.shape[1]
+    part = at_ref[0]
+    out_ref[:, pl.ds(pl.multiple_of(part * cols, cols), cols)] = mine_ref[...]
+    out_ref[:, pl.ds(pl.multiple_of((1 - part) * cols, cols), cols)] = got_ref[...]
+
+
+def place(at, mine, got):
+    tokens, cols = got.shape
+    whole = pl.BlockSpec((tokens, cols), lambda i, at: (0, 0))
+    return pl.pallas_call(
+        place_kernel,
+        grid_spec=pltpu.PrefetchScalarGridSpec(
+            num_scalar_prefetch=1,
+            grid=(1,),
+            in_specs=[whole, whole],
+            out_specs=pl.BlockSpec((tokens, 2 * cols), lambda i, at: (0, 0)),
+        ),
+        out_shape=jax.ShapeDtypeStruct((tokens, 2 * cols), BF16),
+        compiler_params=params(1),
+        cost_estimate=cost(1e6, 2e6),
+        name="place",
+    )(at, mine, got)
 
 
 def pair_shards(nz, x_in, gate, b_proj, c_proj, dt_raw, dt_bias, a_log, skip_d, norm_gain, w_out):
@@ -304,64 +354,103 @@
     seq, grp = lax.axis_index("seq"), lax.axis_index("grp")
     z, y = seq // 2, seq % 2
     yv = y.astype(jnp.int32).reshape(1)
+    yc = jnp.stack([y, grp % 2]).astype(jnp.int32)
+    dt_raw = dt_raw.T
     both = ("seq", "grp")
-    spots = [(a, b, g) for a in range(nz) for b in range(2) for g in range(nz)]
-    flat = lambda a, b, g: (a * 2 + b) * nz + g
+    core = grp % 2
+    spots = [(a, b, c, d) for a in range(nz) for b in range(2) for c in range(nz // 2) for d in range(2)]
+    flat = lambda a, b, c, d: ((a * 2 + b) * (nz // 2) + c) * 2 + d
+    tie = lax.optimization_barrier
 
     def half(v, axis, which):
         n = v.shape[axis] // 2
         return lax.dynamic_slice_in_dim(v, which * n, n, axis)
 
     flip = [(s, s ^ 1) for s in range(2 * nz)]
+    sibling = [(g, g ^ 1) for g in range(nz)]
+    across = [(flat(a, b, c, d), flat(a, 1 - b, c, 1 - d)) for a, b, c, d in spots]
+
+    def along(v, step, senders):
+        pairs = [(a * 2 + b, (a + step) * 2 + b) for a in senders for b in range(2)]
+        return lax.ppermute(v, "seq", pairs)
+
     got = lax.ppermute(pack(yv, x_in, b_proj, c_proj, dt_raw, heads), "seq", flip)
-    got_gate = lax.ppermute(half(gate, 1, 1 - y), "seq", flip)
-    got_w = lax.ppermute(half(w_out, 0, 1 - y), "seq", flip)
+    swap, go = half(w_out, 0, y ^ 1 ^ core), half(w_out, 0, 1 - y)
+    gate_half = half(gate, 1, 1 - y)
     bias, alog = half(dt_bias, 0, y)[None, :], half(a_log, 0, y)[None, :]
     skip = jnp.repeat(half(skip_d, 0, y), CHANNEL_WIDTH)[None, :]
     gain = half(norm_gain, 0, y)[None, :]
-
-    def along(v, step, senders):
-        pairs = [(a * 2 + b, (a + step) * 2 + b) for a in senders for b in range(2)]
-        return lax.ppermute(v, "seq", pairs)
+    got, swap, go, gate_half, bias, alog, skip, gain = tie((got, swap, go, gate_half, bias, alog, skip, gain))
 
     xs, bs, cs, scal, send, s = local_state(yv, x_in, b_proj, c_proj, dt_raw, got, bias, alog, heads)
     one = along(send, 1, range(nz - 1))
+    gate_half, _ = tie((gate_half, send))
+    got_gate = lax.ppermute(gate_half, "seq", flip)
     base = local_y(xs, bs, cs, scal, skip, heads)
-    two = along(join(send, s, one), 2, range(nz - 2))
+    one, got_gate, base, swap, go = tie((one, got_gate, base, swap, go))
+
+    joined = join(send, s, one)
+    two = along(joined, 2, range(nz - 2))
+    swap, go, _ = tie((swap, go, joined))
+    pairs = [(flat(a, b, c, 0), flat(a, 1 - b, c, 1)) for a, b, c, d in spots if d == 0]
+    pairs += [(flat(a, b, c, 1), flat(a, b, c, 0)) for a, b, c, d in spots if d == 0]
+    w0 = lax.ppermute(swap, both, pairs)
+    w1 = lax.ppermute(go, both, [(flat(a, b, c, 1), flat(a, 1 - b, c, 1)) for a, b, c, d in spots if d == 0])
     block = finish(yv, base, cs, scal, one, two, gate, got_gate, gain, heads)
 
+    table = [(0, 1, 2, 3), (1, 2, 3, 0), (2, 1, 0, 3), (3, 2, 1, 0)]
+    cross = lambda value: lax.ppermute(value, "grp", sibling)
+
+    def reduce_y(full, rounded):
+        return (full + lax.ppermute(rounded, both, across).astype(F32)).astype(BF16)
+
+    def deliver(slot, value):
+        parts = []
+        for turn in range(2):
+            pairs = [
+                (flat(a, b, c, d), flat(table[a][slot], b, a // 2, d)) for a, b, c, d in spots if c ^ turn == a // 2
+            ]
+            parts.append(lax.ppermute(value, both, pairs) if slot or turn else value)
+        return parts
+
     up1, down1 = along(block, 1, range(nz - 1)), along(block, -1, range(1, nz))
+    flip0 = cross(block)
+    up1, down1, flip0, block = tie((up1, down1, flip0, block))
     up2, down2 = along(up1, 1, range(1, nz - 1)), along(down1, -1, range(1, nz - 1))
+    slot1 = jnp.where(z < 2, down1, up1)
+    flip1 = cross(slot1)
+    up2, down2, flip1, slot1 = tie((up2, down2, flip1, slot1))
     far = jnp.where(z == 1, down2, up2)
     far = lax.ppermute(far, "seq", [(2 + b, b) for b in range(2)] + [(4 + b, 6 + b) for b in range(2)])
-    table = [(0, 1, 2, 3), (1, 2, 0, 3), (2, 1, 3, 0), (3, 2, 1, 0)]
-    slots = [
-        block,
-        jnp.where(z < 2, down1, up1),
-        jnp.where(z == 0, down2, jnp.where(z == 1, up1, jnp.where(z == 2, down1, up2))),
-        jnp.where(z == 1, down2, jnp.where(z == 2, up2, far)),
-    ]
-    total = None
-    for slot, value in enumerate(slots):
-        full, rounded = project(yv, value, w_out, got_w)
-        owner = lambda a: table[a][slot]
-        pairs = [(flat(a, b, g ^ 1), flat(a, b, g)) for a, b, g in spots if g % 2 == owner(a) % 2]
-        summed = full + lax.ppermute(rounded, both, pairs).astype(F32)
-        pairs = [(flat(a, 1 - b, g), flat(a, b, g)) for a, b, g in spots if g % 2 == owner(a) % 2]
-        r = lax.ppermute(summed[1].astype(BF16), both, pairs).astype(F32)
-        summed = summed[0] + r[::-1]
-        pairs = [(flat(a, b, g ^ 2), flat(a, b, g)) for a, b, g in spots if g == owner(a)]
-        summed = summed + lax.ppermute(summed.astype(BF16), both, pairs).astype(F32)
-        result = summed.astype(BF16)
-        if slot:
-            pairs = [(flat(a, b, g), flat(g, b, a)) for a, b, g in spots if g == owner(a)]
-            result = lax.ppermute(result, both, pairs)
-            total = total + result
-        else:
-            total = jnp.where(z == grp, result, jnp.zeros_like(result))
-    left = jnp.where(y == 0, total[0], total[1])
-    right = jnp.where(y == 0, total[1], total[0])
-    return jnp.concatenate([left, right], axis=1)
+    slot2 = jnp.where(z < 2, down2, up2)
+    flip2 = cross(slot2)
+    a0 = project(yc, block, flip0, w_out, w0, w1)
+    a1 = project(yc, slot1, flip1, w_out, w0, w1)
+    b0 = reduce_y(*a0)
+    far, flip2, a1, b0 = tie((far, flip2, a1, b0))
+    slot3 = jnp.where(z == 1, up1, jnp.where(z == 2, down1, far))
+    flip3 = cross(slot3)
+    b1 = reduce_y(*a1)
+    a2 = project(yc, slot2, flip2, w_out, w0, w1)
+    flip3, slot3, b1, a2 = tie((flip3, slot3, b1, a2))
+    b2 = reduce_y(*a2)
+    a3 = project(yc, slot3, flip3, w_out, w0, w1)
+    r0 = deliver(0, b0)
+    r0, b2, a3 = tie((r0, b2, a3))
+    b3 = reduce_y(*a3)
+    r1 = deliver(1, b1)
+    r1, b3 = tie((r1, b3))
+    results = [r0, r1, deliver(2, b2), deliver(3, b3)]
+    results = [p.astype(F32) + q.astype(F32) for p, q in results]
+    marks = []
+    for slot in range(nz):
+        mark = jnp.int32(-1)
+        for a in range(nz):
+            mark = jnp.where((z == table[a][slot]) & (grp // 2 == a // 2), a % 2, mark)
+        marks.append(mark)
+    pick = lambda which: sum(jnp.where(mark == which, r, 0.0) for mark, r in zip(marks, results)).astype(BF16)
+    at = (y ^ core).astype(jnp.int32).reshape(1)
+    return place(at, pick(core), cross(pick(1 - core)))
 
 
 def prefix(array, axis, combine, identity):

time: 213 us -> 170 us (0.80)
  the two profiles are of different devices: /device:TPU:2 before, /device:TPU:0 now
where the time goes in v2:
time: 170 us; the launch traced here: 169 us
  waiting for transfers between devices  71.1 us (42%)
  starting transfers between devices  52 us (31%)
  Pallas kernels  21.5 us (13%)
  local copies, waits for them, and re-layouts  17.4 us (10%)
  other arithmetic  6.25 us (4%)
    ppermute x6, waiting for transfers between devices, along(): return lax.ppermute(v, 'seq', pairs)  37.8 us
    ppermute x7, waiting for transfers between devices, deliver(): parts.append(lax.ppermute(value, both, pairs) if slot or turn else value)  21.9 us
    ppermute x6, starting transfers between devices, along(): return lax.ppermute(v, 'seq', pairs)  21.4 us
    ppermute x7, starting transfers between devices, deliver(): parts.append(lax.ppermute(value, both, pairs) if slot or turn else value)  18 us
    pallas_call x4, Pallas kernels, project(): pl.pallas_call(project_kernel, grid_spec=pltpu.PrefetchScalarGridSpec(num...  16.9 us
    unnamed x30, local copies, waits for them, and re-layouts  9.41 us
    dynamic_slice x4, local copies, waits for them, and re-layouts, half(): return lax.dynamic_slice_in_dim(v, which * n, n, axis)  7.17 us
    ppermute x4, waiting for transfers between devices, reduce_y(): return (full + lax.ppermute(rounded, both, across).astype(F32)).astype(BF16)  5.11 us
  transfers between devices with their start and end apart: 27, of which 12 were waited for; matrix products, arithmetic and copies ran while one was open for 7% of the time, Pallas kernels for 11%

profile of v2, /device:TPU:0, one launch (start us, length us, event | category | flops | bytes accessed | tf_op | source)
XLA Modules:
  0.0 168.7 jit_solution(1045402370316950129)
XLA Ops:
  3.6 3.0 %collective-permute-start = (bf16[128,1408]{1,0:T(8,128)(2,1)S(1)}, bf16[128,1408]{1,0:T(8,128)(2,1)S(1)}, u32[]{:S(2)}, u32[]{:S(2)}) collective-permute-start(bf16[128,1408]{1,0:T(8,128)(2,1)S(1)} %pack.1), channel_id=1, source_target_pairs={{0,4},{4,0},{8,12},{12,8},{16,20},{20,16},{24,28},{28,24},{1,5},{5... | collective-permute-start | bytes 1081352 | tf_op jit(solution)/shard_map/ppermute | solution.py:377
  9.9 4.8 %constant_dynamic-slice_fusion.1 = (bf16[1024,1024]{1,0:T(8,128)(2,1)}, bf16[1024,1024]{1,0:T(8,128)(2,1)}) fusion(bf16[2048,1024]{1,0:T(8,128)(2,1)} %w_ref.7, s32[]{:T(128)S(6)} %select_n.188, s32[]{:T(128)S(6)} %select_n.187), kind=kLoop, calls=%fused_computation.15 | loop fusion | bytes 8388616 | tf_op jit(solution)/shard_map/dynamic_slice | solution.py:367
  15.2 1.4 local_state.1
  16.6 3.7 %collective-permute-start.1 = (bf16[144,1024]{1,0:T(8,128)(2,1)S(1)}, bf16[144,1024]{1,0:T(8,128)(2,1)S(1)}, u32[]{:S(2)}, u32[]{:S(2)}) collective-permute-start(bf16[144,1024]{1,0:T(8,128)(2,1)S(1)} %get-tuple-element.64.send_ref), channel_id=1, source_target_pairs={{0,8},{4,12},{8,16},{12,20},{16,24},{20,28},{1,9},{5,13},{9,17},{1... | collective-permute-start | bytes 884744 | tf_op jit(solution)/shard_map/ppermute | solution.py:375
  20.3 1.6 collective-permute-start.2
  23.0 4.3 %collective-permute-done.2.refs_7_ = bf16[128,1024]{1,0:T(8,128)(2,1)S(1)} collective-permute-done((bf16[128,1024]{1,0:T(8,128)(2,1)S(1)}, bf16[128,1024]{1,0:T(8,128)(2,1)S(1)}, u32[]{:S(2)}, u32[]{:S(2)}) %collective-permute-start.2) | collective-permute-done | bytes 262176 | tf_op jit(solution)/shard_map/ppermute | solution.py:388
  27.4 2.0 %collective-permute-start.13 = (bf16[1024,1024]{1,0:T(8,128)(2,1)}, bf16[1024,1024]{1,0:T(8,128)(2,1)}, u32[]{:S(2)}, u32[]{:S(2)}) collective-permute-start(bf16[1024,1024]{1,0:T(8,128)(2,1)} %get-tuple-element.88), channel_id=1, source_target_pairs={{1,5},{3,7},{5,1},{7,3},{9,13},{11,15},{13,9},{15,11},{17,21},{19,... | collective-permute-start | bytes 6291464 | tf_op jit(solution)/shard_map/ppermute | solution.py:398
  29.4 4.5 %collective-permute-start.3 = (bf16[128,1024]{1,0:T(8,128)(2,1)S(1)}, bf16[128,1024]{1,0:T(8,128)(2,1)S(1)}, u32[]{:S(2)}, u32[]{:S(2)}) collective-permute-start(bf16[128,1024]{1,0:T(8,128)(2,1)S(1)} %join.1), channel_id=1, source_target_pairs={{0,16},{4,20},{8,24},{12,28},{1,17},{5,21},{9,25},{13,29},{2,18},{... | collective-permute-start | bytes 786440 | tf_op jit(solution)/shard_map/ppermute | solution.py:375
  33.9 6.1 %collective-permute-done.3.refs_5_ = bf16[128,1024]{1,0:T(8,128)(2,1)S(1)} collective-permute-done((bf16[128,1024]{1,0:T(8,128)(2,1)S(1)}, bf16[128,1024]{1,0:T(8,128)(2,1)S(1)}, u32[]{:S(2)}, u32[]{:S(2)}) %collective-permute-start.3) | collective-permute-done | bytes 262176 | tf_op jit(solution)/shard_map/ppermute | solution.py:375
  41.0 9.2 %collective-permute-start.4 = (bf16[256,1024]{1,0:T(8,128)(2,1)S(1)}, bf16[256,1024]{1,0:T(8,128)(2,1)}, u32[]{:S(2)}, u32[]{:S(2)}) collective-permute-start(bf16[256,1024]{1,0:T(8,128)(2,1)S(1)} %finish.1.own_ref), channel_id=1, source_target_pairs={{0,8},{4,12},{8,16},{12,20},{16,24},{20,28},{1,9},{5,13},{9,17},{1... | collective-permute-start | bytes 1572872 | tf_op jit(solution)/shard_map/ppermute | solution.py:375
  52.0 9.4 %collective-permute-done.4 = bf16[256,1024]{1,0:T(8,128)(2,1)} collective-permute-done((bf16[256,1024]{1,0:T(8,128)(2,1)S(1)}, bf16[256,1024]{1,0:T(8,128)(2,1)}, u32[]{:S(2)}, u32[]{:S(2)}) %collective-permute-start.4) | collective-permute-done | bytes 524320 | tf_op jit(solution)/shard_map/ppermute | solution.py:375
  61.4 5.0 %collective-permute-done.5 = bf16[256,1024]{1,0:T(8,128)(2,1)} collective-permute-done((bf16[256,1024]{1,0:T(8,128)(2,1)S(1)}, bf16[256,1024]{1,0:T(8,128)(2,1)}, u32[]{:S(2)}, u32[]{:S(2)}) %collective-permute-start.5) | collective-permute-done | bytes 524320 | tf_op jit(solution)/shard_map/ppermute | solution.py:375
  68.4 1.5 collective-permute-start.7
  71.2 17.3 %collective-permute-done.8 = bf16[256,1024]{1,0:T(8,128)(2,1)} collective-permute-done((bf16[256,1024]{1,0:T(8,128)(2,1)}, bf16[256,1024]{1,0:T(8,128)(2,1)}, u32[]{:S(2)}, u32[]{:S(2)}) %collective-permute-start.8) | collective-permute-done | bytes 524320 | tf_op jit(solution)/shard_map/ppermute | solution.py:375
  88.5 2.3 %broadcast_select_fusion = (bf16[256,1024]{1,0:T(8,128)(2,1)}, bf16[256,1024]{1,0:T(8,128)(2,1)}) fusion(bf16[256,1024]{1,0:T(8,128)(2,1)} %collective-permute-done.8, bf16[256,1024]{1,0:T(8,128)(2,1)} %collective-permute-done.7, pred[]{:T(512)S(6)} %lt.37, pred[]{:T(512)S(6)} %eq.35), kind=kLoop, calls=%fused_computation.11 | loop fusion | flops 524288 | bytes 2097154 | tf_op jit(solution)/shard_map/jit(_where)/select_n | solution.py:425
  92.2 2.2 %copy-done = bf16[2048,1024]{1,0:T(8,128)(2,1)S(1)} copy-done((bf16[2048,1024]{1,0:T(8,128)(2,1)S(1)}, bf16[2048,1024]{1,0:T(8,128)(2,1)}, u32[]{:S(2)}) %copy-start) | copy-done | bytes 4194328
  94.4 4.1 %project.5 = (f32[128,1024]{1,0:T(8,128)S(1)}, bf16[128,1024]{1,0:T(8,128)(2,1)S(1)}) custom-call(s32[2]{0:T(128)S(1)} %pad_add_fusion.yc_ref, bf16[256,1024]{1,0:T(8,128)(2,1)S(1)} %finish.1.own_ref, bf16[256,1024]{1,0:T(8,128)(2,1)S(1)} %copy-done.6, bf16[2048,1024]{1,0:T(8,128)(2,1)S(1)} %copy-done, ...), custom_call_target="tpu_custom_call" | custom-call | flops 1 | bytes 1 | tf_op jit(solution)/shard_map/project/pallas_call | solution.py:300
  99.3 1.6 collective-permute-start.14
  101.0 2.2 %copy-done.1 = bf16[2048,1024]{1,0:T(8,128)(2,1)S(1)} copy-done((bf16[2048,1024]{1,0:T(8,128)(2,1)S(1)}, bf16[2048,1024]{1,0:T(8,128)(2,1)}, u32[]{:S(2)}) %copy-start.1) | copy-done | bytes 4194328
  103.1 4.3 %project.4 = (f32[128,1024]{1,0:T(8,128)S(1)}, bf16[128,1024]{1,0:T(8,128)(2,1)S(1)}) custom-call(s32[2]{0:T(128)S(1)} %pad_add_fusion.yc_ref, bf16[256,1024]{1,0:T(8,128)(2,1)S(1)} %broadcast_select_fusion.1.own_ref, bf16[256,1024]{1,0:T(8,128)(2,1)} %collective-permute-done.9.got_ref, bf16[2048,1024]{1,0:T(8,128)(2,1)S(1)} %copy-done.1, ...), custom_call_target="tpu_custom_call" | custom-call | flops 1 | bytes 1 | tf_op jit(solution)/shard_map/project/pallas_call | solution.py:300
  110.9 4.5 %project.6 = (f32[128,1024]{1,0:T(8,128)S(1)}, bf16[128,1024]{1,0:T(8,128)(2,1)S(1)}) custom-call(s32[2]{0:T(128)S(1)} %pad_add_fusion.yc_ref, bf16[256,1024]{1,0:T(8,128)(2,1)} %get-tuple-element.121.own_ref, bf16[256,1024]{1,0:T(8,128)(2,1)} %collective-permute-done.11.got_ref, bf16[2048,1024]{1,0:T(8,128)(2,1)S(1)} %copy-done.1, ...), custom_call_target="tpu_custom_call" | custom-call | flops 1 | bytes 1 | tf_op jit(solution)/shard_map/project/pallas_call | solution.py:300
  115.3 3.1 %collective-permute-done.17 = bf16[128,1024]{1,0:T(8,128)(2,1)S(1)} collective-permute-done((bf16[128,1024]{1,0:T(8,128)(2,1)S(1)}, bf16[128,1024]{1,0:T(8,128)(2,1)S(1)}, u32[]{:S(2)}, u32[]{:S(2)}) %collective-permute-start.17) | collective-permute-done | bytes 262176 | tf_op jit(solution)/shard_map/ppermute | solution.py:405
  120.7 4.1 %project.7 = (f32[128,1024]{1,0:T(8,128)S(1)}, bf16[128,1024]{1,0:T(8,128)(2,1)S(1)}) custom-call(s32[2]{0:T(128)S(1)} %pad_add_fusion.yc_ref, bf16[256,1024]{1,0:T(8,128)(2,1)S(1)} %select_select_fusion.own_ref, bf16[256,1024]{1,0:T(8,128)(2,1)S(1)} %collective-permute-done.16.got_ref, bf16[2048,1024]{1,0:T(8,128)(2,1)S(1)} %copy-done.1, ...), custom_call_target="tpu_custom_call" | custom-call | flops 1 | bytes 1 | tf_op jit(solution)/shard_map/project/pallas_call | solution.py:300
  124.8 2.1 %collective-permute-done.18 = bf16[128,1024]{1,0:T(8,128)(2,1)S(1)} collective-permute-done((bf16[128,1024]{1,0:T(8,128)(2,1)S(1)}, bf16[128,1024]{1,0:T(8,128)(2,1)S(1)}, u32[]{:S(2)}, u32[]{:S(2)}) %collective-permute-start.18) | collective-permute-done | bytes 262176 | tf_op jit(solution)/shard_map/ppermute | solution.py:405
  126.9 3.0 %collective-permute-done.15 = bf16[128,1024]{1,0:T(8,128)(2,1)S(1)} collective-permute-done((bf16[128,1024]{1,0:T(8,128)(2,1)S(1)}, bf16[128,1024]{1,0:T(8,128)(2,1)S(1)}, u32[]{:S(2)}, u32[]{:S(2)}) %collective-permute-start.15) | collective-permute-done | bytes 262176 | tf_op jit(solution)/shard_map/ppermute | solution.py:413
  129.9 5.4 %collective-permute-start.19 = (bf16[128,1024]{1,0:T(8,128)(2,1)S(1)}, bf16[128,1024]{1,0:T(8,128)(2,1)S(1)}, u32[]{:S(2)}, u32[]{:S(2)}) collective-permute-start(bf16[128,1024]{1,0:T(8,128)(2,1)S(1)} %add_convert_fusion.4), channel_id=1, source_target_pairs={{0,8},{1,9},{4,12},{5,13},{8,16},{9,17},{12,20},{13,21},{18,10},{1... | collective-permute-start | bytes 786440 | tf_op jit(solution)/shard_map/ppermute | solution.py:413
  136.1 3.0 %collective-permute-start.22 = (bf16[128,1024]{1,0:T(8,128)(2,1)S(1)}, bf16[128,1024]{1,0:T(8,128)(2,1)S(1)}, u32[]{:S(2)}, u32[]{:S(2)}) collective-permute-start(bf16[128,1024]{1,0:T(8,128)(2,1)S(1)} %add_convert_fusion.3), channel_id=1, source_target_pairs={{0,16},{1,17},{4,20},{5,21},{8,24},{9,25},{12,28},{13,29},{18,2},{... | collective-permute-start | bytes 786440 | tf_op jit(solution)/shard_map/ppermute | solution.py:413
  139.8 2.2 %collective-permute-done.19 = bf16[128,1024]{1,0:T(8,128)(2,1)S(1)} collective-permute-done((bf16[128,1024]{1,0:T(8,128)(2,1)S(1)}, bf16[128,1024]{1,0:T(8,128)(2,1)S(1)}, u32[]{:S(2)}, u32[]{:S(2)}) %collective-permute-start.19) | collective-permute-done | bytes 262176 | tf_op jit(solution)/shard_map/ppermute | solution.py:413
  142.0 5.7 %collective-permute-start.24 = (bf16[128,1024]{1,0:T(8,128)(2,1)S(1)}, bf16[128,1024]{1,0:T(8,128)(2,1)S(1)}, u32[]{:S(2)}, u32[]{:S(2)}) collective-permute-start(bf16[128,1024]{1,0:T(8,128)(2,1)S(1)} %add_convert_fusion.2), channel_id=1, source_target_pairs={{0,24},{1,25},{4,28},{5,29},{8,0},{9,1},{12,4},{13,5},{18,26},{19,... | collective-permute-start | bytes 786440 | tf_op jit(solution)/shard_map/ppermute | solution.py:413
  147.8 1.3 collective-permute-start.25
  149.2 16.6 %collective-permute-done.24 = bf16[128,1024]{1,0:T(8,128)(2,1)S(1)} collective-permute-done((bf16[128,1024]{1,0:T(8,128)(2,1)S(1)}, bf16[128,1024]{1,0:T(8,128)(2,1)S(1)}, u32[]{:S(2)}, u32[]{:S(2)}) %collective-permute-start.24) | collective-permute-done | bytes 262176 | tf_op jit(solution)/shard_map/ppermute | solution.py:413
  166.4 1.5 collective-permute-done.26.got_ref
  (77 shorter events, 25.3 us)
Async XLA Ops:
  3.6 11.4 %collective-permute-start = (bf16[128,1408]{1,0:T(8,128)(2,1)S(1)}, bf16[128,1408]{1,0:T(8,128)(2,1)S(1)}, u32[]{:S(2)}, u32[]{:S(2)}) collective-permute-start(bf16[128,1408]{1,0:T(8,128)(2,1)S(1)} %pack.1), channel_id=1, source_target_pairs={{0,4},{4,0},{8,12},{12,8},{16,20},{20,16},{24,28},{28,24},{1,5},{5... | collective-permute-start | bytes 1081352 | tf_op jit(solution)/shard_map/ppermute | solution.py:377
  9.8 5.4 %copy-start.3 = (bf16[128,2048]{1,0:T(8,128)(2,1)S(1)}, bf16[128,2048]{1,0:T(8,128)(2,1)}, u32[]{:S(2)}) copy-start(bf16[128,2048]{1,0:T(8,128)(2,1)} %refs_1_.3) | copy-start | bytes 1572868
  9.8 5.3 %copy-start.10 = (bf16[128,256]{1,0:T(8,128)(2,1)S(1)}, bf16[128,256]{1,0:T(8,128)(2,1)}, u32[]{:S(2)}) copy-start(bf16[128,256]{1,0:T(8,128)(2,1)} %refs_2_.3) | copy-start | bytes 196612
  9.8 5.3 %copy-start.12 = (bf16[128,256]{1,0:T(8,128)(2,1)S(1)}, bf16[128,256]{1,0:T(8,128)(2,1)}, u32[]{:S(2)}) copy-start(bf16[128,256]{1,0:T(8,128)(2,1)} %refs_3_.3) | copy-start | bytes 196612
  15.2 24.8 %copy-start.4 = (bf16[128,2048]{1,0:T(8,128)(2,1)S(1)}, bf16[128,2048]{1,0:T(8,128)(2,1)}, u32[]{:S(2)}) copy-start(bf16[128,2048]{1,0:T(8,128)(2,1)} %refs_6_.1) | copy-start | bytes 1572868
  16.6 10.7 %collective-permute-start.1 = (bf16[144,1024]{1,0:T(8,128)(2,1)S(1)}, bf16[144,1024]{1,0:T(8,128)(2,1)S(1)}, u32[]{:S(2)}, u32[]{:S(2)}) collective-permute-start(bf16[144,1024]{1,0:T(8,128)(2,1)S(1)} %get-tuple-element.64.send_ref), channel_id=1, source_target_pairs={{0,8},{4,12},{8,16},{12,20},{16,24},{20,28},{1,9},{5,13},{9,17},{1... | collective-permute-start | bytes 884744 | tf_op jit(solution)/shard_map/ppermute | solution.py:375
  20.3 7.0 %collective-permute-start.2 = (bf16[128,1024]{1,0:T(8,128)(2,1)S(1)}, bf16[128,1024]{1,0:T(8,128)(2,1)S(1)}, u32[]{:S(2)}, u32[]{:S(2)}) collective-permute-start(bf16[128,1024]{1,0:T(8,128)(2,1)S(1)} %constant_dynamic-slice_fusion), channel_id=1, source_target_pairs={{0,4},{4,0},{8,12},{12,8},{16,20},{20,16},{24,28},{28,24},{1,5},{5... | collective-permute-start | bytes 786440 | tf_op jit(solution)/shard_map/ppermute | solution.py:388
  27.3 64.9 %collective-permute-start.12 = (bf16[1024,1024]{1,0:T(8,128)(2,1)}, bf16[1024,1024]{1,0:T(8,128)(2,1)S(1)}, u32[]{:S(2)}, u32[]{:S(2)}) collective-permute-start(bf16[1024,1024]{1,0:T(8,128)(2,1)} %get-tuple-element.87), channel_id=1, source_target_pairs={{0,5},{2,7},{4,1},{6,3},{8,13},{10,15},{12,9},{14,11},{16,21},{18,... | collective-permute-start | bytes 6291464 | tf_op jit(solution)/shard_map/ppermute | solution.py:397
  27.4 64.8 %collective-permute-start.13 = (bf16[1024,1024]{1,0:T(8,128)(2,1)}, bf16[1024,1024]{1,0:T(8,128)(2,1)}, u32[]{:S(2)}, u32[]{:S(2)}) collective-permute-start(bf16[1024,1024]{1,0:T(8,128)(2,1)} %get-tuple-element.88), channel_id=1, source_target_pairs={{1,5},{3,7},{5,1},{7,3},{9,13},{11,15},{13,9},{15,11},{17,21},{19,... | collective-permute-start | bytes 6291464 | tf_op jit(solution)/shard_map/ppermute | solution.py:398
  29.4 10.6 %collective-permute-start.3 = (bf16[128,1024]{1,0:T(8,128)(2,1)S(1)}, bf16[128,1024]{1,0:T(8,128)(2,1)S(1)}, u32[]{:S(2)}, u32[]{:S(2)}) collective-permute-start(bf16[128,1024]{1,0:T(8,128)(2,1)S(1)} %join.1), channel_id=1, source_target_pairs={{0,16},{4,20},{8,24},{12,28},{1,17},{5,21},{9,25},{13,29},{2,18},{... | collective-permute-start | bytes 786440 | tf_op jit(solution)/shard_map/ppermute | solution.py:375
  41.0 20.4 %collective-permute-start.4 = (bf16[256,1024]{1,0:T(8,128)(2,1)S(1)}, bf16[256,1024]{1,0:T(8,128)(2,1)}, u32[]{:S(2)}, u32[]{:S(2)}) collective-permute-start(bf16[256,1024]{1,0:T(8,128)(2,1)S(1)} %finish.1.own_ref), channel_id=1, source_target_pairs={{0,8},{4,12},{8,16},{12,20},{16,24},{20,28},{1,9},{5,13},{9,17},{1... | collective-permute-start | bytes 1572872 | tf_op jit(solution)/shard_map/ppermute | solution.py:375
  50.2 16.3 %collective-permute-start.5 = (bf16[256,1024]{1,0:T(8,128)(2,1)S(1)}, bf16[256,1024]{1,0:T(8,128)(2,1)}, u32[]{:S(2)}, u32[]{:S(2)}) collective-permute-start(bf16[256,1024]{1,0:T(8,128)(2,1)S(1)} %finish.1.own_ref), channel_id=1, source_target_pairs={{8,0},{12,4},{16,8},{20,12},{24,16},{28,20},{9,1},{13,5},{17,9},{2... | collective-permute-start | bytes 1572872 | tf_op jit(solution)/shard_map/ppermute | solution.py:375
  51.4 15.0 %collective-permute-start.6 = (bf16[256,1024]{1,0:T(8,128)(2,1)S(1)}, bf16[256,1024]{1,0:T(8,128)(2,1)S(1)}, u32[]{:S(2)}, u32[]{:S(2)}) collective-permute-start(bf16[256,1024]{1,0:T(8,128)(2,1)S(1)} %finish.1.own_ref), channel_id=1, source_target_pairs={{0,1},{1,0},{2,3},{3,2},{4,5},{5,4},{6,7},{7,6},{8,9},{9,8},{10,11... | collective-permute-start | bytes 1572872 | tf_op jit(solution)/shard_map/ppermute | solution.py:402
  68.3 2.9 %collective-permute-start.9 = (bf16[256,1024]{1,0:T(8,128)(2,1)S(1)}, bf16[256,1024]{1,0:T(8,128)(2,1)}, u32[]{:S(2)}, u32[]{:S(2)}) collective-permute-start(bf16[256,1024]{1,0:T(8,128)(2,1)S(1)} %broadcast_select_fusion.1.own_ref), channel_id=1, source_target_pairs={{0,1},{1,0},{2,3},{3,2},{4,5},{5,4},{6,7},{7,6},{8,9},{9,8},{10,11... | collective-permute-start | bytes 1572872 | tf_op jit(solution)/shard_map/ppermute | solution.py:402
  68.4 2.8 %collective-permute-start.7 = (bf16[256,1024]{1,0:T(8,128)(2,1)}, bf16[256,1024]{1,0:T(8,128)(2,1)}, u32[]{:S(2)}, u32[]{:S(2)}) collective-permute-start(bf16[256,1024]{1,0:T(8,128)(2,1)} %collective-permute-done.4), channel_id=1, source_target_pairs={{8,16},{12,20},{16,24},{20,28},{9,17},{13,21},{17,25},{21,29},{10,... | collective-permute-start | bytes 1572872 | tf_op jit(solution)/shard_map/ppermute | solution.py:375
  69.9 18.6 %collective-permute-start.8 = (bf16[256,1024]{1,0:T(8,128)(2,1)}, bf16[256,1024]{1,0:T(8,128)(2,1)}, u32[]{:S(2)}, u32[]{:S(2)}) collective-permute-start(bf16[256,1024]{1,0:T(8,128)(2,1)} %collective-permute-done.5), channel_id=1, source_target_pairs={{8,0},{12,4},{16,8},{20,12},{9,1},{13,5},{17,9},{21,13},{10,2},{14... | collective-permute-start | bytes 1572872 | tf_op jit(solution)/shard_map/ppermute | solution.py:375
  71.2 21.1 %copy-start.6 = (bf16[256,1024]{1,0:T(8,128)(2,1)S(1)}, bf16[256,1024]{1,0:T(8,128)(2,1)}, u32[]{:S(2)}) copy-start(bf16[256,1024]{1,0:T(8,128)(2,1)} %copy-done.5) | copy-start | bytes 1572868
  90.8 17.7 %collective-permute-start.10 = (bf16[256,1024]{1,0:T(8,128)(2,1)}, bf16[256,1024]{1,0:T(8,128)(2,1)}, u32[]{:S(2)}, u32[]{:S(2)}) collective-permute-start(bf16[256,1024]{1,0:T(8,128)(2,1)} %get-tuple-element.122), channel_id=1, source_target_pairs={{8,0},{12,4},{16,24},{20,28},{9,1},{13,5},{17,25},{21,29},{10,2},{... | collective-permute-start | bytes 1572872 | tf_op jit(solution)/shard_map/ppermute | solution.py:424
  92.1 16.4 %collective-permute-start.11 = (bf16[256,1024]{1,0:T(8,128)(2,1)}, bf16[256,1024]{1,0:T(8,128)(2,1)}, u32[]{:S(2)}, u32[]{:S(2)}) collective-permute-start(bf16[256,1024]{1,0:T(8,128)(2,1)} %get-tuple-element.121.own_ref), channel_id=1, source_target_pairs={{0,1},{1,0},{2,3},{3,2},{4,5},{5,4},{6,7},{7,6},{8,9},{9,8},{10,11... | collective-permute-start | bytes 1572872 | tf_op jit(solution)/shard_map/ppermute | solution.py:402
  99.3 8.1 %collective-permute-start.14 = (bf16[128,1024]{1,0:T(8,128)(2,1)S(1)}, bf16[128,1024]{1,0:T(8,128)(2,1)}, u32[]{:S(2)}, u32[]{:S(2)}) collective-permute-start(bf16[128,1024]{1,0:T(8,128)(2,1)S(1)} %get-tuple-element.94), channel_id=1, source_target_pairs={{0,5},{1,4},{2,7},{3,6},{4,1},{5,0},{6,3},{7,2},{8,13},{9,12},{10,... | collective-permute-start | bytes 786440 | tf_op jit(solution)/shard_map/ppermute | solution.py:405
  109.6 8.8 %collective-permute-start.16 = (bf16[256,1024]{1,0:T(8,128)(2,1)S(1)}, bf16[256,1024]{1,0:T(8,128)(2,1)S(1)}, u32[]{:S(2)}, u32[]{:S(2)}) collective-permute-start(bf16[256,1024]{1,0:T(8,128)(2,1)S(1)} %select_select_fusion.own_ref), channel_id=1, source_target_pairs={{0,1},{1,0},{2,3},{3,2},{4,5},{5,4},{6,7},{7,6},{8,9},{9,8},{10,11... | collective-permute-start | bytes 1572872 | tf_op jit(solution)/shard_map/ppermute | solution.py:402
  110.1 8.3 %collective-permute-start.17 = (bf16[128,1024]{1,0:T(8,128)(2,1)S(1)}, bf16[128,1024]{1,0:T(8,128)(2,1)S(1)}, u32[]{:S(2)}, u32[]{:S(2)}) collective-permute-start(bf16[128,1024]{1,0:T(8,128)(2,1)S(1)} %get-tuple-element.98), channel_id=1, source_target_pairs={{0,5},{1,4},{2,7},{3,6},{4,1},{5,0},{6,3},{7,2},{8,13},{9,12},{10,... | collective-permute-start | bytes 786440 | tf_op jit(solution)/shard_map/ppermute | solution.py:405
  118.5 8.4 %collective-permute-start.18 = (bf16[128,1024]{1,0:T(8,128)(2,1)S(1)}, bf16[128,1024]{1,0:T(8,128)(2,1)S(1)}, u32[]{:S(2)}, u32[]{:S(2)}) collective-permute-start(bf16[128,1024]{1,0:T(8,128)(2,1)S(1)} %get-tuple-element.103), channel_id=1, source_target_pairs={{0,5},{1,4},{2,7},{3,6},{4,1},{5,0},{6,3},{7,2},{8,13},{9,12},{10,... | collective-permute-start | bytes 786440 | tf_op jit(solution)/shard_map/ppermute | solution.py:405
  119.4 10.5 %collective-permute-start.15 = (bf16[128,1024]{1,0:T(8,128)(2,1)S(1)}, bf16[128,1024]{1,0:T(8,128)(2,1)S(1)}, u32[]{:S(2)}, u32[]{:S(2)}) collective-permute-start(bf16[128,1024]{1,0:T(8,128)(2,1)S(1)} %add_convert_fusion.5), channel_id=1, source_target_pairs={{2,0},{3,1},{6,4},{7,5},{10,8},{11,9},{14,12},{15,13},{16,18},{17,... | collective-permute-start | bytes 786440 | tf_op jit(solution)/shard_map/ppermute | solution.py:413
  129.9 9.8 %collective-permute-start.21 = (bf16[128,1024]{1,0:T(8,128)(2,1)S(1)}, bf16[128,1024]{1,0:T(8,128)(2,1)S(1)}, u32[]{:S(2)}, u32[]{:S(2)}) collective-permute-start(bf16[128,1024]{1,0:T(8,128)(2,1)S(1)} %get-tuple-element.112), channel_id=1, source_target_pairs={{0,5},{1,4},{2,7},{3,6},{4,1},{5,0},{6,3},{7,2},{8,13},{9,12},{10,... | collective-permute-start | bytes 786440 | tf_op jit(solution)/shard_map/ppermute | solution.py:405
  129.9 12.1 %collective-permute-start.19 = (bf16[128,1024]{1,0:T(8,128)(2,1)S(1)}, bf16[128,1024]{1,0:T(8,128)(2,1)S(1)}, u32[]{:S(2)}, u32[]{:S(2)}) collective-permute-start(bf16[128,1024]{1,0:T(8,128)(2,1)S(1)} %add_convert_fusion.4), channel_id=1, source_target_pairs={{0,8},{1,9},{4,12},{5,13},{8,16},{9,17},{12,20},{13,21},{18,10},{1... | collective-permute-start | bytes 786440 | tf_op jit(solution)/shard_map/ppermute | solution.py:413
  135.4 6.7 %collective-permute-start.20 = (bf16[128,1024]{1,0:T(8,128)(2,1)S(1)}, bf16[128,1024]{1,0:T(8,128)(2,1)S(1)}, u32[]{:S(2)}, u32[]{:S(2)}) collective-permute-start(bf16[128,1024]{1,0:T(8,128)(2,1)S(1)} %add_convert_fusion.4), channel_id=1, source_target_pairs={{2,8},{3,9},{6,12},{7,13},{10,16},{11,17},{14,20},{15,21},{16,10},... | collective-permute-start | bytes 786440 | tf_op jit(solution)/shard_map/ppermute | solution.py:413
  136.1 13.1 %collective-permute-start.22 = (bf16[128,1024]{1,0:T(8,128)(2,1)S(1)}, bf16[128,1024]{1,0:T(8,128)(2,1)S(1)}, u32[]{:S(2)}, u32[]{:S(2)}) collective-permute-start(bf16[128,1024]{1,0:T(8,128)(2,1)S(1)} %add_convert_fusion.3), channel_id=1, source_target_pairs={{0,16},{1,17},{4,20},{5,21},{8,24},{9,25},{12,28},{13,29},{18,2},{... | collective-permute-start | bytes 786440 | tf_op jit(solution)/shard_map/ppermute | solution.py:413
  139.0 10.1 %collective-permute-start.23 = (bf16[128,1024]{1,0:T(8,128)(2,1)S(1)}, bf16[128,1024]{1,0:T(8,128)(2,1)S(1)}, u32[]{:S(2)}, u32[]{:S(2)}) collective-permute-start(bf16[128,1024]{1,0:T(8,128)(2,1)S(1)} %add_convert_fusion.3), channel_id=1, source_target_pairs={{2,16},{3,17},{6,20},{7,21},{10,24},{11,25},{14,28},{15,29},{16,2}... | collective-permute-start | bytes 786440 | tf_op jit(solution)/shard_map/ppermute | solution.py:413
  142.0 23.8 %collective-permute-start.24 = (bf16[128,1024]{1,0:T(8,128)(2,1)S(1)}, bf16[128,1024]{1,0:T(8,128)(2,1)S(1)}, u32[]{:S(2)}, u32[]{:S(2)}) collective-permute-start(bf16[128,1024]{1,0:T(8,128)(2,1)S(1)} %add_convert_fusion.2), channel_id=1, source_target_pairs={{0,24},{1,25},{4,28},{5,29},{8,0},{9,1},{12,4},{13,5},{18,26},{19,... | collective-permute-start | bytes 786440 | tf_op jit(solution)/shard_map/ppermute | solution.py:413
  147.8 18.1 %collective-permute-start.25 = (bf16[128,1024]{1,0:T(8,128)(2,1)S(1)}, bf16[128,1024]{1,0:T(8,128)(2,1)S(1)}, u32[]{:S(2)}, u32[]{:S(2)}) collective-permute-start(bf16[128,1024]{1,0:T(8,128)(2,1)S(1)} %add_convert_fusion.2), channel_id=1, source_target_pairs={{2,24},{3,25},{6,28},{7,29},{10,0},{11,1},{14,4},{15,5},{16,26},{1... | collective-permute-start | bytes 786440 | tf_op jit(solution)/shard_map/ppermute | solution.py:413
  166.3 1.6 collective-permute-start.26
  (10 other events, 19.0 us)

commit v3 on v2

--- a/solution.py
+++ b/solution.py
@@ -19,9 +19,9 @@
 VMEM_LIMIT = 24 * 2**20
 
 
-def params(grid_dims=0):
+def params(grid_dims=0, limit=VMEM_LIMIT):
     return pltpu.CompilerParams(
-        vmem_limit_bytes=VMEM_LIMIT,
+        vmem_limit_bytes=limit,
         dimension_semantics=("arbitrary",) * grid_dims if grid_dims else None,
     )
 
@@ -79,7 +79,7 @@
             out_specs=pl.BlockSpec((tokens, full), lambda i, y: (0, 0)),
         ),
         out_shape=jax.ShapeDtypeStruct((tokens, full), BF16),
-        compiler_params=params(1),
+        compiler_params=params(1, 60 * 2**20),
         cost_estimate=cost(1e6, 4 * tokens * full),
         name="pack",
     )(y, x, b, c, dt)
@@ -226,11 +226,13 @@
     y = y_ref[0]
     decay = jnp.sum(one_ref[state:, :].astype(F32), axis=0, keepdims=True)
     start = one_ref[:state, :].astype(F32) + decay * two_ref[...].astype(F32)
-    hi = start.astype(BF16)
+    top = start.astype(BF16)
+    low = (start - top.astype(F32)).astype(BF16)
     grow = jnp.exp(scal_ref[:, :heads])
     for k in range(2):
         at = pl.ds(k * tokens, tokens)
-        carried = jnp.dot(cs_ref[at, :], hi, preferred_element_type=F32)
+        carried = jnp.dot(cs_ref[at, :], top, preferred_element_type=F32)
+        carried = carried + jnp.dot(cs_ref[at, :], low, preferred_element_type=F32)
         value = local_ref[at, :] + carried * spread(grow[k * tokens : (k + 1) * tokens, :], CHANNEL_WIDTH)
         gate = jnp.where(y == k, gate_ref[...], got_ref[...]).astype(F32)
         value = value * (gate / (1.0 + jnp.exp(-gate)))
@@ -265,24 +267,28 @@
     )(y, local, cs, scal, one, two, gate, got, gain)
 
 
-def project_kernel(yc_ref, own_ref, got_ref, w_ref, w0_ref, w1_ref, keep_ref, send_ref, both_ref):
-    tokens, depth = keep_ref.shape[0], own_ref.shape[1]
+def project_kernel(yc_ref, *refs):
+    *pair_refs, w_ref, w0_ref, w1_ref, keep_ref, send_ref, both_ref = refs
+    slots, depth = len(pair_refs) // 2, pair_refs[0].shape[1]
+    kept = keep_ref.shape[0]
+    tokens = kept // slots
     y, core = yc_ref[0], yc_ref[1]
 
     @pl.when(pl.program_id(0) == 0)
     def _():
-        for k in range(2):
-            at = pl.multiple_of(jnp.where(y == 0, k, 1 - k) * tokens, tokens)
-            rows = pl.ds(k * tokens, tokens)
-            own, got = own_ref[pl.ds(at, tokens), :], got_ref[pl.ds(at, tokens), :]
-            both_ref[rows, :depth] = jnp.where(core == 0, own, got)
-            both_ref[rows, depth:] = jnp.where(core == 0, got, own)
+        for slot in range(slots):
+            own_ref, got_ref = pair_refs[2 * slot], pair_refs[2 * slot + 1]
+            for k in range(2):
+                at = pl.ds(pl.multiple_of(jnp.where(y == 0, k, 1 - k) * tokens, tokens), tokens)
+                rows = pl.ds(k * kept + slot * tokens, tokens)
+                both_ref[rows, :depth] = jnp.where(core == 0, own_ref[at, :], got_ref[at, :])
+                both_ref[rows, depth:] = jnp.where(core == 0, got_ref[at, :], own_ref[at, :])
 
     def multiply(first, second):
         part = jnp.dot(both_ref[:, :depth], first[...], preferred_element_type=F32)
         part = part + jnp.dot(both_ref[:, depth:], second[...], preferred_element_type=F32)
-        keep_ref[...] = part[:tokens, :]
-        send_ref[...] = part[tokens:, :].astype(BF16)
+        keep_ref[...] = part[:kept, :]
+        send_ref[...] = part[kept:, :].astype(BF16)
 
     @pl.when(core == 0)
     def _():
@@ -293,8 +299,9 @@
         multiply(w0_ref, w1_ref)
 
 
-def project(yc, own, got, w, w0, w1):
-    tokens, depth = own.shape[0] // 2, own.shape[1]
+def project(yc, pairs, w, w0, w1):
+    length, depth = pairs[0][0].shape
+    kept = len(pairs) * length // 2
     cols = w.shape[1]
     tile = min(cols, 256)
     return pl.pallas_call(
@@ -302,24 +309,23 @@
         grid_spec=pltpu.PrefetchScalarGridSpec(
             num_scalar_prefetch=1,
             grid=(cols // tile,),
-            in_specs=[
-                pl.BlockSpec(own.shape, lambda i, yc: (0, 0)),
-                pl.BlockSpec(own.shape, lambda i, yc: (0, 0)),
+            in_specs=[pl.BlockSpec((length, depth), lambda i, yc: (0, 0))] * (2 * len(pairs))
+            + [
                 pl.BlockSpec((depth, tile), lambda i, yc: (yc[0], jnp.where(yc[1] == 0, i, 0))),
                 pl.BlockSpec((depth, tile), lambda i, yc: (0, i)),
                 pl.BlockSpec((depth, tile), lambda i, yc: (0, jnp.where(yc[1] == 1, i, 0))),
             ],
             out_specs=[
-                pl.BlockSpec((tokens, tile), lambda i, yc: (0, i)),
-                pl.BlockSpec((tokens, tile), lambda i, yc: (0, i)),
+                pl.BlockSpec((kept, tile), lambda i, yc: (0, i)),
+                pl.BlockSpec((kept, tile), lambda i, yc: (0, i)),
             ],
-            scratch_shapes=[pltpu.VMEM((2 * tokens, 2 * depth), BF16)],
+            scratch_shapes=[pltpu.VMEM((2 * kept, 2 * depth), BF16)],
         ),
-        out_shape=[jax.ShapeDtypeStruct((tokens, cols), F32), jax.ShapeDtypeStruct((tokens, cols), BF16)],
+        out_shape=[jax.ShapeDtypeStruct((kept, cols), F32), jax.ShapeDtypeStruct((kept, cols), BF16)],
         compiler_params=params(1),
-        cost_estimate=cost(8.0 * tokens * depth * cols, 6e6),
+        cost_estimate=cost(8.0 * kept * depth * cols, 6e6),
         name="project",
-    )(yc, own, got, w, w0, w1)
+    )(yc, *[v for pair in pairs for v in pair], w, w0, w1)
 
 
 def place_kernel(at_ref, mine_ref, got_ref, out_ref):
@@ -380,18 +386,16 @@
     bias, alog = half(dt_bias, 0, y)[None, :], half(a_log, 0, y)[None, :]
     skip = jnp.repeat(half(skip_d, 0, y), CHANNEL_WIDTH)[None, :]
     gain = half(norm_gain, 0, y)[None, :]
-    got, swap, go, gate_half, bias, alog, skip, gain = tie((got, swap, go, gate_half, bias, alog, skip, gain))
+    got_gate = lax.ppermute(gate_half, "seq", flip)
+    got, swap, go, bias, alog, skip, gain = tie((got, swap, go, bias, alog, skip, gain))
 
     xs, bs, cs, scal, send, s = local_state(yv, x_in, b_proj, c_proj, dt_raw, got, bias, alog, heads)
     one = along(send, 1, range(nz - 1))
-    gate_half, _ = tie((gate_half, send))
-    got_gate = lax.ppermute(gate_half, "seq", flip)
-    base = local_y(xs, bs, cs, scal, skip, heads)
+    got_gate, after = tie((got_gate, xs))
+    base = local_y(after, bs, cs, scal, skip, heads)
     one, got_gate, base, swap, go = tie((one, got_gate, base, swap, go))
 
-    joined = join(send, s, one)
-    two = along(joined, 2, range(nz - 2))
-    swap, go, _ = tie((swap, go, joined))
+    two = along(join(send, s, one), 2, range(nz - 2))
     pairs = [(flat(a, b, c, 0), flat(a, 1 - b, c, 1)) for a, b, c, d in spots if d == 0]
     pairs += [(flat(a, b, c, 1), flat(a, b, c, 0)) for a, b, c, d in spots if d == 0]
     w0 = lax.ppermute(swap, both, pairs)
@@ -404,44 +408,39 @@
     def reduce_y(full, rounded):
         return (full + lax.ppermute(rounded, both, across).astype(F32)).astype(BF16)
 
-    def deliver(slot, value):
-        parts = []
-        for turn in range(2):
-            pairs = [
-                (flat(a, b, c, d), flat(table[a][slot], b, a // 2, d)) for a, b, c, d in spots if c ^ turn == a // 2
-            ]
-            parts.append(lax.ppermute(value, both, pairs) if slot or turn else value)
-        return parts
+    def deliver(slot, value, turn):
+        pairs = [(flat(a, b, c, d), flat(table[a][slot], b, a // 2, d)) for a, b, c, d in spots if c ^ turn == a // 2]
+        return lax.ppermute(value, both, pairs).astype(F32)
 
     up1, down1 = along(block, 1, range(nz - 1)), along(block, -1, range(1, nz))
-    flip0 = cross(block)
-    up1, down1, flip0, block = tie((up1, down1, flip0, block))
+    up1, down1, block = tie((up1, down1, block))
     up2, down2 = along(up1, 1, range(1, nz - 1)), along(down1, -1, range(1, nz - 1))
     slot1 = jnp.where(z < 2, down1, up1)
-    flip1 = cross(slot1)
-    up2, down2, flip1, slot1 = tie((up2, down2, flip1, slot1))
-    far = jnp.where(z == 1, down2, up2)
-    far = lax.ppermute(far, "seq", [(2 + b, b) for b in range(2)] + [(4 + b, 6 + b) for b in range(2)])
+    flip0, flip1 = cross(block), cross(slot1)
+    up2, down2, w0, w1 = tie((up2, down2, w0, w1))
+    moves = [(2, 3), (1, 0), (0, 1), (3, 2)]
+    slot3 = jnp.where(z == 1, down2, jnp.where(z == 2, up2, block))
+    slot3 = lax.ppermute(slot3, "seq", [(i * 2 + b, j * 2 + b) for i, j in moves for b in range(2)])
     slot2 = jnp.where(z < 2, down2, up2)
     flip2 = cross(slot2)
-    a0 = project(yc, block, flip0, w_out, w0, w1)
-    a1 = project(yc, slot1, flip1, w_out, w0, w1)
+    a0 = project(yc, [(block, flip0), (slot1, flip1)], w_out, w0, w1)
+    flip2, slot2, a0 = tie((flip2, slot2, a0))
+    a2 = project(yc, [(slot2, flip2)], w_out, w0, w1)
+    slot3, a2 = tie((slot3, a2))
+    flip3 = cross(slot3)
     b0 = reduce_y(*a0)
-    far, flip2, a1, b0 = tie((far, flip2, a1, b0))
-    slot3 = jnp.where(z == 1, up1, jnp.where(z == 2, down1, far))
-    flip3 = cross(slot3)
-    b1 = reduce_y(*a1)
-    a2 = project(yc, slot2, flip2, w_out, w0, w1)
-    flip3, slot3, b1, a2 = tie((flip3, slot3, b1, a2))
+    flip3, slot3, b0 = tie((flip3, slot3, b0))
+    a3 = project(yc, [(slot3, flip3)], w_out, w0, w1)
     b2 = reduce_y(*a2)
-    a3 = project(yc, slot3, flip3, w_out, w0, w1)
-    r0 = deliver(0, b0)
-    r0, b2, a3 = tie((r0, b2, a3))
+    chips = [(flat(a, b, 1 - c, d), flat(a, b, c, d)) for a, b, c, d in spots if c == a // 2]
+    c0 = b0.astype(F32) + lax.ppermute(b0, both, chips).astype(F32)
+    a3, b2 = tie((a3, b2))
     b3 = reduce_y(*a3)
-    r1 = deliver(1, b1)
-    r1, b3 = tie((r1, b3))
-    results = [r0, r1, deliver(2, b2), deliver(3, b3)]
-    results = [p.astype(F32) + q.astype(F32) for p, q in results]
+    b3, c0 = tie((b3, c0))
+    r1 = deliver(1, c0[tokens:].astype(BF16), 0)
+    r2 = [deliver(2, b2, turn) for turn in range(2)]
+    r3 = [deliver(3, b3, turn) for turn in range(2)]
+    results = [c0[:tokens], r1, r2[0] + r2[1], r3[0] + r3[1]]
     marks = []
     for slot in range(nz):
         mark = jnp.int32(-1)

time: 170 us -> 150 us (0.88)
  starting transfers between devices: 52 us -> 40.2 us
  local copies, waits for them, and re-layouts: 17.4 us -> 7.08 us
  waiting for transfers between devices: 71.1 us -> 79.3 us
  other arithmetic: 6.25 us -> 2.25 us
    ppermute x4 -> x3, waiting for transfers between devices: 5.11 us -> 14.8 us  [reduce_y(): return (full + lax.ppermute(rounded, both, across).astype(F32)).astype(BF16)]
    unnamed x30 -> x12, local copies, waits for them, and re-layouts: 9.41 us -> 0.03 us
    ppermute x8 -> x7, starting transfers between devices: 19.3 us -> 10.5 us  [the longest x5 7.41 us: deliver(): return lax.ppermute(value, both, pairs).astype(F32)]
    pallas_call x4 -> x3, Pallas kernels: 16.9 us -> 13.6 us  [project(): pl.pallas_call(project_kernel, grid_spec=pltpu.PrefetchScalarGridSpec(num...]
    ppermute x8 -> x7, waiting for transfers between devices: 21.9 us -> 19.7 us  [the longest x5 17.2 us: deliver(): return lax.ppermute(value, both, pairs).astype(F32)]
    pallas_call x1, Pallas kernels: 0.22 us -> 1.93 us  [pack(): pl.pallas_call(lambda *refs: pack_kernel(*refs, heads=heads), grid_spec=p...]
  transfers between devices with their start and end apart: 27 -> 25, of which waited for: 12 -> 13; matrix products, arithmetic and copies ran while one was open for 7% -> 6% of each run, Pallas kernels for 11% -> 11%
where the time goes in v3:
time: 150 us; the launch traced here: 149 us
  waiting for transfers between devices  79.3 us (53%)
  starting transfers between devices  40.2 us (27%)
  Pallas kernels  20 us (13%)
  local copies, waits for them, and re-layouts  7.08 us (5%)
  other arithmetic  2.25 us (2%)
    ppermute x6, waiting for transfers between devices, along(): return lax.ppermute(v, 'seq', pairs)  36.2 us
    ppermute x6, starting transfers between devices, along(): return lax.ppermute(v, 'seq', pairs)  20.2 us
    ppermute x5, waiting for transfers between devices, deliver(): return lax.ppermute(value, both, pairs).astype(F32)  17.2 us
    ppermute x3, waiting for transfers between devices, reduce_y(): return (full + lax.ppermute(rounded, both, across).astype(F32)).astype(BF16)  14.8 us
    pallas_call x3, Pallas kernels, project(): pl.pallas_call(project_kernel, grid_spec=pltpu.PrefetchScalarGridSpec(num...  13.6 us
    ppermute x5, starting transfers between devices, deliver(): return lax.ppermute(value, both, pairs).astype(F32)  7.41 us
    dynamic_slice x4, local copies, waits for them, and re-layouts, half(): return lax.dynamic_slice_in_dim(v, which * n, n, axis)  6.2 us
    ppermute x1, waiting for transfers between devices, pair_shards(): got_gate = lax.ppermute(gate_half, 'seq', flip)  5.38 us
  transfers between devices with their start and end apart: 25, of which 13 were waited for; matrix products, arithmetic and copies ran while one was open for 6% of the time, Pallas kernels for 11%

profile of v3, /device:TPU:0, one launch (start us, length us, event | category | flops | bytes accessed | tf_op | source)
XLA Modules:
  0.0 149.2 jit_solution(15216962774846420692)
XLA Ops:
  0.0 1.9 %pack.1 = bf16[128,1408]{1,0:T(8,128)(2,1)} custom-call(s32[1]{0:T(128)} %bitcast.1.refs_0_, bf16[128,2048]{1,0:T(8,128)(2,1)} %refs_1_.3, bf16[128,256]{1,0:T(8,128)(2,1)} %refs_2_.5, bf16[128,256]{1,0:T(8,128)(2,1)} %refs_3_.3, f32[16,128]{1,0:T(8,128)} %bitcast.10), custom_call_target="tpu_custom_call" | custom-call | flops 1 | bytes 1 | tf_op jit(solution)/shard_map/pack/pallas_call | solution.py:68
  1.9 3.0 %collective-permute-start = (bf16[128,1408]{1,0:T(8,128)(2,1)}, bf16[128,1408]{1,0:T(8,128)(2,1)S(1)}, u32[]{:S(2)}, u32[]{:S(2)}) collective-permute-start(bf16[128,1408]{1,0:T(8,128)(2,1)} %pack.1), channel_id=1, source_target_pairs={{0,4},{4,0},{8,12},{12,8},{16,20},{20,16},{24,28},{28,24},{1,5},{5... | collective-permute-start | bytes 1081352 | tf_op jit(solution)/shard_map/ppermute | solution.py:383
  7.1 4.8 %constant_dynamic-slice_fusion.1 = (bf16[1024,1024]{1,0:T(8,128)(2,1)}, bf16[1024,1024]{1,0:T(8,128)(2,1)}) fusion(bf16[2048,1024]{1,0:T(8,128)(2,1)} %refs_2_.7, s32[]{:T(128)S(6)} %select_n.184, s32[]{:T(128)S(6)} %select_n.183), kind=kLoop, calls=%fused_computation.21 | loop fusion | bytes 8388616 | tf_op jit(solution)/shard_map/dynamic_slice | solution.py:373
  11.8 1.7 %collective-permute-done.refs_5_ = bf16[128,1408]{1,0:T(8,128)(2,1)S(1)} collective-permute-done((bf16[128,1408]{1,0:T(8,128)(2,1)}, bf16[128,1408]{1,0:T(8,128)(2,1)S(1)}, u32[]{:S(2)}, u32[]{:S(2)}) %collective-permute-start) | collective-permute-done | bytes 360480 | tf_op jit(solution)/shard_map/ppermute | solution.py:383
  13.6 1.4 local_state.1
  15.0 3.7 %collective-permute-start.1 = (bf16[144,1024]{1,0:T(8,128)(2,1)S(1)}, bf16[144,1024]{1,0:T(8,128)(2,1)S(1)}, u32[]{:S(2)}, u32[]{:S(2)}) collective-permute-start(bf16[144,1024]{1,0:T(8,128)(2,1)S(1)} %get-tuple-element.56.send_ref), channel_id=1, source_target_pairs={{0,8},{4,12},{8,16},{12,20},{16,24},{20,28},{1,9},{5,13},{9,17},{1... | collective-permute-start | bytes 884744 | tf_op jit(solution)/shard_map/ppermute | solution.py:381
  18.8 1.6 %collective-permute-start.2 = (bf16[128,1024]{1,0:T(8,128)(2,1)S(1)}, bf16[128,1024]{1,0:T(8,128)(2,1)S(1)}, u32[]{:S(2)}, u32[]{:S(2)}) collective-permute-start(bf16[128,1024]{1,0:T(8,128)(2,1)S(1)} %constant_dynamic-slice_fusion), channel_id=1, source_target_pairs={{0,4},{4,0},{8,12},{12,8},{16,20},{20,16},{24,28},{28,24},{1,5},{5... | collective-permute-start | bytes 786440 | tf_op jit(solution)/shard_map/ppermute | solution.py:389
  20.4 5.4 %collective-permute-done.2.refs_7_ = bf16[128,1024]{1,0:T(8,128)(2,1)S(1)} collective-permute-done((bf16[128,1024]{1,0:T(8,128)(2,1)S(1)}, bf16[128,1024]{1,0:T(8,128)(2,1)S(1)}, u32[]{:S(2)}, u32[]{:S(2)}) %collective-permute-start.2) | collective-permute-done | bytes 262176 | tf_op jit(solution)/shard_map/ppermute | solution.py:389
  26.9 2.0 %collective-permute-start.9 = (bf16[1024,1024]{1,0:T(8,128)(2,1)}, bf16[1024,1024]{1,0:T(8,128)(2,1)}, u32[]{:S(2)}, u32[]{:S(2)}) collective-permute-start(bf16[1024,1024]{1,0:T(8,128)(2,1)} %get-tuple-element.74), channel_id=1, source_target_pairs={{1,5},{3,7},{5,1},{7,3},{9,13},{11,15},{13,9},{15,11},{17,21},{19,... | collective-permute-start | bytes 6291464 | tf_op jit(solution)/shard_map/ppermute | solution.py:402
  29.0 4.5 %collective-permute-start.3 = (bf16[128,1024]{1,0:T(8,128)(2,1)S(1)}, bf16[128,1024]{1,0:T(8,128)(2,1)S(1)}, u32[]{:S(2)}, u32[]{:S(2)}) collective-permute-start(bf16[128,1024]{1,0:T(8,128)(2,1)S(1)} %join.1), channel_id=1, source_target_pairs={{0,16},{4,20},{8,24},{12,28},{1,17},{5,21},{9,25},{13,29},{2,18},{... | collective-permute-start | bytes 786440 | tf_op jit(solution)/shard_map/ppermute | solution.py:381
  33.5 6.1 %collective-permute-done.3.refs_5_ = bf16[128,1024]{1,0:T(8,128)(2,1)S(1)} collective-permute-done((bf16[128,1024]{1,0:T(8,128)(2,1)S(1)}, bf16[128,1024]{1,0:T(8,128)(2,1)S(1)}, u32[]{:S(2)}, u32[]{:S(2)}) %collective-permute-start.3) | collective-permute-done | bytes 262176 | tf_op jit(solution)/shard_map/ppermute | solution.py:381
  40.7 8.0 %collective-permute-start.4 = (bf16[256,1024]{1,0:T(8,128)(2,1)S(1)}, bf16[256,1024]{1,0:T(8,128)(2,1)}, u32[]{:S(2)}, u32[]{:S(2)}) collective-permute-start(bf16[256,1024]{1,0:T(8,128)(2,1)S(1)} %finish.1.refs_0_), channel_id=1, source_target_pairs={{0,8},{4,12},{8,16},{12,20},{16,24},{20,28},{1,9},{5,13},{9,17},{1... | collective-permute-start | bytes 1572872 | tf_op jit(solution)/shard_map/ppermute | solution.py:381
  49.9 9.9 %collective-permute-done.4 = bf16[256,1024]{1,0:T(8,128)(2,1)} collective-permute-done((bf16[256,1024]{1,0:T(8,128)(2,1)S(1)}, bf16[256,1024]{1,0:T(8,128)(2,1)}, u32[]{:S(2)}, u32[]{:S(2)}) %collective-permute-start.4) | collective-permute-done | bytes 524320 | tf_op jit(solution)/shard_map/ppermute | solution.py:381
  59.9 4.9 %collective-permute-done.5 = bf16[256,1024]{1,0:T(8,128)(2,1)S(1)} collective-permute-done((bf16[256,1024]{1,0:T(8,128)(2,1)S(1)}, bf16[256,1024]{1,0:T(8,128)(2,1)S(1)}, u32[]{:S(2)}, u32[]{:S(2)}) %collective-permute-start.5) | collective-permute-done | bytes 524320 | tf_op jit(solution)/shard_map/ppermute | solution.py:381
  64.8 1.4 collective-permute-start.6
  68.2 15.2 %collective-permute-done.7 = bf16[256,1024]{1,0:T(8,128)(2,1)} collective-permute-done((bf16[256,1024]{1,0:T(8,128)(2,1)S(1)}, bf16[256,1024]{1,0:T(8,128)(2,1)}, u32[]{:S(2)}, u32[]{:S(2)}) %collective-permute-start.7) | collective-permute-done | bytes 524320 | tf_op jit(solution)/shard_map/ppermute | solution.py:381
  84.8 1.8 %collective-permute-start.10 = (bf16[256,1024]{1,0:T(8,128)(2,1)S(1)}, bf16[256,1024]{1,0:T(8,128)(2,1)S(1)}, u32[]{:S(2)}, u32[]{:S(2)}) collective-permute-start(bf16[256,1024]{1,0:T(8,128)(2,1)S(1)} %get-tuple-element.106), channel_id=1, source_target_pairs={{16,24},{20,28},{8,0},{12,4},{0,8},{4,12},{24,16},{28,20},{17,25},... | collective-permute-start | bytes 1572872 | tf_op jit(solution)/shard_map/ppermute | solution.py:423
  86.7 5.4 %project.3 = (f32[256,1024]{1,0:T(8,128)S(1)}, bf16[256,1024]{1,0:T(8,128)(2,1)S(1)}) custom-call(s32[2]{0:T(128)S(1)} %pad_add_fusion.yc_ref, bf16[256,1024]{1,0:T(8,128)(2,1)S(1)} %finish.1.refs_0_, bf16[256,1024]{1,0:T(8,128)(2,1)S(1)} %collective-permute-done.12.refs_1_, bf16[256,1024]{1,0:T(8,128)(2,1)S(1)} %broadcast_select_fusion.refs_2_, ...), custom_call_target="tpu_custom_call" | custom-call | flops 1 | bytes 1 | tf_op jit(solution)/shard_map/project/pallas_call | solution.py:307
  92.6 4.1 %project.4 = (f32[128,1024]{1,0:T(8,128)S(1)}, bf16[128,1024]{1,0:T(8,128)(2,1)S(1)}) custom-call(s32[2]{0:T(128)S(1)} %pad_add_fusion.yc_ref, bf16[256,1024]{1,0:T(8,128)(2,1)S(1)} %get-tuple-element.82.refs_0_, bf16[256,1024]{1,0:T(8,128)(2,1)S(1)} %collective-permute-done.11.refs_1_, bf16[2048,1024]{1,0:T(8,128)(2,1)S(1)} %copy-done, ...), custom_call_target="tpu_custom_call" | custom-call | flops 1 | bytes 1 | tf_op jit(solution)/shard_map/project/pallas_call | solution.py:307
  96.7 2.5 %collective-permute-done.10.refs_0_ = bf16[256,1024]{1,0:T(8,128)(2,1)S(1)} collective-permute-done((bf16[256,1024]{1,0:T(8,128)(2,1)S(1)}, bf16[256,1024]{1,0:T(8,128)(2,1)S(1)}, u32[]{:S(2)}, u32[]{:S(2)}) %collective-permute-start.10) | collective-permute-done | bytes 524320 | tf_op jit(solution)/shard_map/ppermute | solution.py:423
  99.8 6.2 %collective-permute-done.15 = bf16[256,1024]{1,0:T(8,128)(2,1)S(1)} collective-permute-done((bf16[256,1024]{1,0:T(8,128)(2,1)S(1)}, bf16[256,1024]{1,0:T(8,128)(2,1)S(1)}, u32[]{:S(2)}, u32[]{:S(2)}) %collective-permute-start.15) | collective-permute-done | bytes 524320 | tf_op jit(solution)/shard_map/ppermute | solution.py:409
  106.2 1.3 collective-permute-start.18
  107.5 4.2 %collective-permute-done.16 = bf16[128,1024]{1,0:T(8,128)(2,1)S(1)} collective-permute-done((bf16[128,1024]{1,0:T(8,128)(2,1)S(1)}, bf16[128,1024]{1,0:T(8,128)(2,1)S(1)}, u32[]{:S(2)}, u32[]{:S(2)}) %collective-permute-start.16) | collective-permute-done | bytes 262176 | tf_op jit(solution)/shard_map/ppermute | solution.py:409
  111.7 4.2 %project.5 = (f32[128,1024]{1,0:T(8,128)S(1)}, bf16[128,1024]{1,0:T(8,128)(2,1)S(1)}) custom-call(s32[2]{0:T(128)S(1)} %pad_add_fusion.yc_ref, bf16[256,1024]{1,0:T(8,128)(2,1)S(1)} %collective-permute-done.10.refs_0_, bf16[256,1024]{1,0:T(8,128)(2,1)S(1)} %collective-permute-done.14.refs_1_, bf16[2048,1024]{1,0:T(8,128)(2,1)S(1)} %copy-done, ...), custom_call_target="tpu_custom_call" | custom-call | flops 1 | bytes 1 | tf_op jit(solution)/shard_map/project/pallas_call | solution.py:307
  116.9 1.3 collective-permute-start.20
  118.9 4.4 %collective-permute-done.17 = bf16[128,1024]{1,0:T(8,128)(2,1)S(1)} collective-permute-done((bf16[128,1024]{1,0:T(8,128)(2,1)S(1)}, bf16[128,1024]{1,0:T(8,128)(2,1)S(1)}, u32[]{:S(2)}, u32[]{:S(2)}) %collective-permute-start.17) | collective-permute-done | bytes 262176 | tf_op jit(solution)/shard_map/ppermute | solution.py:409
  123.7 2.2 %collective-permute-start.19 = (bf16[128,1024]{1,0:T(8,128)(2,1)S(1)}, bf16[128,1024]{1,0:T(8,128)(2,1)S(1)}, u32[]{:S(2)}, u32[]{:S(2)}) collective-permute-start(bf16[128,1024]{1,0:T(8,128)(2,1)S(1)} %slice.13), channel_id=1, source_target_pairs={{0,8},{1,9},{4,12},{5,13},{8,16},{9,17},{12,20},{13,21},{18,10},{1... | collective-permute-start | bytes 786440 | tf_op jit(solution)/shard_map/ppermute | solution.py:413
  125.9 1.9 %collective-permute-start.22 = (bf16[128,1024]{1,0:T(8,128)(2,1)S(1)}, bf16[128,1024]{1,0:T(8,128)(2,1)S(1)}, u32[]{:S(2)}, u32[]{:S(2)}) collective-permute-start(bf16[128,1024]{1,0:T(8,128)(2,1)S(1)} %add_convert_fusion.1), channel_id=1, source_target_pairs={{0,24},{1,25},{4,28},{5,29},{8,0},{9,1},{12,4},{13,5},{18,26},{19,... | collective-permute-start | bytes 786440 | tf_op jit(solution)/shard_map/ppermute | solution.py:413
  127.8 1.3 collective-permute-start.23
  129.2 3.3 %collective-permute-done.19 = bf16[128,1024]{1,0:T(8,128)(2,1)S(1)} collective-permute-done((bf16[128,1024]{1,0:T(8,128)(2,1)S(1)}, bf16[128,1024]{1,0:T(8,128)(2,1)S(1)}, u32[]{:S(2)}, u32[]{:S(2)}) %collective-permute-start.19) | collective-permute-done | bytes 262176 | tf_op jit(solution)/shard_map/ppermute | solution.py:413
  132.6 13.9 %collective-permute-done.22 = bf16[128,1024]{1,0:T(8,128)(2,1)S(1)} collective-permute-done((bf16[128,1024]{1,0:T(8,128)(2,1)S(1)}, bf16[128,1024]{1,0:T(8,128)(2,1)S(1)}, u32[]{:S(2)}, u32[]{:S(2)}) %collective-permute-start.22) | collective-permute-done | bytes 262176 | tf_op jit(solution)/shard_map/ppermute | solution.py:413
  147.0 1.4 collective-permute-done.24.got_ref
  (54 shorter events, 13.8 us)
Async XLA Ops:
  1.9 11.6 %collective-permute-start = (bf16[128,1408]{1,0:T(8,128)(2,1)}, bf16[128,1408]{1,0:T(8,128)(2,1)S(1)}, u32[]{:S(2)}, u32[]{:S(2)}) collective-permute-start(bf16[128,1408]{1,0:T(8,128)(2,1)} %pack.1), channel_id=1, source_target_pairs={{0,4},{4,0},{8,12},{12,8},{16,20},{20,16},{24,28},{28,24},{1,5},{5... | collective-permute-start | bytes 1081352 | tf_op jit(solution)/shard_map/ppermute | solution.py:383
  7.1 6.5 %copy-start.1 = (bf16[128,2048]{1,0:T(8,128)(2,1)S(1)}, bf16[128,2048]{1,0:T(8,128)(2,1)}, u32[]{:S(2)}) copy-start(bf16[128,2048]{1,0:T(8,128)(2,1)} %refs_1_.3) | copy-start | bytes 1572868
  7.1 6.5 %copy-start.3 = (bf16[128,256]{1,0:T(8,128)(2,1)S(1)}, bf16[128,256]{1,0:T(8,128)(2,1)}, u32[]{:S(2)}) copy-start(bf16[128,256]{1,0:T(8,128)(2,1)} %refs_2_.5) | copy-start | bytes 196612
  7.1 6.5 %copy-start.4 = (bf16[128,256]{1,0:T(8,128)(2,1)S(1)}, bf16[128,256]{1,0:T(8,128)(2,1)}, u32[]{:S(2)}) copy-start(bf16[128,256]{1,0:T(8,128)(2,1)} %refs_3_.3) | copy-start | bytes 196612
  7.1 6.5 %copy-start.5 = (f32[128,16]{0,1:T(8,128)S(1)}, f32[128,16]{0,1:T(8,128)}, u32[]{:S(2)}) copy-start(f32[128,16]{0,1:T(8,128)} %param.14) | copy-start | bytes 24580
  7.1 11.7 %copy-start.2 = (bf16[128,2048]{1,0:T(8,128)(2,1)S(1)}, bf16[128,2048]{1,0:T(8,128)(2,1)}, u32[]{:S(2)}) copy-start(bf16[128,2048]{1,0:T(8,128)(2,1)} %refs_6_.1) | copy-start | bytes 1572868
  15.0 11.9 %collective-permute-start.1 = (bf16[144,1024]{1,0:T(8,128)(2,1)S(1)}, bf16[144,1024]{1,0:T(8,128)(2,1)S(1)}, u32[]{:S(2)}, u32[]{:S(2)}) collective-permute-start(bf16[144,1024]{1,0:T(8,128)(2,1)S(1)} %get-tuple-element.56.send_ref), channel_id=1, source_target_pairs={{0,8},{4,12},{8,16},{12,20},{16,24},{20,28},{1,9},{5,13},{9,17},{1... | collective-permute-start | bytes 884744 | tf_op jit(solution)/shard_map/ppermute | solution.py:381
  18.8 7.0 %collective-permute-start.2 = (bf16[128,1024]{1,0:T(8,128)(2,1)S(1)}, bf16[128,1024]{1,0:T(8,128)(2,1)S(1)}, u32[]{:S(2)}, u32[]{:S(2)}) collective-permute-start(bf16[128,1024]{1,0:T(8,128)(2,1)S(1)} %constant_dynamic-slice_fusion), channel_id=1, source_target_pairs={{0,4},{4,0},{8,12},{12,8},{16,20},{20,16},{24,28},{28,24},{1,5},{5... | collective-permute-start | bytes 786440 | tf_op jit(solution)/shard_map/ppermute | solution.py:389
  26.9 56.6 %collective-permute-start.8 = (bf16[1024,1024]{1,0:T(8,128)(2,1)}, bf16[1024,1024]{1,0:T(8,128)(2,1)S(1)}, u32[]{:S(2)}, u32[]{:S(2)}) collective-permute-start(bf16[1024,1024]{1,0:T(8,128)(2,1)} %get-tuple-element.73), channel_id=1, source_target_pairs={{0,5},{2,7},{4,1},{6,3},{8,13},{10,15},{12,9},{14,11},{16,21},{18,... | collective-permute-start | bytes 6291464 | tf_op jit(solution)/shard_map/ppermute | solution.py:401
  26.9 56.5 %collective-permute-start.9 = (bf16[1024,1024]{1,0:T(8,128)(2,1)}, bf16[1024,1024]{1,0:T(8,128)(2,1)}, u32[]{:S(2)}, u32[]{:S(2)}) collective-permute-start(bf16[1024,1024]{1,0:T(8,128)(2,1)} %get-tuple-element.74), channel_id=1, source_target_pairs={{1,5},{3,7},{5,1},{7,3},{9,13},{11,15},{13,9},{15,11},{17,21},{19,... | collective-permute-start | bytes 6291464 | tf_op jit(solution)/shard_map/ppermute | solution.py:402
  29.0 10.6 %collective-permute-start.3 = (bf16[128,1024]{1,0:T(8,128)(2,1)S(1)}, bf16[128,1024]{1,0:T(8,128)(2,1)S(1)}, u32[]{:S(2)}, u32[]{:S(2)}) collective-permute-start(bf16[128,1024]{1,0:T(8,128)(2,1)S(1)} %join.1), channel_id=1, source_target_pairs={{0,16},{4,20},{8,24},{12,28},{1,17},{5,21},{9,25},{13,29},{2,18},{... | collective-permute-start | bytes 786440 | tf_op jit(solution)/shard_map/ppermute | solution.py:381
  40.7 19.2 %collective-permute-start.4 = (bf16[256,1024]{1,0:T(8,128)(2,1)S(1)}, bf16[256,1024]{1,0:T(8,128)(2,1)}, u32[]{:S(2)}, u32[]{:S(2)}) collective-permute-start(bf16[256,1024]{1,0:T(8,128)(2,1)S(1)} %finish.1.refs_0_), channel_id=1, source_target_pairs={{0,8},{4,12},{8,16},{12,20},{16,24},{20,28},{1,9},{5,13},{9,17},{1... | collective-permute-start | bytes 1572872 | tf_op jit(solution)/shard_map/ppermute | solution.py:381
  48.7 16.1 %collective-permute-start.5 = (bf16[256,1024]{1,0:T(8,128)(2,1)S(1)}, bf16[256,1024]{1,0:T(8,128)(2,1)S(1)}, u32[]{:S(2)}, u32[]{:S(2)}) collective-permute-start(bf16[256,1024]{1,0:T(8,128)(2,1)S(1)} %finish.1.refs_0_), channel_id=1, source_target_pairs={{8,0},{12,4},{16,8},{20,12},{24,16},{28,20},{9,1},{13,5},{17,9},{2... | collective-permute-start | bytes 1572872 | tf_op jit(solution)/shard_map/ppermute | solution.py:381
  64.8 2.9 %collective-permute-start.6 = (bf16[256,1024]{1,0:T(8,128)(2,1)}, bf16[256,1024]{1,0:T(8,128)(2,1)}, u32[]{:S(2)}, u32[]{:S(2)}) collective-permute-start(bf16[256,1024]{1,0:T(8,128)(2,1)} %collective-permute-done.4), channel_id=1, source_target_pairs={{8,16},{12,20},{16,24},{20,28},{9,17},{13,21},{17,25},{21,29},{10,... | collective-permute-start | bytes 1572872 | tf_op jit(solution)/shard_map/ppermute | solution.py:381
  66.2 17.2 %collective-permute-start.7 = (bf16[256,1024]{1,0:T(8,128)(2,1)S(1)}, bf16[256,1024]{1,0:T(8,128)(2,1)}, u32[]{:S(2)}, u32[]{:S(2)}) collective-permute-start(bf16[256,1024]{1,0:T(8,128)(2,1)S(1)} %collective-permute-done.5), channel_id=1, source_target_pairs={{8,0},{12,4},{16,8},{20,12},{9,1},{13,5},{17,9},{21,13},{10,2},{14... | collective-permute-start | bytes 1572872 | tf_op jit(solution)/shard_map/ppermute | solution.py:381
  67.6 19.2 %copy-start = (bf16[2048,1024]{1,0:T(8,128)(2,1)S(1)}, bf16[2048,1024]{1,0:T(8,128)(2,1)}, u32[]{:S(2)}) copy-start(bf16[2048,1024]{1,0:T(8,128)(2,1)} %refs_2_.7) | copy-start | bytes 12582916
  67.6 19.1 %collective-permute-start.13 = (bf16[256,1024]{1,0:T(8,128)(2,1)S(1)}, bf16[256,1024]{1,0:T(8,128)(2,1)S(1)}, u32[]{:S(2)}, u32[]{:S(2)}) collective-permute-start(bf16[256,1024]{1,0:T(8,128)(2,1)S(1)} %broadcast_select_fusion.refs_2_), channel_id=1, source_target_pairs={{0,1},{1,0},{2,3},{3,2},{4,5},{5,4},{6,7},{7,6},{8,9},{9,8},{10,11... | collective-permute-start | bytes 1572872 | tf_op jit(solution)/shard_map/ppermute | solution.py:406
  67.7 19.0 %collective-permute-start.12 = (bf16[256,1024]{1,0:T(8,128)(2,1)S(1)}, bf16[256,1024]{1,0:T(8,128)(2,1)S(1)}, u32[]{:S(2)}, u32[]{:S(2)}) collective-permute-start(bf16[256,1024]{1,0:T(8,128)(2,1)S(1)} %finish.1.refs_0_), channel_id=1, source_target_pairs={{0,1},{1,0},{2,3},{3,2},{4,5},{5,4},{6,7},{7,6},{8,9},{9,8},{10,11... | collective-permute-start | bytes 1572872 | tf_op jit(solution)/shard_map/ppermute | solution.py:406
  84.8 7.4 %collective-permute-start.11 = (bf16[256,1024]{1,0:T(8,128)(2,1)S(1)}, bf16[256,1024]{1,0:T(8,128)(2,1)S(1)}, u32[]{:S(2)}, u32[]{:S(2)}) collective-permute-start(bf16[256,1024]{1,0:T(8,128)(2,1)S(1)} %get-tuple-element.82.refs_0_), channel_id=1, source_target_pairs={{0,1},{1,0},{2,3},{3,2},{4,5},{5,4},{6,7},{7,6},{8,9},{9,8},{10,11... | collective-permute-start | bytes 1572872 | tf_op jit(solution)/shard_map/ppermute | solution.py:406
  84.8 14.3 %collective-permute-start.10 = (bf16[256,1024]{1,0:T(8,128)(2,1)S(1)}, bf16[256,1024]{1,0:T(8,128)(2,1)S(1)}, u32[]{:S(2)}, u32[]{:S(2)}) collective-permute-start(bf16[256,1024]{1,0:T(8,128)(2,1)S(1)} %get-tuple-element.106), channel_id=1, source_target_pairs={{16,24},{20,28},{8,0},{12,4},{0,8},{4,12},{24,16},{28,20},{17,25},... | collective-permute-start | bytes 1572872 | tf_op jit(solution)/shard_map/ppermute | solution.py:423
  92.1 13.9 %collective-permute-start.15 = (bf16[256,1024]{1,0:T(8,128)(2,1)S(1)}, bf16[256,1024]{1,0:T(8,128)(2,1)S(1)}, u32[]{:S(2)}, u32[]{:S(2)}) collective-permute-start(bf16[256,1024]{1,0:T(8,128)(2,1)S(1)} %get-tuple-element.88), channel_id=1, source_target_pairs={{0,5},{1,4},{2,7},{3,6},{4,1},{5,0},{6,3},{7,2},{8,13},{9,12},{10,... | collective-permute-start | bytes 1572872 | tf_op jit(solution)/shard_map/ppermute | solution.py:409
  99.2 7.0 %collective-permute-start.14 = (bf16[256,1024]{1,0:T(8,128)(2,1)S(1)}, bf16[256,1024]{1,0:T(8,128)(2,1)S(1)}, u32[]{:S(2)}, u32[]{:S(2)}) collective-permute-start(bf16[256,1024]{1,0:T(8,128)(2,1)S(1)} %collective-permute-done.10.refs_0_), channel_id=1, source_target_pairs={{0,1},{1,0},{2,3},{3,2},{4,5},{5,4},{6,7},{7,6},{8,9},{9,8},{10,11... | collective-permute-start | bytes 1572872 | tf_op jit(solution)/shard_map/ppermute | solution.py:406
  99.2 12.4 %collective-permute-start.16 = (bf16[128,1024]{1,0:T(8,128)(2,1)S(1)}, bf16[128,1024]{1,0:T(8,128)(2,1)S(1)}, u32[]{:S(2)}, u32[]{:S(2)}) collective-permute-start(bf16[128,1024]{1,0:T(8,128)(2,1)S(1)} %get-tuple-element.94), channel_id=1, source_target_pairs={{0,5},{1,4},{2,7},{3,6},{4,1},{5,0},{6,3},{7,2},{8,13},{9,12},{10,... | collective-permute-start | bytes 786440 | tf_op jit(solution)/shard_map/ppermute | solution.py:409
  106.2 17.3 %collective-permute-start.18 = (bf16[256,1024]{1,0:T(8,128)(2,1)S(1)}, bf16[256,1024]{1,0:T(8,128)(2,1)S(1)}, u32[]{:S(2)}, u32[]{:S(2)}) collective-permute-start(bf16[256,1024]{1,0:T(8,128)(2,1)S(1)} %add_convert_fusion), channel_id=1, source_target_pairs={{2,0},{3,1},{6,4},{7,5},{10,8},{11,9},{14,12},{15,13},{16,18},{17,... | collective-permute-start | bytes 1572872 | tf_op jit(solution)/shard_map/ppermute | solution.py:436
  115.8 7.5 %collective-permute-start.17 = (bf16[128,1024]{1,0:T(8,128)(2,1)S(1)}, bf16[128,1024]{1,0:T(8,128)(2,1)S(1)}, u32[]{:S(2)}, u32[]{:S(2)}) collective-permute-start(bf16[128,1024]{1,0:T(8,128)(2,1)S(1)} %get-tuple-element.96), channel_id=1, source_target_pairs={{0,5},{1,4},{2,7},{3,6},{4,1},{5,0},{6,3},{7,2},{8,13},{9,12},{10,... | collective-permute-start | bytes 786440 | tf_op jit(solution)/shard_map/ppermute | solution.py:409
  116.9 12.3 %collective-permute-start.20 = (bf16[128,1024]{1,0:T(8,128)(2,1)S(1)}, bf16[128,1024]{1,0:T(8,128)(2,1)S(1)}, u32[]{:S(2)}, u32[]{:S(2)}) collective-permute-start(bf16[128,1024]{1,0:T(8,128)(2,1)S(1)} %add_convert_fusion.2), channel_id=1, source_target_pairs={{0,16},{1,17},{4,20},{5,21},{8,24},{9,25},{12,28},{13,29},{18,2},{... | collective-permute-start | bytes 786440 | tf_op jit(solution)/shard_map/ppermute | solution.py:413
  118.2 11.0 %collective-permute-start.21 = (bf16[128,1024]{1,0:T(8,128)(2,1)S(1)}, bf16[128,1024]{1,0:T(8,128)(2,1)S(1)}, u32[]{:S(2)}, u32[]{:S(2)}) collective-permute-start(bf16[128,1024]{1,0:T(8,128)(2,1)S(1)} %add_convert_fusion.2), channel_id=1, source_target_pairs={{2,16},{3,17},{6,20},{7,21},{10,24},{11,25},{14,28},{15,29},{16,2}... | collective-permute-start | bytes 786440 | tf_op jit(solution)/shard_map/ppermute | solution.py:413
  123.7 8.9 %collective-permute-start.19 = (bf16[128,1024]{1,0:T(8,128)(2,1)S(1)}, bf16[128,1024]{1,0:T(8,128)(2,1)S(1)}, u32[]{:S(2)}, u32[]{:S(2)}) collective-permute-start(bf16[128,1024]{1,0:T(8,128)(2,1)S(1)} %slice.13), channel_id=1, source_target_pairs={{0,8},{1,9},{4,12},{5,13},{8,16},{9,17},{12,20},{13,21},{18,10},{1... | collective-permute-start | bytes 786440 | tf_op jit(solution)/shard_map/ppermute | solution.py:413
  125.9 20.5 %collective-permute-start.22 = (bf16[128,1024]{1,0:T(8,128)(2,1)S(1)}, bf16[128,1024]{1,0:T(8,128)(2,1)S(1)}, u32[]{:S(2)}, u32[]{:S(2)}) collective-permute-start(bf16[128,1024]{1,0:T(8,128)(2,1)S(1)} %add_convert_fusion.1), channel_id=1, source_target_pairs={{0,24},{1,25},{4,28},{5,29},{8,0},{9,1},{12,4},{13,5},{18,26},{19,... | collective-permute-start | bytes 786440 | tf_op jit(solution)/shard_map/ppermute | solution.py:413
  127.8 18.6 %collective-permute-start.23 = (bf16[128,1024]{1,0:T(8,128)(2,1)S(1)}, bf16[128,1024]{1,0:T(8,128)(2,1)S(1)}, u32[]{:S(2)}, u32[]{:S(2)}) collective-permute-start(bf16[128,1024]{1,0:T(8,128)(2,1)S(1)} %add_convert_fusion.1), channel_id=1, source_target_pairs={{2,24},{3,25},{6,28},{7,29},{10,0},{11,1},{14,4},{15,5},{16,26},{1... | collective-permute-start | bytes 786440 | tf_op jit(solution)/shard_map/ppermute | solution.py:413
  146.8 1.6 %collective-permute-start.24 = (bf16[128,1024]{1,0:T(8,128)(2,1)S(1)}, bf16[128,1024]{1,0:T(8,128)(2,1)S(1)}, u32[]{:S(2)}, u32[]{:S(2)}) collective-permute-start(bf16[128,1024]{1,0:T(8,128)(2,1)S(1)} %get-tuple-element.103), channel_id=1, source_target_pairs={{0,1},{1,0},{2,3},{3,2},{4,5},{5,4},{6,7},{7,6},{8,9},{9,8},{10,11... | collective-permute-start | bytes 786440 | tf_op jit(solution)/shard_map/ppermute | solution.py:406

commit v4 on v3

--- a/solution.py
+++ b/solution.py
@@ -48,37 +48,46 @@
     return hi, mid, (rest - mid.astype(F32)).astype(BF16)
 
 
-def pack_kernel(y_ref, x_ref, b_ref, c_ref, dt_ref, out_ref, *, heads):
-    width, state = x_ref.shape[1], b_ref.shape[1]
-    out_ref[:, :width] = x_ref[...]
-    out_ref[:, width : width + state] = b_ref[...]
-    out_ref[:, width + state : width + 2 * state] = c_ref[...]
-    other = 1 - y_ref[0]
+def pack_kernel(y_ref, x_ref, b_ref, c_ref, dt_ref, own_ref, out_ref, *, heads):
+    width, state = x_ref.shape[1] // 2, b_ref.shape[1] // 2
     rows, cols = iota((2 * heads, 128), 0), iota((2 * heads, 128), 1)
-    total = jnp.zeros((x_ref.shape[0], 128), F32)
-    for part, value in enumerate(split3(dt_ref[...])):
-        place = (cols == rows - other * heads + part * heads) & (rows // heads == other)
-        total = total + lax.dot_general(value, place.astype(BF16), TN, preferred_element_type=F32)
-    out_ref[:, width + 2 * state :] = total.astype(BF16)
+    parts = split3(dt_ref[...])
+    for group in range(2):
+        total = jnp.zeros((x_ref.shape[0], 128), F32)
+        for part, value in enumerate(parts):
+            where = (cols == rows - group * heads + part * heads) & (rows // heads == group)
+            total = total + lax.dot_general(value, where.astype(BF16), TN, preferred_element_type=F32)
+        steps = total.astype(BF16)
+
+        def fill(ref):
+            ref[:, :width] = x_ref[:, group * width : (group + 1) * width]
+            ref[:, width : width + state] = b_ref[:, group * state : (group + 1) * state]
+            ref[:, width + state : width + 2 * state] = c_ref[:, group * state : (group + 1) * state]
+            ref[:, width + 2 * state :] = steps
+
+        @pl.when(y_ref[0] == group)
+        def _():
+            fill(own_ref)
+
+        @pl.when(y_ref[0] != group)
+        def _():
+            fill(out_ref)
 
 
 def pack(y, x, b, c, dt, heads):
-    tokens, width, state = x.shape[0], heads * CHANNEL_WIDTH, STATE
-    full = width + 2 * state + 128
+    tokens = x.shape[0]
+    full = heads * CHANNEL_WIDTH + 2 * STATE + 128
+    whole = lambda a: pl.BlockSpec(a.shape, lambda i, y: (0,) * a.ndim)
+    out = jax.ShapeDtypeStruct((tokens, full), BF16)
     return pl.pallas_call(
         lambda *refs: pack_kernel(*refs, heads=heads),
         grid_spec=pltpu.PrefetchScalarGridSpec(
             num_scalar_prefetch=1,
             grid=(1,),
-            in_specs=[
-                pl.BlockSpec((tokens, width), lambda i, y: (0, 1 - y[0])),
-                pl.BlockSpec((tokens, state), lambda i, y: (0, 1 - y[0])),
-                pl.BlockSpec((tokens, state), lambda i, y: (0, 1 - y[0])),
-                pl.BlockSpec(dt.shape, lambda i, y: (0, 0)),
-            ],
-            out_specs=pl.BlockSpec((tokens, full), lambda i, y: (0, 0)),
+            in_specs=[whole(x), whole(b), whole(c), whole(dt)],
+            out_specs=[whole(out), whole(out)],
         ),
-        out_shape=jax.ShapeDtypeStruct((tokens, full), BF16),
+        out_shape=[out, out],
         compiler_params=params(1, 60 * 2**20),
         cost_estimate=cost(1e6, 4 * tokens * full),
         name="pack",
@@ -86,24 +95,21 @@
 
 
 def local_state_kernel(
-    y_ref, x_ref, b_ref, c_ref, dt_ref, pk_ref, bias_ref, alog_ref,
-    xs_ref, bs_ref, cs_ref, scal_ref, send_ref, s_ref, *, heads,
+    y_ref, own_ref, pk_ref, bias_ref, alog_ref, xs_ref, bs_ref, cs_ref, scal_ref, send_ref, s_ref, *, heads,
 ):
-    tokens, width = x_ref.shape
-    state = b_ref.shape[1]
+    tokens = own_ref.shape[0]
+    width, state = xs_ref.shape[1], bs_ref.shape[1]
     y = y_ref[0]
-    mine, theirs = pl.multiple_of(y * tokens, tokens), pl.multiple_of((1 - y) * tokens, tokens)
-    xs_ref[pl.ds(mine, tokens), :] = x_ref[...]
-    xs_ref[pl.ds(theirs, tokens), :] = pk_ref[:, :width]
-    bs_ref[pl.ds(mine, tokens), :] = b_ref[...]
-    bs_ref[pl.ds(theirs, tokens), :] = pk_ref[:, width : width + state]
-    cs_ref[pl.ds(mine, tokens), :] = c_ref[...]
-    cs_ref[pl.ds(theirs, tokens), :] = pk_ref[:, width + state : width + 2 * state]
-    rows, cols = iota((2 * heads, heads), 0), iota((2 * heads, heads), 1)
-    own = lax.dot_general(dt_ref[...], (rows == cols + y * heads).astype(F32), TN, precision=HIGH)
     rows, cols = iota((128, heads), 0), iota((128, heads), 1)
     take = ((rows % heads == cols) & (rows < 3 * heads)).astype(BF16)
-    other = jnp.dot(pk_ref[:, width + 2 * state :], take, preferred_element_type=F32)
+    steps = []
+    for ref, place in ((own_ref, y), (pk_ref, 1 - y)):
+        at = pl.ds(pl.multiple_of(place * tokens, tokens), tokens)
+        xs_ref[at, :] = ref[:, :width]
+        bs_ref[at, :] = ref[:, width : width + state]
+        cs_ref[at, :] = ref[:, width + state : width + 2 * state]
+        steps.append(jnp.dot(ref[:, width + 2 * state :], take, preferred_element_type=F32))
+    own, other = steps
     raw = jnp.concatenate([jnp.where(y == 0, own, other), jnp.where(y == 0, other, own)], axis=0)
     raw = raw + bias_ref[...]
     dt = jnp.maximum(raw, 0.0) + jnp.log1p(jnp.exp(-jnp.abs(raw)))
@@ -127,8 +133,8 @@
     send_ref[state:, :] = jnp.where(which < 3, parts, 0.0).astype(BF16)
 
 
-def local_state(y, x, b, c, dt, pk, bias, alog, heads):
-    tokens, width, state = x.shape[0], heads * CHANNEL_WIDTH, STATE
+def local_state(y, own, pk, bias, alog, heads):
+    tokens, width, state = own.shape[0], heads * CHANNEL_WIDTH, STATE
     whole = lambda a: pl.BlockSpec(a.shape, lambda i, y: (0,) * a.ndim)
     outs = [
         jax.ShapeDtypeStruct((2 * tokens, width), BF16),
@@ -143,22 +149,14 @@
         grid_spec=pltpu.PrefetchScalarGridSpec(
             num_scalar_prefetch=1,
             grid=(1,),
-            in_specs=[
-                pl.BlockSpec((tokens, width), lambda i, y: (0, y[0])),
-                pl.BlockSpec((tokens, state), lambda i, y: (0, y[0])),
-                pl.BlockSpec((tokens, state), lambda i, y: (0, y[0])),
-                whole(dt),
-                whole(pk),
-                whole(bias),
-                whole(alog),
-            ],
+            in_specs=[whole(own), whole(pk), whole(bias), whole(alog)],
             out_specs=[whole(o) for o in outs],
         ),
         out_shape=outs,
         compiler_params=params(1),
         cost_estimate=cost(2e8, 3e6),
         name="local_state",
-    )(y, x, b, c, dt, pk, bias, alog)
+    )(y, own, pk, bias, alog)
 
 
 def local_y_kernel(xs_ref, bs_ref, cs_ref, scal_ref, skip_ref, out_ref, *, heads, tokens):
@@ -268,38 +266,29 @@
 
 
 def project_kernel(yc_ref, *refs):
-    *pair_refs, w_ref, w0_ref, w1_ref, keep_ref, send_ref, both_ref = refs
+    *pair_refs, first_ref, second_ref, keep_ref, send_ref, both_ref = refs
     slots, depth = len(pair_refs) // 2, pair_refs[0].shape[1]
     kept = keep_ref.shape[0]
     tokens = kept // slots
-    y, core = yc_ref[0], yc_ref[1]
+    core = yc_ref[1]
 
     @pl.when(pl.program_id(0) == 0)
     def _():
         for slot in range(slots):
             own_ref, got_ref = pair_refs[2 * slot], pair_refs[2 * slot + 1]
             for k in range(2):
-                at = pl.ds(pl.multiple_of(jnp.where(y == 0, k, 1 - k) * tokens, tokens), tokens)
+                at = pl.ds(pl.multiple_of(jnp.where(core == 0, k, 1 - k) * tokens, tokens), tokens)
                 rows = pl.ds(k * kept + slot * tokens, tokens)
-                both_ref[rows, :depth] = jnp.where(core == 0, own_ref[at, :], got_ref[at, :])
-                both_ref[rows, depth:] = jnp.where(core == 0, got_ref[at, :], own_ref[at, :])
-
-    def multiply(first, second):
-        part = jnp.dot(both_ref[:, :depth], first[...], preferred_element_type=F32)
-        part = part + jnp.dot(both_ref[:, depth:], second[...], preferred_element_type=F32)
-        keep_ref[...] = part[:kept, :]
-        send_ref[...] = part[kept:, :].astype(BF16)
-
-    @pl.when(core == 0)
-    def _():
-        multiply(w_ref, w0_ref)
-
-    @pl.when(core == 1)
-    def _():
-        multiply(w0_ref, w1_ref)
-
-
-def project(yc, pairs, w, w0, w1):
+                both_ref[rows, :depth] = own_ref[at, :]
+                both_ref[rows, depth:] = got_ref[at, :]
+
+    part = jnp.dot(both_ref[:, :depth], first_ref[...], preferred_element_type=F32)
+    part = part + jnp.dot(both_ref[:, depth:], second_ref[...], preferred_element_type=F32)
+    keep_ref[...] = part[:kept, :]
+    send_ref[...] = part[kept:, :].astype(BF16)
+
+
+def project(yc, pairs, w):
     length, depth = pairs[0][0].shape
     kept = len(pairs) * length // 2
     cols = w.shape[1]
@@ -311,9 +300,8 @@
             grid=(cols // tile,),
             in_specs=[pl.BlockSpec((length, depth), lambda i, yc: (0, 0))] * (2 * len(pairs))
             + [
-                pl.BlockSpec((depth, tile), lambda i, yc: (yc[0], jnp.where(yc[1] == 0, i, 0))),
-                pl.BlockSpec((depth, tile), lambda i, yc: (0, i)),
-                pl.BlockSpec((depth, tile), lambda i, yc: (0, jnp.where(yc[1] == 1, i, 0))),
+                pl.BlockSpec((depth, tile), lambda i, yc: (yc[0], i)),
+                pl.BlockSpec((depth, tile), lambda i, yc: (1 - yc[0], i)),
             ],
             out_specs=[
                 pl.BlockSpec((kept, tile), lambda i, yc: (0, i)),
@@ -325,7 +313,7 @@
         compiler_params=params(1),
         cost_estimate=cost(8.0 * kept * depth * cols, 6e6),
         name="project",
-    )(yc, *[v for pair in pairs for v in pair], w, w0, w1)
+    )(yc, *[v for pair in pairs for v in pair], w, w)
 
 
 def place_kernel(at_ref, mine_ref, got_ref, out_ref):
@@ -374,82 +362,74 @@
 
     flip = [(s, s ^ 1) for s in range(2 * nz)]
     sibling = [(g, g ^ 1) for g in range(nz)]
-    across = [(flat(a, b, c, d), flat(a, 1 - b, c, 1 - d)) for a, b, c, d in spots]
-
     def along(v, step, senders):
         pairs = [(a * 2 + b, (a + step) * 2 + b) for a in senders for b in range(2)]
         return lax.ppermute(v, "seq", pairs)
 
-    got = lax.ppermute(pack(yv, x_in, b_proj, c_proj, dt_raw, heads), "seq", flip)
-    swap, go = half(w_out, 0, y ^ 1 ^ core), half(w_out, 0, 1 - y)
+    own, packed = pack(yv, x_in, b_proj, c_proj, dt_raw, heads)
+    got = lax.ppermute(packed, "seq", flip)
     gate_half = half(gate, 1, 1 - y)
     bias, alog = half(dt_bias, 0, y)[None, :], half(a_log, 0, y)[None, :]
     skip = jnp.repeat(half(skip_d, 0, y), CHANNEL_WIDTH)[None, :]
     gain = half(norm_gain, 0, y)[None, :]
     got_gate = lax.ppermute(gate_half, "seq", flip)
-    got, swap, go, bias, alog, skip, gain = tie((got, swap, go, bias, alog, skip, gain))
-
-    xs, bs, cs, scal, send, s = local_state(yv, x_in, b_proj, c_proj, dt_raw, got, bias, alog, heads)
+    got, bias, alog, skip, gain = tie((got, bias, alog, skip, gain))
+
+    xs, bs, cs, scal, send, s = local_state(yv, own, got, bias, alog, heads)
     one = along(send, 1, range(nz - 1))
-    got_gate, after = tie((got_gate, xs))
-    base = local_y(after, bs, cs, scal, skip, heads)
-    one, got_gate, base, swap, go = tie((one, got_gate, base, swap, go))
+    base = local_y(xs, bs, cs, scal, skip, heads)
+    one, base = tie((one, base))
 
     two = along(join(send, s, one), 2, range(nz - 2))
-    pairs = [(flat(a, b, c, 0), flat(a, 1 - b, c, 1)) for a, b, c, d in spots if d == 0]
-    pairs += [(flat(a, b, c, 1), flat(a, b, c, 0)) for a, b, c, d in spots if d == 0]
-    w0 = lax.ppermute(swap, both, pairs)
-    w1 = lax.ppermute(go, both, [(flat(a, b, c, 1), flat(a, 1 - b, c, 1)) for a, b, c, d in spots if d == 0])
     block = finish(yv, base, cs, scal, one, two, gate, got_gate, gain, heads)
 
-    table = [(0, 1, 2, 3), (1, 2, 3, 0), (2, 1, 0, 3), (3, 2, 1, 0)]
+    hop = lambda value, *moves: lax.ppermute(value, "seq", [(i * 2 + b, j * 2 + b) for i, j in moves for b in range(2)])
+    inner = (z == 1) | (z == 2)
+    across = lambda value: lax.ppermute(value, "seq", flip)
     cross = lambda value: lax.ppermute(value, "grp", sibling)
 
-    def reduce_y(full, rounded):
-        return (full + lax.ppermute(rounded, both, across).astype(F32)).astype(BF16)
-
-    def deliver(slot, value, turn):
-        pairs = [(flat(a, b, c, d), flat(table[a][slot], b, a // 2, d)) for a, b, c, d in spots if c ^ turn == a // 2]
-        return lax.ppermute(value, both, pairs).astype(F32)
-
-    up1, down1 = along(block, 1, range(nz - 1)), along(block, -1, range(1, nz))
-    up1, down1, block = tie((up1, down1, block))
-    up2, down2 = along(up1, 1, range(1, nz - 1)), along(down1, -1, range(1, nz - 1))
-    slot1 = jnp.where(z < 2, down1, up1)
-    flip0, flip1 = cross(block), cross(slot1)
-    up2, down2, w0, w1 = tie((up2, down2, w0, w1))
-    moves = [(2, 3), (1, 0), (0, 1), (3, 2)]
-    slot3 = jnp.where(z == 1, down2, jnp.where(z == 2, up2, block))
-    slot3 = lax.ppermute(slot3, "seq", [(i * 2 + b, j * 2 + b) for i, j in moves for b in range(2)])
-    slot2 = jnp.where(z < 2, down2, up2)
-    flip2 = cross(slot2)
-    a0 = project(yc, [(block, flip0), (slot1, flip1)], w_out, w0, w1)
-    flip2, slot2, a0 = tie((flip2, slot2, a0))
-    a2 = project(yc, [(slot2, flip2)], w_out, w0, w1)
-    slot3, a2 = tie((slot3, a2))
-    flip3 = cross(slot3)
-    b0 = reduce_y(*a0)
-    flip3, slot3, b0 = tie((flip3, slot3, b0))
-    a3 = project(yc, [(slot3, flip3)], w_out, w0, w1)
-    b2 = reduce_y(*a2)
-    chips = [(flat(a, b, 1 - c, d), flat(a, b, c, d)) for a, b, c, d in spots if c == a // 2]
-    c0 = b0.astype(F32) + lax.ppermute(b0, both, chips).astype(F32)
-    a3, b2 = tie((a3, b2))
-    b3 = reduce_y(*a3)
-    b3, c0 = tie((b3, c0))
-    r1 = deliver(1, c0[tokens:].astype(BF16), 0)
-    r2 = [deliver(2, b2, turn) for turn in range(2)]
-    r3 = [deliver(3, b3, turn) for turn in range(2)]
-    results = [c0[:tokens], r1, r2[0] + r2[1], r3[0] + r3[1]]
-    marks = []
-    for slot in range(nz):
-        mark = jnp.int32(-1)
-        for a in range(nz):
-            mark = jnp.where((z == table[a][slot]) & (grp // 2 == a // 2), a % 2, mark)
-        marks.append(mark)
-    pick = lambda which: sum(jnp.where(mark == which, r, 0.0) for mark, r in zip(marks, results)).astype(BF16)
-    at = (y ^ core).astype(jnp.int32).reshape(1)
-    return place(at, pick(core), cross(pick(1 - core)))
+    def reduce_core(full, rounded):
+        return (full + cross(rounded).astype(F32)).astype(BF16)
+
+    def deliver(slot, near, distant):
+        near_x, total = grp // 2 == z // 2, 0.0
+        for turn in range(2):
+            pairs = []
+            for a, b, c, d in spots:
+                at = slot if c ^ turn == a // 2 else slot + 2
+                pairs.append((flat(a, b, c, d), flat(a ^ at, d, a // 2, b)))
+            value = jnp.where(near_x, near, distant) if turn == 0 else jnp.where(near_x, distant, near)
+            moved = lax.ppermute(value, both, [(i, j) for i, j in pairs if i != j])
+            if any(i == j for i, j in pairs):
+                moved = jnp.where(near_x & (y == core), near, moved)
+            total = total + moved.astype(F32)
+        return total
+
+    slot1 = hop(block, (0, 1), (1, 0), (2, 3), (3, 2))
+    middle = hop(block, (1, 2), (2, 1))
+    other0 = across(block)
+    inward, outward = hop(slot1, (1, 2), (2, 1)), hop(middle, (1, 0), (2, 3))
+    other1 = across(slot1)
+    a0 = project(yc, [(block, other0)], w_out)
+    inward, outward, other1, a0 = tie((inward, outward, other1, a0))
+    last = hop(inward, (1, 0), (2, 3))
+    slot2 = jnp.where(inner, inward, outward)
+    other2 = across(slot2)
+    a1 = project(yc, [(slot1, other1)], w_out)
+    b0 = reduce_core(*a0)
+    last, other2, a1, b0 = tie((last, other2, a1, b0))
+    slot3 = jnp.where(inner, middle, last)
+    other3 = across(slot3)
+    b1 = reduce_core(*a1)
+    b2 = reduce_core(*project(yc, [(slot2, other2)], w_out))
+    other3, b2, b1 = tie((other3, b2, b1))
+    b3 = reduce_core(*project(yc, [(slot3, other3)], w_out))
+    even = deliver(0, b0, b2)
+    b3, = tie((b3,))
+    odd = deliver(1, b1, b3)
+    here = core == z % 2
+    mine, theirs = jnp.where(here, even, odd), jnp.where(here, odd, even)
+    return place(core.astype(jnp.int32).reshape(1), mine.astype(BF16), cross(theirs.astype(BF16)))
 
 
 def prefix(array, axis, combine, identity):

time: 150 us -> 138 us (0.920)
  the two profiles are of different devices: /device:TPU:0 before, /device:TPU:21 now
where the time goes in v4:
time: 138 us; the launch traced here: 137 us
  waiting for transfers between devices  67.8 us (49%)
  starting transfers between devices  43.3 us (31%)
  Pallas kernels  19 us (14%)
  local copies, waits for them, and re-layouts  6.38 us (5%)
    ppermute x4, waiting for transfers between devices, deliver(): moved = lax.ppermute(value, both, [(i, j) for i, j in pairs if i != j])  21.8 us
    ppermute x5, starting transfers between devices, pair_shards(): lax.ppermute(value, 'seq', [(i * 2 + b, j * 2 + b) for i, j in moves for...  18.2 us
    ppermute x5, waiting for transfers between devices, pair_shards(): lax.ppermute(value, 'seq', [(i * 2 + b, j * 2 + b) for i, j in moves for...  14.8 us
    pallas_call x4, Pallas kernels, project(): pl.pallas_call(project_kernel, grid_spec=pltpu.PrefetchScalarGridSpec(num...  12.4 us
    ppermute x4, waiting for transfers between devices, pair_shards(): across = lambda value: lax.ppermute(value, 'seq', flip)  11.7 us
    ppermute x5, starting transfers between devices, pair_shards(): cross = lambda value: lax.ppermute(value, 'grp', sibling)  10.4 us
    ppermute x2, waiting for transfers between devices, along(): return lax.ppermute(v, 'seq', pairs)  10.1 us
    ppermute x4, starting transfers between devices, deliver(): moved = lax.ppermute(value, both, [(i, j) for i, j in pairs if i != j])  7.54 us
  transfers between devices with their start and end apart: 22, of which 14 were waited for; matrix products, arithmetic and copies ran while one was open for 3% of the time, Pallas kernels for 8%

profile of v4, /device:TPU:21, one launch (start us, length us, event | category | flops | bytes accessed | tf_op | source)
XLA Modules:
  0.0 137.5 jit_solution(8852109833186560031)
XLA Ops:
  0.0 2.4 %pack.1 = (bf16[128,1408]{1,0:T(8,128)(2,1)}, bf16[128,1408]{1,0:T(8,128)(2,1)}) custom-call(s32[1]{0:T(128)} %bitcast.1.refs_0_, bf16[128,2048]{1,0:T(8,128)(2,1)} %refs_1_.1, bf16[128,256]{1,0:T(8,128)(2,1)} %refs_2_.5, bf16[128,256]{1,0:T(8,128)(2,1)} %refs_3_.5, f32[16,128]{1,0:T(8,128)} %bitcast.11), custom_call_target="tpu_custom_call" | custom-call | flops 1 | bytes 1 | tf_op jit(solution)/shard_map/pack/pallas_call | solution.py:82
  4.8 7.1 %collective-permute-done.refs_2_ = bf16[128,1408]{1,0:T(8,128)(2,1)S(1)} collective-permute-done((bf16[128,1408]{1,0:T(8,128)(2,1)}, bf16[128,1408]{1,0:T(8,128)(2,1)S(1)}, u32[]{:S(2)}, u32[]{:S(2)}) %collective-permute-start) | collective-permute-done | bytes 360480 | tf_op jit(solution)/shard_map/ppermute | solution.py:370
  13.0 1.2 local_state.1
  14.2 3.2 %collective-permute-start.1 = (bf16[144,1024]{1,0:T(8,128)(2,1)S(1)}, bf16[144,1024]{1,0:T(8,128)(2,1)S(1)}, u32[]{:S(2)}, u32[]{:S(2)}) collective-permute-start(bf16[144,1024]{1,0:T(8,128)(2,1)S(1)} %get-tuple-element.46.send_ref), channel_id=1, source_target_pairs={{0,8},{4,12},{8,16},{12,20},{16,24},{20,28},{1,9},{5,13},{9,17},{1... | collective-permute-start | bytes 884744 | tf_op jit(solution)/shard_map/ppermute | solution.py:367
  19.7 3.3 %collective-permute-done.1.got_ref.refs_4_ = bf16[144,1024]{1,0:T(8,128)(2,1)S(1)} collective-permute-done((bf16[144,1024]{1,0:T(8,128)(2,1)S(1)}, bf16[144,1024]{1,0:T(8,128)(2,1)S(1)}, u32[]{:S(2)}, u32[]{:S(2)}) %collective-permute-start.1) | collective-permute-done | bytes 294944 | tf_op jit(solution)/shard_map/ppermute | solution.py:367
  23.1 1.3 collective-permute-start.2
  24.4 6.8 %collective-permute-done.2.refs_5_ = bf16[128,1024]{1,0:T(8,128)(2,1)S(1)} collective-permute-done((bf16[128,1024]{1,0:T(8,128)(2,1)S(1)}, bf16[128,1024]{1,0:T(8,128)(2,1)S(1)}, u32[]{:S(2)}, u32[]{:S(2)}) %collective-permute-start.2) | collective-permute-done | bytes 262176 | tf_op jit(solution)/shard_map/ppermute | solution.py:367
  32.2 9.7 %collective-permute-start.4 = (bf16[256,1024]{1,0:T(8,128)(2,1)S(1)}, bf16[256,1024]{1,0:T(8,128)(2,1)S(1)}, u32[]{:S(2)}, u32[]{:S(2)}) collective-permute-start(bf16[256,1024]{1,0:T(8,128)(2,1)S(1)} %finish.1.refs_0_), channel_id=1, source_target_pairs={{0,8},{4,12},{8,0},{12,4},{16,24},{20,28},{24,16},{28,20},{1,9},{5... | collective-permute-start | bytes 1572872 | tf_op jit(solution)/shard_map/ppermute | solution.py:386
  42.0 1.9 %collective-permute-start.6 = (bf16[256,1024]{1,0:T(8,128)(2,1)S(1)}, bf16[256,1024]{1,0:T(8,128)(2,1)S(1)}, u32[]{:S(2)}, u32[]{:S(2)}) collective-permute-start(bf16[256,1024]{1,0:T(8,128)(2,1)S(1)} %finish.1.refs_0_), channel_id=1, source_target_pairs={{8,16},{12,20},{16,8},{20,12},{9,17},{13,21},{17,9},{21,13},{10,18... | collective-permute-start | bytes 1572872 | tf_op jit(solution)/shard_map/ppermute | solution.py:386
  44.2 9.6 %collective-permute-done.4.refs_0_ = bf16[256,1024]{1,0:T(8,128)(2,1)S(1)} collective-permute-done((bf16[256,1024]{1,0:T(8,128)(2,1)S(1)}, bf16[256,1024]{1,0:T(8,128)(2,1)S(1)}, u32[]{:S(2)}, u32[]{:S(2)}) %collective-permute-start.4) | collective-permute-done | bytes 524320 | tf_op jit(solution)/shard_map/ppermute | solution.py:386
  53.8 1.9 %collective-permute-start.5 = (bf16[256,1024]{1,0:T(8,128)(2,1)S(1)}, bf16[256,1024]{1,0:T(8,128)(2,1)S(1)}, u32[]{:S(2)}, u32[]{:S(2)}) collective-permute-start(bf16[256,1024]{1,0:T(8,128)(2,1)S(1)} %collective-permute-done.4.refs_0_), channel_id=1, source_target_pairs={{8,16},{12,20},{16,8},{20,12},{9,17},{13,21},{17,9},{21,13},{10,18... | collective-permute-start | bytes 1572872 | tf_op jit(solution)/shard_map/ppermute | solution.py:386
  56.5 2.1 %collective-permute-start.7 = (bf16[256,1024]{1,0:T(8,128)(2,1)S(1)}, bf16[256,1024]{1,0:T(8,128)(2,1)}, u32[]{:S(2)}, u32[]{:S(2)}) collective-permute-start(bf16[256,1024]{1,0:T(8,128)(2,1)S(1)} %collective-permute-done.6), channel_id=1, source_target_pairs={{8,0},{12,4},{16,24},{20,28},{9,1},{13,5},{17,25},{21,29},{10,2},{... | collective-permute-start | bytes 1572872 | tf_op jit(solution)/shard_map/ppermute | solution.py:386
  58.9 2.2 %copy-done = bf16[2048,1024]{1,0:T(8,128)(2,1)S(1)} copy-done((bf16[2048,1024]{1,0:T(8,128)(2,1)S(1)}, bf16[2048,1024]{1,0:T(8,128)(2,1)}, u32[]{:S(2)}) %copy-start) | copy-done | bytes 4194328
  61.1 3.1 %project.4 = (f32[128,1024]{1,0:T(8,128)S(1)}, bf16[128,1024]{1,0:T(8,128)(2,1)S(1)}) custom-call(s32[2]{0:T(128)S(1)} %pad_add_fusion.yc_ref, bf16[256,1024]{1,0:T(8,128)(2,1)S(1)} %finish.1.refs_0_, bf16[256,1024]{1,0:T(8,128)(2,1)S(1)} %collective-permute-done.9.refs_1_, bf16[2048,1024]{1,0:T(8,128)(2,1)S(1)} %copy-done, bf16[2048,1024]{1,0:T(8,128)(2,1)S(1)} %copy-done), custom_call_target="tpu_custom_call" | custom-call | flops 1 | bytes 1 | tf_op jit(solution)/shard_map/project/pallas_call | solution.py:296
  64.2 3.8 %collective-permute-done.5 = bf16[256,1024]{1,0:T(8,128)(2,1)S(1)} collective-permute-done((bf16[256,1024]{1,0:T(8,128)(2,1)S(1)}, bf16[256,1024]{1,0:T(8,128)(2,1)S(1)}, u32[]{:S(2)}, u32[]{:S(2)}) %collective-permute-start.5) | collective-permute-done | bytes 524320 | tf_op jit(solution)/shard_map/ppermute | solution.py:386
  68.0 2.3 %collective-permute-done.8.refs_1_ = bf16[256,1024]{1,0:T(8,128)(2,1)S(1)} collective-permute-done((bf16[256,1024]{1,0:T(8,128)(2,1)S(1)}, bf16[256,1024]{1,0:T(8,128)(2,1)S(1)}, u32[]{:S(2)}, u32[]{:S(2)}) %collective-permute-start.8) | collective-permute-done | bytes 524320 | tf_op jit(solution)/shard_map/ppermute | solution.py:388
  70.7 2.5 %collective-permute-start.10 = (bf16[256,1024]{1,0:T(8,128)(2,1)S(1)}, bf16[256,1024]{1,0:T(8,128)(2,1)S(1)}, u32[]{:S(2)}, u32[]{:S(2)}) collective-permute-start(bf16[256,1024]{1,0:T(8,128)(2,1)S(1)} %collective-permute-done.5), channel_id=1, source_target_pairs={{8,0},{12,4},{16,24},{20,28},{9,1},{13,5},{17,25},{21,29},{10,2},{... | collective-permute-start | bytes 1572872 | tf_op jit(solution)/shard_map/ppermute | solution.py:386
  73.2 3.0 %collective-permute-start.12 = (bf16[128,1024]{1,0:T(8,128)(2,1)S(1)}, bf16[128,1024]{1,0:T(8,128)(2,1)S(1)}, u32[]{:S(2)}, u32[]{:S(2)}) collective-permute-start(bf16[128,1024]{1,0:T(8,128)(2,1)S(1)} %get-tuple-element.64), channel_id=1, source_target_pairs={{0,1},{1,0},{2,3},{3,2},{4,5},{5,4},{6,7},{7,6},{8,9},{9,8},{10,11... | collective-permute-start | bytes 786440 | tf_op jit(solution)/shard_map/ppermute | solution.py:389
  76.2 3.1 %project.5 = (f32[128,1024]{1,0:T(8,128)S(1)}, bf16[128,1024]{1,0:T(8,128)(2,1)S(1)}) custom-call(s32[2]{0:T(128)S(1)} %pad_add_fusion.yc_ref, bf16[256,1024]{1,0:T(8,128)(2,1)S(1)} %collective-permute-done.4.refs_0_, bf16[256,1024]{1,0:T(8,128)(2,1)S(1)} %collective-permute-done.8.refs_1_, bf16[2048,1024]{1,0:T(8,128)(2,1)S(1)} %copy-done.1, ...), custom_call_target="tpu_custom_call" | custom-call | flops 1 | bytes 1 | tf_op jit(solution)/shard_map/project/pallas_call | solution.py:296
  79.4 1.8 %collective-permute-done.11.refs_1_ = bf16[256,1024]{1,0:T(8,128)(2,1)S(1)} collective-permute-done((bf16[256,1024]{1,0:T(8,128)(2,1)S(1)}, bf16[256,1024]{1,0:T(8,128)(2,1)S(1)}, u32[]{:S(2)}, u32[]{:S(2)}) %collective-permute-start.11) | collective-permute-done | bytes 524320 | tf_op jit(solution)/shard_map/ppermute | solution.py:388
  81.8 3.5 %collective-permute-start.15 = (bf16[128,1024]{1,0:T(8,128)(2,1)S(1)}, bf16[128,1024]{1,0:T(8,128)(2,1)S(1)}, u32[]{:S(2)}, u32[]{:S(2)}) collective-permute-start(bf16[128,1024]{1,0:T(8,128)(2,1)S(1)} %get-tuple-element.71), channel_id=1, source_target_pairs={{0,1},{1,0},{2,3},{3,2},{4,5},{5,4},{6,7},{7,6},{8,9},{9,8},{10,11... | collective-permute-start | bytes 786440 | tf_op jit(solution)/shard_map/ppermute | solution.py:389
  85.4 1.3 collective-permute-start.13
  86.7 3.1 %project.6 = (f32[128,1024]{1,0:T(8,128)S(1)}, bf16[128,1024]{1,0:T(8,128)(2,1)S(1)}) custom-call(s32[2]{0:T(128)S(1)} %pad_add_fusion.yc_ref, bf16[256,1024]{1,0:T(8,128)(2,1)S(1)} %broadcast_select_fusion.1.refs_0_, bf16[256,1024]{1,0:T(8,128)(2,1)S(1)} %collective-permute-done.11.refs_1_, bf16[2048,1024]{1,0:T(8,128)(2,1)S(1)} %copy-done.1, ...), custom_call_target="tpu_custom_call" | custom-call | flops 1 | bytes 1 | tf_op jit(solution)/shard_map/project/pallas_call | solution.py:296
  90.2 1.2 collective-permute-done.14
  91.4 7.6 %collective-permute-done.13.refs_1_ = bf16[256,1024]{1,0:T(8,128)(2,1)S(1)} collective-permute-done((bf16[256,1024]{1,0:T(8,128)(2,1)S(1)}, bf16[256,1024]{1,0:T(8,128)(2,1)S(1)}, u32[]{:S(2)}, u32[]{:S(2)}) %collective-permute-start.13) | collective-permute-done | bytes 524320 | tf_op jit(solution)/shard_map/ppermute | solution.py:388
  99.0 3.1 %project.7 = (f32[128,1024]{1,0:T(8,128)S(1)}, bf16[128,1024]{1,0:T(8,128)(2,1)S(1)}) custom-call(s32[2]{0:T(128)S(1)} %pad_add_fusion.yc_ref, bf16[256,1024]{1,0:T(8,128)(2,1)S(1)} %broadcast_select_fusion.refs_0_, bf16[256,1024]{1,0:T(8,128)(2,1)S(1)} %collective-permute-done.13.refs_1_, bf16[2048,1024]{1,0:T(8,128)(2,1)S(1)} %copy-done.1, ...), custom_call_target="tpu_custom_call" | custom-call | flops 1 | bytes 1 | tf_op jit(solution)/shard_map/project/pallas_call | solution.py:296
  103.0 5.8 %collective-permute-start.16 = (bf16[128,1024]{1,0:T(8,128)(2,1)S(1)}, bf16[128,1024]{1,0:T(8,128)(2,1)S(1)}, u32[]{:S(2)}, u32[]{:S(2)}) collective-permute-start(bf16[128,1024]{1,0:T(8,128)(2,1)S(1)} %get-tuple-element.79), channel_id=1, source_target_pairs={{1,4},{2,16},{3,20},{4,1},{6,17},{7,21},{9,12},{10,24},{11,28},{12... | collective-permute-start | bytes 786440 | tf_op jit(solution)/shard_map/ppermute | solution.py:402
  109.5 1.2 collective-permute-start.20
  110.7 14.4 %collective-permute-done.16 = bf16[128,1024]{1,0:T(8,128)(2,1)S(1)} collective-permute-done((bf16[128,1024]{1,0:T(8,128)(2,1)S(1)}, bf16[128,1024]{1,0:T(8,128)(2,1)S(1)}, u32[]{:S(2)}, u32[]{:S(2)}) %collective-permute-start.16) | collective-permute-done | bytes 262176 | tf_op jit(solution)/shard_map/ppermute | solution.py:402
  125.1 7.4 %collective-permute-done.19 = bf16[128,1024]{1,0:T(8,128)(2,1)S(1)} collective-permute-done((bf16[128,1024]{1,0:T(8,128)(2,1)S(1)}, bf16[128,1024]{1,0:T(8,128)(2,1)S(1)}, u32[]{:S(2)}, u32[]{:S(2)}) %collective-permute-start.19) | collective-permute-done | bytes 262176 | tf_op jit(solution)/shard_map/ppermute | solution.py:402
  132.7 2.8 %collective-permute-start.21 = (bf16[128,1024]{1,0:T(8,128)(2,1)S(1)}, bf16[128,1024]{1,0:T(8,128)(2,1)S(1)}, u32[]{:S(2)}, u32[]{:S(2)}) collective-permute-start(bf16[128,1024]{1,0:T(8,128)(2,1)S(1)} %get-tuple-element.77), channel_id=1, source_target_pairs={{0,1},{1,0},{2,3},{3,2},{4,5},{5,4},{6,7},{7,6},{8,9},{9,8},{10,11... | collective-permute-start | bytes 786440 | tf_op jit(solution)/shard_map/ppermute | solution.py:389
  135.5 1.2 collective-permute-done.21.got_ref
  (45 shorter events, 12.5 us)
Async XLA Ops:
  0.0 31.2 %copy-start.2 = (bf16[128,2048]{1,0:T(8,128)(2,1)S(1)}, bf16[128,2048]{1,0:T(8,128)(2,1)}, u32[]{:S(2)}) copy-start(bf16[128,2048]{1,0:T(8,128)(2,1)} %refs_6_.1) | copy-start | bytes 1572868
  2.4 9.5 %collective-permute-start = (bf16[128,1408]{1,0:T(8,128)(2,1)}, bf16[128,1408]{1,0:T(8,128)(2,1)S(1)}, u32[]{:S(2)}, u32[]{:S(2)}) collective-permute-start(bf16[128,1408]{1,0:T(8,128)(2,1)} %get-tuple-element.42), channel_id=1, source_target_pairs={{0,4},{4,0},{8,12},{12,8},{16,20},{20,16},{24,28},{28,24},{1,5},{5... | collective-permute-start | bytes 1081352 | tf_op jit(solution)/shard_map/ppermute | solution.py:370
  12.0 1.0 copy-start.3
  14.2 8.8 %collective-permute-start.1 = (bf16[144,1024]{1,0:T(8,128)(2,1)S(1)}, bf16[144,1024]{1,0:T(8,128)(2,1)S(1)}, u32[]{:S(2)}, u32[]{:S(2)}) collective-permute-start(bf16[144,1024]{1,0:T(8,128)(2,1)S(1)} %get-tuple-element.46.send_ref), channel_id=1, source_target_pairs={{0,8},{4,12},{8,16},{12,20},{16,24},{20,28},{1,9},{5,13},{9,17},{1... | collective-permute-start | bytes 884744 | tf_op jit(solution)/shard_map/ppermute | solution.py:367
  18.4 6.0 %collective-permute-start.3 = (bf16[128,1024]{1,0:T(8,128)(2,1)S(1)}, bf16[128,1024]{1,0:T(8,128)(2,1)S(1)}, u32[]{:S(2)}, u32[]{:S(2)}) collective-permute-start(bf16[128,1024]{1,0:T(8,128)(2,1)S(1)} %constant_dynamic-slice_fusion), channel_id=1, source_target_pairs={{0,4},{4,0},{8,12},{12,8},{16,20},{20,16},{24,28},{28,24},{1,5},{5... | collective-permute-start | bytes 786440 | tf_op jit(solution)/shard_map/ppermute | solution.py:375
  23.1 8.1 %collective-permute-start.2 = (bf16[128,1024]{1,0:T(8,128)(2,1)S(1)}, bf16[128,1024]{1,0:T(8,128)(2,1)S(1)}, u32[]{:S(2)}, u32[]{:S(2)}) collective-permute-start(bf16[128,1024]{1,0:T(8,128)(2,1)S(1)} %join.1), channel_id=1, source_target_pairs={{0,16},{4,20},{8,24},{12,28},{1,17},{5,21},{9,25},{13,29},{2,18},{... | collective-permute-start | bytes 786440 | tf_op jit(solution)/shard_map/ppermute | solution.py:367
  32.2 21.6 %collective-permute-start.4 = (bf16[256,1024]{1,0:T(8,128)(2,1)S(1)}, bf16[256,1024]{1,0:T(8,128)(2,1)S(1)}, u32[]{:S(2)}, u32[]{:S(2)}) collective-permute-start(bf16[256,1024]{1,0:T(8,128)(2,1)S(1)} %finish.1.refs_0_), channel_id=1, source_target_pairs={{0,8},{4,12},{8,0},{12,4},{16,24},{20,28},{24,16},{28,20},{1,9},{5... | collective-permute-start | bytes 1572872 | tf_op jit(solution)/shard_map/ppermute | solution.py:386
  42.0 14.5 %collective-permute-start.6 = (bf16[256,1024]{1,0:T(8,128)(2,1)S(1)}, bf16[256,1024]{1,0:T(8,128)(2,1)S(1)}, u32[]{:S(2)}, u32[]{:S(2)}) collective-permute-start(bf16[256,1024]{1,0:T(8,128)(2,1)S(1)} %finish.1.refs_0_), channel_id=1, source_target_pairs={{8,16},{12,20},{16,8},{20,12},{9,17},{13,21},{17,9},{21,13},{10,18... | collective-permute-start | bytes 1572872 | tf_op jit(solution)/shard_map/ppermute | solution.py:386
  43.9 15.0 %collective-permute-start.9 = (bf16[256,1024]{1,0:T(8,128)(2,1)S(1)}, bf16[256,1024]{1,0:T(8,128)(2,1)S(1)}, u32[]{:S(2)}, u32[]{:S(2)}) collective-permute-start(bf16[256,1024]{1,0:T(8,128)(2,1)S(1)} %finish.1.refs_0_), channel_id=1, source_target_pairs={{0,4},{4,0},{8,12},{12,8},{16,20},{20,16},{24,28},{28,24},{1,5},{5... | collective-permute-start | bytes 1572872 | tf_op jit(solution)/shard_map/ppermute | solution.py:388
  53.8 14.2 %collective-permute-start.5 = (bf16[256,1024]{1,0:T(8,128)(2,1)S(1)}, bf16[256,1024]{1,0:T(8,128)(2,1)S(1)}, u32[]{:S(2)}, u32[]{:S(2)}) collective-permute-start(bf16[256,1024]{1,0:T(8,128)(2,1)S(1)} %collective-permute-done.4.refs_0_), channel_id=1, source_target_pairs={{8,16},{12,20},{16,8},{20,12},{9,17},{13,21},{17,9},{21,13},{10,18... | collective-permute-start | bytes 1572872 | tf_op jit(solution)/shard_map/ppermute | solution.py:386
  56.5 11.5 %collective-permute-start.7 = (bf16[256,1024]{1,0:T(8,128)(2,1)S(1)}, bf16[256,1024]{1,0:T(8,128)(2,1)}, u32[]{:S(2)}, u32[]{:S(2)}) collective-permute-start(bf16[256,1024]{1,0:T(8,128)(2,1)S(1)} %collective-permute-done.6), channel_id=1, source_target_pairs={{8,0},{12,4},{16,24},{20,28},{9,1},{13,5},{17,25},{21,29},{10,2},{... | collective-permute-start | bytes 1572872 | tf_op jit(solution)/shard_map/ppermute | solution.py:386
  58.6 11.7 %collective-permute-start.8 = (bf16[256,1024]{1,0:T(8,128)(2,1)S(1)}, bf16[256,1024]{1,0:T(8,128)(2,1)S(1)}, u32[]{:S(2)}, u32[]{:S(2)}) collective-permute-start(bf16[256,1024]{1,0:T(8,128)(2,1)S(1)} %collective-permute-done.4.refs_0_), channel_id=1, source_target_pairs={{0,4},{4,0},{8,12},{12,8},{16,20},{20,16},{24,28},{28,24},{1,5},{5... | collective-permute-start | bytes 1572872 | tf_op jit(solution)/shard_map/ppermute | solution.py:388
  58.9 2.2 %copy-start = (bf16[2048,1024]{1,0:T(8,128)(2,1)S(1)}, bf16[2048,1024]{1,0:T(8,128)(2,1)}, u32[]{:S(2)}) copy-start(bf16[2048,1024]{1,0:T(8,128)(2,1)} %refs_3_.9) | copy-start | bytes 12582916
  61.1 15.1 %copy-start.1 = (bf16[2048,1024]{1,0:T(8,128)(2,1)S(1)}, bf16[2048,1024]{1,0:T(8,128)(2,1)}, u32[]{:S(2)}) copy-start(bf16[2048,1024]{1,0:T(8,128)(2,1)} %refs_3_.9) | copy-start | bytes 12582916
  70.3 10.9 %collective-permute-start.11 = (bf16[256,1024]{1,0:T(8,128)(2,1)S(1)}, bf16[256,1024]{1,0:T(8,128)(2,1)S(1)}, u32[]{:S(2)}, u32[]{:S(2)}) collective-permute-start(bf16[256,1024]{1,0:T(8,128)(2,1)S(1)} %broadcast_select_fusion.1.refs_0_), channel_id=1, source_target_pairs={{0,4},{4,0},{8,12},{12,8},{16,20},{20,16},{24,28},{28,24},{1,5},{5... | collective-permute-start | bytes 1572872 | tf_op jit(solution)/shard_map/ppermute | solution.py:388
  70.7 11.1 %collective-permute-start.10 = (bf16[256,1024]{1,0:T(8,128)(2,1)S(1)}, bf16[256,1024]{1,0:T(8,128)(2,1)S(1)}, u32[]{:S(2)}, u32[]{:S(2)}) collective-permute-start(bf16[256,1024]{1,0:T(8,128)(2,1)S(1)} %collective-permute-done.5), channel_id=1, source_target_pairs={{8,0},{12,4},{16,24},{20,28},{9,1},{13,5},{17,25},{21,29},{10,2},{... | collective-permute-start | bytes 1572872 | tf_op jit(solution)/shard_map/ppermute | solution.py:386
  73.2 6.1 %collective-permute-start.12 = (bf16[128,1024]{1,0:T(8,128)(2,1)S(1)}, bf16[128,1024]{1,0:T(8,128)(2,1)S(1)}, u32[]{:S(2)}, u32[]{:S(2)}) collective-permute-start(bf16[128,1024]{1,0:T(8,128)(2,1)S(1)} %get-tuple-element.64), channel_id=1, source_target_pairs={{0,1},{1,0},{2,3},{3,2},{4,5},{5,4},{6,7},{7,6},{8,9},{9,8},{10,11... | collective-permute-start | bytes 786440 | tf_op jit(solution)/shard_map/ppermute | solution.py:389
  81.8 8.3 %collective-permute-start.15 = (bf16[128,1024]{1,0:T(8,128)(2,1)S(1)}, bf16[128,1024]{1,0:T(8,128)(2,1)S(1)}, u32[]{:S(2)}, u32[]{:S(2)}) collective-permute-start(bf16[128,1024]{1,0:T(8,128)(2,1)S(1)} %get-tuple-element.71), channel_id=1, source_target_pairs={{0,1},{1,0},{2,3},{3,2},{4,5},{5,4},{6,7},{7,6},{8,9},{9,8},{10,11... | collective-permute-start | bytes 786440 | tf_op jit(solution)/shard_map/ppermute | solution.py:389
  85.4 13.6 %collective-permute-start.13 = (bf16[256,1024]{1,0:T(8,128)(2,1)S(1)}, bf16[256,1024]{1,0:T(8,128)(2,1)S(1)}, u32[]{:S(2)}, u32[]{:S(2)}) collective-permute-start(bf16[256,1024]{1,0:T(8,128)(2,1)S(1)} %broadcast_select_fusion.refs_0_), channel_id=1, source_target_pairs={{0,4},{4,0},{8,12},{12,8},{16,20},{20,16},{24,28},{28,24},{1,5},{5... | collective-permute-start | bytes 1572872 | tf_op jit(solution)/shard_map/ppermute | solution.py:388
  89.8 1.6 %collective-permute-start.14 = (bf16[128,1024]{1,0:T(8,128)(2,1)S(1)}, bf16[128,1024]{1,0:T(8,128)(2,1)S(1)}, u32[]{:S(2)}, u32[]{:S(2)}) collective-permute-start(bf16[128,1024]{1,0:T(8,128)(2,1)S(1)} %get-tuple-element.69), channel_id=1, source_target_pairs={{0,1},{1,0},{2,3},{3,2},{4,5},{5,4},{6,7},{7,6},{8,9},{9,8},{10,11... | collective-permute-start | bytes 786440 | tf_op jit(solution)/shard_map/ppermute | solution.py:389
  102.1 6.8 %collective-permute-start.18 = (bf16[128,1024]{1,0:T(8,128)(2,1)S(1)}, bf16[128,1024]{1,0:T(8,128)(2,1)S(1)}, u32[]{:S(2)}, u32[]{:S(2)}) collective-permute-start(bf16[128,1024]{1,0:T(8,128)(2,1)S(1)} %get-tuple-element.76), channel_id=1, source_target_pairs={{0,1},{1,0},{2,3},{3,2},{4,5},{5,4},{6,7},{7,6},{8,9},{9,8},{10,11... | collective-permute-start | bytes 786440 | tf_op jit(solution)/shard_map/ppermute | solution.py:389
  103.0 22.1 %collective-permute-start.16 = (bf16[128,1024]{1,0:T(8,128)(2,1)S(1)}, bf16[128,1024]{1,0:T(8,128)(2,1)S(1)}, u32[]{:S(2)}, u32[]{:S(2)}) collective-permute-start(bf16[128,1024]{1,0:T(8,128)(2,1)S(1)} %get-tuple-element.79), channel_id=1, source_target_pairs={{1,4},{2,16},{3,20},{4,1},{6,17},{7,21},{9,12},{10,24},{11,28},{12... | collective-permute-start | bytes 786440 | tf_op jit(solution)/shard_map/ppermute | solution.py:402
  108.8 16.3 %collective-permute-start.17 = (bf16[128,1024]{1,0:T(8,128)(2,1)S(1)}, bf16[128,1024]{1,0:T(8,128)(2,1)S(1)}, u32[]{:S(2)}, u32[]{:S(2)}) collective-permute-start(bf16[128,1024]{1,0:T(8,128)(2,1)S(1)} %get-tuple-element.80), channel_id=1, source_target_pairs={{0,16},{1,20},{2,0},{3,4},{4,17},{5,21},{6,1},{7,5},{8,24},{9,28},... | collective-permute-start | bytes 786440 | tf_op jit(solution)/shard_map/ppermute | solution.py:402
  109.0 23.5 %collective-permute-start.19 = (bf16[128,1024]{1,0:T(8,128)(2,1)S(1)}, bf16[128,1024]{1,0:T(8,128)(2,1)S(1)}, u32[]{:S(2)}, u32[]{:S(2)}) collective-permute-start(bf16[128,1024]{1,0:T(8,128)(2,1)S(1)} %get-tuple-element.81), channel_id=1, source_target_pairs={{0,8},{1,12},{2,24},{3,28},{4,9},{5,13},{6,25},{7,29},{8,0},{9,4},... | collective-permute-start | bytes 786440 | tf_op jit(solution)/shard_map/ppermute | solution.py:402
  109.5 23.0 %collective-permute-start.20 = (bf16[128,1024]{1,0:T(8,128)(2,1)S(1)}, bf16[128,1024]{1,0:T(8,128)(2,1)S(1)}, u32[]{:S(2)}, u32[]{:S(2)}) collective-permute-start(bf16[128,1024]{1,0:T(8,128)(2,1)S(1)} %get-tuple-element.82), channel_id=1, source_target_pairs={{0,24},{1,28},{2,8},{3,12},{4,25},{5,29},{6,9},{7,13},{8,16},{9,20... | collective-permute-start | bytes 786440 | tf_op jit(solution)/shard_map/ppermute | solution.py:402
  132.7 3.9 %collective-permute-start.21 = (bf16[128,1024]{1,0:T(8,128)(2,1)S(1)}, bf16[128,1024]{1,0:T(8,128)(2,1)S(1)}, u32[]{:S(2)}, u32[]{:S(2)}) collective-permute-start(bf16[128,1024]{1,0:T(8,128)(2,1)S(1)} %get-tuple-element.77), channel_id=1, source_target_pairs={{0,1},{1,0},{2,3},{3,2},{4,5},{5,4},{6,7},{7,6},{8,9},{9,8},{10,11... | collective-permute-start | bytes 786440 | tf_op jit(solution)/shard_map/ppermute | solution.py:389

commit v5 on v4

--- a/solution.py
+++ b/solution.py
@@ -265,55 +265,60 @@
     )(y, local, cs, scal, one, two, gate, got, gain)
 
 
-def project_kernel(yc_ref, *refs):
-    *pair_refs, first_ref, second_ref, keep_ref, send_ref, both_ref = refs
-    slots, depth = len(pair_refs) // 2, pair_refs[0].shape[1]
-    kept = keep_ref.shape[0]
-    tokens = kept // slots
+def project_kernel(yc_ref, own_ref, *refs):
+    *got_refs, first_ref, second_ref, keep_ref, send_ref, both_ref = refs
+    tokens, depth = keep_ref.shape[0], own_ref.shape[1]
     core = yc_ref[1]
 
     @pl.when(pl.program_id(0) == 0)
     def _():
-        for slot in range(slots):
-            own_ref, got_ref = pair_refs[2 * slot], pair_refs[2 * slot + 1]
+        def fill(lower, upper):
             for k in range(2):
-                at = pl.ds(pl.multiple_of(jnp.where(core == 0, k, 1 - k) * tokens, tokens), tokens)
-                rows = pl.ds(k * kept + slot * tokens, tokens)
-                both_ref[rows, :depth] = own_ref[at, :]
-                both_ref[rows, depth:] = got_ref[at, :]
+                rows = pl.ds(pl.multiple_of(jnp.where(core == 0, k, 1 - k) * tokens, tokens), tokens)
+                both_ref[rows, :depth] = own_ref[k * tokens : (k + 1) * tokens, :]
+                both_ref[rows, depth:] = (lower, upper)[k]()
+
+        whole = got_refs[0]
+        halves = lambda: fill(lambda: whole[:tokens, :], lambda: whole[tokens:, :])
+        if len(got_refs) == 1:
+            halves()
+        else:
+            pl.when(yc_ref[2] == 1)(halves)
+            pl.when(yc_ref[2] == 0)(lambda: fill(lambda: got_refs[1][...], lambda: got_refs[2][...]))
 
     part = jnp.dot(both_ref[:, :depth], first_ref[...], preferred_element_type=F32)
     part = part + jnp.dot(both_ref[:, depth:], second_ref[...], preferred_element_type=F32)
-    keep_ref[...] = part[:kept, :]
-    send_ref[...] = part[kept:, :].astype(BF16)
-
-
-def project(yc, pairs, w):
-    length, depth = pairs[0][0].shape
-    kept = len(pairs) * length // 2
-    cols = w.shape[1]
+    keep_ref[...] = part[:tokens, :]
+    send_ref[...] = part[tokens:, :].astype(BF16)
+
+
+def project(yc, own, got, w):
+    length, depth = own.shape
+    tokens, cols = length // 2, w.shape[1]
     tile = min(cols, 256)
+    whole = lambda a: pl.BlockSpec(a.shape, lambda i, yc: (0, 0))
     return pl.pallas_call(
         project_kernel,
         grid_spec=pltpu.PrefetchScalarGridSpec(
             num_scalar_prefetch=1,
             grid=(cols // tile,),
-            in_specs=[pl.BlockSpec((length, depth), lambda i, yc: (0, 0))] * (2 * len(pairs))
+            in_specs=[whole(own)]
+            + [whole(v) for v in got]
             + [
                 pl.BlockSpec((depth, tile), lambda i, yc: (yc[0], i)),
                 pl.BlockSpec((depth, tile), lambda i, yc: (1 - yc[0], i)),
             ],
             out_specs=[
-                pl.BlockSpec((kept, tile), lambda i, yc: (0, i)),
-                pl.BlockSpec((kept, tile), lambda i, yc: (0, i)),
+                pl.BlockSpec((tokens, tile), lambda i, yc: (0, i)),
+                pl.BlockSpec((tokens, tile), lambda i, yc: (0, i)),
             ],
-            scratch_shapes=[pltpu.VMEM((2 * kept, 2 * depth), BF16)],
+            scratch_shapes=[pltpu.VMEM((length, 2 * depth), BF16)],
         ),
-        out_shape=[jax.ShapeDtypeStruct((kept, cols), F32), jax.ShapeDtypeStruct((kept, cols), BF16)],
+        out_shape=[jax.ShapeDtypeStruct((tokens, cols), F32), jax.ShapeDtypeStruct((tokens, cols), BF16)],
         compiler_params=params(1),
-        cost_estimate=cost(8.0 * kept * depth * cols, 6e6),
+        cost_estimate=cost(4.0 * length * depth * cols, 6e6),
         name="project",
-    )(yc, *[v for pair in pairs for v in pair], w, w)
+    )(yc, own, *got, w, w)
 
 
 def place_kernel(at_ref, mine_ref, got_ref, out_ref):
@@ -348,7 +353,6 @@
     seq, grp = lax.axis_index("seq"), lax.axis_index("grp")
     z, y = seq // 2, seq % 2
     yv = y.astype(jnp.int32).reshape(1)
-    yc = jnp.stack([y, grp % 2]).astype(jnp.int32)
     dt_raw = dt_raw.T
     both = ("seq", "grp")
     core = grp % 2
@@ -385,6 +389,7 @@
 
     hop = lambda value, *moves: lax.ppermute(value, "seq", [(i * 2 + b, j * 2 + b) for i, j in moves for b in range(2)])
     inner = (z == 1) | (z == 2)
+    yc = jnp.stack([y, core, inner]).astype(jnp.int32)
     across = lambda value: lax.ppermute(value, "seq", flip)
     cross = lambda value: lax.ppermute(value, "grp", sibling)
 
@@ -410,20 +415,23 @@
     other0 = across(block)
     inward, outward = hop(slot1, (1, 2), (2, 1)), hop(middle, (1, 0), (2, 3))
     other1 = across(slot1)
-    a0 = project(yc, [(block, other0)], w_out)
+    a0 = project(yc, block, [other0], w_out)
     inward, outward, other1, a0 = tie((inward, outward, other1, a0))
     last = hop(inward, (1, 0), (2, 3))
     slot2 = jnp.where(inner, inward, outward)
     other2 = across(slot2)
-    a1 = project(yc, [(slot1, other1)], w_out)
+    a1 = project(yc, slot1, [other1], w_out)
     b0 = reduce_core(*a0)
-    last, other2, a1, b0 = tie((last, other2, a1, b0))
+    inner3 = hop(other0, (1, 2), (2, 1))
+    last, other2, inner3, a1, b0 = tie((last, other2, inner3, a1, b0))
     slot3 = jnp.where(inner, middle, last)
-    other3 = across(slot3)
+    lower3 = lax.ppermute(last[:tokens], "seq", [(i * 2 + b, i * 2 + 1 - b) for i in (0, 3) for b in range(2)])
+    upper3 = hop(other2[tokens:], (1, 0), (2, 3))
     b1 = reduce_core(*a1)
-    b2 = reduce_core(*project(yc, [(slot2, other2)], w_out))
-    other3, b2, b1 = tie((other3, b2, b1))
-    b3 = reduce_core(*project(yc, [(slot3, other3)], w_out))
+    a2 = project(yc, slot2, [other2], w_out)
+    lower3, upper3, a2, b1 = tie((lower3, upper3, a2, b1))
+    b2 = reduce_core(*a2)
+    b3 = reduce_core(*project(yc, slot3, [inner3, lower3, upper3], w_out))
     even = deliver(0, b0, b2)
     b3, = tie((b3,))
     odd = deliver(1, b1, b3)

time: 138 us -> 136 us (0.986)
  the two profiles are of different devices: /device:TPU:21 before, /device:TPU:2 now
where the time goes in v5:
time: 136 us; the launch traced here: 135 us
  waiting for transfers between devices  68 us (50%)
  starting transfers between devices  39.4 us (29%)
  Pallas kernels  19 us (14%)
  local copies, waits for them, and re-layouts  6.41 us (5%)
  other arithmetic  1.84 us (1%)
    ppermute x7, waiting for transfers between devices, pair_shards(): lax.ppermute(value, 'seq', [(i * 2 + b, j * 2 + b) for i, j in moves for...  24 us
    ppermute x4, waiting for transfers between devices, deliver(): moved = lax.ppermute(value, both, [(i, j) for i, j in pairs if i != j])  19.7 us
    ppermute x7, starting transfers between devices, pair_shards(): lax.ppermute(value, 'seq', [(i * 2 + b, j * 2 + b) for i, j in moves for...  12.9 us
    pallas_call x4, Pallas kernels, project(): pl.pallas_call(project_kernel, grid_spec=pltpu.PrefetchScalarGridSpec(num...  12.4 us
    ppermute x2, starting transfers between devices, along(): return lax.ppermute(v, 'seq', pairs)  8.91 us
    ppermute x1, waiting for transfers between devices, pair_shards(): got = lax.ppermute(packed, 'seq', flip)  6.69 us
    ppermute x3, waiting for transfers between devices, pair_shards(): across = lambda value: lax.ppermute(value, 'seq', flip)  6.3 us
    ppermute x4, starting transfers between devices, deliver(): moved = lax.ppermute(value, both, [(i, j) for i, j in pairs if i != j])  6.08 us
  transfers between devices with their start and end apart: 24, of which 15 were waited for; matrix products, arithmetic and copies ran while one was open for 4% of the time, Pallas kernels for 8%

profile of v5, /device:TPU:2, one launch (start us, length us, event | category | flops | bytes accessed | tf_op | source)
XLA Modules:
  0.0 135.0 jit_solution(14152439970612961827)
XLA Ops:
  0.0 2.4 %pack.1 = (bf16[128,1408]{1,0:T(8,128)(2,1)}, bf16[128,1408]{1,0:T(8,128)(2,1)}) custom-call(s32[1]{0:T(128)} %bitcast.1.refs_0_, bf16[128,2048]{1,0:T(8,128)(2,1)} %refs_1_.4, bf16[128,256]{1,0:T(8,128)(2,1)} %refs_2_.4, bf16[128,256]{1,0:T(8,128)(2,1)} %refs_3_.2, f32[16,128]{1,0:T(8,128)} %bitcast.12), custom_call_target="tpu_custom_call" | custom-call | flops 1 | bytes 1 | tf_op jit(solution)/shard_map/pack/pallas_call | solution.py:82
  2.4 1.5 %collective-permute-start = (bf16[128,1408]{1,0:T(8,128)(2,1)}, bf16[128,1408]{1,0:T(8,128)(2,1)S(1)}, u32[]{:S(2)}, u32[]{:S(2)}) collective-permute-start(bf16[128,1408]{1,0:T(8,128)(2,1)} %get-tuple-element.45), channel_id=1, source_target_pairs={{0,4},{4,0},{8,12},{12,8},{16,20},{20,16},{24,28},{28,24},{1,5},{5... | collective-permute-start | bytes 1081352 | tf_op jit(solution)/shard_map/ppermute | solution.py:374
  6.1 6.7 %collective-permute-done.refs_2_ = bf16[128,1408]{1,0:T(8,128)(2,1)S(1)} collective-permute-done((bf16[128,1408]{1,0:T(8,128)(2,1)}, bf16[128,1408]{1,0:T(8,128)(2,1)S(1)}, u32[]{:S(2)}, u32[]{:S(2)}) %collective-permute-start) | collective-permute-done | bytes 360480 | tf_op jit(solution)/shard_map/ppermute | solution.py:374
  15.0 3.5 %collective-permute-start.1 = (bf16[144,1024]{1,0:T(8,128)(2,1)S(1)}, bf16[144,1024]{1,0:T(8,128)(2,1)S(1)}, u32[]{:S(2)}, u32[]{:S(2)}) collective-permute-start(bf16[144,1024]{1,0:T(8,128)(2,1)S(1)} %get-tuple-element.49.send_ref), channel_id=1, source_target_pairs={{0,8},{4,12},{8,16},{12,20},{16,24},{20,28},{1,9},{5,13},{9,17},{1... | collective-permute-start | bytes 884744 | tf_op jit(solution)/shard_map/ppermute | solution.py:371
  19.5 1.6 %collective-permute-start.3 = (bf16[128,1024]{1,0:T(8,128)(2,1)S(1)}, bf16[128,1024]{1,0:T(8,128)(2,1)S(1)}, u32[]{:S(2)}, u32[]{:S(2)}) collective-permute-start(bf16[128,1024]{1,0:T(8,128)(2,1)S(1)} %constant_dynamic-slice_fusion), channel_id=1, source_target_pairs={{0,4},{4,0},{8,12},{12,8},{16,20},{20,16},{24,28},{28,24},{1,5},{5... | collective-permute-start | bytes 786440 | tf_op jit(solution)/shard_map/ppermute | solution.py:379
  22.2 1.7 %collective-permute-done.1.got_ref.refs_4_ = bf16[144,1024]{1,0:T(8,128)(2,1)S(1)} collective-permute-done((bf16[144,1024]{1,0:T(8,128)(2,1)S(1)}, bf16[144,1024]{1,0:T(8,128)(2,1)S(1)}, u32[]{:S(2)}, u32[]{:S(2)}) %collective-permute-start.1) | collective-permute-done | bytes 294944 | tf_op jit(solution)/shard_map/ppermute | solution.py:371
  24.0 5.4 %collective-permute-start.2 = (bf16[128,1024]{1,0:T(8,128)(2,1)S(1)}, bf16[128,1024]{1,0:T(8,128)(2,1)S(1)}, u32[]{:S(2)}, u32[]{:S(2)}) collective-permute-start(bf16[128,1024]{1,0:T(8,128)(2,1)S(1)} %join.1), channel_id=1, source_target_pairs={{0,16},{4,20},{8,24},{12,28},{1,17},{5,21},{9,25},{13,29},{2,18},{... | collective-permute-start | bytes 786440 | tf_op jit(solution)/shard_map/ppermute | solution.py:371
  29.4 3.8 %collective-permute-done.2.refs_5_ = bf16[128,1024]{1,0:T(8,128)(2,1)S(1)} collective-permute-done((bf16[128,1024]{1,0:T(8,128)(2,1)S(1)}, bf16[128,1024]{1,0:T(8,128)(2,1)S(1)}, u32[]{:S(2)}, u32[]{:S(2)}) %collective-permute-start.2) | collective-permute-done | bytes 262176 | tf_op jit(solution)/shard_map/ppermute | solution.py:371
  34.3 7.0 %collective-permute-start.4 = (bf16[256,1024]{1,0:T(8,128)(2,1)S(1)}, bf16[256,1024]{1,0:T(8,128)(2,1)S(1)}, u32[]{:S(2)}, u32[]{:S(2)}) collective-permute-start(bf16[256,1024]{1,0:T(8,128)(2,1)S(1)} %finish.1.own_ref), channel_id=1, source_target_pairs={{0,8},{4,12},{8,0},{12,4},{16,24},{20,28},{24,16},{28,20},{1,9},{5... | collective-permute-start | bytes 1572872 | tf_op jit(solution)/shard_map/ppermute | solution.py:390
  42.0 1.6 %collective-permute-start.9 = (bf16[256,1024]{1,0:T(8,128)(2,1)S(1)}, bf16[256,1024]{1,0:T(8,128)(2,1)S(1)}, u32[]{:S(2)}, u32[]{:S(2)}) collective-permute-start(bf16[256,1024]{1,0:T(8,128)(2,1)S(1)} %finish.1.own_ref), channel_id=1, source_target_pairs={{0,4},{4,0},{8,12},{12,8},{16,20},{20,16},{24,28},{28,24},{1,5},{5... | collective-permute-start | bytes 1572872 | tf_op jit(solution)/shard_map/ppermute | solution.py:393
  43.6 9.8 %collective-permute-done.4.own_ref = bf16[256,1024]{1,0:T(8,128)(2,1)S(1)} collective-permute-done((bf16[256,1024]{1,0:T(8,128)(2,1)S(1)}, bf16[256,1024]{1,0:T(8,128)(2,1)S(1)}, u32[]{:S(2)}, u32[]{:S(2)}) %collective-permute-start.4) | collective-permute-done | bytes 524320 | tf_op jit(solution)/shard_map/ppermute | solution.py:390
  54.1 1.3 collective-permute-start.7
  55.4 1.6 %collective-permute-start.8 = (bf16[256,1024]{1,0:T(8,128)(2,1)S(1)}, bf16[256,1024]{1,0:T(8,128)(2,1)S(1)}, u32[]{:S(2)}, u32[]{:S(2)}) collective-permute-start(bf16[256,1024]{1,0:T(8,128)(2,1)S(1)} %collective-permute-done.4.own_ref), channel_id=1, source_target_pairs={{0,4},{4,0},{8,12},{12,8},{16,20},{20,16},{24,28},{28,24},{1,5},{5... | collective-permute-start | bytes 1572872 | tf_op jit(solution)/shard_map/ppermute | solution.py:393
  57.8 2.2 %copy-done = bf16[2048,1024]{1,0:T(8,128)(2,1)S(1)} copy-done((bf16[2048,1024]{1,0:T(8,128)(2,1)S(1)}, bf16[2048,1024]{1,0:T(8,128)(2,1)}, u32[]{:S(2)}) %copy-start) | copy-done | bytes 4194328
  59.9 3.1 %project.4 = (f32[128,1024]{1,0:T(8,128)S(1)}, bf16[128,1024]{1,0:T(8,128)(2,1)S(1)}) custom-call(s32[3]{0:T(128)S(1)} %pad_add_fusion.yc_ref, bf16[256,1024]{1,0:T(8,128)(2,1)S(1)} %finish.1.own_ref, bf16[256,1024]{1,0:T(8,128)(2,1)S(1)} %collective-permute-done.9.refs_0_, bf16[2048,1024]{1,0:T(8,128)(2,1)S(1)} %copy-done, bf16[2048,1024]{1,0:T(8,128)(2,1)S(1)} %copy-done), custom_call_target="tpu_custom_call" | custom-call | flops 1 | bytes 1 | tf_op jit(solution)/shard_map/project/pallas_call | solution.py:300
  63.1 8.9 %collective-permute-done.7 = bf16[256,1024]{1,0:T(8,128)(2,1)} collective-permute-done((bf16[256,1024]{1,0:T(8,128)(2,1)S(1)}, bf16[256,1024]{1,0:T(8,128)(2,1)}, u32[]{:S(2)}, u32[]{:S(2)}) %collective-permute-start.7) | collective-permute-done | bytes 524320 | tf_op jit(solution)/shard_map/ppermute | solution.py:390
  73.0 1.6 %collective-permute-start.11 = (bf16[256,1024]{1,0:T(8,128)(2,1)S(1)}, bf16[256,1024]{1,0:T(8,128)(2,1)S(1)}, u32[]{:S(2)}, u32[]{:S(2)}) collective-permute-start(bf16[256,1024]{1,0:T(8,128)(2,1)S(1)} %broadcast_select_fusion.1.own_ref), channel_id=1, source_target_pairs={{0,4},{4,0},{8,12},{12,8},{16,20},{20,16},{24,28},{28,24},{1,5},{5... | collective-permute-start | bytes 1572872 | tf_op jit(solution)/shard_map/ppermute | solution.py:393
  74.6 1.3 collective-permute-start.10
  76.0 3.1 %project.5 = (f32[128,1024]{1,0:T(8,128)S(1)}, bf16[128,1024]{1,0:T(8,128)(2,1)S(1)}) custom-call(s32[3]{0:T(128)S(1)} %pad_add_fusion.yc_ref, bf16[256,1024]{1,0:T(8,128)(2,1)S(1)} %collective-permute-done.4.own_ref, bf16[256,1024]{1,0:T(8,128)(2,1)S(1)} %collective-permute-done.8.refs_0_, bf16[2048,1024]{1,0:T(8,128)(2,1)S(1)} %copy-done.1, ...), custom_call_target="tpu_custom_call" | custom-call | flops 1 | bytes 1 | tf_op jit(solution)/shard_map/project/pallas_call | solution.py:300
  79.2 6.3 %collective-permute-done.11.refs_0_ = bf16[256,1024]{1,0:T(8,128)(2,1)S(1)} collective-permute-done((bf16[256,1024]{1,0:T(8,128)(2,1)S(1)}, bf16[256,1024]{1,0:T(8,128)(2,1)S(1)}, u32[]{:S(2)}, u32[]{:S(2)}) %collective-permute-start.11) | collective-permute-done | bytes 524320 | tf_op jit(solution)/shard_map/ppermute | solution.py:393
  85.5 3.1 %collective-permute-done.10 = bf16[256,1024]{1,0:T(8,128)(2,1)S(1)} collective-permute-done((bf16[256,1024]{1,0:T(8,128)(2,1)S(1)}, bf16[256,1024]{1,0:T(8,128)(2,1)S(1)}, u32[]{:S(2)}, u32[]{:S(2)}) %collective-permute-start.10) | collective-permute-done | bytes 524320 | tf_op jit(solution)/shard_map/ppermute | solution.py:390
  88.6 2.4 %collective-permute-start.14 = (bf16[128,1024]{1,0:T(8,128)(2,1)S(1)}, bf16[128,1024]{1,0:T(8,128)(2,1)S(1)}, u32[]{:S(2)}, u32[]{:S(2)}) collective-permute-start(bf16[128,1024]{1,0:T(8,128)(2,1)S(1)} %slice.6), channel_id=1, source_target_pairs={{0,4},{4,0},{24,28},{28,24},{1,5},{5,1},{25,29},{29,25},{2,6},{6,2... | collective-permute-start | bytes 786440 | tf_op jit(solution)/shard_map/ppermute | solution.py:428
  91.1 1.3 collective-permute-start.15
  92.4 3.1 %project.6 = (f32[128,1024]{1,0:T(8,128)S(1)}, bf16[128,1024]{1,0:T(8,128)(2,1)S(1)}) custom-call(s32[3]{0:T(128)S(1)} %pad_add_fusion.yc_ref, bf16[256,1024]{1,0:T(8,128)(2,1)S(1)} %broadcast_select_fusion.1.own_ref, bf16[256,1024]{1,0:T(8,128)(2,1)S(1)} %collective-permute-done.11.refs_0_, bf16[2048,1024]{1,0:T(8,128)(2,1)S(1)} %copy-done.1, ...), custom_call_target="tpu_custom_call" | custom-call | flops 1 | bytes 1 | tf_op jit(solution)/shard_map/project/pallas_call | solution.py:300
  95.6 3.6 %collective-permute-done.14.refs_1_ = bf16[128,1024]{1,0:T(8,128)(2,1)S(1)} collective-permute-done((bf16[128,1024]{1,0:T(8,128)(2,1)S(1)}, bf16[128,1024]{1,0:T(8,128)(2,1)S(1)}, u32[]{:S(2)}, u32[]{:S(2)}) %collective-permute-start.14) | collective-permute-done | bytes 262176 | tf_op jit(solution)/shard_map/ppermute | solution.py:428
  99.2 2.2 %collective-permute-done.15.refs_2_ = bf16[128,1024]{1,0:T(8,128)(2,1)S(1)} collective-permute-done((bf16[128,1024]{1,0:T(8,128)(2,1)S(1)}, bf16[128,1024]{1,0:T(8,128)(2,1)S(1)}, u32[]{:S(2)}, u32[]{:S(2)}) %collective-permute-start.15) | collective-permute-done | bytes 262176 | tf_op jit(solution)/shard_map/ppermute | solution.py:390
  101.4 3.1 %project.7 = (f32[128,1024]{1,0:T(8,128)S(1)}, bf16[128,1024]{1,0:T(8,128)(2,1)S(1)}) custom-call(s32[3]{0:T(128)S(1)} %pad_add_fusion.yc_ref, bf16[256,1024]{1,0:T(8,128)(2,1)S(1)} %broadcast_select_fusion.own_ref, bf16[256,1024]{1,0:T(8,128)(2,1)S(1)} %collective-permute-done.12.refs_0_, bf16[128,1024]{1,0:T(8,128)(2,1)S(1)} %collective-permute-done.14.refs_1_, ...), custom_call_target="tpu_custom_call" | custom-call | flops 1 | bytes 1 | tf_op jit(solution)/shard_map/project/pallas_call | solution.py:300
  106.2 1.6 %collective-permute-start.21 = (bf16[128,1024]{1,0:T(8,128)(2,1)S(1)}, bf16[128,1024]{1,0:T(8,128)(2,1)S(1)}, u32[]{:S(2)}, u32[]{:S(2)}) collective-permute-start(bf16[128,1024]{1,0:T(8,128)(2,1)S(1)} %get-tuple-element.87), channel_id=1, source_target_pairs={{0,8},{1,12},{2,24},{3,28},{4,9},{5,13},{6,25},{7,29},{8,0},{9,4},... | collective-permute-start | bytes 786440 | tf_op jit(solution)/shard_map/ppermute | solution.py:407
  108.4 3.0 %collective-permute-start.18 = (bf16[128,1024]{1,0:T(8,128)(2,1)S(1)}, bf16[128,1024]{1,0:T(8,128)(2,1)S(1)}, u32[]{:S(2)}, u32[]{:S(2)}) collective-permute-start(bf16[128,1024]{1,0:T(8,128)(2,1)S(1)} %get-tuple-element.85), channel_id=1, source_target_pairs={{1,4},{2,16},{3,20},{4,1},{6,17},{7,21},{9,12},{10,24},{11,28},{12... | collective-permute-start | bytes 786440 | tf_op jit(solution)/shard_map/ppermute | solution.py:407
  112.4 5.5 %collective-permute-done.21 = bf16[128,1024]{1,0:T(8,128)(2,1)S(1)} collective-permute-done((bf16[128,1024]{1,0:T(8,128)(2,1)S(1)}, bf16[128,1024]{1,0:T(8,128)(2,1)S(1)}, u32[]{:S(2)}, u32[]{:S(2)}) %collective-permute-start.21) | collective-permute-done | bytes 262176 | tf_op jit(solution)/shard_map/ppermute | solution.py:407
  118.0 2.8 %collective-permute-done.22 = bf16[128,1024]{1,0:T(8,128)(2,1)S(1)} collective-permute-done((bf16[128,1024]{1,0:T(8,128)(2,1)S(1)}, bf16[128,1024]{1,0:T(8,128)(2,1)S(1)}, u32[]{:S(2)}, u32[]{:S(2)}) %collective-permute-start.22) | collective-permute-done | bytes 262176 | tf_op jit(solution)/shard_map/ppermute | solution.py:407
  120.8 11.2 %collective-permute-done.18 = bf16[128,1024]{1,0:T(8,128)(2,1)S(1)} collective-permute-done((bf16[128,1024]{1,0:T(8,128)(2,1)S(1)}, bf16[128,1024]{1,0:T(8,128)(2,1)S(1)}, u32[]{:S(2)}, u32[]{:S(2)}) %collective-permute-start.18) | collective-permute-done | bytes 262176 | tf_op jit(solution)/shard_map/ppermute | solution.py:407
  (50 shorter events, 17.3 us)
Async XLA Ops:
  0.0 33.3 %copy-start.2 = (bf16[128,2048]{1,0:T(8,128)(2,1)S(1)}, bf16[128,2048]{1,0:T(8,128)(2,1)}, u32[]{:S(2)}) copy-start(bf16[128,2048]{1,0:T(8,128)(2,1)} %refs_6_.1) | copy-start | bytes 1572868
  2.4 10.4 %collective-permute-start = (bf16[128,1408]{1,0:T(8,128)(2,1)}, bf16[128,1408]{1,0:T(8,128)(2,1)S(1)}, u32[]{:S(2)}, u32[]{:S(2)}) collective-permute-start(bf16[128,1408]{1,0:T(8,128)(2,1)} %get-tuple-element.45), channel_id=1, source_target_pairs={{0,4},{4,0},{8,12},{12,8},{16,20},{20,16},{24,28},{28,24},{1,5},{5... | collective-permute-start | bytes 1081352 | tf_op jit(solution)/shard_map/ppermute | solution.py:374
  12.9 1.0 copy-start.3
  15.0 8.9 %collective-permute-start.1 = (bf16[144,1024]{1,0:T(8,128)(2,1)S(1)}, bf16[144,1024]{1,0:T(8,128)(2,1)S(1)}, u32[]{:S(2)}, u32[]{:S(2)}) collective-permute-start(bf16[144,1024]{1,0:T(8,128)(2,1)S(1)} %get-tuple-element.49.send_ref), channel_id=1, source_target_pairs={{0,8},{4,12},{8,16},{12,20},{16,24},{20,28},{1,9},{5,13},{9,17},{1... | collective-permute-start | bytes 884744 | tf_op jit(solution)/shard_map/ppermute | solution.py:371
  19.5 9.9 %collective-permute-start.3 = (bf16[128,1024]{1,0:T(8,128)(2,1)S(1)}, bf16[128,1024]{1,0:T(8,128)(2,1)S(1)}, u32[]{:S(2)}, u32[]{:S(2)}) collective-permute-start(bf16[128,1024]{1,0:T(8,128)(2,1)S(1)} %constant_dynamic-slice_fusion), channel_id=1, source_target_pairs={{0,4},{4,0},{8,12},{12,8},{16,20},{20,16},{24,28},{28,24},{1,5},{5... | collective-permute-start | bytes 786440 | tf_op jit(solution)/shard_map/ppermute | solution.py:379
  24.0 9.3 %collective-permute-start.2 = (bf16[128,1024]{1,0:T(8,128)(2,1)S(1)}, bf16[128,1024]{1,0:T(8,128)(2,1)S(1)}, u32[]{:S(2)}, u32[]{:S(2)}) collective-permute-start(bf16[128,1024]{1,0:T(8,128)(2,1)S(1)} %join.1), channel_id=1, source_target_pairs={{0,16},{4,20},{8,24},{12,28},{1,17},{5,21},{9,25},{13,29},{2,18},{... | collective-permute-start | bytes 786440 | tf_op jit(solution)/shard_map/ppermute | solution.py:371
  34.3 19.1 %collective-permute-start.4 = (bf16[256,1024]{1,0:T(8,128)(2,1)S(1)}, bf16[256,1024]{1,0:T(8,128)(2,1)S(1)}, u32[]{:S(2)}, u32[]{:S(2)}) collective-permute-start(bf16[256,1024]{1,0:T(8,128)(2,1)S(1)} %finish.1.own_ref), channel_id=1, source_target_pairs={{0,8},{4,12},{8,0},{12,4},{16,24},{20,28},{24,16},{28,20},{1,9},{5... | collective-permute-start | bytes 1572872 | tf_op jit(solution)/shard_map/ppermute | solution.py:390
  41.3 12.8 %collective-permute-start.6 = (bf16[256,1024]{1,0:T(8,128)(2,1)S(1)}, bf16[256,1024]{1,0:T(8,128)(2,1)S(1)}, u32[]{:S(2)}, u32[]{:S(2)}) collective-permute-start(bf16[256,1024]{1,0:T(8,128)(2,1)S(1)} %finish.1.own_ref), channel_id=1, source_target_pairs={{8,16},{12,20},{16,8},{20,12},{9,17},{13,21},{17,9},{21,13},{10,18... | collective-permute-start | bytes 1572872 | tf_op jit(solution)/shard_map/ppermute | solution.py:390
  42.0 15.1 %collective-permute-start.9 = (bf16[256,1024]{1,0:T(8,128)(2,1)S(1)}, bf16[256,1024]{1,0:T(8,128)(2,1)S(1)}, u32[]{:S(2)}, u32[]{:S(2)}) collective-permute-start(bf16[256,1024]{1,0:T(8,128)(2,1)S(1)} %finish.1.own_ref), channel_id=1, source_target_pairs={{0,4},{4,0},{8,12},{12,8},{16,20},{20,16},{24,28},{28,24},{1,5},{5... | collective-permute-start | bytes 1572872 | tf_op jit(solution)/shard_map/ppermute | solution.py:393
  53.4 9.7 %collective-permute-start.5 = (bf16[256,1024]{1,0:T(8,128)(2,1)S(1)}, bf16[256,1024]{1,0:T(8,128)(2,1)S(1)}, u32[]{:S(2)}, u32[]{:S(2)}) collective-permute-start(bf16[256,1024]{1,0:T(8,128)(2,1)S(1)} %collective-permute-done.4.own_ref), channel_id=1, source_target_pairs={{8,16},{12,20},{16,8},{20,12},{9,17},{13,21},{17,9},{21,13},{10,18... | collective-permute-start | bytes 1572872 | tf_op jit(solution)/shard_map/ppermute | solution.py:390
  54.1 17.8 %collective-permute-start.7 = (bf16[256,1024]{1,0:T(8,128)(2,1)S(1)}, bf16[256,1024]{1,0:T(8,128)(2,1)}, u32[]{:S(2)}, u32[]{:S(2)}) collective-permute-start(bf16[256,1024]{1,0:T(8,128)(2,1)S(1)} %collective-permute-done.6), channel_id=1, source_target_pairs={{8,0},{12,4},{16,24},{20,28},{9,1},{13,5},{17,25},{21,29},{10,2},{... | collective-permute-start | bytes 1572872 | tf_op jit(solution)/shard_map/ppermute | solution.py:390
  55.4 16.5 %collective-permute-start.8 = (bf16[256,1024]{1,0:T(8,128)(2,1)S(1)}, bf16[256,1024]{1,0:T(8,128)(2,1)S(1)}, u32[]{:S(2)}, u32[]{:S(2)}) collective-permute-start(bf16[256,1024]{1,0:T(8,128)(2,1)S(1)} %collective-permute-done.4.own_ref), channel_id=1, source_target_pairs={{0,4},{4,0},{8,12},{12,8},{16,20},{20,16},{24,28},{28,24},{1,5},{5... | collective-permute-start | bytes 1572872 | tf_op jit(solution)/shard_map/ppermute | solution.py:393
  57.0 22.1 %collective-permute-start.12 = (bf16[256,1024]{1,0:T(8,128)(2,1)S(1)}, bf16[256,1024]{1,0:T(8,128)(2,1)S(1)}, u32[]{:S(2)}, u32[]{:S(2)}) collective-permute-start(bf16[256,1024]{1,0:T(8,128)(2,1)S(1)} %collective-permute-done.9.refs_0_), channel_id=1, source_target_pairs={{8,16},{12,20},{16,8},{20,12},{9,17},{13,21},{17,9},{21,13},{10,18... | collective-permute-start | bytes 1572872 | tf_op jit(solution)/shard_map/ppermute | solution.py:390
  57.7 2.2 %copy-start = (bf16[2048,1024]{1,0:T(8,128)(2,1)S(1)}, bf16[2048,1024]{1,0:T(8,128)(2,1)}, u32[]{:S(2)}) copy-start(bf16[2048,1024]{1,0:T(8,128)(2,1)} %refs_4_.1) | copy-start | bytes 12582916
  59.9 16.0 %copy-start.1 = (bf16[2048,1024]{1,0:T(8,128)(2,1)S(1)}, bf16[2048,1024]{1,0:T(8,128)(2,1)}, u32[]{:S(2)}) copy-start(bf16[2048,1024]{1,0:T(8,128)(2,1)} %refs_4_.1) | copy-start | bytes 12582916
  73.0 12.4 %collective-permute-start.11 = (bf16[256,1024]{1,0:T(8,128)(2,1)S(1)}, bf16[256,1024]{1,0:T(8,128)(2,1)S(1)}, u32[]{:S(2)}, u32[]{:S(2)}) collective-permute-start(bf16[256,1024]{1,0:T(8,128)(2,1)S(1)} %broadcast_select_fusion.1.own_ref), channel_id=1, source_target_pairs={{0,4},{4,0},{8,12},{12,8},{16,20},{20,16},{24,28},{28,24},{1,5},{5... | collective-permute-start | bytes 1572872 | tf_op jit(solution)/shard_map/ppermute | solution.py:393
  74.6 14.0 %collective-permute-start.10 = (bf16[256,1024]{1,0:T(8,128)(2,1)S(1)}, bf16[256,1024]{1,0:T(8,128)(2,1)S(1)}, u32[]{:S(2)}, u32[]{:S(2)}) collective-permute-start(bf16[256,1024]{1,0:T(8,128)(2,1)S(1)} %collective-permute-done.5), channel_id=1, source_target_pairs={{8,0},{12,4},{16,24},{20,28},{9,1},{13,5},{17,25},{21,29},{10,2},{... | collective-permute-start | bytes 1572872 | tf_op jit(solution)/shard_map/ppermute | solution.py:390
  75.9 3.2 %collective-permute-start.13 = (bf16[128,1024]{1,0:T(8,128)(2,1)S(1)}, bf16[128,1024]{1,0:T(8,128)(2,1)S(1)}, u32[]{:S(2)}, u32[]{:S(2)}) collective-permute-start(bf16[128,1024]{1,0:T(8,128)(2,1)S(1)} %get-tuple-element.67), channel_id=1, source_target_pairs={{0,1},{1,0},{2,3},{3,2},{4,5},{5,4},{6,7},{7,6},{8,9},{9,8},{10,11... | collective-permute-start | bytes 786440 | tf_op jit(solution)/shard_map/ppermute | solution.py:394
  88.6 7.0 %collective-permute-start.16 = (bf16[128,1024]{1,0:T(8,128)(2,1)S(1)}, bf16[128,1024]{1,0:T(8,128)(2,1)S(1)}, u32[]{:S(2)}, u32[]{:S(2)}) collective-permute-start(bf16[128,1024]{1,0:T(8,128)(2,1)S(1)} %get-tuple-element.74), channel_id=1, source_target_pairs={{0,1},{1,0},{2,3},{3,2},{4,5},{5,4},{6,7},{7,6},{8,9},{9,8},{10,11... | collective-permute-start | bytes 786440 | tf_op jit(solution)/shard_map/ppermute | solution.py:394
  88.6 10.6 %collective-permute-start.14 = (bf16[128,1024]{1,0:T(8,128)(2,1)S(1)}, bf16[128,1024]{1,0:T(8,128)(2,1)S(1)}, u32[]{:S(2)}, u32[]{:S(2)}) collective-permute-start(bf16[128,1024]{1,0:T(8,128)(2,1)S(1)} %slice.6), channel_id=1, source_target_pairs={{0,4},{4,0},{24,28},{28,24},{1,5},{5,1},{25,29},{29,25},{2,6},{6,2... | collective-permute-start | bytes 786440 | tf_op jit(solution)/shard_map/ppermute | solution.py:428
  91.1 10.3 %collective-permute-start.15 = (bf16[128,1024]{1,0:T(8,128)(2,1)S(1)}, bf16[128,1024]{1,0:T(8,128)(2,1)S(1)}, u32[]{:S(2)}, u32[]{:S(2)}) collective-permute-start(bf16[128,1024]{1,0:T(8,128)(2,1)S(1)} %slice.7), channel_id=1, source_target_pairs={{8,0},{12,4},{16,24},{20,28},{9,1},{13,5},{17,25},{21,29},{10,2},{... | collective-permute-start | bytes 786440 | tf_op jit(solution)/shard_map/ppermute | solution.py:390
  104.5 1.6 %collective-permute-start.20 = (bf16[128,1024]{1,0:T(8,128)(2,1)S(1)}, bf16[128,1024]{1,0:T(8,128)(2,1)S(1)}, u32[]{:S(2)}, u32[]{:S(2)}) collective-permute-start(bf16[128,1024]{1,0:T(8,128)(2,1)S(1)} %get-tuple-element.82), channel_id=1, source_target_pairs={{0,1},{1,0},{2,3},{3,2},{4,5},{5,4},{6,7},{7,6},{8,9},{9,8},{10,11... | collective-permute-start | bytes 786440 | tf_op jit(solution)/shard_map/ppermute | solution.py:394
  104.6 3.7 %collective-permute-start.17 = (bf16[128,1024]{1,0:T(8,128)(2,1)S(1)}, bf16[128,1024]{1,0:T(8,128)(2,1)S(1)}, u32[]{:S(2)}, u32[]{:S(2)}) collective-permute-start(bf16[128,1024]{1,0:T(8,128)(2,1)S(1)} %get-tuple-element.76), channel_id=1, source_target_pairs={{0,1},{1,0},{2,3},{3,2},{4,5},{5,4},{6,7},{7,6},{8,9},{9,8},{10,11... | collective-permute-start | bytes 786440 | tf_op jit(solution)/shard_map/ppermute | solution.py:394
  106.2 11.8 %collective-permute-start.21 = (bf16[128,1024]{1,0:T(8,128)(2,1)S(1)}, bf16[128,1024]{1,0:T(8,128)(2,1)S(1)}, u32[]{:S(2)}, u32[]{:S(2)}) collective-permute-start(bf16[128,1024]{1,0:T(8,128)(2,1)S(1)} %get-tuple-element.87), channel_id=1, source_target_pairs={{0,8},{1,12},{2,24},{3,28},{4,9},{5,13},{6,25},{7,29},{8,0},{9,4},... | collective-permute-start | bytes 786440 | tf_op jit(solution)/shard_map/ppermute | solution.py:407
  107.9 12.9 %collective-permute-start.22 = (bf16[128,1024]{1,0:T(8,128)(2,1)S(1)}, bf16[128,1024]{1,0:T(8,128)(2,1)S(1)}, u32[]{:S(2)}, u32[]{:S(2)}) collective-permute-start(bf16[128,1024]{1,0:T(8,128)(2,1)S(1)} %get-tuple-element.88), channel_id=1, source_target_pairs={{0,24},{1,28},{2,8},{3,12},{4,25},{5,29},{6,9},{7,13},{8,16},{9,20... | collective-permute-start | bytes 786440 | tf_op jit(solution)/shard_map/ppermute | solution.py:407
  108.4 23.5 %collective-permute-start.18 = (bf16[128,1024]{1,0:T(8,128)(2,1)S(1)}, bf16[128,1024]{1,0:T(8,128)(2,1)S(1)}, u32[]{:S(2)}, u32[]{:S(2)}) collective-permute-start(bf16[128,1024]{1,0:T(8,128)(2,1)S(1)} %get-tuple-element.85), channel_id=1, source_target_pairs={{1,4},{2,16},{3,20},{4,1},{6,17},{7,21},{9,12},{10,24},{11,28},{12... | collective-permute-start | bytes 786440 | tf_op jit(solution)/shard_map/ppermute | solution.py:407
  111.5 20.7 %collective-permute-start.19 = (bf16[128,1024]{1,0:T(8,128)(2,1)S(1)}, bf16[128,1024]{1,0:T(8,128)(2,1)S(1)}, u32[]{:S(2)}, u32[]{:S(2)}) collective-permute-start(bf16[128,1024]{1,0:T(8,128)(2,1)S(1)} %get-tuple-element.86), channel_id=1, source_target_pairs={{0,16},{1,20},{2,0},{3,4},{4,17},{5,21},{6,1},{7,5},{8,24},{9,28},... | collective-permute-start | bytes 786440 | tf_op jit(solution)/shard_map/ppermute | solution.py:407
  132.4 1.7 %collective-permute-start.23 = (bf16[128,1024]{1,0:T(8,128)(2,1)S(1)}, bf16[128,1024]{1,0:T(8,128)(2,1)S(1)}, u32[]{:S(2)}, u32[]{:S(2)}) collective-permute-start(bf16[128,1024]{1,0:T(8,128)(2,1)S(1)} %get-tuple-element.83), channel_id=1, source_target_pairs={{0,1},{1,0},{2,3},{3,2},{4,5},{5,4},{6,7},{7,6},{8,9},{9,8},{10,11... | collective-permute-start | bytes 786440 | tf_op jit(solution)/shard_map/ppermute | solution.py:394

commit v6 on v5

--- a/solution.py
+++ b/solution.py
@@ -48,50 +48,41 @@
     return hi, mid, (rest - mid.astype(F32)).astype(BF16)
 
 
-def pack_kernel(y_ref, x_ref, b_ref, c_ref, dt_ref, own_ref, out_ref, *, heads):
-    width, state = x_ref.shape[1] // 2, b_ref.shape[1] // 2
+def pack_kernel(group_ref, x_ref, b_ref, c_ref, dt_ref, out_ref, *, heads):
+    width, state = x_ref.shape[1], b_ref.shape[1]
+    out_ref[:, :width] = x_ref[...]
+    out_ref[:, width : width + state] = b_ref[...]
+    out_ref[:, width + state : width + 2 * state] = c_ref[...]
+    group = group_ref[0]
     rows, cols = iota((2 * heads, 128), 0), iota((2 * heads, 128), 1)
-    parts = split3(dt_ref[...])
-    for group in range(2):
-        total = jnp.zeros((x_ref.shape[0], 128), F32)
-        for part, value in enumerate(parts):
-            where = (cols == rows - group * heads + part * heads) & (rows // heads == group)
-            total = total + lax.dot_general(value, where.astype(BF16), TN, preferred_element_type=F32)
-        steps = total.astype(BF16)
-
-        def fill(ref):
-            ref[:, :width] = x_ref[:, group * width : (group + 1) * width]
-            ref[:, width : width + state] = b_ref[:, group * state : (group + 1) * state]
-            ref[:, width + state : width + 2 * state] = c_ref[:, group * state : (group + 1) * state]
-            ref[:, width + 2 * state :] = steps
-
-        @pl.when(y_ref[0] == group)
-        def _():
-            fill(own_ref)
-
-        @pl.when(y_ref[0] != group)
-        def _():
-            fill(out_ref)
-
-
-def pack(y, x, b, c, dt, heads):
-    tokens = x.shape[0]
-    full = heads * CHANNEL_WIDTH + 2 * STATE + 128
-    whole = lambda a: pl.BlockSpec(a.shape, lambda i, y: (0,) * a.ndim)
-    out = jax.ShapeDtypeStruct((tokens, full), BF16)
+    total = jnp.zeros((x_ref.shape[0], 128), F32)
+    for part, value in enumerate(split3(dt_ref[...])):
+        where = (cols == rows - group * heads + part * heads) & (rows // heads == group)
+        total = total + lax.dot_general(value, where.astype(BF16), TN, preferred_element_type=F32)
+    out_ref[:, width + 2 * state :] = total.astype(BF16)
+
+
+def pack(group, x, b, c, dt, heads, limit):
+    tokens, width, state = x.shape[0], heads * CHANNEL_WIDTH, STATE
+    out = jax.ShapeDtypeStruct((tokens, width + 2 * state + 128), BF16)
     return pl.pallas_call(
         lambda *refs: pack_kernel(*refs, heads=heads),
         grid_spec=pltpu.PrefetchScalarGridSpec(
             num_scalar_prefetch=1,
             grid=(1,),
-            in_specs=[whole(x), whole(b), whole(c), whole(dt)],
-            out_specs=[whole(out), whole(out)],
+            in_specs=[
+                pl.BlockSpec((tokens, width), lambda i, g: (0, g[0])),
+                pl.BlockSpec((tokens, state), lambda i, g: (0, g[0])),
+                pl.BlockSpec((tokens, state), lambda i, g: (0, g[0])),
+                pl.BlockSpec(dt.shape, lambda i, g: (0, 0)),
+            ],
+            out_specs=pl.BlockSpec(out.shape, lambda i, g: (0, 0)),
         ),
-        out_shape=[out, out],
-        compiler_params=params(1, 60 * 2**20),
-        cost_estimate=cost(1e6, 4 * tokens * full),
+        out_shape=out,
+        compiler_params=params(1, limit),
+        cost_estimate=cost(1e6, 1e6),
         name="pack",
-    )(y, x, b, c, dt)
+    )(group, x, b, c, dt)
 
 
 def local_state_kernel(
@@ -370,14 +361,14 @@
         pairs = [(a * 2 + b, (a + step) * 2 + b) for a in senders for b in range(2)]
         return lax.ppermute(v, "seq", pairs)
 
-    own, packed = pack(yv, x_in, b_proj, c_proj, dt_raw, heads)
-    got = lax.ppermute(packed, "seq", flip)
+    got = lax.ppermute(pack(1 - yv, x_in, b_proj, c_proj, dt_raw, heads, 60 * 2**20), "seq", flip)
+    own = pack(yv, x_in, b_proj, c_proj, dt_raw, heads, VMEM_LIMIT)
     gate_half = half(gate, 1, 1 - y)
     bias, alog = half(dt_bias, 0, y)[None, :], half(a_log, 0, y)[None, :]
     skip = jnp.repeat(half(skip_d, 0, y), CHANNEL_WIDTH)[None, :]
     gain = half(norm_gain, 0, y)[None, :]
     got_gate = lax.ppermute(gate_half, "seq", flip)
-    got, bias, alog, skip, gain = tie((got, bias, alog, skip, gain))
+    got, own, bias, alog, skip, gain = tie((got, own, bias, alog, skip, gain))
 
     xs, bs, cs, scal, send, s = local_state(yv, own, got, bias, alog, heads)
     one = along(send, 1, range(nz - 1))
@@ -416,14 +407,14 @@
     inward, outward = hop(slot1, (1, 2), (2, 1)), hop(middle, (1, 0), (2, 3))
     other1 = across(slot1)
     a0 = project(yc, block, [other0], w_out)
-    inward, outward, other1, a0 = tie((inward, outward, other1, a0))
+    inward, outward, a0 = tie((inward, outward, a0))
     last = hop(inward, (1, 0), (2, 3))
     slot2 = jnp.where(inner, inward, outward)
     other2 = across(slot2)
     a1 = project(yc, slot1, [other1], w_out)
     b0 = reduce_core(*a0)
     inner3 = hop(other0, (1, 2), (2, 1))
-    last, other2, inner3, a1, b0 = tie((last, other2, inner3, a1, b0))
+    last, inner3, a1, b0 = tie((last, inner3, a1, b0))
     slot3 = jnp.where(inner, middle, last)
     lower3 = lax.ppermute(last[:tokens], "seq", [(i * 2 + b, i * 2 + 1 - b) for i in (0, 3) for b in range(2)])
     upper3 = hop(other2[tokens:], (1, 0), (2, 3))

time: 136 us -> 131 us (0.963)
  waiting for transfers between devices: 68 us -> 61.2 us
  local copies, waits for them, and re-layouts: 6.41 us -> 8.85 us
    ppermute x3, waiting for transfers between devices: 6.3 us -> 0.01 us  [pair_shards(): across = lambda value: lax.ppermute(value, 'seq', flip)]
    ppermute x7, waiting for transfers between devices: 24 us -> 29.3 us  [pair_shards(): lax.ppermute(value, 'seq', [(i * 2 + b, j * 2 + b) for i, j in moves for...]
    ppermute x1, waiting for transfers between devices: 6.69 us -> 3.02 us  [pair_shards(): lax.ppermute(pack(1 - yv, x_in, b_proj, c_proj, dt_raw, heads, 60 * 2 **...]
    unnamed x8 -> x14, local copies, waits for them, and re-layouts: 3.17 us -> 5.61 us
    ppermute x1, waiting for transfers between devices: 3.57 us -> 1.33 us  [pair_shards(): lax.ppermute(last[:tokens], 'seq', [(i * 2 + b, i * 2 + 1 - b) for i in (...]
  transfers between devices with their start and end apart: 24 -> 24, of which waited for: 15 -> 14; matrix products, arithmetic and copies ran while one was open for 4% -> 3% of each run, Pallas kernels for 8% -> 8%
where the time goes in v6:
time: 131 us; the launch traced here: 130 us
  waiting for transfers between devices  61.2 us (47%)
  starting transfers between devices  40 us (31%)
  Pallas kernels  18.8 us (14%)
  local copies, waits for them, and re-layouts  8.85 us (7%)
    ppermute x7, waiting for transfers between devices, pair_shards(): lax.ppermute(value, 'seq', [(i * 2 + b, j * 2 + b) for i, j in moves for...  29.3 us
    ppermute x4, waiting for transfers between devices, deliver(): moved = lax.ppermute(value, both, [(i, j) for i, j in pairs if i != j])  19.7 us
    ppermute x7, starting transfers between devices, pair_shards(): lax.ppermute(value, 'seq', [(i * 2 + b, j * 2 + b) for i, j in moves for...  12.9 us
    pallas_call x4, Pallas kernels, project(): pl.pallas_call(project_kernel, grid_spec=pltpu.PrefetchScalarGridSpec(num...  12.4 us
    ppermute x2, starting transfers between devices, along(): return lax.ppermute(v, 'seq', pairs)  8.91 us
    ppermute x4, starting transfers between devices, deliver(): moved = lax.ppermute(value, both, [(i, j) for i, j in pairs if i != j])  6.08 us
    unnamed x14, local copies, waits for them, and re-layouts  5.61 us
    ppermute x2, waiting for transfers between devices, along(): return lax.ppermute(v, 'seq', pairs)  5.52 us
  transfers between devices with their start and end apart: 24, of which 14 were waited for; matrix products, arithmetic and copies ran while one was open for 3% of the time, Pallas kernels for 8%

profile of v6, /device:TPU:2, one launch (start us, length us, event | category | flops | bytes accessed | tf_op | source)
XLA Modules:
  0.0 130.0 jit_solution(10612951657257602244)
XLA Ops:
  0.0 2.0 %pack.2 = bf16[128,1408]{1,0:T(8,128)(2,1)} custom-call(s32[1]{0:T(128)S(6)} %sub.21.refs_0_, bf16[128,2048]{1,0:T(8,128)(2,1)} %refs_1_.6, bf16[128,256]{1,0:T(8,128)(2,1)} %refs_2_.6, bf16[128,256]{1,0:T(8,128)(2,1)} %refs_3_.4, f32[16,128]{1,0:T(8,128)} %bitcast.10), custom_call_target="tpu_custom_call" | custom-call | flops 1 | bytes 1 | tf_op jit(solution)/shard_map/pack/pallas_call | solution.py:68
  2.0 1.5 %collective-permute-start = (bf16[128,1408]{1,0:T(8,128)(2,1)}, bf16[128,1408]{1,0:T(8,128)(2,1)S(1)}, u32[]{:S(2)}, u32[]{:S(2)}) collective-permute-start(bf16[128,1408]{1,0:T(8,128)(2,1)} %pack.2), channel_id=1, source_target_pairs={{0,4},{4,0},{8,12},{12,8},{16,20},{20,16},{24,28},{28,24},{1,5},{5... | collective-permute-start | bytes 1081352 | tf_op jit(solution)/shard_map/ppermute | solution.py:364
  9.3 3.0 %collective-permute-done.refs_2_ = bf16[128,1408]{1,0:T(8,128)(2,1)S(1)} collective-permute-done((bf16[128,1408]{1,0:T(8,128)(2,1)}, bf16[128,1408]{1,0:T(8,128)(2,1)S(1)}, u32[]{:S(2)}, u32[]{:S(2)}) %collective-permute-start) | collective-permute-done | bytes 360480 | tf_op jit(solution)/shard_map/ppermute | solution.py:364
  13.6 3.5 %collective-permute-start.1 = (bf16[144,1024]{1,0:T(8,128)(2,1)S(1)}, bf16[144,1024]{1,0:T(8,128)(2,1)S(1)}, u32[]{:S(2)}, u32[]{:S(2)}) collective-permute-start(bf16[144,1024]{1,0:T(8,128)(2,1)S(1)} %get-tuple-element.45.send_ref), channel_id=1, source_target_pairs={{0,8},{4,12},{8,16},{12,20},{16,24},{20,28},{1,9},{5,13},{9,17},{1... | collective-permute-start | bytes 884744 | tf_op jit(solution)/shard_map/ppermute | solution.py:362
  18.1 1.6 %collective-permute-start.3 = (bf16[128,1024]{1,0:T(8,128)(2,1)S(1)}, bf16[128,1024]{1,0:T(8,128)(2,1)S(1)}, u32[]{:S(2)}, u32[]{:S(2)}) collective-permute-start(bf16[128,1024]{1,0:T(8,128)(2,1)S(1)} %constant_dynamic-slice_fusion), channel_id=1, source_target_pairs={{0,4},{4,0},{8,12},{12,8},{16,20},{20,16},{24,28},{28,24},{1,5},{5... | collective-permute-start | bytes 786440 | tf_op jit(solution)/shard_map/ppermute | solution.py:370
  20.8 1.7 %collective-permute-done.1.got_ref.refs_4_ = bf16[144,1024]{1,0:T(8,128)(2,1)S(1)} collective-permute-done((bf16[144,1024]{1,0:T(8,128)(2,1)S(1)}, bf16[144,1024]{1,0:T(8,128)(2,1)S(1)}, u32[]{:S(2)}, u32[]{:S(2)}) %collective-permute-start.1) | collective-permute-done | bytes 294944 | tf_op jit(solution)/shard_map/ppermute | solution.py:362
  22.6 5.4 %collective-permute-start.2 = (bf16[128,1024]{1,0:T(8,128)(2,1)S(1)}, bf16[128,1024]{1,0:T(8,128)(2,1)S(1)}, u32[]{:S(2)}, u32[]{:S(2)}) collective-permute-start(bf16[128,1024]{1,0:T(8,128)(2,1)S(1)} %join.1), channel_id=1, source_target_pairs={{0,16},{4,20},{8,24},{12,28},{1,17},{5,21},{9,25},{13,29},{2,18},{... | collective-permute-start | bytes 786440 | tf_op jit(solution)/shard_map/ppermute | solution.py:362
  28.0 3.8 %collective-permute-done.2.refs_5_ = bf16[128,1024]{1,0:T(8,128)(2,1)S(1)} collective-permute-done((bf16[128,1024]{1,0:T(8,128)(2,1)S(1)}, bf16[128,1024]{1,0:T(8,128)(2,1)S(1)}, u32[]{:S(2)}, u32[]{:S(2)}) %collective-permute-start.2) | collective-permute-done | bytes 262176 | tf_op jit(solution)/shard_map/ppermute | solution.py:362
  32.8 7.0 %collective-permute-start.4 = (bf16[256,1024]{1,0:T(8,128)(2,1)S(1)}, bf16[256,1024]{1,0:T(8,128)(2,1)S(1)}, u32[]{:S(2)}, u32[]{:S(2)}) collective-permute-start(bf16[256,1024]{1,0:T(8,128)(2,1)S(1)} %finish.1.own_ref), channel_id=1, source_target_pairs={{0,8},{4,12},{8,0},{12,4},{16,24},{20,28},{24,16},{28,20},{1,9},{5... | collective-permute-start | bytes 1572872 | tf_op jit(solution)/shard_map/ppermute | solution.py:381
  40.5 1.6 %collective-permute-start.8 = (bf16[256,1024]{1,0:T(8,128)(2,1)S(1)}, bf16[256,1024]{1,0:T(8,128)(2,1)S(1)}, u32[]{:S(2)}, u32[]{:S(2)}) collective-permute-start(bf16[256,1024]{1,0:T(8,128)(2,1)S(1)} %finish.1.own_ref), channel_id=1, source_target_pairs={{0,4},{4,0},{8,12},{12,8},{16,20},{20,16},{24,28},{28,24},{1,5},{5... | collective-permute-start | bytes 1572872 | tf_op jit(solution)/shard_map/ppermute | solution.py:384
  42.1 9.8 %collective-permute-done.4.own_ref = bf16[256,1024]{1,0:T(8,128)(2,1)S(1)} collective-permute-done((bf16[256,1024]{1,0:T(8,128)(2,1)S(1)}, bf16[256,1024]{1,0:T(8,128)(2,1)S(1)}, u32[]{:S(2)}, u32[]{:S(2)}) %collective-permute-start.4) | collective-permute-done | bytes 524320 | tf_op jit(solution)/shard_map/ppermute | solution.py:381
  52.6 1.3 collective-permute-start.7
  54.0 1.5 %collective-permute-start.11 = (bf16[256,1024]{1,0:T(8,128)(2,1)S(1)}, bf16[256,1024]{1,0:T(8,128)(2,1)S(1)}, u32[]{:S(2)}, u32[]{:S(2)}) collective-permute-start(bf16[256,1024]{1,0:T(8,128)(2,1)S(1)} %collective-permute-done.4.own_ref), channel_id=1, source_target_pairs={{0,4},{4,0},{8,12},{12,8},{16,20},{20,16},{24,28},{28,24},{1,5},{5... | collective-permute-start | bytes 1572872 | tf_op jit(solution)/shard_map/ppermute | solution.py:384
  56.3 2.2 %copy-done = bf16[2048,1024]{1,0:T(8,128)(2,1)S(1)} copy-done((bf16[2048,1024]{1,0:T(8,128)(2,1)S(1)}, bf16[2048,1024]{1,0:T(8,128)(2,1)}, u32[]{:S(2)}) %copy-start) | copy-done | bytes 4194328
  58.5 3.1 %project.4 = (f32[128,1024]{1,0:T(8,128)S(1)}, bf16[128,1024]{1,0:T(8,128)(2,1)S(1)}) custom-call(s32[3]{0:T(128)S(1)} %pad_add_fusion.yc_ref, bf16[256,1024]{1,0:T(8,128)(2,1)S(1)} %finish.1.own_ref, bf16[256,1024]{1,0:T(8,128)(2,1)S(1)} %collective-permute-done.8.refs_0_, bf16[2048,1024]{1,0:T(8,128)(2,1)S(1)} %copy-done, bf16[2048,1024]{1,0:T(8,128)(2,1)S(1)} %copy-done), custom_call_target="tpu_custom_call" | custom-call | flops 1 | bytes 1 | tf_op jit(solution)/shard_map/project/pallas_call | solution.py:291
  61.6 8.8 %collective-permute-done.7 = bf16[256,1024]{1,0:T(8,128)(2,1)S(1)} collective-permute-done((bf16[256,1024]{1,0:T(8,128)(2,1)S(1)}, bf16[256,1024]{1,0:T(8,128)(2,1)S(1)}, u32[]{:S(2)}, u32[]{:S(2)}) %collective-permute-start.7) | collective-permute-done | bytes 524320 | tf_op jit(solution)/shard_map/ppermute | solution.py:381
  71.7 1.6 %collective-permute-start.14 = (bf16[256,1024]{1,0:T(8,128)(2,1)S(1)}, bf16[256,1024]{1,0:T(8,128)(2,1)S(1)}, u32[]{:S(2)}, u32[]{:S(2)}) collective-permute-start(bf16[256,1024]{1,0:T(8,128)(2,1)S(1)} %broadcast_select_fusion.1.own_ref), channel_id=1, source_target_pairs={{0,4},{4,0},{8,12},{12,8},{16,20},{20,16},{24,28},{28,24},{1,5},{5... | collective-permute-start | bytes 1572872 | tf_op jit(solution)/shard_map/ppermute | solution.py:384
  73.3 3.1 %project.5 = (f32[128,1024]{1,0:T(8,128)S(1)}, bf16[128,1024]{1,0:T(8,128)(2,1)S(1)}) custom-call(s32[3]{0:T(128)S(1)} %pad_add_fusion.yc_ref, bf16[256,1024]{1,0:T(8,128)(2,1)S(1)} %collective-permute-done.4.own_ref, bf16[256,1024]{1,0:T(8,128)(2,1)S(1)} %collective-permute-done.11.refs_0_, bf16[2048,1024]{1,0:T(8,128)(2,1)S(1)} %copy-done.1, ...), custom_call_target="tpu_custom_call" | custom-call | flops 1 | bytes 1 | tf_op jit(solution)/shard_map/project/pallas_call | solution.py:291
  76.5 8.1 %collective-permute-done.9 = bf16[256,1024]{1,0:T(8,128)(2,1)S(1)} collective-permute-done((bf16[256,1024]{1,0:T(8,128)(2,1)S(1)}, bf16[256,1024]{1,0:T(8,128)(2,1)S(1)}, u32[]{:S(2)}, u32[]{:S(2)}) %collective-permute-start.9) | collective-permute-done | bytes 524320 | tf_op jit(solution)/shard_map/ppermute | solution.py:381
  84.6 1.3 collective-permute-start.15
  85.9 3.4 %collective-permute-start.13 = (bf16[128,1024]{1,0:T(8,128)(2,1)S(1)}, bf16[128,1024]{1,0:T(8,128)(2,1)S(1)}, u32[]{:S(2)}, u32[]{:S(2)}) collective-permute-start(bf16[128,1024]{1,0:T(8,128)(2,1)S(1)} %slice.6), channel_id=1, source_target_pairs={{0,4},{4,0},{24,28},{28,24},{1,5},{5,1},{25,29},{29,25},{2,6},{6,2... | collective-permute-start | bytes 786440 | tf_op jit(solution)/shard_map/ppermute | solution.py:419
  89.5 3.1 %project.6 = (f32[128,1024]{1,0:T(8,128)S(1)}, bf16[128,1024]{1,0:T(8,128)(2,1)S(1)}) custom-call(s32[3]{0:T(128)S(1)} %pad_add_fusion.yc_ref, bf16[256,1024]{1,0:T(8,128)(2,1)S(1)} %broadcast_select_fusion.1.own_ref, bf16[256,1024]{1,0:T(8,128)(2,1)S(1)} %collective-permute-done.14.refs_0_, bf16[2048,1024]{1,0:T(8,128)(2,1)S(1)} %copy-done.1, ...), custom_call_target="tpu_custom_call" | custom-call | flops 1 | bytes 1 | tf_op jit(solution)/shard_map/project/pallas_call | solution.py:291
  92.7 2.6 %collective-permute-done.15.refs_2_ = bf16[128,1024]{1,0:T(8,128)(2,1)S(1)} collective-permute-done((bf16[128,1024]{1,0:T(8,128)(2,1)S(1)}, bf16[128,1024]{1,0:T(8,128)(2,1)S(1)}, u32[]{:S(2)}, u32[]{:S(2)}) %collective-permute-start.15) | collective-permute-done | bytes 262176 | tf_op jit(solution)/shard_map/ppermute | solution.py:381
  95.2 1.3 %collective-permute-done.13.refs_1_ = bf16[128,1024]{1,0:T(8,128)(2,1)S(1)} collective-permute-done((bf16[128,1024]{1,0:T(8,128)(2,1)S(1)}, bf16[128,1024]{1,0:T(8,128)(2,1)S(1)}, u32[]{:S(2)}, u32[]{:S(2)}) %collective-permute-start.13) | collective-permute-done | bytes 262176 | tf_op jit(solution)/shard_map/ppermute | solution.py:419
  96.6 3.1 %project.7 = (f32[128,1024]{1,0:T(8,128)S(1)}, bf16[128,1024]{1,0:T(8,128)(2,1)S(1)}) custom-call(s32[3]{0:T(128)S(1)} %pad_add_fusion.yc_ref, bf16[256,1024]{1,0:T(8,128)(2,1)S(1)} %broadcast_select_fusion.own_ref, bf16[256,1024]{1,0:T(8,128)(2,1)S(1)} %collective-permute-done.10.refs_0_, bf16[128,1024]{1,0:T(8,128)(2,1)S(1)} %collective-permute-done.13.refs_1_, ...), custom_call_target="tpu_custom_call" | custom-call | flops 1 | bytes 1 | tf_op jit(solution)/shard_map/project/pallas_call | solution.py:291
  101.4 1.6 %collective-permute-start.21 = (bf16[128,1024]{1,0:T(8,128)(2,1)S(1)}, bf16[128,1024]{1,0:T(8,128)(2,1)S(1)}, u32[]{:S(2)}, u32[]{:S(2)}) collective-permute-start(bf16[128,1024]{1,0:T(8,128)(2,1)S(1)} %get-tuple-element.81), channel_id=1, source_target_pairs={{0,8},{1,12},{2,24},{3,28},{4,9},{5,13},{6,25},{7,29},{8,0},{9,4},... | collective-permute-start | bytes 786440 | tf_op jit(solution)/shard_map/ppermute | solution.py:398
  103.6 3.0 %collective-permute-start.18 = (bf16[128,1024]{1,0:T(8,128)(2,1)S(1)}, bf16[128,1024]{1,0:T(8,128)(2,1)S(1)}, u32[]{:S(2)}, u32[]{:S(2)}) collective-permute-start(bf16[128,1024]{1,0:T(8,128)(2,1)S(1)} %get-tuple-element.79), channel_id=1, source_target_pairs={{1,4},{2,16},{3,20},{4,1},{6,17},{7,21},{9,12},{10,24},{11,28},{12... | collective-permute-start | bytes 786440 | tf_op jit(solution)/shard_map/ppermute | solution.py:398
  107.6 5.5 %collective-permute-done.21 = bf16[128,1024]{1,0:T(8,128)(2,1)S(1)} collective-permute-done((bf16[128,1024]{1,0:T(8,128)(2,1)S(1)}, bf16[128,1024]{1,0:T(8,128)(2,1)S(1)}, u32[]{:S(2)}, u32[]{:S(2)}) %collective-permute-start.21) | collective-permute-done | bytes 262176 | tf_op jit(solution)/shard_map/ppermute | solution.py:398
  113.2 2.7 %collective-permute-done.22 = bf16[128,1024]{1,0:T(8,128)(2,1)S(1)} collective-permute-done((bf16[128,1024]{1,0:T(8,128)(2,1)S(1)}, bf16[128,1024]{1,0:T(8,128)(2,1)S(1)}, u32[]{:S(2)}, u32[]{:S(2)}) %collective-permute-start.22) | collective-permute-done | bytes 262176 | tf_op jit(solution)/shard_map/ppermute | solution.py:398
  115.9 9.9 %collective-permute-done.18 = bf16[128,1024]{1,0:T(8,128)(2,1)S(1)} collective-permute-done((bf16[128,1024]{1,0:T(8,128)(2,1)S(1)}, bf16[128,1024]{1,0:T(8,128)(2,1)S(1)}, u32[]{:S(2)}, u32[]{:S(2)}) %collective-permute-start.18) | collective-permute-done | bytes 262176 | tf_op jit(solution)/shard_map/ppermute | solution.py:398
  125.8 1.5 %collective-permute-done.19 = bf16[128,1024]{1,0:T(8,128)(2,1)S(1)} collective-permute-done((bf16[128,1024]{1,0:T(8,128)(2,1)S(1)}, bf16[128,1024]{1,0:T(8,128)(2,1)S(1)}, u32[]{:S(2)}, u32[]{:S(2)}) %collective-permute-start.19) | collective-permute-done | bytes 262176 | tf_op jit(solution)/shard_map/ppermute | solution.py:398
  127.9 1.3 collective-permute-done.23.got_ref
  (57 shorter events, 18.5 us)
Async XLA Ops:
  0.0 31.8 %copy-start.3 = (bf16[128,2048]{1,0:T(8,128)(2,1)S(1)}, bf16[128,2048]{1,0:T(8,128)(2,1)}, u32[]{:S(2)}) copy-start(bf16[128,2048]{1,0:T(8,128)(2,1)} %refs_6_.1) | copy-start | bytes 1572868
  2.0 10.4 %collective-permute-start = (bf16[128,1408]{1,0:T(8,128)(2,1)}, bf16[128,1408]{1,0:T(8,128)(2,1)S(1)}, u32[]{:S(2)}, u32[]{:S(2)}) collective-permute-start(bf16[128,1408]{1,0:T(8,128)(2,1)} %pack.2), channel_id=1, source_target_pairs={{0,4},{4,0},{8,12},{12,8},{16,20},{20,16},{24,28},{28,24},{1,5},{5... | collective-permute-start | bytes 1081352 | tf_op jit(solution)/shard_map/ppermute | solution.py:364
  3.5 1.0 copy-start.2
  4.6 0.8 copy-start.4
  5.4 0.8 copy-start.5
  6.2 0.7 copy-start.6
  13.6 8.9 %collective-permute-start.1 = (bf16[144,1024]{1,0:T(8,128)(2,1)S(1)}, bf16[144,1024]{1,0:T(8,128)(2,1)S(1)}, u32[]{:S(2)}, u32[]{:S(2)}) collective-permute-start(bf16[144,1024]{1,0:T(8,128)(2,1)S(1)} %get-tuple-element.45.send_ref), channel_id=1, source_target_pairs={{0,8},{4,12},{8,16},{12,20},{16,24},{20,28},{1,9},{5,13},{9,17},{1... | collective-permute-start | bytes 884744 | tf_op jit(solution)/shard_map/ppermute | solution.py:362
  18.1 9.9 %collective-permute-start.3 = (bf16[128,1024]{1,0:T(8,128)(2,1)S(1)}, bf16[128,1024]{1,0:T(8,128)(2,1)S(1)}, u32[]{:S(2)}, u32[]{:S(2)}) collective-permute-start(bf16[128,1024]{1,0:T(8,128)(2,1)S(1)} %constant_dynamic-slice_fusion), channel_id=1, source_target_pairs={{0,4},{4,0},{8,12},{12,8},{16,20},{20,16},{24,28},{28,24},{1,5},{5... | collective-permute-start | bytes 786440 | tf_op jit(solution)/shard_map/ppermute | solution.py:370
  22.6 9.3 %collective-permute-start.2 = (bf16[128,1024]{1,0:T(8,128)(2,1)S(1)}, bf16[128,1024]{1,0:T(8,128)(2,1)S(1)}, u32[]{:S(2)}, u32[]{:S(2)}) collective-permute-start(bf16[128,1024]{1,0:T(8,128)(2,1)S(1)} %join.1), channel_id=1, source_target_pairs={{0,16},{4,20},{8,24},{12,28},{1,17},{5,21},{9,25},{13,29},{2,18},{... | collective-permute-start | bytes 786440 | tf_op jit(solution)/shard_map/ppermute | solution.py:362
  32.8 19.1 %collective-permute-start.4 = (bf16[256,1024]{1,0:T(8,128)(2,1)S(1)}, bf16[256,1024]{1,0:T(8,128)(2,1)S(1)}, u32[]{:S(2)}, u32[]{:S(2)}) collective-permute-start(bf16[256,1024]{1,0:T(8,128)(2,1)S(1)} %finish.1.own_ref), channel_id=1, source_target_pairs={{0,8},{4,12},{8,0},{12,4},{16,24},{20,28},{24,16},{28,20},{1,9},{5... | collective-permute-start | bytes 1572872 | tf_op jit(solution)/shard_map/ppermute | solution.py:381
  39.9 12.8 %collective-permute-start.6 = (bf16[256,1024]{1,0:T(8,128)(2,1)S(1)}, bf16[256,1024]{1,0:T(8,128)(2,1)S(1)}, u32[]{:S(2)}, u32[]{:S(2)}) collective-permute-start(bf16[256,1024]{1,0:T(8,128)(2,1)S(1)} %finish.1.own_ref), channel_id=1, source_target_pairs={{8,16},{12,20},{16,8},{20,12},{9,17},{13,21},{17,9},{21,13},{10,18... | collective-permute-start | bytes 1572872 | tf_op jit(solution)/shard_map/ppermute | solution.py:381
  40.5 15.0 %collective-permute-start.8 = (bf16[256,1024]{1,0:T(8,128)(2,1)S(1)}, bf16[256,1024]{1,0:T(8,128)(2,1)S(1)}, u32[]{:S(2)}, u32[]{:S(2)}) collective-permute-start(bf16[256,1024]{1,0:T(8,128)(2,1)S(1)} %finish.1.own_ref), channel_id=1, source_target_pairs={{0,4},{4,0},{8,12},{12,8},{16,20},{20,16},{24,28},{28,24},{1,5},{5... | collective-permute-start | bytes 1572872 | tf_op jit(solution)/shard_map/ppermute | solution.py:384
  51.9 9.6 %collective-permute-start.5 = (bf16[256,1024]{1,0:T(8,128)(2,1)S(1)}, bf16[256,1024]{1,0:T(8,128)(2,1)S(1)}, u32[]{:S(2)}, u32[]{:S(2)}) collective-permute-start(bf16[256,1024]{1,0:T(8,128)(2,1)S(1)} %collective-permute-done.4.own_ref), channel_id=1, source_target_pairs={{8,16},{12,20},{16,8},{20,12},{9,17},{13,21},{17,9},{21,13},{10,18... | collective-permute-start | bytes 1572872 | tf_op jit(solution)/shard_map/ppermute | solution.py:381
  52.6 17.7 %collective-permute-start.7 = (bf16[256,1024]{1,0:T(8,128)(2,1)S(1)}, bf16[256,1024]{1,0:T(8,128)(2,1)S(1)}, u32[]{:S(2)}, u32[]{:S(2)}) collective-permute-start(bf16[256,1024]{1,0:T(8,128)(2,1)S(1)} %collective-permute-done.6), channel_id=1, source_target_pairs={{8,0},{12,4},{16,24},{20,28},{9,1},{13,5},{17,25},{21,29},{10,2},{... | collective-permute-start | bytes 1572872 | tf_op jit(solution)/shard_map/ppermute | solution.py:381
  54.0 19.2 %collective-permute-start.11 = (bf16[256,1024]{1,0:T(8,128)(2,1)S(1)}, bf16[256,1024]{1,0:T(8,128)(2,1)S(1)}, u32[]{:S(2)}, u32[]{:S(2)}) collective-permute-start(bf16[256,1024]{1,0:T(8,128)(2,1)S(1)} %collective-permute-done.4.own_ref), channel_id=1, source_target_pairs={{0,4},{4,0},{8,12},{12,8},{16,20},{20,16},{24,28},{28,24},{1,5},{5... | collective-permute-start | bytes 1572872 | tf_op jit(solution)/shard_map/ppermute | solution.py:384
  55.6 20.9 %collective-permute-start.10 = (bf16[256,1024]{1,0:T(8,128)(2,1)S(1)}, bf16[256,1024]{1,0:T(8,128)(2,1)S(1)}, u32[]{:S(2)}, u32[]{:S(2)}) collective-permute-start(bf16[256,1024]{1,0:T(8,128)(2,1)S(1)} %collective-permute-done.8.refs_0_), channel_id=1, source_target_pairs={{8,16},{12,20},{16,8},{20,12},{9,17},{13,21},{17,9},{21,13},{10,18... | collective-permute-start | bytes 1572872 | tf_op jit(solution)/shard_map/ppermute | solution.py:381
  56.3 2.2 %copy-start = (bf16[2048,1024]{1,0:T(8,128)(2,1)S(1)}, bf16[2048,1024]{1,0:T(8,128)(2,1)}, u32[]{:S(2)}) copy-start(bf16[2048,1024]{1,0:T(8,128)(2,1)} %refs_4_.1) | copy-start | bytes 12582916
  58.5 14.8 %copy-start.1 = (bf16[2048,1024]{1,0:T(8,128)(2,1)S(1)}, bf16[2048,1024]{1,0:T(8,128)(2,1)}, u32[]{:S(2)}) copy-start(bf16[2048,1024]{1,0:T(8,128)(2,1)} %refs_4_.1) | copy-start | bytes 12582916
  70.3 14.3 %collective-permute-start.9 = (bf16[256,1024]{1,0:T(8,128)(2,1)S(1)}, bf16[256,1024]{1,0:T(8,128)(2,1)S(1)}, u32[]{:S(2)}, u32[]{:S(2)}) collective-permute-start(bf16[256,1024]{1,0:T(8,128)(2,1)S(1)} %collective-permute-done.5), channel_id=1, source_target_pairs={{8,0},{12,4},{16,24},{20,28},{9,1},{13,5},{17,25},{21,29},{10,2},{... | collective-permute-start | bytes 1572872 | tf_op jit(solution)/shard_map/ppermute | solution.py:381
  71.7 12.9 %collective-permute-start.14 = (bf16[256,1024]{1,0:T(8,128)(2,1)S(1)}, bf16[256,1024]{1,0:T(8,128)(2,1)S(1)}, u32[]{:S(2)}, u32[]{:S(2)}) collective-permute-start(bf16[256,1024]{1,0:T(8,128)(2,1)S(1)} %broadcast_select_fusion.1.own_ref), channel_id=1, source_target_pairs={{0,4},{4,0},{8,12},{12,8},{16,20},{20,16},{24,28},{28,24},{1,5},{5... | collective-permute-start | bytes 1572872 | tf_op jit(solution)/shard_map/ppermute | solution.py:384
  73.3 3.1 %collective-permute-start.12 = (bf16[128,1024]{1,0:T(8,128)(2,1)S(1)}, bf16[128,1024]{1,0:T(8,128)(2,1)S(1)}, u32[]{:S(2)}, u32[]{:S(2)}) collective-permute-start(bf16[128,1024]{1,0:T(8,128)(2,1)S(1)} %get-tuple-element.61), channel_id=1, source_target_pairs={{0,1},{1,0},{2,3},{3,2},{4,5},{5,4},{6,7},{7,6},{8,9},{9,8},{10,11... | collective-permute-start | bytes 786440 | tf_op jit(solution)/shard_map/ppermute | solution.py:385
  84.6 8.0 %collective-permute-start.16 = (bf16[128,1024]{1,0:T(8,128)(2,1)S(1)}, bf16[128,1024]{1,0:T(8,128)(2,1)S(1)}, u32[]{:S(2)}, u32[]{:S(2)}) collective-permute-start(bf16[128,1024]{1,0:T(8,128)(2,1)S(1)} %get-tuple-element.68), channel_id=1, source_target_pairs={{0,1},{1,0},{2,3},{3,2},{4,5},{5,4},{6,7},{7,6},{8,9},{9,8},{10,11... | collective-permute-start | bytes 786440 | tf_op jit(solution)/shard_map/ppermute | solution.py:385
  84.6 10.6 %collective-permute-start.15 = (bf16[128,1024]{1,0:T(8,128)(2,1)S(1)}, bf16[128,1024]{1,0:T(8,128)(2,1)S(1)}, u32[]{:S(2)}, u32[]{:S(2)}) collective-permute-start(bf16[128,1024]{1,0:T(8,128)(2,1)S(1)} %slice.8), channel_id=1, source_target_pairs={{8,0},{12,4},{16,24},{20,28},{9,1},{13,5},{17,25},{21,29},{10,2},{... | collective-permute-start | bytes 786440 | tf_op jit(solution)/shard_map/ppermute | solution.py:381
  85.9 10.6 %collective-permute-start.13 = (bf16[128,1024]{1,0:T(8,128)(2,1)S(1)}, bf16[128,1024]{1,0:T(8,128)(2,1)S(1)}, u32[]{:S(2)}, u32[]{:S(2)}) collective-permute-start(bf16[128,1024]{1,0:T(8,128)(2,1)S(1)} %slice.6), channel_id=1, source_target_pairs={{0,4},{4,0},{24,28},{28,24},{1,5},{5,1},{25,29},{29,25},{2,6},{6,2... | collective-permute-start | bytes 786440 | tf_op jit(solution)/shard_map/ppermute | solution.py:419
  99.7 1.6 %collective-permute-start.20 = (bf16[128,1024]{1,0:T(8,128)(2,1)S(1)}, bf16[128,1024]{1,0:T(8,128)(2,1)S(1)}, u32[]{:S(2)}, u32[]{:S(2)}) collective-permute-start(bf16[128,1024]{1,0:T(8,128)(2,1)S(1)} %get-tuple-element.76), channel_id=1, source_target_pairs={{0,1},{1,0},{2,3},{3,2},{4,5},{5,4},{6,7},{7,6},{8,9},{9,8},{10,11... | collective-permute-start | bytes 786440 | tf_op jit(solution)/shard_map/ppermute | solution.py:385
  99.8 3.7 %collective-permute-start.17 = (bf16[128,1024]{1,0:T(8,128)(2,1)S(1)}, bf16[128,1024]{1,0:T(8,128)(2,1)S(1)}, u32[]{:S(2)}, u32[]{:S(2)}) collective-permute-start(bf16[128,1024]{1,0:T(8,128)(2,1)S(1)} %get-tuple-element.70), channel_id=1, source_target_pairs={{0,1},{1,0},{2,3},{3,2},{4,5},{5,4},{6,7},{7,6},{8,9},{9,8},{10,11... | collective-permute-start | bytes 786440 | tf_op jit(solution)/shard_map/ppermute | solution.py:385
  101.4 11.8 %collective-permute-start.21 = (bf16[128,1024]{1,0:T(8,128)(2,1)S(1)}, bf16[128,1024]{1,0:T(8,128)(2,1)S(1)}, u32[]{:S(2)}, u32[]{:S(2)}) collective-permute-start(bf16[128,1024]{1,0:T(8,128)(2,1)S(1)} %get-tuple-element.81), channel_id=1, source_target_pairs={{0,8},{1,12},{2,24},{3,28},{4,9},{5,13},{6,25},{7,29},{8,0},{9,4},... | collective-permute-start | bytes 786440 | tf_op jit(solution)/shard_map/ppermute | solution.py:398
  103.1 12.8 %collective-permute-start.22 = (bf16[128,1024]{1,0:T(8,128)(2,1)S(1)}, bf16[128,1024]{1,0:T(8,128)(2,1)S(1)}, u32[]{:S(2)}, u32[]{:S(2)}) collective-permute-start(bf16[128,1024]{1,0:T(8,128)(2,1)S(1)} %get-tuple-element.82), channel_id=1, source_target_pairs={{0,24},{1,28},{2,8},{3,12},{4,25},{5,29},{6,9},{7,13},{8,16},{9,20... | collective-permute-start | bytes 786440 | tf_op jit(solution)/shard_map/ppermute | solution.py:398
  103.6 22.2 %collective-permute-start.18 = (bf16[128,1024]{1,0:T(8,128)(2,1)S(1)}, bf16[128,1024]{1,0:T(8,128)(2,1)S(1)}, u32[]{:S(2)}, u32[]{:S(2)}) collective-permute-start(bf16[128,1024]{1,0:T(8,128)(2,1)S(1)} %get-tuple-element.79), channel_id=1, source_target_pairs={{1,4},{2,16},{3,20},{4,1},{6,17},{7,21},{9,12},{10,24},{11,28},{12... | collective-permute-start | bytes 786440 | tf_op jit(solution)/shard_map/ppermute | solution.py:398
  106.7 20.7 %collective-permute-start.19 = (bf16[128,1024]{1,0:T(8,128)(2,1)S(1)}, bf16[128,1024]{1,0:T(8,128)(2,1)S(1)}, u32[]{:S(2)}, u32[]{:S(2)}) collective-permute-start(bf16[128,1024]{1,0:T(8,128)(2,1)S(1)} %get-tuple-element.80), channel_id=1, source_target_pairs={{0,16},{1,20},{2,0},{3,4},{4,17},{5,21},{6,1},{7,5},{8,24},{9,28},... | collective-permute-start | bytes 786440 | tf_op jit(solution)/shard_map/ppermute | solution.py:398
  127.6 1.6 %collective-permute-start.23 = (bf16[128,1024]{1,0:T(8,128)(2,1)S(1)}, bf16[128,1024]{1,0:T(8,128)(2,1)S(1)}, u32[]{:S(2)}, u32[]{:S(2)}) collective-permute-start(bf16[128,1024]{1,0:T(8,128)(2,1)S(1)} %get-tuple-element.77), channel_id=1, source_target_pairs={{0,1},{1,0},{2,3},{3,2},{4,5},{5,4},{6,7},{7,6},{8,9},{9,8},{10,11... | collective-permute-start | bytes 786440 | tf_op jit(solution)/shard_map/ppermute | solution.py:385

commit v7 on v6

--- a/solution.py
+++ b/solution.py
@@ -407,7 +407,7 @@
     inward, outward = hop(slot1, (1, 2), (2, 1)), hop(middle, (1, 0), (2, 3))
     other1 = across(slot1)
     a0 = project(yc, block, [other0], w_out)
-    inward, outward, a0 = tie((inward, outward, a0))
+    inward, a0 = tie((inward, a0))
     last = hop(inward, (1, 0), (2, 3))
     slot2 = jnp.where(inner, inward, outward)
     other2 = across(slot2)
@@ -418,14 +418,15 @@
     slot3 = jnp.where(inner, middle, last)
     lower3 = lax.ppermute(last[:tokens], "seq", [(i * 2 + b, i * 2 + 1 - b) for i in (0, 3) for b in range(2)])
     upper3 = hop(other2[tokens:], (1, 0), (2, 3))
-    b1 = reduce_core(*a1)
     a2 = project(yc, slot2, [other2], w_out)
-    lower3, upper3, a2, b1 = tie((lower3, upper3, a2, b1))
-    b2 = reduce_core(*a2)
+    rounded = jnp.concatenate([a1[1], a2[1]])
+    lower3, upper3, rounded = tie((lower3, upper3, rounded))
+    sums = cross(rounded).reshape(2, tokens, -1)
+    b1, b2 = ((part[0] + v.astype(F32)).astype(BF16) for part, v in zip((a1, a2), sums))
     b3 = reduce_core(*project(yc, slot3, [inner3, lower3, upper3], w_out))
+    b0, b1, b2, b3 = tie((b0, b1, b2, b3))
+    odd = deliver(1, b1, b3)
     even = deliver(0, b0, b2)
-    b3, = tie((b3,))
-    odd = deliver(1, b1, b3)
     here = core == z % 2
     mine, theirs = jnp.where(here, even, odd), jnp.where(here, odd, even)
     return place(core.astype(jnp.int32).reshape(1), mine.astype(BF16), cross(theirs.astype(BF16)))

time: 131 us -> 129 us (0.985)
  waiting for transfers between devices: 61.2 us -> 57.3 us
    ppermute x7, waiting for transfers between devices: 29.3 us -> 24 us  [pair_shards(): lax.ppermute(value, 'seq', [(i * 2 + b, j * 2 + b) for i, j in moves for...]
  transfers between devices with their start and end apart: 24 -> 23, of which waited for: 14 -> 15; matrix products, arithmetic and copies ran while one was open for 3% -> 3% of each run, Pallas kernels for 8% -> 11%
where the time goes in v7:
time: 129 us; the launch traced here: 127 us
  waiting for transfers between devices  57.3 us (44%)
  starting transfers between devices  40.2 us (31%)
  Pallas kernels  18.8 us (15%)
  local copies, waits for them, and re-layouts  8.85 us (7%)
  other arithmetic  1.84 us (1%)
    ppermute x7, waiting for transfers between devices, pair_shards(): lax.ppermute(value, 'seq', [(i * 2 + b, j * 2 + b) for i, j in moves for...  24 us
    ppermute x4, waiting for transfers between devices, deliver(): moved = lax.ppermute(value, both, [(i, j) for i, j in pairs if i != j])  19.8 us
    ppermute x7, starting transfers between devices, pair_shards(): lax.ppermute(value, 'seq', [(i * 2 + b, j * 2 + b) for i, j in moves for...  13 us
    pallas_call x4, Pallas kernels, project(): pl.pallas_call(project_kernel, grid_spec=pltpu.PrefetchScalarGridSpec(num...  12.4 us
    ppermute x2, starting transfers between devices, along(): return lax.ppermute(v, 'seq', pairs)  8.91 us
    ppermute x4, starting transfers between devices, deliver(): moved = lax.ppermute(value, both, [(i, j) for i, j in pairs if i != j])  6.08 us
    unnamed x14, local copies, waits for them, and re-layouts  5.61 us
    ppermute x2, waiting for transfers between devices, along(): return lax.ppermute(v, 'seq', pairs)  5.54 us
  transfers between devices with their start and end apart: 23, of which 15 were waited for; matrix products, arithmetic and copies ran while one was open for 3% of the time, Pallas kernels for 11%

profile of v7, /device:TPU:2, one launch (start us, length us, event | category | flops | bytes accessed | tf_op | source)
XLA Modules:
  0.0 127.4 jit_solution(6685779124949532227)
XLA Ops:
  0.0 2.0 %pack.2 = bf16[128,1408]{1,0:T(8,128)(2,1)} custom-call(s32[1]{0:T(128)S(6)} %sub.21.refs_0_, bf16[128,2048]{1,0:T(8,128)(2,1)} %refs_1_.6, bf16[128,256]{1,0:T(8,128)(2,1)} %refs_2_.6, bf16[128,256]{1,0:T(8,128)(2,1)} %refs_3_.4, f32[16,128]{1,0:T(8,128)} %bitcast.10), custom_call_target="tpu_custom_call" | custom-call | flops 1 | bytes 1 | tf_op jit(solution)/shard_map/pack/pallas_call | solution.py:68
  2.0 1.5 %collective-permute-start = (bf16[128,1408]{1,0:T(8,128)(2,1)}, bf16[128,1408]{1,0:T(8,128)(2,1)S(1)}, u32[]{:S(2)}, u32[]{:S(2)}) collective-permute-start(bf16[128,1408]{1,0:T(8,128)(2,1)} %pack.2), channel_id=1, source_target_pairs={{0,4},{4,0},{8,12},{12,8},{16,20},{20,16},{24,28},{28,24},{1,5},{5... | collective-permute-start | bytes 1081352 | tf_op jit(solution)/shard_map/ppermute | solution.py:364
  9.3 3.0 %collective-permute-done.refs_2_ = bf16[128,1408]{1,0:T(8,128)(2,1)S(1)} collective-permute-done((bf16[128,1408]{1,0:T(8,128)(2,1)}, bf16[128,1408]{1,0:T(8,128)(2,1)S(1)}, u32[]{:S(2)}, u32[]{:S(2)}) %collective-permute-start) | collective-permute-done | bytes 360480 | tf_op jit(solution)/shard_map/ppermute | solution.py:364
  13.6 3.5 %collective-permute-start.1 = (bf16[144,1024]{1,0:T(8,128)(2,1)S(1)}, bf16[144,1024]{1,0:T(8,128)(2,1)S(1)}, u32[]{:S(2)}, u32[]{:S(2)}) collective-permute-start(bf16[144,1024]{1,0:T(8,128)(2,1)S(1)} %get-tuple-element.46.send_ref), channel_id=1, source_target_pairs={{0,8},{4,12},{8,16},{12,20},{16,24},{20,28},{1,9},{5,13},{9,17},{1... | collective-permute-start | bytes 884744 | tf_op jit(solution)/shard_map/ppermute | solution.py:362
  18.1 1.6 %collective-permute-start.3 = (bf16[128,1024]{1,0:T(8,128)(2,1)S(1)}, bf16[128,1024]{1,0:T(8,128)(2,1)S(1)}, u32[]{:S(2)}, u32[]{:S(2)}) collective-permute-start(bf16[128,1024]{1,0:T(8,128)(2,1)S(1)} %constant_dynamic-slice_fusion), channel_id=1, source_target_pairs={{0,4},{4,0},{8,12},{12,8},{16,20},{20,16},{24,28},{28,24},{1,5},{5... | collective-permute-start | bytes 786440 | tf_op jit(solution)/shard_map/ppermute | solution.py:370
  20.8 1.7 %collective-permute-done.1.got_ref.refs_4_ = bf16[144,1024]{1,0:T(8,128)(2,1)S(1)} collective-permute-done((bf16[144,1024]{1,0:T(8,128)(2,1)S(1)}, bf16[144,1024]{1,0:T(8,128)(2,1)S(1)}, u32[]{:S(2)}, u32[]{:S(2)}) %collective-permute-start.1) | collective-permute-done | bytes 294944 | tf_op jit(solution)/shard_map/ppermute | solution.py:362
  22.6 5.4 %collective-permute-start.2 = (bf16[128,1024]{1,0:T(8,128)(2,1)S(1)}, bf16[128,1024]{1,0:T(8,128)(2,1)S(1)}, u32[]{:S(2)}, u32[]{:S(2)}) collective-permute-start(bf16[128,1024]{1,0:T(8,128)(2,1)S(1)} %join.1), channel_id=1, source_target_pairs={{0,16},{4,20},{8,24},{12,28},{1,17},{5,21},{9,25},{13,29},{2,18},{... | collective-permute-start | bytes 786440 | tf_op jit(solution)/shard_map/ppermute | solution.py:362
  28.0 3.8 %collective-permute-done.2.refs_5_ = bf16[128,1024]{1,0:T(8,128)(2,1)S(1)} collective-permute-done((bf16[128,1024]{1,0:T(8,128)(2,1)S(1)}, bf16[128,1024]{1,0:T(8,128)(2,1)S(1)}, u32[]{:S(2)}, u32[]{:S(2)}) %collective-permute-start.2) | collective-permute-done | bytes 262176 | tf_op jit(solution)/shard_map/ppermute | solution.py:362
  32.8 7.0 %collective-permute-start.4 = (bf16[256,1024]{1,0:T(8,128)(2,1)S(1)}, bf16[256,1024]{1,0:T(8,128)(2,1)S(1)}, u32[]{:S(2)}, u32[]{:S(2)}) collective-permute-start(bf16[256,1024]{1,0:T(8,128)(2,1)S(1)} %finish.1.own_ref), channel_id=1, source_target_pairs={{0,8},{4,12},{8,0},{12,4},{16,24},{20,28},{24,16},{28,20},{1,9},{5... | collective-permute-start | bytes 1572872 | tf_op jit(solution)/shard_map/ppermute | solution.py:381
  40.5 1.6 %collective-permute-start.6 = (bf16[256,1024]{1,0:T(8,128)(2,1)S(1)}, bf16[256,1024]{1,0:T(8,128)(2,1)S(1)}, u32[]{:S(2)}, u32[]{:S(2)}) collective-permute-start(bf16[256,1024]{1,0:T(8,128)(2,1)S(1)} %finish.1.own_ref), channel_id=1, source_target_pairs={{0,4},{4,0},{8,12},{12,8},{16,20},{20,16},{24,28},{28,24},{1,5},{5... | collective-permute-start | bytes 1572872 | tf_op jit(solution)/shard_map/ppermute | solution.py:384
  42.1 9.8 %collective-permute-done.4.own_ref = bf16[256,1024]{1,0:T(8,128)(2,1)S(1)} collective-permute-done((bf16[256,1024]{1,0:T(8,128)(2,1)S(1)}, bf16[256,1024]{1,0:T(8,128)(2,1)S(1)}, u32[]{:S(2)}, u32[]{:S(2)}) %collective-permute-start.4) | collective-permute-done | bytes 524320 | tf_op jit(solution)/shard_map/ppermute | solution.py:381
  52.6 1.3 %collective-permute-start.13 = (bf16[256,1024]{1,0:T(8,128)(2,1)S(1)}, bf16[256,1024]{1,0:T(8,128)(2,1)S(1)}, u32[]{:S(2)}, u32[]{:S(2)}) collective-permute-start(bf16[256,1024]{1,0:T(8,128)(2,1)S(1)} %collective-permute-done.12), channel_id=1, source_target_pairs={{8,0},{12,4},{16,24},{20,28},{9,1},{13,5},{17,25},{21,29},{10,2},{... | collective-permute-start | bytes 1572872 | tf_op jit(solution)/shard_map/ppermute | solution.py:381
  54.0 1.5 %collective-permute-start.9 = (bf16[256,1024]{1,0:T(8,128)(2,1)S(1)}, bf16[256,1024]{1,0:T(8,128)(2,1)S(1)}, u32[]{:S(2)}, u32[]{:S(2)}) collective-permute-start(bf16[256,1024]{1,0:T(8,128)(2,1)S(1)} %collective-permute-done.4.own_ref), channel_id=1, source_target_pairs={{0,4},{4,0},{8,12},{12,8},{16,20},{20,16},{24,28},{28,24},{1,5},{5... | collective-permute-start | bytes 1572872 | tf_op jit(solution)/shard_map/ppermute | solution.py:384
  56.3 2.2 %copy-done = bf16[2048,1024]{1,0:T(8,128)(2,1)S(1)} copy-done((bf16[2048,1024]{1,0:T(8,128)(2,1)S(1)}, bf16[2048,1024]{1,0:T(8,128)(2,1)}, u32[]{:S(2)}) %copy-start) | copy-done | bytes 4194328
  58.4 3.1 %project.4 = (f32[128,1024]{1,0:T(8,128)S(1)}, bf16[128,1024]{1,0:T(8,128)(2,1)S(1)}) custom-call(s32[3]{0:T(128)S(1)} %pad_add_fusion.yc_ref, bf16[256,1024]{1,0:T(8,128)(2,1)S(1)} %finish.1.own_ref, bf16[256,1024]{1,0:T(8,128)(2,1)S(1)} %collective-permute-done.6.refs_0_, bf16[2048,1024]{1,0:T(8,128)(2,1)S(1)} %copy-done, bf16[2048,1024]{1,0:T(8,128)(2,1)S(1)} %copy-done), custom_call_target="tpu_custom_call" | custom-call | flops 1 | bytes 1 | tf_op jit(solution)/shard_map/project/pallas_call | solution.py:291
  61.6 1.3 %collective-permute-start.7 = (bf16[256,1024]{1,0:T(8,128)(2,1)S(1)}, bf16[256,1024]{1,0:T(8,128)(2,1)S(1)}, u32[]{:S(2)}, u32[]{:S(2)}) collective-permute-start(bf16[256,1024]{1,0:T(8,128)(2,1)S(1)} %collective-permute-done.5), channel_id=1, source_target_pairs={{8,0},{12,4},{16,24},{20,28},{9,1},{13,5},{17,25},{21,29},{10,2},{... | collective-permute-start | bytes 1572872 | tf_op jit(solution)/shard_map/ppermute | solution.py:381
  62.9 7.4 %collective-permute-done.13 = bf16[256,1024]{1,0:T(8,128)(2,1)S(1)} collective-permute-done((bf16[256,1024]{1,0:T(8,128)(2,1)S(1)}, bf16[256,1024]{1,0:T(8,128)(2,1)S(1)}, u32[]{:S(2)}, u32[]{:S(2)}) %collective-permute-start.13) | collective-permute-done | bytes 524320 | tf_op jit(solution)/shard_map/ppermute | solution.py:381
  70.4 1.6 %collective-permute-start.14 = (bf16[256,1024]{1,0:T(8,128)(2,1)S(1)}, bf16[256,1024]{1,0:T(8,128)(2,1)S(1)}, u32[]{:S(2)}, u32[]{:S(2)}) collective-permute-start(bf16[256,1024]{1,0:T(8,128)(2,1)S(1)} %broadcast_select_fusion.1.own_ref), channel_id=1, source_target_pairs={{0,4},{4,0},{8,12},{12,8},{16,20},{20,16},{24,28},{28,24},{1,5},{5... | collective-permute-start | bytes 1572872 | tf_op jit(solution)/shard_map/ppermute | solution.py:384
  72.0 3.1 %project.5 = (f32[128,1024]{1,0:T(8,128)S(1)}, bf16[128,1024]{1,0:T(8,128)(2,1)S(1)}) custom-call(s32[3]{0:T(128)S(1)} %pad_add_fusion.yc_ref, bf16[256,1024]{1,0:T(8,128)(2,1)S(1)} %collective-permute-done.4.own_ref, bf16[256,1024]{1,0:T(8,128)(2,1)S(1)} %collective-permute-done.9.refs_0_, bf16[2048,1024]{1,0:T(8,128)(2,1)S(1)} %copy-done.1, ...), custom_call_target="tpu_custom_call" | custom-call | flops 1 | bytes 1 | tf_op jit(solution)/shard_map/project/pallas_call | solution.py:291
  75.2 6.4 %collective-permute-done.7 = bf16[256,1024]{1,0:T(8,128)(2,1)S(1)} collective-permute-done((bf16[256,1024]{1,0:T(8,128)(2,1)S(1)}, bf16[256,1024]{1,0:T(8,128)(2,1)S(1)}, u32[]{:S(2)}, u32[]{:S(2)}) %collective-permute-start.7) | collective-permute-done | bytes 524320 | tf_op jit(solution)/shard_map/ppermute | solution.py:381
  81.6 1.3 collective-permute-done.14.refs_0_
  82.8 1.3 %collective-permute-start.15 = (bf16[128,1024]{1,0:T(8,128)(2,1)S(1)}, bf16[128,1024]{1,0:T(8,128)(2,1)S(1)}, u32[]{:S(2)}, u32[]{:S(2)}) collective-permute-start(bf16[128,1024]{1,0:T(8,128)(2,1)S(1)} %slice.10), channel_id=1, source_target_pairs={{8,0},{12,4},{16,24},{20,28},{9,1},{13,5},{17,25},{21,29},{10,2},{... | collective-permute-start | bytes 786440 | tf_op jit(solution)/shard_map/ppermute | solution.py:381
  84.2 3.4 %collective-permute-start.11 = (bf16[128,1024]{1,0:T(8,128)(2,1)S(1)}, bf16[128,1024]{1,0:T(8,128)(2,1)S(1)}, u32[]{:S(2)}, u32[]{:S(2)}) collective-permute-start(bf16[128,1024]{1,0:T(8,128)(2,1)S(1)} %slice.8), channel_id=1, source_target_pairs={{0,4},{4,0},{24,28},{28,24},{1,5},{5,1},{25,29},{29,25},{2,6},{6,2... | collective-permute-start | bytes 786440 | tf_op jit(solution)/shard_map/ppermute | solution.py:419
  87.6 3.1 %project.6 = (f32[128,1024]{1,0:T(8,128)S(1)}, bf16[128,1024]{1,0:T(8,128)(2,1)S(1)}) custom-call(s32[3]{0:T(128)S(1)} %pad_add_fusion.yc_ref, bf16[256,1024]{1,0:T(8,128)(2,1)S(1)} %broadcast_select_fusion.1.own_ref, bf16[256,1024]{1,0:T(8,128)(2,1)S(1)} %collective-permute-done.14.refs_0_, bf16[2048,1024]{1,0:T(8,128)(2,1)S(1)} %copy-done.1, ...), custom_call_target="tpu_custom_call" | custom-call | flops 1 | bytes 1 | tf_op jit(solution)/shard_map/project/pallas_call | solution.py:291
  91.1 1.3 %collective-permute-done.11.refs_1_ = bf16[128,1024]{1,0:T(8,128)(2,1)S(1)} collective-permute-done((bf16[128,1024]{1,0:T(8,128)(2,1)S(1)}, bf16[128,1024]{1,0:T(8,128)(2,1)S(1)}, u32[]{:S(2)}, u32[]{:S(2)}) %collective-permute-start.11) | collective-permute-done | bytes 262176 | tf_op jit(solution)/shard_map/ppermute | solution.py:419
  92.5 3.1 %project.7 = (f32[128,1024]{1,0:T(8,128)S(1)}, bf16[128,1024]{1,0:T(8,128)(2,1)S(1)}) custom-call(s32[3]{0:T(128)S(1)} %pad_add_fusion.yc_ref, bf16[256,1024]{1,0:T(8,128)(2,1)S(1)} %broadcast_select_fusion.own_ref, bf16[256,1024]{1,0:T(8,128)(2,1)S(1)} %collective-permute-done.8.refs_0_, bf16[128,1024]{1,0:T(8,128)(2,1)S(1)} %collective-permute-done.11.refs_1_, ...), custom_call_target="tpu_custom_call" | custom-call | flops 1 | bytes 1 | tf_op jit(solution)/shard_map/project/pallas_call | solution.py:291
  98.7 1.6 %collective-permute-start.20 = (bf16[128,1024]{1,0:T(8,128)(2,1)S(1)}, bf16[128,1024]{1,0:T(8,128)(2,1)S(1)}, u32[]{:S(2)}, u32[]{:S(2)}) collective-permute-start(bf16[128,1024]{1,0:T(8,128)(2,1)S(1)} %get-tuple-element.83), channel_id=1, source_target_pairs={{0,8},{1,12},{2,24},{3,28},{4,9},{5,13},{6,25},{7,29},{8,0},{9,4},... | collective-permute-start | bytes 786440 | tf_op jit(solution)/shard_map/ppermute | solution.py:398
  100.8 3.0 %collective-permute-start.18 = (bf16[128,1024]{1,0:T(8,128)(2,1)S(1)}, bf16[128,1024]{1,0:T(8,128)(2,1)S(1)}, u32[]{:S(2)}, u32[]{:S(2)}) collective-permute-start(bf16[128,1024]{1,0:T(8,128)(2,1)S(1)} %get-tuple-element.81), channel_id=1, source_target_pairs={{1,4},{2,16},{3,20},{4,1},{6,17},{7,21},{9,12},{10,24},{11,28},{12... | collective-permute-start | bytes 786440 | tf_op jit(solution)/shard_map/ppermute | solution.py:398
  104.8 5.6 %collective-permute-done.20 = bf16[128,1024]{1,0:T(8,128)(2,1)S(1)} collective-permute-done((bf16[128,1024]{1,0:T(8,128)(2,1)S(1)}, bf16[128,1024]{1,0:T(8,128)(2,1)S(1)}, u32[]{:S(2)}, u32[]{:S(2)}) %collective-permute-start.20) | collective-permute-done | bytes 262176 | tf_op jit(solution)/shard_map/ppermute | solution.py:398
  110.4 2.8 %collective-permute-done.21 = bf16[128,1024]{1,0:T(8,128)(2,1)S(1)} collective-permute-done((bf16[128,1024]{1,0:T(8,128)(2,1)S(1)}, bf16[128,1024]{1,0:T(8,128)(2,1)S(1)}, u32[]{:S(2)}, u32[]{:S(2)}) %collective-permute-start.21) | collective-permute-done | bytes 262176 | tf_op jit(solution)/shard_map/ppermute | solution.py:398
  113.2 10.0 %collective-permute-done.18 = bf16[128,1024]{1,0:T(8,128)(2,1)S(1)} collective-permute-done((bf16[128,1024]{1,0:T(8,128)(2,1)S(1)}, bf16[128,1024]{1,0:T(8,128)(2,1)S(1)}, u32[]{:S(2)}, u32[]{:S(2)}) %collective-permute-start.18) | collective-permute-done | bytes 262176 | tf_op jit(solution)/shard_map/ppermute | solution.py:398
  123.2 1.5 %collective-permute-done.19 = bf16[128,1024]{1,0:T(8,128)(2,1)S(1)} collective-permute-done((bf16[128,1024]{1,0:T(8,128)(2,1)S(1)}, bf16[128,1024]{1,0:T(8,128)(2,1)S(1)}, u32[]{:S(2)}, u32[]{:S(2)}) %collective-permute-start.19) | collective-permute-done | bytes 262176 | tf_op jit(solution)/shard_map/ppermute | solution.py:398
  (56 shorter events, 20.1 us)
Async XLA Ops:
  0.0 31.8 %copy-start.3 = (bf16[128,2048]{1,0:T(8,128)(2,1)S(1)}, bf16[128,2048]{1,0:T(8,128)(2,1)}, u32[]{:S(2)}) copy-start(bf16[128,2048]{1,0:T(8,128)(2,1)} %refs_6_.1) | copy-start | bytes 1572868
  2.0 10.4 %collective-permute-start = (bf16[128,1408]{1,0:T(8,128)(2,1)}, bf16[128,1408]{1,0:T(8,128)(2,1)S(1)}, u32[]{:S(2)}, u32[]{:S(2)}) collective-permute-start(bf16[128,1408]{1,0:T(8,128)(2,1)} %pack.2), channel_id=1, source_target_pairs={{0,4},{4,0},{8,12},{12,8},{16,20},{20,16},{24,28},{28,24},{1,5},{5... | collective-permute-start | bytes 1081352 | tf_op jit(solution)/shard_map/ppermute | solution.py:364
  3.5 1.0 copy-start.2
  4.6 0.8 copy-start.4
  5.4 0.8 copy-start.5
  6.2 0.7 copy-start.6
  13.6 8.9 %collective-permute-start.1 = (bf16[144,1024]{1,0:T(8,128)(2,1)S(1)}, bf16[144,1024]{1,0:T(8,128)(2,1)S(1)}, u32[]{:S(2)}, u32[]{:S(2)}) collective-permute-start(bf16[144,1024]{1,0:T(8,128)(2,1)S(1)} %get-tuple-element.46.send_ref), channel_id=1, source_target_pairs={{0,8},{4,12},{8,16},{12,20},{16,24},{20,28},{1,9},{5,13},{9,17},{1... | collective-permute-start | bytes 884744 | tf_op jit(solution)/shard_map/ppermute | solution.py:362
  18.1 9.9 %collective-permute-start.3 = (bf16[128,1024]{1,0:T(8,128)(2,1)S(1)}, bf16[128,1024]{1,0:T(8,128)(2,1)S(1)}, u32[]{:S(2)}, u32[]{:S(2)}) collective-permute-start(bf16[128,1024]{1,0:T(8,128)(2,1)S(1)} %constant_dynamic-slice_fusion), channel_id=1, source_target_pairs={{0,4},{4,0},{8,12},{12,8},{16,20},{20,16},{24,28},{28,24},{1,5},{5... | collective-permute-start | bytes 786440 | tf_op jit(solution)/shard_map/ppermute | solution.py:370
  22.6 9.3 %collective-permute-start.2 = (bf16[128,1024]{1,0:T(8,128)(2,1)S(1)}, bf16[128,1024]{1,0:T(8,128)(2,1)S(1)}, u32[]{:S(2)}, u32[]{:S(2)}) collective-permute-start(bf16[128,1024]{1,0:T(8,128)(2,1)S(1)} %join.1), channel_id=1, source_target_pairs={{0,16},{4,20},{8,24},{12,28},{1,17},{5,21},{9,25},{13,29},{2,18},{... | collective-permute-start | bytes 786440 | tf_op jit(solution)/shard_map/ppermute | solution.py:362
  32.8 19.1 %collective-permute-start.4 = (bf16[256,1024]{1,0:T(8,128)(2,1)S(1)}, bf16[256,1024]{1,0:T(8,128)(2,1)S(1)}, u32[]{:S(2)}, u32[]{:S(2)}) collective-permute-start(bf16[256,1024]{1,0:T(8,128)(2,1)S(1)} %finish.1.own_ref), channel_id=1, source_target_pairs={{0,8},{4,12},{8,0},{12,4},{16,24},{20,28},{24,16},{28,20},{1,9},{5... | collective-permute-start | bytes 1572872 | tf_op jit(solution)/shard_map/ppermute | solution.py:381
  39.8 12.8 %collective-permute-start.12 = (bf16[256,1024]{1,0:T(8,128)(2,1)S(1)}, bf16[256,1024]{1,0:T(8,128)(2,1)S(1)}, u32[]{:S(2)}, u32[]{:S(2)}) collective-permute-start(bf16[256,1024]{1,0:T(8,128)(2,1)S(1)} %finish.1.own_ref), channel_id=1, source_target_pairs={{8,16},{12,20},{16,8},{20,12},{9,17},{13,21},{17,9},{21,13},{10,18... | collective-permute-start | bytes 1572872 | tf_op jit(solution)/shard_map/ppermute | solution.py:381
  40.5 15.0 %collective-permute-start.6 = (bf16[256,1024]{1,0:T(8,128)(2,1)S(1)}, bf16[256,1024]{1,0:T(8,128)(2,1)S(1)}, u32[]{:S(2)}, u32[]{:S(2)}) collective-permute-start(bf16[256,1024]{1,0:T(8,128)(2,1)S(1)} %finish.1.own_ref), channel_id=1, source_target_pairs={{0,4},{4,0},{8,12},{12,8},{16,20},{20,16},{24,28},{28,24},{1,5},{5... | collective-permute-start | bytes 1572872 | tf_op jit(solution)/shard_map/ppermute | solution.py:384
  51.9 9.6 %collective-permute-start.5 = (bf16[256,1024]{1,0:T(8,128)(2,1)S(1)}, bf16[256,1024]{1,0:T(8,128)(2,1)S(1)}, u32[]{:S(2)}, u32[]{:S(2)}) collective-permute-start(bf16[256,1024]{1,0:T(8,128)(2,1)S(1)} %collective-permute-done.4.own_ref), channel_id=1, source_target_pairs={{8,16},{12,20},{16,8},{20,12},{9,17},{13,21},{17,9},{21,13},{10,18... | collective-permute-start | bytes 1572872 | tf_op jit(solution)/shard_map/ppermute | solution.py:381
  52.6 17.7 %collective-permute-start.13 = (bf16[256,1024]{1,0:T(8,128)(2,1)S(1)}, bf16[256,1024]{1,0:T(8,128)(2,1)S(1)}, u32[]{:S(2)}, u32[]{:S(2)}) collective-permute-start(bf16[256,1024]{1,0:T(8,128)(2,1)S(1)} %collective-permute-done.12), channel_id=1, source_target_pairs={{8,0},{12,4},{16,24},{20,28},{9,1},{13,5},{17,25},{21,29},{10,2},{... | collective-permute-start | bytes 1572872 | tf_op jit(solution)/shard_map/ppermute | solution.py:381
  54.0 17.9 %collective-permute-start.9 = (bf16[256,1024]{1,0:T(8,128)(2,1)S(1)}, bf16[256,1024]{1,0:T(8,128)(2,1)S(1)}, u32[]{:S(2)}, u32[]{:S(2)}) collective-permute-start(bf16[256,1024]{1,0:T(8,128)(2,1)S(1)} %collective-permute-done.4.own_ref), channel_id=1, source_target_pairs={{0,4},{4,0},{8,12},{12,8},{16,20},{20,16},{24,28},{28,24},{1,5},{5... | collective-permute-start | bytes 1572872 | tf_op jit(solution)/shard_map/ppermute | solution.py:384
  55.6 19.6 %collective-permute-start.8 = (bf16[256,1024]{1,0:T(8,128)(2,1)S(1)}, bf16[256,1024]{1,0:T(8,128)(2,1)S(1)}, u32[]{:S(2)}, u32[]{:S(2)}) collective-permute-start(bf16[256,1024]{1,0:T(8,128)(2,1)S(1)} %collective-permute-done.6.refs_0_), channel_id=1, source_target_pairs={{8,16},{12,20},{16,8},{20,12},{9,17},{13,21},{17,9},{21,13},{10,18... | collective-permute-start | bytes 1572872 | tf_op jit(solution)/shard_map/ppermute | solution.py:381
  56.3 2.2 %copy-start = (bf16[2048,1024]{1,0:T(8,128)(2,1)S(1)}, bf16[2048,1024]{1,0:T(8,128)(2,1)}, u32[]{:S(2)}) copy-start(bf16[2048,1024]{1,0:T(8,128)(2,1)} %refs_4_.1) | copy-start | bytes 12582916
  58.4 13.5 %copy-start.1 = (bf16[2048,1024]{1,0:T(8,128)(2,1)S(1)}, bf16[2048,1024]{1,0:T(8,128)(2,1)}, u32[]{:S(2)}) copy-start(bf16[2048,1024]{1,0:T(8,128)(2,1)} %refs_4_.1) | copy-start | bytes 12582916
  61.6 20.0 %collective-permute-start.7 = (bf16[256,1024]{1,0:T(8,128)(2,1)S(1)}, bf16[256,1024]{1,0:T(8,128)(2,1)S(1)}, u32[]{:S(2)}, u32[]{:S(2)}) collective-permute-start(bf16[256,1024]{1,0:T(8,128)(2,1)S(1)} %collective-permute-done.5), channel_id=1, source_target_pairs={{8,0},{12,4},{16,24},{20,28},{9,1},{13,5},{17,25},{21,29},{10,2},{... | collective-permute-start | bytes 1572872 | tf_op jit(solution)/shard_map/ppermute | solution.py:381
  70.4 12.4 %collective-permute-start.14 = (bf16[256,1024]{1,0:T(8,128)(2,1)S(1)}, bf16[256,1024]{1,0:T(8,128)(2,1)S(1)}, u32[]{:S(2)}, u32[]{:S(2)}) collective-permute-start(bf16[256,1024]{1,0:T(8,128)(2,1)S(1)} %broadcast_select_fusion.1.own_ref), channel_id=1, source_target_pairs={{0,4},{4,0},{8,12},{12,8},{16,20},{20,16},{24,28},{28,24},{1,5},{5... | collective-permute-start | bytes 1572872 | tf_op jit(solution)/shard_map/ppermute | solution.py:384
  72.0 3.1 %collective-permute-start.10 = (bf16[128,1024]{1,0:T(8,128)(2,1)S(1)}, bf16[128,1024]{1,0:T(8,128)(2,1)S(1)}, u32[]{:S(2)}, u32[]{:S(2)}) collective-permute-start(bf16[128,1024]{1,0:T(8,128)(2,1)S(1)} %get-tuple-element.62), channel_id=1, source_target_pairs={{0,1},{1,0},{2,3},{3,2},{4,5},{5,4},{6,7},{7,6},{8,9},{9,8},{10,11... | collective-permute-start | bytes 786440 | tf_op jit(solution)/shard_map/ppermute | solution.py:385
  82.8 8.3 %collective-permute-start.15 = (bf16[128,1024]{1,0:T(8,128)(2,1)S(1)}, bf16[128,1024]{1,0:T(8,128)(2,1)S(1)}, u32[]{:S(2)}, u32[]{:S(2)}) collective-permute-start(bf16[128,1024]{1,0:T(8,128)(2,1)S(1)} %slice.10), channel_id=1, source_target_pairs={{8,0},{12,4},{16,24},{20,28},{9,1},{13,5},{17,25},{21,29},{10,2},{... | collective-permute-start | bytes 786440 | tf_op jit(solution)/shard_map/ppermute | solution.py:381
  84.2 8.3 %collective-permute-start.11 = (bf16[128,1024]{1,0:T(8,128)(2,1)S(1)}, bf16[128,1024]{1,0:T(8,128)(2,1)S(1)}, u32[]{:S(2)}, u32[]{:S(2)}) collective-permute-start(bf16[128,1024]{1,0:T(8,128)(2,1)S(1)} %slice.8), channel_id=1, source_target_pairs={{0,4},{4,0},{24,28},{28,24},{1,5},{5,1},{25,29},{29,25},{2,6},{6,2... | collective-permute-start | bytes 786440 | tf_op jit(solution)/shard_map/ppermute | solution.py:419
  92.4 5.0 %collective-permute-start.16 = (bf16[256,1024]{1,0:T(8,128)(2,1)S(1)}, bf16[256,1024]{1,0:T(8,128)(2,1)}, u32[]{:S(2)}, u32[]{:S(2)}) collective-permute-start(bf16[256,1024]{1,0:T(8,128)(2,1)S(1)} %pad_maximum_fusion), channel_id=1, source_target_pairs={{0,1},{1,0},{2,3},{3,2},{4,5},{5,4},{6,7},{7,6},{8,9},{9,8},{10,11... | collective-permute-start | bytes 1572872 | tf_op jit(solution)/shard_map/ppermute | solution.py:385
  95.6 1.7 %collective-permute-start.17 = (bf16[128,1024]{1,0:T(8,128)(2,1)S(1)}, bf16[128,1024]{1,0:T(8,128)(2,1)S(1)}, u32[]{:S(2)}, u32[]{:S(2)}) collective-permute-start(bf16[128,1024]{1,0:T(8,128)(2,1)S(1)} %get-tuple-element.74), channel_id=1, source_target_pairs={{0,1},{1,0},{2,3},{3,2},{4,5},{5,4},{6,7},{7,6},{8,9},{9,8},{10,11... | collective-permute-start | bytes 786440 | tf_op jit(solution)/shard_map/ppermute | solution.py:385
  98.7 11.8 %collective-permute-start.20 = (bf16[128,1024]{1,0:T(8,128)(2,1)S(1)}, bf16[128,1024]{1,0:T(8,128)(2,1)S(1)}, u32[]{:S(2)}, u32[]{:S(2)}) collective-permute-start(bf16[128,1024]{1,0:T(8,128)(2,1)S(1)} %get-tuple-element.83), channel_id=1, source_target_pairs={{0,8},{1,12},{2,24},{3,28},{4,9},{5,13},{6,25},{7,29},{8,0},{9,4},... | collective-permute-start | bytes 786440 | tf_op jit(solution)/shard_map/ppermute | solution.py:398
  100.3 12.9 %collective-permute-start.21 = (bf16[128,1024]{1,0:T(8,128)(2,1)S(1)}, bf16[128,1024]{1,0:T(8,128)(2,1)S(1)}, u32[]{:S(2)}, u32[]{:S(2)}) collective-permute-start(bf16[128,1024]{1,0:T(8,128)(2,1)S(1)} %get-tuple-element.84), channel_id=1, source_target_pairs={{0,24},{1,28},{2,8},{3,12},{4,25},{5,29},{6,9},{7,13},{8,16},{9,20... | collective-permute-start | bytes 786440 | tf_op jit(solution)/shard_map/ppermute | solution.py:398
  100.8 22.4 %collective-permute-start.18 = (bf16[128,1024]{1,0:T(8,128)(2,1)S(1)}, bf16[128,1024]{1,0:T(8,128)(2,1)S(1)}, u32[]{:S(2)}, u32[]{:S(2)}) collective-permute-start(bf16[128,1024]{1,0:T(8,128)(2,1)S(1)} %get-tuple-element.81), channel_id=1, source_target_pairs={{1,4},{2,16},{3,20},{4,1},{6,17},{7,21},{9,12},{10,24},{11,28},{12... | collective-permute-start | bytes 786440 | tf_op jit(solution)/shard_map/ppermute | solution.py:398
  103.8 20.8 %collective-permute-start.19 = (bf16[128,1024]{1,0:T(8,128)(2,1)S(1)}, bf16[128,1024]{1,0:T(8,128)(2,1)S(1)}, u32[]{:S(2)}, u32[]{:S(2)}) collective-permute-start(bf16[128,1024]{1,0:T(8,128)(2,1)S(1)} %get-tuple-element.82), channel_id=1, source_target_pairs={{0,16},{1,20},{2,0},{3,4},{4,17},{5,21},{6,1},{7,5},{8,24},{9,28},... | collective-permute-start | bytes 786440 | tf_op jit(solution)/shard_map/ppermute | solution.py:398
  124.9 1.7 %collective-permute-start.22 = (bf16[128,1024]{1,0:T(8,128)(2,1)S(1)}, bf16[128,1024]{1,0:T(8,128)(2,1)S(1)}, u32[]{:S(2)}, u32[]{:S(2)}) collective-permute-start(bf16[128,1024]{1,0:T(8,128)(2,1)S(1)} %get-tuple-element.79), channel_id=1, source_target_pairs={{0,1},{1,0},{2,3},{3,2},{4,5},{5,4},{6,7},{7,6},{8,9},{9,8},{10,11... | collective-permute-start | bytes 786440 | tf_op jit(solution)/shard_map/ppermute | solution.py:385

commit v8 on v7

--- a/solution.py
+++ b/solution.py
@@ -27,7 +27,7 @@
 
 
 def cost(flops, moved):
-    return pl.CostEstimate(flops=1, bytes_accessed=1, transcendentals=0)
+    return pl.CostEstimate(flops=int(flops), bytes_accessed=int(moved), transcendentals=0)
 
 
 def iota(shape, axis):

time: 129 us -> 127 us (0.984)
  no operation moved by 1% of the time
where the time goes in v8:
time: 127 us; the launch traced here: 126 us
  waiting for transfers between devices  57.3 us (45%)
  starting transfers between devices  40.2 us (32%)
  Pallas kernels  18.8 us (15%)
  local copies, waits for them, and re-layouts  8.85 us (7%)
    ppermute x7, waiting for transfers between devices, pair_shards(): lax.ppermute(value, 'seq', [(i * 2 + b, j * 2 + b) for i, j in moves for...  23.9 us
    ppermute x4, waiting for transfers between devices, deliver(): moved = lax.ppermute(value, both, [(i, j) for i, j in pairs if i != j])  19.8 us
    ppermute x7, starting transfers between devices, pair_shards(): lax.ppermute(value, 'seq', [(i * 2 + b, j * 2 + b) for i, j in moves for...  13 us
    pallas_call x4, Pallas kernels, project(): pl.pallas_call(project_kernel, grid_spec=pltpu.PrefetchScalarGridSpec(num...  12.4 us
    ppermute x2, starting transfers between devices, along(): return lax.ppermute(v, 'seq', pairs)  8.91 us
    ppermute x4, starting transfers between devices, deliver(): moved = lax.ppermute(value, both, [(i, j) for i, j in pairs if i != j])  6.08 us
    unnamed x14, local copies, waits for them, and re-layouts  5.61 us
    ppermute x2, waiting for transfers between devices, along(): return lax.ppermute(v, 'seq', pairs)  5.54 us
  transfers between devices with their start and end apart: 23, of which 15 were waited for; matrix products, arithmetic and copies ran while one was open for 3% of the time, Pallas kernels for 11%

profile of v8, /device:TPU:2, one launch (start us, length us, event | category | flops | bytes accessed | tf_op | source)
XLA Modules:
  0.0 126.3 jit_solution(1063013026436760537)
XLA Ops:
  0.0 2.0 %pack.2 = bf16[128,1408]{1,0:T(8,128)(2,1)} custom-call(s32[1]{0:T(128)S(6)} %sub.21.refs_0_, bf16[128,2048]{1,0:T(8,128)(2,1)} %refs_1_.6, bf16[128,256]{1,0:T(8,128)(2,1)} %refs_2_.6, bf16[128,256]{1,0:T(8,128)(2,1)} %refs_3_.4, f32[16,128]{1,0:T(8,128)} %bitcast.10), custom_call_target="tpu_custom_call" | custom-call | flops 1000000 | bytes 1000000 | tf_op jit(solution)/shard_map/pack/pallas_call | solution.py:68
  2.0 1.5 %collective-permute-start = (bf16[128,1408]{1,0:T(8,128)(2,1)}, bf16[128,1408]{1,0:T(8,128)(2,1)S(1)}, u32[]{:S(2)}, u32[]{:S(2)}) collective-permute-start(bf16[128,1408]{1,0:T(8,128)(2,1)} %pack.2), channel_id=1, source_target_pairs={{0,4},{4,0},{8,12},{12,8},{16,20},{20,16},{24,28},{28,24},{1,5},{5... | collective-permute-start | bytes 1081352 | tf_op jit(solution)/shard_map/ppermute | solution.py:364
  9.3 3.0 %collective-permute-done.refs_2_ = bf16[128,1408]{1,0:T(8,128)(2,1)S(1)} collective-permute-done((bf16[128,1408]{1,0:T(8,128)(2,1)}, bf16[128,1408]{1,0:T(8,128)(2,1)S(1)}, u32[]{:S(2)}, u32[]{:S(2)}) %collective-permute-start) | collective-permute-done | bytes 360480 | tf_op jit(solution)/shard_map/ppermute | solution.py:364
  13.6 3.5 %collective-permute-start.1 = (bf16[144,1024]{1,0:T(8,128)(2,1)S(1)}, bf16[144,1024]{1,0:T(8,128)(2,1)S(1)}, u32[]{:S(2)}, u32[]{:S(2)}) collective-permute-start(bf16[144,1024]{1,0:T(8,128)(2,1)S(1)} %get-tuple-element.46.send_ref), channel_id=1, source_target_pairs={{0,8},{4,12},{8,16},{12,20},{16,24},{20,28},{1,9},{5,13},{9,17},{1... | collective-permute-start | bytes 884744 | tf_op jit(solution)/shard_map/ppermute | solution.py:362
  18.1 1.6 %collective-permute-start.3 = (bf16[128,1024]{1,0:T(8,128)(2,1)S(1)}, bf16[128,1024]{1,0:T(8,128)(2,1)S(1)}, u32[]{:S(2)}, u32[]{:S(2)}) collective-permute-start(bf16[128,1024]{1,0:T(8,128)(2,1)S(1)} %constant_dynamic-slice_fusion), channel_id=1, source_target_pairs={{0,4},{4,0},{8,12},{12,8},{16,20},{20,16},{24,28},{28,24},{1,5},{5... | collective-permute-start | bytes 786440 | tf_op jit(solution)/shard_map/ppermute | solution.py:370
  20.8 1.7 %collective-permute-done.1.got_ref.refs_4_ = bf16[144,1024]{1,0:T(8,128)(2,1)S(1)} collective-permute-done((bf16[144,1024]{1,0:T(8,128)(2,1)S(1)}, bf16[144,1024]{1,0:T(8,128)(2,1)S(1)}, u32[]{:S(2)}, u32[]{:S(2)}) %collective-permute-start.1) | collective-permute-done | bytes 294944 | tf_op jit(solution)/shard_map/ppermute | solution.py:362
  22.6 5.4 %collective-permute-start.2 = (bf16[128,1024]{1,0:T(8,128)(2,1)S(1)}, bf16[128,1024]{1,0:T(8,128)(2,1)S(1)}, u32[]{:S(2)}, u32[]{:S(2)}) collective-permute-start(bf16[128,1024]{1,0:T(8,128)(2,1)S(1)} %join.1), channel_id=1, source_target_pairs={{0,16},{4,20},{8,24},{12,28},{1,17},{5,21},{9,25},{13,29},{2,18},{... | collective-permute-start | bytes 786440 | tf_op jit(solution)/shard_map/ppermute | solution.py:362
  28.0 3.8 %collective-permute-done.2.refs_5_ = bf16[128,1024]{1,0:T(8,128)(2,1)S(1)} collective-permute-done((bf16[128,1024]{1,0:T(8,128)(2,1)S(1)}, bf16[128,1024]{1,0:T(8,128)(2,1)S(1)}, u32[]{:S(2)}, u32[]{:S(2)}) %collective-permute-start.2) | collective-permute-done | bytes 262176 | tf_op jit(solution)/shard_map/ppermute | solution.py:362
  32.8 7.0 %collective-permute-start.4 = (bf16[256,1024]{1,0:T(8,128)(2,1)S(1)}, bf16[256,1024]{1,0:T(8,128)(2,1)S(1)}, u32[]{:S(2)}, u32[]{:S(2)}) collective-permute-start(bf16[256,1024]{1,0:T(8,128)(2,1)S(1)} %finish.1.own_ref), channel_id=1, source_target_pairs={{0,8},{4,12},{8,0},{12,4},{16,24},{20,28},{24,16},{28,20},{1,9},{5... | collective-permute-start | bytes 1572872 | tf_op jit(solution)/shard_map/ppermute | solution.py:381
  40.5 1.6 %collective-permute-start.6 = (bf16[256,1024]{1,0:T(8,128)(2,1)S(1)}, bf16[256,1024]{1,0:T(8,128)(2,1)S(1)}, u32[]{:S(2)}, u32[]{:S(2)}) collective-permute-start(bf16[256,1024]{1,0:T(8,128)(2,1)S(1)} %finish.1.own_ref), channel_id=1, source_target_pairs={{0,4},{4,0},{8,12},{12,8},{16,20},{20,16},{24,28},{28,24},{1,5},{5... | collective-permute-start | bytes 1572872 | tf_op jit(solution)/shard_map/ppermute | solution.py:384
  42.1 9.8 %collective-permute-done.4.own_ref = bf16[256,1024]{1,0:T(8,128)(2,1)S(1)} collective-permute-done((bf16[256,1024]{1,0:T(8,128)(2,1)S(1)}, bf16[256,1024]{1,0:T(8,128)(2,1)S(1)}, u32[]{:S(2)}, u32[]{:S(2)}) %collective-permute-start.4) | collective-permute-done | bytes 524320 | tf_op jit(solution)/shard_map/ppermute | solution.py:381
  52.6 1.3 %collective-permute-start.13 = (bf16[256,1024]{1,0:T(8,128)(2,1)S(1)}, bf16[256,1024]{1,0:T(8,128)(2,1)S(1)}, u32[]{:S(2)}, u32[]{:S(2)}) collective-permute-start(bf16[256,1024]{1,0:T(8,128)(2,1)S(1)} %collective-permute-done.12), channel_id=1, source_target_pairs={{8,0},{12,4},{16,24},{20,28},{9,1},{13,5},{17,25},{21,29},{10,2},{... | collective-permute-start | bytes 1572872 | tf_op jit(solution)/shard_map/ppermute | solution.py:381
  54.0 1.5 %collective-permute-start.9 = (bf16[256,1024]{1,0:T(8,128)(2,1)S(1)}, bf16[256,1024]{1,0:T(8,128)(2,1)S(1)}, u32[]{:S(2)}, u32[]{:S(2)}) collective-permute-start(bf16[256,1024]{1,0:T(8,128)(2,1)S(1)} %collective-permute-done.4.own_ref), channel_id=1, source_target_pairs={{0,4},{4,0},{8,12},{12,8},{16,20},{20,16},{24,28},{28,24},{1,5},{5... | collective-permute-start | bytes 1572872 | tf_op jit(solution)/shard_map/ppermute | solution.py:384
  56.3 2.2 %copy-done = bf16[2048,1024]{1,0:T(8,128)(2,1)S(1)} copy-done((bf16[2048,1024]{1,0:T(8,128)(2,1)S(1)}, bf16[2048,1024]{1,0:T(8,128)(2,1)}, u32[]{:S(2)}) %copy-start) | copy-done | bytes 4194328
  58.4 3.1 %project.4 = (f32[128,1024]{1,0:T(8,128)S(1)}, bf16[128,1024]{1,0:T(8,128)(2,1)S(1)}) custom-call(s32[3]{0:T(128)S(1)} %pad_add_fusion.yc_ref, bf16[256,1024]{1,0:T(8,128)(2,1)S(1)} %finish.1.own_ref, bf16[256,1024]{1,0:T(8,128)(2,1)S(1)} %collective-permute-done.6.refs_0_, bf16[2048,1024]{1,0:T(8,128)(2,1)S(1)} %copy-done, bf16[2048,1024]{1,0:T(8,128)(2,1)S(1)} %copy-done), custom_call_target="tpu_custom_call" | custom-call | flops 1073741824 | bytes 6000000 | tf_op jit(solution)/shard_map/project/pallas_call | solution.py:291
  61.6 1.3 %collective-permute-start.7 = (bf16[256,1024]{1,0:T(8,128)(2,1)S(1)}, bf16[256,1024]{1,0:T(8,128)(2,1)S(1)}, u32[]{:S(2)}, u32[]{:S(2)}) collective-permute-start(bf16[256,1024]{1,0:T(8,128)(2,1)S(1)} %collective-permute-done.5), channel_id=1, source_target_pairs={{8,0},{12,4},{16,24},{20,28},{9,1},{13,5},{17,25},{21,29},{10,2},{... | collective-permute-start | bytes 1572872 | tf_op jit(solution)/shard_map/ppermute | solution.py:381
  62.9 7.4 %collective-permute-done.13 = bf16[256,1024]{1,0:T(8,128)(2,1)S(1)} collective-permute-done((bf16[256,1024]{1,0:T(8,128)(2,1)S(1)}, bf16[256,1024]{1,0:T(8,128)(2,1)S(1)}, u32[]{:S(2)}, u32[]{:S(2)}) %collective-permute-start.13) | collective-permute-done | bytes 524320 | tf_op jit(solution)/shard_map/ppermute | solution.py:381
  70.4 1.6 %collective-permute-start.14 = (bf16[256,1024]{1,0:T(8,128)(2,1)S(1)}, bf16[256,1024]{1,0:T(8,128)(2,1)S(1)}, u32[]{:S(2)}, u32[]{:S(2)}) collective-permute-start(bf16[256,1024]{1,0:T(8,128)(2,1)S(1)} %broadcast_select_fusion.1.own_ref), channel_id=1, source_target_pairs={{0,4},{4,0},{8,12},{12,8},{16,20},{20,16},{24,28},{28,24},{1,5},{5... | collective-permute-start | bytes 1572872 | tf_op jit(solution)/shard_map/ppermute | solution.py:384
  72.0 3.1 %project.5 = (f32[128,1024]{1,0:T(8,128)S(1)}, bf16[128,1024]{1,0:T(8,128)(2,1)S(1)}) custom-call(s32[3]{0:T(128)S(1)} %pad_add_fusion.yc_ref, bf16[256,1024]{1,0:T(8,128)(2,1)S(1)} %collective-permute-done.4.own_ref, bf16[256,1024]{1,0:T(8,128)(2,1)S(1)} %collective-permute-done.9.refs_0_, bf16[2048,1024]{1,0:T(8,128)(2,1)S(1)} %copy-done.1, ...), custom_call_target="tpu_custom_call" | custom-call | flops 1073741824 | bytes 6000000 | tf_op jit(solution)/shard_map/project/pallas_call | solution.py:291
  75.2 6.4 %collective-permute-done.7 = bf16[256,1024]{1,0:T(8,128)(2,1)S(1)} collective-permute-done((bf16[256,1024]{1,0:T(8,128)(2,1)S(1)}, bf16[256,1024]{1,0:T(8,128)(2,1)S(1)}, u32[]{:S(2)}, u32[]{:S(2)}) %collective-permute-start.7) | collective-permute-done | bytes 524320 | tf_op jit(solution)/shard_map/ppermute | solution.py:381
  81.6 1.3 collective-permute-done.14.refs_0_
  82.8 1.3 %collective-permute-start.15 = (bf16[128,1024]{1,0:T(8,128)(2,1)S(1)}, bf16[128,1024]{1,0:T(8,128)(2,1)S(1)}, u32[]{:S(2)}, u32[]{:S(2)}) collective-permute-start(bf16[128,1024]{1,0:T(8,128)(2,1)S(1)} %slice.10), channel_id=1, source_target_pairs={{8,0},{12,4},{16,24},{20,28},{9,1},{13,5},{17,25},{21,29},{10,2},{... | collective-permute-start | bytes 786440 | tf_op jit(solution)/shard_map/ppermute | solution.py:381
  84.2 3.4 %collective-permute-start.11 = (bf16[128,1024]{1,0:T(8,128)(2,1)S(1)}, bf16[128,1024]{1,0:T(8,128)(2,1)S(1)}, u32[]{:S(2)}, u32[]{:S(2)}) collective-permute-start(bf16[128,1024]{1,0:T(8,128)(2,1)S(1)} %slice.8), channel_id=1, source_target_pairs={{0,4},{4,0},{24,28},{28,24},{1,5},{5,1},{25,29},{29,25},{2,6},{6,2... | collective-permute-start | bytes 786440 | tf_op jit(solution)/shard_map/ppermute | solution.py:419
  87.6 3.1 %project.6 = (f32[128,1024]{1,0:T(8,128)S(1)}, bf16[128,1024]{1,0:T(8,128)(2,1)S(1)}) custom-call(s32[3]{0:T(128)S(1)} %pad_add_fusion.yc_ref, bf16[256,1024]{1,0:T(8,128)(2,1)S(1)} %broadcast_select_fusion.1.own_ref, bf16[256,1024]{1,0:T(8,128)(2,1)S(1)} %collective-permute-done.14.refs_0_, bf16[2048,1024]{1,0:T(8,128)(2,1)S(1)} %copy-done.1, ...), custom_call_target="tpu_custom_call" | custom-call | flops 1073741824 | bytes 6000000 | tf_op jit(solution)/shard_map/project/pallas_call | solution.py:291
  91.1 1.3 %collective-permute-done.11.refs_1_ = bf16[128,1024]{1,0:T(8,128)(2,1)S(1)} collective-permute-done((bf16[128,1024]{1,0:T(8,128)(2,1)S(1)}, bf16[128,1024]{1,0:T(8,128)(2,1)S(1)}, u32[]{:S(2)}, u32[]{:S(2)}) %collective-permute-start.11) | collective-permute-done | bytes 262176 | tf_op jit(solution)/shard_map/ppermute | solution.py:419
  92.4 3.1 %project.7 = (f32[128,1024]{1,0:T(8,128)S(1)}, bf16[128,1024]{1,0:T(8,128)(2,1)S(1)}) custom-call(s32[3]{0:T(128)S(1)} %pad_add_fusion.yc_ref, bf16[256,1024]{1,0:T(8,128)(2,1)S(1)} %broadcast_select_fusion.own_ref, bf16[256,1024]{1,0:T(8,128)(2,1)S(1)} %collective-permute-done.8.refs_0_, bf16[128,1024]{1,0:T(8,128)(2,1)S(1)} %collective-permute-done.11.refs_1_, ...), custom_call_target="tpu_custom_call" | custom-call | flops 1073741824 | bytes 6000000 | tf_op jit(solution)/shard_map/project/pallas_call | solution.py:291
  97.6 1.6 %collective-permute-start.20 = (bf16[128,1024]{1,0:T(8,128)(2,1)S(1)}, bf16[128,1024]{1,0:T(8,128)(2,1)S(1)}, u32[]{:S(2)}, u32[]{:S(2)}) collective-permute-start(bf16[128,1024]{1,0:T(8,128)(2,1)S(1)} %get-tuple-element.83), channel_id=1, source_target_pairs={{0,8},{1,12},{2,24},{3,28},{4,9},{5,13},{6,25},{7,29},{8,0},{9,4},... | collective-permute-start | bytes 786440 | tf_op jit(solution)/shard_map/ppermute | solution.py:398
  99.7 3.0 %collective-permute-start.18 = (bf16[128,1024]{1,0:T(8,128)(2,1)S(1)}, bf16[128,1024]{1,0:T(8,128)(2,1)S(1)}, u32[]{:S(2)}, u32[]{:S(2)}) collective-permute-start(bf16[128,1024]{1,0:T(8,128)(2,1)S(1)} %get-tuple-element.81), channel_id=1, source_target_pairs={{1,4},{2,16},{3,20},{4,1},{6,17},{7,21},{9,12},{10,24},{11,28},{12... | collective-permute-start | bytes 786440 | tf_op jit(solution)/shard_map/ppermute | solution.py:398
  103.7 5.6 %collective-permute-done.20 = bf16[128,1024]{1,0:T(8,128)(2,1)S(1)} collective-permute-done((bf16[128,1024]{1,0:T(8,128)(2,1)S(1)}, bf16[128,1024]{1,0:T(8,128)(2,1)S(1)}, u32[]{:S(2)}, u32[]{:S(2)}) %collective-permute-start.20) | collective-permute-done | bytes 262176 | tf_op jit(solution)/shard_map/ppermute | solution.py:398
  109.3 2.8 %collective-permute-done.21 = bf16[128,1024]{1,0:T(8,128)(2,1)S(1)} collective-permute-done((bf16[128,1024]{1,0:T(8,128)(2,1)S(1)}, bf16[128,1024]{1,0:T(8,128)(2,1)S(1)}, u32[]{:S(2)}, u32[]{:S(2)}) %collective-permute-start.21) | collective-permute-done | bytes 262176 | tf_op jit(solution)/shard_map/ppermute | solution.py:398
  112.1 10.0 %collective-permute-done.18 = bf16[128,1024]{1,0:T(8,128)(2,1)S(1)} collective-permute-done((bf16[128,1024]{1,0:T(8,128)(2,1)S(1)}, bf16[128,1024]{1,0:T(8,128)(2,1)S(1)}, u32[]{:S(2)}, u32[]{:S(2)}) %collective-permute-start.18) | collective-permute-done | bytes 262176 | tf_op jit(solution)/shard_map/ppermute | solution.py:398
  122.1 1.4 %collective-permute-done.19 = bf16[128,1024]{1,0:T(8,128)(2,1)S(1)} collective-permute-done((bf16[128,1024]{1,0:T(8,128)(2,1)S(1)}, bf16[128,1024]{1,0:T(8,128)(2,1)S(1)}, u32[]{:S(2)}, u32[]{:S(2)}) %collective-permute-start.19) | collective-permute-done | bytes 262176 | tf_op jit(solution)/shard_map/ppermute | solution.py:398
  (56 shorter events, 19.0 us)
Async XLA Ops:
  0.0 31.8 %copy-start.3 = (bf16[128,2048]{1,0:T(8,128)(2,1)S(1)}, bf16[128,2048]{1,0:T(8,128)(2,1)}, u32[]{:S(2)}) copy-start(bf16[128,2048]{1,0:T(8,128)(2,1)} %refs_6_.1) | copy-start | bytes 1572868
  2.0 10.4 %collective-permute-start = (bf16[128,1408]{1,0:T(8,128)(2,1)}, bf16[128,1408]{1,0:T(8,128)(2,1)S(1)}, u32[]{:S(2)}, u32[]{:S(2)}) collective-permute-start(bf16[128,1408]{1,0:T(8,128)(2,1)} %pack.2), channel_id=1, source_target_pairs={{0,4},{4,0},{8,12},{12,8},{16,20},{20,16},{24,28},{28,24},{1,5},{5... | collective-permute-start | bytes 1081352 | tf_op jit(solution)/shard_map/ppermute | solution.py:364
  4.9 1.0 copy-start.2
  6.0 0.8 copy-start.4
  6.8 0.8 copy-start.5
  7.6 0.7 copy-start.6
  13.6 8.9 %collective-permute-start.1 = (bf16[144,1024]{1,0:T(8,128)(2,1)S(1)}, bf16[144,1024]{1,0:T(8,128)(2,1)S(1)}, u32[]{:S(2)}, u32[]{:S(2)}) collective-permute-start(bf16[144,1024]{1,0:T(8,128)(2,1)S(1)} %get-tuple-element.46.send_ref), channel_id=1, source_target_pairs={{0,8},{4,12},{8,16},{12,20},{16,24},{20,28},{1,9},{5,13},{9,17},{1... | collective-permute-start | bytes 884744 | tf_op jit(solution)/shard_map/ppermute | solution.py:362
  18.1 9.9 %collective-permute-start.3 = (bf16[128,1024]{1,0:T(8,128)(2,1)S(1)}, bf16[128,1024]{1,0:T(8,128)(2,1)S(1)}, u32[]{:S(2)}, u32[]{:S(2)}) collective-permute-start(bf16[128,1024]{1,0:T(8,128)(2,1)S(1)} %constant_dynamic-slice_fusion), channel_id=1, source_target_pairs={{0,4},{4,0},{8,12},{12,8},{16,20},{20,16},{24,28},{28,24},{1,5},{5... | collective-permute-start | bytes 786440 | tf_op jit(solution)/shard_map/ppermute | solution.py:370
  22.6 9.3 %collective-permute-start.2 = (bf16[128,1024]{1,0:T(8,128)(2,1)S(1)}, bf16[128,1024]{1,0:T(8,128)(2,1)S(1)}, u32[]{:S(2)}, u32[]{:S(2)}) collective-permute-start(bf16[128,1024]{1,0:T(8,128)(2,1)S(1)} %join.1), channel_id=1, source_target_pairs={{0,16},{4,20},{8,24},{12,28},{1,17},{5,21},{9,25},{13,29},{2,18},{... | collective-permute-start | bytes 786440 | tf_op jit(solution)/shard_map/ppermute | solution.py:362
  32.8 19.1 %collective-permute-start.4 = (bf16[256,1024]{1,0:T(8,128)(2,1)S(1)}, bf16[256,1024]{1,0:T(8,128)(2,1)S(1)}, u32[]{:S(2)}, u32[]{:S(2)}) collective-permute-start(bf16[256,1024]{1,0:T(8,128)(2,1)S(1)} %finish.1.own_ref), channel_id=1, source_target_pairs={{0,8},{4,12},{8,0},{12,4},{16,24},{20,28},{24,16},{28,20},{1,9},{5... | collective-permute-start | bytes 1572872 | tf_op jit(solution)/shard_map/ppermute | solution.py:381
  39.8 12.8 %collective-permute-start.12 = (bf16[256,1024]{1,0:T(8,128)(2,1)S(1)}, bf16[256,1024]{1,0:T(8,128)(2,1)S(1)}, u32[]{:S(2)}, u32[]{:S(2)}) collective-permute-start(bf16[256,1024]{1,0:T(8,128)(2,1)S(1)} %finish.1.own_ref), channel_id=1, source_target_pairs={{8,16},{12,20},{16,8},{20,12},{9,17},{13,21},{17,9},{21,13},{10,18... | collective-permute-start | bytes 1572872 | tf_op jit(solution)/shard_map/ppermute | solution.py:381
  40.5 15.0 %collective-permute-start.6 = (bf16[256,1024]{1,0:T(8,128)(2,1)S(1)}, bf16[256,1024]{1,0:T(8,128)(2,1)S(1)}, u32[]{:S(2)}, u32[]{:S(2)}) collective-permute-start(bf16[256,1024]{1,0:T(8,128)(2,1)S(1)} %finish.1.own_ref), channel_id=1, source_target_pairs={{0,4},{4,0},{8,12},{12,8},{16,20},{20,16},{24,28},{28,24},{1,5},{5... | collective-permute-start | bytes 1572872 | tf_op jit(solution)/shard_map/ppermute | solution.py:384
  51.9 9.6 %collective-permute-start.5 = (bf16[256,1024]{1,0:T(8,128)(2,1)S(1)}, bf16[256,1024]{1,0:T(8,128)(2,1)S(1)}, u32[]{:S(2)}, u32[]{:S(2)}) collective-permute-start(bf16[256,1024]{1,0:T(8,128)(2,1)S(1)} %collective-permute-done.4.own_ref), channel_id=1, source_target_pairs={{8,16},{12,20},{16,8},{20,12},{9,17},{13,21},{17,9},{21,13},{10,18... | collective-permute-start | bytes 1572872 | tf_op jit(solution)/shard_map/ppermute | solution.py:381
  52.6 17.7 %collective-permute-start.13 = (bf16[256,1024]{1,0:T(8,128)(2,1)S(1)}, bf16[256,1024]{1,0:T(8,128)(2,1)S(1)}, u32[]{:S(2)}, u32[]{:S(2)}) collective-permute-start(bf16[256,1024]{1,0:T(8,128)(2,1)S(1)} %collective-permute-done.12), channel_id=1, source_target_pairs={{8,0},{12,4},{16,24},{20,28},{9,1},{13,5},{17,25},{21,29},{10,2},{... | collective-permute-start | bytes 1572872 | tf_op jit(solution)/shard_map/ppermute | solution.py:381
  54.0 17.9 %collective-permute-start.9 = (bf16[256,1024]{1,0:T(8,128)(2,1)S(1)}, bf16[256,1024]{1,0:T(8,128)(2,1)S(1)}, u32[]{:S(2)}, u32[]{:S(2)}) collective-permute-start(bf16[256,1024]{1,0:T(8,128)(2,1)S(1)} %collective-permute-done.4.own_ref), channel_id=1, source_target_pairs={{0,4},{4,0},{8,12},{12,8},{16,20},{20,16},{24,28},{28,24},{1,5},{5... | collective-permute-start | bytes 1572872 | tf_op jit(solution)/shard_map/ppermute | solution.py:384
  55.6 19.6 %collective-permute-start.8 = (bf16[256,1024]{1,0:T(8,128)(2,1)S(1)}, bf16[256,1024]{1,0:T(8,128)(2,1)S(1)}, u32[]{:S(2)}, u32[]{:S(2)}) collective-permute-start(bf16[256,1024]{1,0:T(8,128)(2,1)S(1)} %collective-permute-done.6.refs_0_), channel_id=1, source_target_pairs={{8,16},{12,20},{16,8},{20,12},{9,17},{13,21},{17,9},{21,13},{10,18... | collective-permute-start | bytes 1572872 | tf_op jit(solution)/shard_map/ppermute | solution.py:381
  56.3 2.2 %copy-start = (bf16[2048,1024]{1,0:T(8,128)(2,1)S(1)}, bf16[2048,1024]{1,0:T(8,128)(2,1)}, u32[]{:S(2)}) copy-start(bf16[2048,1024]{1,0:T(8,128)(2,1)} %refs_4_.1) | copy-start | bytes 12582916
  58.4 13.5 %copy-start.1 = (bf16[2048,1024]{1,0:T(8,128)(2,1)S(1)}, bf16[2048,1024]{1,0:T(8,128)(2,1)}, u32[]{:S(2)}) copy-start(bf16[2048,1024]{1,0:T(8,128)(2,1)} %refs_4_.1) | copy-start | bytes 12582916
  61.6 20.0 %collective-permute-start.7 = (bf16[256,1024]{1,0:T(8,128)(2,1)S(1)}, bf16[256,1024]{1,0:T(8,128)(2,1)S(1)}, u32[]{:S(2)}, u32[]{:S(2)}) collective-permute-start(bf16[256,1024]{1,0:T(8,128)(2,1)S(1)} %collective-permute-done.5), channel_id=1, source_target_pairs={{8,0},{12,4},{16,24},{20,28},{9,1},{13,5},{17,25},{21,29},{10,2},{... | collective-permute-start | bytes 1572872 | tf_op jit(solution)/shard_map/ppermute | solution.py:381
  70.4 12.4 %collective-permute-start.14 = (bf16[256,1024]{1,0:T(8,128)(2,1)S(1)}, bf16[256,1024]{1,0:T(8,128)(2,1)S(1)}, u32[]{:S(2)}, u32[]{:S(2)}) collective-permute-start(bf16[256,1024]{1,0:T(8,128)(2,1)S(1)} %broadcast_select_fusion.1.own_ref), channel_id=1, source_target_pairs={{0,4},{4,0},{8,12},{12,8},{16,20},{20,16},{24,28},{28,24},{1,5},{5... | collective-permute-start | bytes 1572872 | tf_op jit(solution)/shard_map/ppermute | solution.py:384
  72.0 3.1 %collective-permute-start.10 = (bf16[128,1024]{1,0:T(8,128)(2,1)S(1)}, bf16[128,1024]{1,0:T(8,128)(2,1)S(1)}, u32[]{:S(2)}, u32[]{:S(2)}) collective-permute-start(bf16[128,1024]{1,0:T(8,128)(2,1)S(1)} %get-tuple-element.62), channel_id=1, source_target_pairs={{0,1},{1,0},{2,3},{3,2},{4,5},{5,4},{6,7},{7,6},{8,9},{9,8},{10,11... | collective-permute-start | bytes 786440 | tf_op jit(solution)/shard_map/ppermute | solution.py:385
  82.8 8.3 %collective-permute-start.15 = (bf16[128,1024]{1,0:T(8,128)(2,1)S(1)}, bf16[128,1024]{1,0:T(8,128)(2,1)S(1)}, u32[]{:S(2)}, u32[]{:S(2)}) collective-permute-start(bf16[128,1024]{1,0:T(8,128)(2,1)S(1)} %slice.10), channel_id=1, source_target_pairs={{8,0},{12,4},{16,24},{20,28},{9,1},{13,5},{17,25},{21,29},{10,2},{... | collective-permute-start | bytes 786440 | tf_op jit(solution)/shard_map/ppermute | solution.py:381
  84.2 8.3 %collective-permute-start.11 = (bf16[128,1024]{1,0:T(8,128)(2,1)S(1)}, bf16[128,1024]{1,0:T(8,128)(2,1)S(1)}, u32[]{:S(2)}, u32[]{:S(2)}) collective-permute-start(bf16[128,1024]{1,0:T(8,128)(2,1)S(1)} %slice.8), channel_id=1, source_target_pairs={{0,4},{4,0},{24,28},{28,24},{1,5},{5,1},{25,29},{29,25},{2,6},{6,2... | collective-permute-start | bytes 786440 | tf_op jit(solution)/shard_map/ppermute | solution.py:419
  92.4 4.9 %collective-permute-start.16 = (bf16[256,1024]{1,0:T(8,128)(2,1)S(1)}, bf16[256,1024]{1,0:T(8,128)(2,1)S(1)}, u32[]{:S(2)}, u32[]{:S(2)}) collective-permute-start(bf16[256,1024]{1,0:T(8,128)(2,1)S(1)} %pad_maximum_fusion), channel_id=1, source_target_pairs={{0,1},{1,0},{2,3},{3,2},{4,5},{5,4},{6,7},{7,6},{8,9},{9,8},{10,11... | collective-permute-start | bytes 1572872 | tf_op jit(solution)/shard_map/ppermute | solution.py:385
  95.6 1.7 %collective-permute-start.17 = (bf16[128,1024]{1,0:T(8,128)(2,1)S(1)}, bf16[128,1024]{1,0:T(8,128)(2,1)S(1)}, u32[]{:S(2)}, u32[]{:S(2)}) collective-permute-start(bf16[128,1024]{1,0:T(8,128)(2,1)S(1)} %get-tuple-element.74), channel_id=1, source_target_pairs={{0,1},{1,0},{2,3},{3,2},{4,5},{5,4},{6,7},{7,6},{8,9},{9,8},{10,11... | collective-permute-start | bytes 786440 | tf_op jit(solution)/shard_map/ppermute | solution.py:385
  97.6 11.8 %collective-permute-start.20 = (bf16[128,1024]{1,0:T(8,128)(2,1)S(1)}, bf16[128,1024]{1,0:T(8,128)(2,1)S(1)}, u32[]{:S(2)}, u32[]{:S(2)}) collective-permute-start(bf16[128,1024]{1,0:T(8,128)(2,1)S(1)} %get-tuple-element.83), channel_id=1, source_target_pairs={{0,8},{1,12},{2,24},{3,28},{4,9},{5,13},{6,25},{7,29},{8,0},{9,4},... | collective-permute-start | bytes 786440 | tf_op jit(solution)/shard_map/ppermute | solution.py:398
  99.2 12.9 %collective-permute-start.21 = (bf16[128,1024]{1,0:T(8,128)(2,1)S(1)}, bf16[128,1024]{1,0:T(8,128)(2,1)S(1)}, u32[]{:S(2)}, u32[]{:S(2)}) collective-permute-start(bf16[128,1024]{1,0:T(8,128)(2,1)S(1)} %get-tuple-element.84), channel_id=1, source_target_pairs={{0,24},{1,28},{2,8},{3,12},{4,25},{5,29},{6,9},{7,13},{8,16},{9,20... | collective-permute-start | bytes 786440 | tf_op jit(solution)/shard_map/ppermute | solution.py:398
  99.7 22.5 %collective-permute-start.18 = (bf16[128,1024]{1,0:T(8,128)(2,1)S(1)}, bf16[128,1024]{1,0:T(8,128)(2,1)S(1)}, u32[]{:S(2)}, u32[]{:S(2)}) collective-permute-start(bf16[128,1024]{1,0:T(8,128)(2,1)S(1)} %get-tuple-element.81), channel_id=1, source_target_pairs={{1,4},{2,16},{3,20},{4,1},{6,17},{7,21},{9,12},{10,24},{11,28},{12... | collective-permute-start | bytes 786440 | tf_op jit(solution)/shard_map/ppermute | solution.py:398
  102.7 20.8 %collective-permute-start.19 = (bf16[128,1024]{1,0:T(8,128)(2,1)S(1)}, bf16[128,1024]{1,0:T(8,128)(2,1)S(1)}, u32[]{:S(2)}, u32[]{:S(2)}) collective-permute-start(bf16[128,1024]{1,0:T(8,128)(2,1)S(1)} %get-tuple-element.82), channel_id=1, source_target_pairs={{0,16},{1,20},{2,0},{3,4},{4,17},{5,21},{6,1},{7,5},{8,24},{9,28},... | collective-permute-start | bytes 786440 | tf_op jit(solution)/shard_map/ppermute | solution.py:398
  123.8 1.7 %collective-permute-start.22 = (bf16[128,1024]{1,0:T(8,128)(2,1)S(1)}, bf16[128,1024]{1,0:T(8,128)(2,1)S(1)}, u32[]{:S(2)}, u32[]{:S(2)}) collective-permute-start(bf16[128,1024]{1,0:T(8,128)(2,1)S(1)} %get-tuple-element.79), channel_id=1, source_target_pairs={{0,1},{1,0},{2,3},{3,2},{4,5},{5,4},{6,7},{7,6},{8,9},{9,8},{10,11... | collective-permute-start | bytes 786440 | tf_op jit(solution)/shard_map/ppermute | solution.py:385

commit v9 on v8

--- a/solution.py
+++ b/solution.py
@@ -387,12 +387,12 @@
     def reduce_core(full, rounded):
         return (full + cross(rounded).astype(F32)).astype(BF16)
 
-    def deliver(slot, near, distant):
+    def deliver(slot, far, near, distant):
         near_x, total = grp // 2 == z // 2, 0.0
         for turn in range(2):
             pairs = []
             for a, b, c, d in spots:
-                at = slot if c ^ turn == a // 2 else slot + 2
+                at = slot if c ^ turn == a // 2 else far
                 pairs.append((flat(a, b, c, d), flat(a ^ at, d, a // 2, b)))
             value = jnp.where(near_x, near, distant) if turn == 0 else jnp.where(near_x, distant, near)
             moved = lax.ppermute(value, both, [(i, j) for i, j in pairs if i != j])
@@ -425,10 +425,10 @@
     b1, b2 = ((part[0] + v.astype(F32)).astype(BF16) for part, v in zip((a1, a2), sums))
     b3 = reduce_core(*project(yc, slot3, [inner3, lower3, upper3], w_out))
     b0, b1, b2, b3 = tie((b0, b1, b2, b3))
-    odd = deliver(1, b1, b3)
-    even = deliver(0, b0, b2)
-    here = core == z % 2
-    mine, theirs = jnp.where(here, even, odd), jnp.where(here, odd, even)
+    last_sums = deliver(0, 3, b0, b3)
+    early_sums = deliver(1, 2, b1, b2)
+    here = (core == z % 2) == (grp // 2 == z // 2)
+    mine, theirs = jnp.where(here, last_sums, early_sums), jnp.where(here, early_sums, last_sums)
     return place(core.astype(jnp.int32).reshape(1), mine.astype(BF16), cross(theirs.astype(BF16)))
 
 

time: 127 us -> 127 us (level)
  the two profiles are of different devices: /device:TPU:2 before, /device:TPU:11 now
where the time goes in v9:
time: 127 us
  waiting for transfers between devices  49.4 us (39%)
  starting transfers between devices  48.5 us (38%)
  Pallas kernels  18.8 us (15%)
  local copies, waits for them, and re-layouts  8.85 us (7%)
    ppermute x4, waiting for transfers between devices, deliver(): moved = lax.ppermute(value, both, [(i, j) for i, j in pairs if i != j])  20.3 us
    ppermute x7, starting transfers between devices, pair_shards(): lax.ppermute(value, 'seq', [(i * 2 + b, j * 2 + b) for i, j in moves for...  18.7 us
    ppermute x2, waiting for transfers between devices, along(): return lax.ppermute(v, 'seq', pairs)  13.7 us
    pallas_call x4, Pallas kernels, project(): pl.pallas_call(project_kernel, grid_spec=pltpu.PrefetchScalarGridSpec(num...  12.4 us
    ppermute x7, waiting for transfers between devices, pair_shards(): lax.ppermute(value, 'seq', [(i * 2 + b, j * 2 + b) for i, j in moves for...  9.09 us
    ppermute x4, starting transfers between devices, deliver(): moved = lax.ppermute(value, both, [(i, j) for i, j in pairs if i != j])  8.65 us
    ppermute x2, starting transfers between devices, along(): return lax.ppermute(v, 'seq', pairs)  7.43 us
    ppermute x4, starting transfers between devices, pair_shards(): cross = lambda value: lax.ppermute(value, 'grp', sibling)  6.65 us
  transfers between devices with their start and end apart: 23, of which 13 were waited for; matrix products, arithmetic and copies ran while one was open for 3% of the time, Pallas kernels for 11%

profile of v9, /device:TPU:11, one launch (start us, length us, event | category | flops | bytes accessed | tf_op | source)
XLA Modules:
  0.0 126.7 jit_solution(1791067032459560697)
XLA Ops:
  0.0 2.0 %pack.2 = bf16[128,1408]{1,0:T(8,128)(2,1)} custom-call(s32[1]{0:T(128)S(6)} %sub.23.refs_0_, bf16[128,2048]{1,0:T(8,128)(2,1)} %refs_1_.6, bf16[128,256]{1,0:T(8,128)(2,1)} %refs_2_.6, bf16[128,256]{1,0:T(8,128)(2,1)} %refs_3_.4, f32[16,128]{1,0:T(8,128)} %bitcast.10), custom_call_target="tpu_custom_call" | custom-call | flops 1000000 | bytes 1000000 | tf_op jit(solution)/shard_map/pack/pallas_call | solution.py:68
  9.0 2.4 %collective-permute-done.refs_2_ = bf16[128,1408]{1,0:T(8,128)(2,1)S(1)} collective-permute-done((bf16[128,1408]{1,0:T(8,128)(2,1)}, bf16[128,1408]{1,0:T(8,128)(2,1)S(1)}, u32[]{:S(2)}, u32[]{:S(2)}) %collective-permute-start) | collective-permute-done | bytes 360480 | tf_op jit(solution)/shard_map/ppermute | solution.py:364
  12.7 3.2 %collective-permute-start.1 = (bf16[144,1024]{1,0:T(8,128)(2,1)S(1)}, bf16[144,1024]{1,0:T(8,128)(2,1)S(1)}, u32[]{:S(2)}, u32[]{:S(2)}) collective-permute-start(bf16[144,1024]{1,0:T(8,128)(2,1)S(1)} %get-tuple-element.46.send_ref), channel_id=1, source_target_pairs={{0,8},{4,12},{8,16},{12,20},{16,24},{20,28},{1,9},{5,13},{9,17},{1... | collective-permute-start | bytes 884744 | tf_op jit(solution)/shard_map/ppermute | solution.py:362
  16.9 1.3 %collective-permute-start.3 = (bf16[128,1024]{1,0:T(8,128)(2,1)S(1)}, bf16[128,1024]{1,0:T(8,128)(2,1)S(1)}, u32[]{:S(2)}, u32[]{:S(2)}) collective-permute-start(bf16[128,1024]{1,0:T(8,128)(2,1)S(1)} %constant_dynamic-slice_fusion), channel_id=1, source_target_pairs={{0,4},{4,0},{8,12},{12,8},{16,20},{20,16},{24,28},{28,24},{1,5},{5... | collective-permute-start | bytes 786440 | tf_op jit(solution)/shard_map/ppermute | solution.py:370
  19.3 2.3 %collective-permute-done.1.got_ref.refs_4_ = bf16[144,1024]{1,0:T(8,128)(2,1)S(1)} collective-permute-done((bf16[144,1024]{1,0:T(8,128)(2,1)S(1)}, bf16[144,1024]{1,0:T(8,128)(2,1)S(1)}, u32[]{:S(2)}, u32[]{:S(2)}) %collective-permute-start.1) | collective-permute-done | bytes 294944 | tf_op jit(solution)/shard_map/ppermute | solution.py:362
  21.7 4.2 %collective-permute-start.2 = (bf16[128,1024]{1,0:T(8,128)(2,1)S(1)}, bf16[128,1024]{1,0:T(8,128)(2,1)S(1)}, u32[]{:S(2)}, u32[]{:S(2)}) collective-permute-start(bf16[128,1024]{1,0:T(8,128)(2,1)S(1)} %join.1), channel_id=1, source_target_pairs={{0,16},{4,20},{8,24},{12,28},{1,17},{5,21},{9,25},{13,29},{2,18},{... | collective-permute-start | bytes 786440 | tf_op jit(solution)/shard_map/ppermute | solution.py:362
  25.9 11.5 %collective-permute-done.2.refs_5_ = bf16[128,1024]{1,0:T(8,128)(2,1)S(1)} collective-permute-done((bf16[128,1024]{1,0:T(8,128)(2,1)S(1)}, bf16[128,1024]{1,0:T(8,128)(2,1)S(1)}, u32[]{:S(2)}, u32[]{:S(2)}) %collective-permute-start.2) | collective-permute-done | bytes 262176 | tf_op jit(solution)/shard_map/ppermute | solution.py:362
  38.4 5.3 %collective-permute-start.12 = (bf16[256,1024]{1,0:T(8,128)(2,1)S(1)}, bf16[256,1024]{1,0:T(8,128)(2,1)S(1)}, u32[]{:S(2)}, u32[]{:S(2)}) collective-permute-start(bf16[256,1024]{1,0:T(8,128)(2,1)S(1)} %finish.1.own_ref), channel_id=1, source_target_pairs={{8,16},{12,20},{16,8},{20,12},{9,17},{13,21},{17,9},{21,13},{10,18... | collective-permute-start | bytes 1572872 | tf_op jit(solution)/shard_map/ppermute | solution.py:381
  43.7 1.3 %collective-permute-start.6 = (bf16[256,1024]{1,0:T(8,128)(2,1)S(1)}, bf16[256,1024]{1,0:T(8,128)(2,1)S(1)}, u32[]{:S(2)}, u32[]{:S(2)}) collective-permute-start(bf16[256,1024]{1,0:T(8,128)(2,1)S(1)} %finish.1.own_ref), channel_id=1, source_target_pairs={{0,4},{4,0},{8,12},{12,8},{16,20},{20,16},{24,28},{28,24},{1,5},{5... | collective-permute-start | bytes 1572872 | tf_op jit(solution)/shard_map/ppermute | solution.py:384
  45.0 6.4 %collective-permute-done.4.own_ref = bf16[256,1024]{1,0:T(8,128)(2,1)S(1)} collective-permute-done((bf16[256,1024]{1,0:T(8,128)(2,1)S(1)}, bf16[256,1024]{1,0:T(8,128)(2,1)S(1)}, u32[]{:S(2)}, u32[]{:S(2)}) %collective-permute-start.4) | collective-permute-done | bytes 524320 | tf_op jit(solution)/shard_map/ppermute | solution.py:381
  51.4 4.1 %collective-permute-start.5 = (bf16[256,1024]{1,0:T(8,128)(2,1)S(1)}, bf16[256,1024]{1,0:T(8,128)(2,1)S(1)}, u32[]{:S(2)}, u32[]{:S(2)}) collective-permute-start(bf16[256,1024]{1,0:T(8,128)(2,1)S(1)} %collective-permute-done.4.own_ref), channel_id=1, source_target_pairs={{8,16},{12,20},{16,8},{20,12},{9,17},{13,21},{17,9},{21,13},{10,18... | collective-permute-start | bytes 1572872 | tf_op jit(solution)/shard_map/ppermute | solution.py:381
  55.5 1.3 %collective-permute-start.13 = (bf16[256,1024]{1,0:T(8,128)(2,1)S(1)}, bf16[256,1024]{1,0:T(8,128)(2,1)S(1)}, u32[]{:S(2)}, u32[]{:S(2)}) collective-permute-start(bf16[256,1024]{1,0:T(8,128)(2,1)S(1)} %collective-permute-done.12), channel_id=1, source_target_pairs={{8,0},{12,4},{16,24},{20,28},{9,1},{13,5},{17,25},{21,29},{10,2},{... | collective-permute-start | bytes 1572872 | tf_op jit(solution)/shard_map/ppermute | solution.py:381
  57.0 1.2 collective-permute-start.9
  58.2 2.7 %collective-permute-start.8 = (bf16[256,1024]{1,0:T(8,128)(2,1)S(1)}, bf16[256,1024]{1,0:T(8,128)(2,1)S(1)}, u32[]{:S(2)}, u32[]{:S(2)}) collective-permute-start(bf16[256,1024]{1,0:T(8,128)(2,1)S(1)} %collective-permute-done.6.refs_0_), channel_id=1, source_target_pairs={{8,16},{12,20},{16,8},{20,12},{9,17},{13,21},{17,9},{21,13},{10,18... | collective-permute-start | bytes 1572872 | tf_op jit(solution)/shard_map/ppermute | solution.py:381
  60.9 2.2 %copy-done = bf16[2048,1024]{1,0:T(8,128)(2,1)S(1)} copy-done((bf16[2048,1024]{1,0:T(8,128)(2,1)S(1)}, bf16[2048,1024]{1,0:T(8,128)(2,1)}, u32[]{:S(2)}) %copy-start) | copy-done | bytes 4194328
  63.1 3.1 %project.4 = (f32[128,1024]{1,0:T(8,128)S(1)}, bf16[128,1024]{1,0:T(8,128)(2,1)S(1)}) custom-call(s32[3]{0:T(128)S(1)} %pad_add_fusion.yc_ref, bf16[256,1024]{1,0:T(8,128)(2,1)S(1)} %finish.1.own_ref, bf16[256,1024]{1,0:T(8,128)(2,1)S(1)} %collective-permute-done.6.refs_0_, bf16[2048,1024]{1,0:T(8,128)(2,1)S(1)} %copy-done, bf16[2048,1024]{1,0:T(8,128)(2,1)S(1)} %copy-done), custom_call_target="tpu_custom_call" | custom-call | flops 1073741824 | bytes 6000000 | tf_op jit(solution)/shard_map/project/pallas_call | solution.py:291
  66.7 1.3 %collective-permute-start.7 = (bf16[256,1024]{1,0:T(8,128)(2,1)S(1)}, bf16[256,1024]{1,0:T(8,128)(2,1)S(1)}, u32[]{:S(2)}, u32[]{:S(2)}) collective-permute-start(bf16[256,1024]{1,0:T(8,128)(2,1)S(1)} %collective-permute-done.5), channel_id=1, source_target_pairs={{8,0},{12,4},{16,24},{20,28},{9,1},{13,5},{17,25},{21,29},{10,2},{... | collective-permute-start | bytes 1572872 | tf_op jit(solution)/shard_map/ppermute | solution.py:381
  68.1 1.3 %collective-permute-start.14 = (bf16[256,1024]{1,0:T(8,128)(2,1)S(1)}, bf16[256,1024]{1,0:T(8,128)(2,1)S(1)}, u32[]{:S(2)}, u32[]{:S(2)}) collective-permute-start(bf16[256,1024]{1,0:T(8,128)(2,1)S(1)} %broadcast_select_fusion.1.own_ref), channel_id=1, source_target_pairs={{0,4},{4,0},{8,12},{12,8},{16,20},{20,16},{24,28},{28,24},{1,5},{5... | collective-permute-start | bytes 1572872 | tf_op jit(solution)/shard_map/ppermute | solution.py:384
  69.4 3.2 %collective-permute-start.10 = (bf16[128,1024]{1,0:T(8,128)(2,1)S(1)}, bf16[128,1024]{1,0:T(8,128)(2,1)S(1)}, u32[]{:S(2)}, u32[]{:S(2)}) collective-permute-start(bf16[128,1024]{1,0:T(8,128)(2,1)S(1)} %get-tuple-element.62), channel_id=1, source_target_pairs={{0,1},{1,0},{2,3},{3,2},{4,5},{5,4},{6,7},{7,6},{8,9},{9,8},{10,11... | collective-permute-start | bytes 786440 | tf_op jit(solution)/shard_map/ppermute | solution.py:385
  72.6 3.1 %project.5 = (f32[128,1024]{1,0:T(8,128)S(1)}, bf16[128,1024]{1,0:T(8,128)(2,1)S(1)}) custom-call(s32[3]{0:T(128)S(1)} %pad_add_fusion.yc_ref, bf16[256,1024]{1,0:T(8,128)(2,1)S(1)} %collective-permute-done.4.own_ref, bf16[256,1024]{1,0:T(8,128)(2,1)S(1)} %collective-permute-done.9.refs_0_, bf16[2048,1024]{1,0:T(8,128)(2,1)S(1)} %copy-done.1, ...), custom_call_target="tpu_custom_call" | custom-call | flops 1073741824 | bytes 6000000 | tf_op jit(solution)/shard_map/project/pallas_call | solution.py:291
  75.8 2.2 %collective-permute-done.8.refs_0_ = bf16[256,1024]{1,0:T(8,128)(2,1)S(1)} collective-permute-done((bf16[256,1024]{1,0:T(8,128)(2,1)S(1)}, bf16[256,1024]{1,0:T(8,128)(2,1)S(1)}, u32[]{:S(2)}, u32[]{:S(2)}) %collective-permute-start.8) | collective-permute-done | bytes 524320 | tf_op jit(solution)/shard_map/ppermute | solution.py:381
  78.8 3.9 %collective-permute-start.15 = (bf16[128,1024]{1,0:T(8,128)(2,1)S(1)}, bf16[128,1024]{1,0:T(8,128)(2,1)S(1)}, u32[]{:S(2)}, u32[]{:S(2)}) collective-permute-start(bf16[128,1024]{1,0:T(8,128)(2,1)S(1)} %slice.10), channel_id=1, source_target_pairs={{8,0},{12,4},{16,24},{20,28},{9,1},{13,5},{17,25},{21,29},{10,2},{... | collective-permute-start | bytes 786440 | tf_op jit(solution)/shard_map/ppermute | solution.py:381
  83.4 3.1 %project.6 = (f32[128,1024]{1,0:T(8,128)S(1)}, bf16[128,1024]{1,0:T(8,128)(2,1)S(1)}) custom-call(s32[3]{0:T(128)S(1)} %pad_add_fusion.yc_ref, bf16[256,1024]{1,0:T(8,128)(2,1)S(1)} %broadcast_select_fusion.1.own_ref, bf16[256,1024]{1,0:T(8,128)(2,1)S(1)} %collective-permute-done.14.refs_0_, bf16[2048,1024]{1,0:T(8,128)(2,1)S(1)} %copy-done.1, ...), custom_call_target="tpu_custom_call" | custom-call | flops 1073741824 | bytes 6000000 | tf_op jit(solution)/shard_map/project/pallas_call | solution.py:291
  86.7 3.2 %collective-permute-start.16 = (bf16[256,1024]{1,0:T(8,128)(2,1)S(1)}, bf16[256,1024]{1,0:T(8,128)(2,1)S(1)}, u32[]{:S(2)}, u32[]{:S(2)}) collective-permute-start(bf16[256,1024]{1,0:T(8,128)(2,1)S(1)} %pad_maximum_fusion), channel_id=1, source_target_pairs={{0,1},{1,0},{2,3},{3,2},{4,5},{5,4},{6,7},{7,6},{8,9},{9,8},{10,11... | collective-permute-start | bytes 1572872 | tf_op jit(solution)/shard_map/ppermute | solution.py:385
  89.9 3.1 %project.7 = (f32[128,1024]{1,0:T(8,128)S(1)}, bf16[128,1024]{1,0:T(8,128)(2,1)S(1)}) custom-call(s32[3]{0:T(128)S(1)} %pad_add_fusion.yc_ref, bf16[256,1024]{1,0:T(8,128)(2,1)S(1)} %broadcast_select_fusion.own_ref, bf16[256,1024]{1,0:T(8,128)(2,1)S(1)} %collective-permute-done.8.refs_0_, bf16[128,1024]{1,0:T(8,128)(2,1)S(1)} %collective-permute-done.11.refs_1_, ...), custom_call_target="tpu_custom_call" | custom-call | flops 1073741824 | bytes 6000000 | tf_op jit(solution)/shard_map/project/pallas_call | solution.py:291
  93.2 1.5 %collective-permute-done.17 = bf16[128,1024]{1,0:T(8,128)(2,1)S(1)} collective-permute-done((bf16[128,1024]{1,0:T(8,128)(2,1)S(1)}, bf16[128,1024]{1,0:T(8,128)(2,1)S(1)}, u32[]{:S(2)}, u32[]{:S(2)}) %collective-permute-start.17) | collective-permute-done | bytes 262176 | tf_op jit(solution)/shard_map/ppermute | solution.py:385
  94.9 4.5 %collective-permute-start.20 = (bf16[128,1024]{1,0:T(8,128)(2,1)S(1)}, bf16[128,1024]{1,0:T(8,128)(2,1)S(1)}, u32[]{:S(2)}, u32[]{:S(2)}) collective-permute-start(bf16[128,1024]{1,0:T(8,128)(2,1)S(1)} %get-tuple-element.83), channel_id=1, source_target_pairs={{0,8},{1,12},{2,16},{3,20},{4,9},{5,13},{6,17},{7,21},{8,0},{9,4},... | collective-permute-start | bytes 786440 | tf_op jit(solution)/shard_map/ppermute | solution.py:398
  99.5 4.1 %collective-permute-start.18 = (bf16[128,1024]{1,0:T(8,128)(2,1)S(1)}, bf16[128,1024]{1,0:T(8,128)(2,1)S(1)}, u32[]{:S(2)}, u32[]{:S(2)}) collective-permute-start(bf16[128,1024]{1,0:T(8,128)(2,1)S(1)} %get-tuple-element.81), channel_id=1, source_target_pairs={{1,4},{2,24},{3,28},{4,1},{6,25},{7,29},{9,12},{10,16},{11,20},{12... | collective-permute-start | bytes 786440 | tf_op jit(solution)/shard_map/ppermute | solution.py:398
  103.6 6.3 %collective-permute-done.20 = bf16[128,1024]{1,0:T(8,128)(2,1)S(1)} collective-permute-done((bf16[128,1024]{1,0:T(8,128)(2,1)S(1)}, bf16[128,1024]{1,0:T(8,128)(2,1)S(1)}, u32[]{:S(2)}, u32[]{:S(2)}) %collective-permute-start.20) | collective-permute-done | bytes 262176 | tf_op jit(solution)/shard_map/ppermute | solution.py:398
  110.0 2.0 %collective-permute-done.21 = bf16[128,1024]{1,0:T(8,128)(2,1)S(1)} collective-permute-done((bf16[128,1024]{1,0:T(8,128)(2,1)S(1)}, bf16[128,1024]{1,0:T(8,128)(2,1)S(1)}, u32[]{:S(2)}, u32[]{:S(2)}) %collective-permute-start.21) | collective-permute-done | bytes 262176 | tf_op jit(solution)/shard_map/ppermute | solution.py:398
  112.0 10.9 %collective-permute-done.18 = bf16[128,1024]{1,0:T(8,128)(2,1)S(1)} collective-permute-done((bf16[128,1024]{1,0:T(8,128)(2,1)S(1)}, bf16[128,1024]{1,0:T(8,128)(2,1)S(1)}, u32[]{:S(2)}, u32[]{:S(2)}) %collective-permute-start.18) | collective-permute-done | bytes 262176 | tf_op jit(solution)/shard_map/ppermute | solution.py:398
  124.4 1.5 %collective-permute-done.22.got_ref = bf16[128,1024]{1,0:T(8,128)(2,1)S(1)} collective-permute-done((bf16[128,1024]{1,0:T(8,128)(2,1)S(1)}, bf16[128,1024]{1,0:T(8,128)(2,1)S(1)}, u32[]{:S(2)}, u32[]{:S(2)}) %collective-permute-start.22) | collective-permute-done | bytes 262176 | tf_op jit(solution)/shard_map/ppermute | solution.py:385
  (56 shorter events, 16.5 us)
Async XLA Ops:
  0.0 37.4 %copy-start.3 = (bf16[128,2048]{1,0:T(8,128)(2,1)S(1)}, bf16[128,2048]{1,0:T(8,128)(2,1)}, u32[]{:S(2)}) copy-start(bf16[128,2048]{1,0:T(8,128)(2,1)} %refs_6_.1) | copy-start | bytes 1572868
  2.0 9.5 %collective-permute-start = (bf16[128,1408]{1,0:T(8,128)(2,1)}, bf16[128,1408]{1,0:T(8,128)(2,1)S(1)}, u32[]{:S(2)}, u32[]{:S(2)}) collective-permute-start(bf16[128,1408]{1,0:T(8,128)(2,1)} %pack.2), channel_id=1, source_target_pairs={{0,4},{4,0},{8,12},{12,8},{16,20},{20,16},{24,28},{28,24},{1,5},{5... | collective-permute-start | bytes 1081352 | tf_op jit(solution)/shard_map/ppermute | solution.py:364
  4.6 1.0 copy-start.2
  5.7 0.8 copy-start.4
  6.5 0.8 copy-start.5
  7.4 0.7 copy-start.6
  12.7 8.8 %collective-permute-start.1 = (bf16[144,1024]{1,0:T(8,128)(2,1)S(1)}, bf16[144,1024]{1,0:T(8,128)(2,1)S(1)}, u32[]{:S(2)}, u32[]{:S(2)}) collective-permute-start(bf16[144,1024]{1,0:T(8,128)(2,1)S(1)} %get-tuple-element.46.send_ref), channel_id=1, source_target_pairs={{0,8},{4,12},{8,16},{12,20},{16,24},{20,28},{1,9},{5,13},{9,17},{1... | collective-permute-start | bytes 884744 | tf_op jit(solution)/shard_map/ppermute | solution.py:362
  16.9 9.0 %collective-permute-start.3 = (bf16[128,1024]{1,0:T(8,128)(2,1)S(1)}, bf16[128,1024]{1,0:T(8,128)(2,1)S(1)}, u32[]{:S(2)}, u32[]{:S(2)}) collective-permute-start(bf16[128,1024]{1,0:T(8,128)(2,1)S(1)} %constant_dynamic-slice_fusion), channel_id=1, source_target_pairs={{0,4},{4,0},{8,12},{12,8},{16,20},{20,16},{24,28},{28,24},{1,5},{5... | collective-permute-start | bytes 786440 | tf_op jit(solution)/shard_map/ppermute | solution.py:370
  21.7 15.7 %collective-permute-start.2 = (bf16[128,1024]{1,0:T(8,128)(2,1)S(1)}, bf16[128,1024]{1,0:T(8,128)(2,1)S(1)}, u32[]{:S(2)}, u32[]{:S(2)}) collective-permute-start(bf16[128,1024]{1,0:T(8,128)(2,1)S(1)} %join.1), channel_id=1, source_target_pairs={{0,16},{4,20},{8,24},{12,28},{1,17},{5,21},{9,25},{13,29},{2,18},{... | collective-permute-start | bytes 786440 | tf_op jit(solution)/shard_map/ppermute | solution.py:362
  38.4 13.0 %collective-permute-start.4 = (bf16[256,1024]{1,0:T(8,128)(2,1)S(1)}, bf16[256,1024]{1,0:T(8,128)(2,1)S(1)}, u32[]{:S(2)}, u32[]{:S(2)}) collective-permute-start(bf16[256,1024]{1,0:T(8,128)(2,1)S(1)} %finish.1.own_ref), channel_id=1, source_target_pairs={{0,8},{4,12},{8,0},{12,4},{16,24},{20,28},{24,16},{28,20},{1,9},{5... | collective-permute-start | bytes 1572872 | tf_op jit(solution)/shard_map/ppermute | solution.py:381
  38.4 17.1 %collective-permute-start.12 = (bf16[256,1024]{1,0:T(8,128)(2,1)S(1)}, bf16[256,1024]{1,0:T(8,128)(2,1)S(1)}, u32[]{:S(2)}, u32[]{:S(2)}) collective-permute-start(bf16[256,1024]{1,0:T(8,128)(2,1)S(1)} %finish.1.own_ref), channel_id=1, source_target_pairs={{8,16},{12,20},{16,8},{20,12},{9,17},{13,21},{17,9},{21,13},{10,18... | collective-permute-start | bytes 1572872 | tf_op jit(solution)/shard_map/ppermute | solution.py:381
  43.7 14.5 %collective-permute-start.6 = (bf16[256,1024]{1,0:T(8,128)(2,1)S(1)}, bf16[256,1024]{1,0:T(8,128)(2,1)S(1)}, u32[]{:S(2)}, u32[]{:S(2)}) collective-permute-start(bf16[256,1024]{1,0:T(8,128)(2,1)S(1)} %finish.1.own_ref), channel_id=1, source_target_pairs={{0,4},{4,0},{8,12},{12,8},{16,20},{20,16},{24,28},{28,24},{1,5},{5... | collective-permute-start | bytes 1572872 | tf_op jit(solution)/shard_map/ppermute | solution.py:384
  51.4 15.4 %collective-permute-start.5 = (bf16[256,1024]{1,0:T(8,128)(2,1)S(1)}, bf16[256,1024]{1,0:T(8,128)(2,1)S(1)}, u32[]{:S(2)}, u32[]{:S(2)}) collective-permute-start(bf16[256,1024]{1,0:T(8,128)(2,1)S(1)} %collective-permute-done.4.own_ref), channel_id=1, source_target_pairs={{8,16},{12,20},{16,8},{20,12},{9,17},{13,21},{17,9},{21,13},{10,18... | collective-permute-start | bytes 1572872 | tf_op jit(solution)/shard_map/ppermute | solution.py:381
  55.5 12.5 %collective-permute-start.13 = (bf16[256,1024]{1,0:T(8,128)(2,1)S(1)}, bf16[256,1024]{1,0:T(8,128)(2,1)S(1)}, u32[]{:S(2)}, u32[]{:S(2)}) collective-permute-start(bf16[256,1024]{1,0:T(8,128)(2,1)S(1)} %collective-permute-done.12), channel_id=1, source_target_pairs={{8,0},{12,4},{16,24},{20,28},{9,1},{13,5},{17,25},{21,29},{10,2},{... | collective-permute-start | bytes 1572872 | tf_op jit(solution)/shard_map/ppermute | solution.py:381
  57.0 15.7 %collective-permute-start.9 = (bf16[256,1024]{1,0:T(8,128)(2,1)S(1)}, bf16[256,1024]{1,0:T(8,128)(2,1)S(1)}, u32[]{:S(2)}, u32[]{:S(2)}) collective-permute-start(bf16[256,1024]{1,0:T(8,128)(2,1)S(1)} %collective-permute-done.4.own_ref), channel_id=1, source_target_pairs={{0,4},{4,0},{8,12},{12,8},{16,20},{20,16},{24,28},{28,24},{1,5},{5... | collective-permute-start | bytes 1572872 | tf_op jit(solution)/shard_map/ppermute | solution.py:384
  58.2 19.8 %collective-permute-start.8 = (bf16[256,1024]{1,0:T(8,128)(2,1)S(1)}, bf16[256,1024]{1,0:T(8,128)(2,1)S(1)}, u32[]{:S(2)}, u32[]{:S(2)}) collective-permute-start(bf16[256,1024]{1,0:T(8,128)(2,1)S(1)} %collective-permute-done.6.refs_0_), channel_id=1, source_target_pairs={{8,16},{12,20},{16,8},{20,12},{9,17},{13,21},{17,9},{21,13},{10,18... | collective-permute-start | bytes 1572872 | tf_op jit(solution)/shard_map/ppermute | solution.py:381
  60.9 2.2 %copy-start = (bf16[2048,1024]{1,0:T(8,128)(2,1)S(1)}, bf16[2048,1024]{1,0:T(8,128)(2,1)}, u32[]{:S(2)}) copy-start(bf16[2048,1024]{1,0:T(8,128)(2,1)} %refs_4_.1) | copy-start | bytes 12582916
  63.1 9.5 %copy-start.1 = (bf16[2048,1024]{1,0:T(8,128)(2,1)S(1)}, bf16[2048,1024]{1,0:T(8,128)(2,1)}, u32[]{:S(2)}) copy-start(bf16[2048,1024]{1,0:T(8,128)(2,1)} %refs_4_.1) | copy-start | bytes 12582916
  66.7 11.2 %collective-permute-start.7 = (bf16[256,1024]{1,0:T(8,128)(2,1)S(1)}, bf16[256,1024]{1,0:T(8,128)(2,1)S(1)}, u32[]{:S(2)}, u32[]{:S(2)}) collective-permute-start(bf16[256,1024]{1,0:T(8,128)(2,1)S(1)} %collective-permute-done.5), channel_id=1, source_target_pairs={{8,0},{12,4},{16,24},{20,28},{9,1},{13,5},{17,25},{21,29},{10,2},{... | collective-permute-start | bytes 1572872 | tf_op jit(solution)/shard_map/ppermute | solution.py:381
  68.1 10.6 %collective-permute-start.14 = (bf16[256,1024]{1,0:T(8,128)(2,1)S(1)}, bf16[256,1024]{1,0:T(8,128)(2,1)S(1)}, u32[]{:S(2)}, u32[]{:S(2)}) collective-permute-start(bf16[256,1024]{1,0:T(8,128)(2,1)S(1)} %broadcast_select_fusion.1.own_ref), channel_id=1, source_target_pairs={{0,4},{4,0},{8,12},{12,8},{16,20},{20,16},{24,28},{28,24},{1,5},{5... | collective-permute-start | bytes 1572872 | tf_op jit(solution)/shard_map/ppermute | solution.py:384
  69.4 6.3 %collective-permute-start.10 = (bf16[128,1024]{1,0:T(8,128)(2,1)S(1)}, bf16[128,1024]{1,0:T(8,128)(2,1)S(1)}, u32[]{:S(2)}, u32[]{:S(2)}) collective-permute-start(bf16[128,1024]{1,0:T(8,128)(2,1)S(1)} %get-tuple-element.62), channel_id=1, source_target_pairs={{0,1},{1,0},{2,3},{3,2},{4,5},{5,4},{6,7},{7,6},{8,9},{9,8},{10,11... | collective-permute-start | bytes 786440 | tf_op jit(solution)/shard_map/ppermute | solution.py:385
  78.8 7.9 %collective-permute-start.15 = (bf16[128,1024]{1,0:T(8,128)(2,1)S(1)}, bf16[128,1024]{1,0:T(8,128)(2,1)S(1)}, u32[]{:S(2)}, u32[]{:S(2)}) collective-permute-start(bf16[128,1024]{1,0:T(8,128)(2,1)S(1)} %slice.10), channel_id=1, source_target_pairs={{8,0},{12,4},{16,24},{20,28},{9,1},{13,5},{17,25},{21,29},{10,2},{... | collective-permute-start | bytes 786440 | tf_op jit(solution)/shard_map/ppermute | solution.py:381
  82.7 3.9 %collective-permute-start.11 = (bf16[128,1024]{1,0:T(8,128)(2,1)S(1)}, bf16[128,1024]{1,0:T(8,128)(2,1)S(1)}, u32[]{:S(2)}, u32[]{:S(2)}) collective-permute-start(bf16[128,1024]{1,0:T(8,128)(2,1)S(1)} %slice.8), channel_id=1, source_target_pairs={{0,4},{4,0},{24,28},{28,24},{1,5},{5,1},{25,29},{29,25},{2,6},{6,2... | collective-permute-start | bytes 786440 | tf_op jit(solution)/shard_map/ppermute | solution.py:419
  86.7 8.0 %collective-permute-start.16 = (bf16[256,1024]{1,0:T(8,128)(2,1)S(1)}, bf16[256,1024]{1,0:T(8,128)(2,1)S(1)}, u32[]{:S(2)}, u32[]{:S(2)}) collective-permute-start(bf16[256,1024]{1,0:T(8,128)(2,1)S(1)} %pad_maximum_fusion), channel_id=1, source_target_pairs={{0,1},{1,0},{2,3},{3,2},{4,5},{5,4},{6,7},{7,6},{8,9},{9,8},{10,11... | collective-permute-start | bytes 1572872 | tf_op jit(solution)/shard_map/ppermute | solution.py:385
  93.0 1.6 %collective-permute-start.17 = (bf16[128,1024]{1,0:T(8,128)(2,1)S(1)}, bf16[128,1024]{1,0:T(8,128)(2,1)S(1)}, u32[]{:S(2)}, u32[]{:S(2)}) collective-permute-start(bf16[128,1024]{1,0:T(8,128)(2,1)S(1)} %get-tuple-element.74), channel_id=1, source_target_pairs={{0,1},{1,0},{2,3},{3,2},{4,5},{5,4},{6,7},{7,6},{8,9},{9,8},{10,11... | collective-permute-start | bytes 786440 | tf_op jit(solution)/shard_map/ppermute | solution.py:385
  94.9 15.1 %collective-permute-start.20 = (bf16[128,1024]{1,0:T(8,128)(2,1)S(1)}, bf16[128,1024]{1,0:T(8,128)(2,1)S(1)}, u32[]{:S(2)}, u32[]{:S(2)}) collective-permute-start(bf16[128,1024]{1,0:T(8,128)(2,1)S(1)} %get-tuple-element.83), channel_id=1, source_target_pairs={{0,8},{1,12},{2,16},{3,20},{4,9},{5,13},{6,17},{7,21},{8,0},{9,4},... | collective-permute-start | bytes 786440 | tf_op jit(solution)/shard_map/ppermute | solution.py:398
  99.4 12.6 %collective-permute-start.21 = (bf16[128,1024]{1,0:T(8,128)(2,1)S(1)}, bf16[128,1024]{1,0:T(8,128)(2,1)S(1)}, u32[]{:S(2)}, u32[]{:S(2)}) collective-permute-start(bf16[128,1024]{1,0:T(8,128)(2,1)S(1)} %get-tuple-element.84), channel_id=1, source_target_pairs={{0,16},{1,20},{2,8},{3,12},{4,17},{5,21},{6,9},{7,13},{8,24},{9,28... | collective-permute-start | bytes 786440 | tf_op jit(solution)/shard_map/ppermute | solution.py:398
  99.5 23.4 %collective-permute-start.18 = (bf16[128,1024]{1,0:T(8,128)(2,1)S(1)}, bf16[128,1024]{1,0:T(8,128)(2,1)S(1)}, u32[]{:S(2)}, u32[]{:S(2)}) collective-permute-start(bf16[128,1024]{1,0:T(8,128)(2,1)S(1)} %get-tuple-element.81), channel_id=1, source_target_pairs={{1,4},{2,24},{3,28},{4,1},{6,25},{7,29},{9,12},{10,16},{11,20},{12... | collective-permute-start | bytes 786440 | tf_op jit(solution)/shard_map/ppermute | solution.py:398
  103.6 20.4 %collective-permute-start.19 = (bf16[128,1024]{1,0:T(8,128)(2,1)S(1)}, bf16[128,1024]{1,0:T(8,128)(2,1)S(1)}, u32[]{:S(2)}, u32[]{:S(2)}) collective-permute-start(bf16[128,1024]{1,0:T(8,128)(2,1)S(1)} %get-tuple-element.82), channel_id=1, source_target_pairs={{0,24},{1,28},{2,0},{3,4},{4,25},{5,29},{6,1},{7,5},{8,16},{9,20},... | collective-permute-start | bytes 786440 | tf_op jit(solution)/shard_map/ppermute | solution.py:398
  124.2 1.6 %collective-permute-start.22 = (bf16[128,1024]{1,0:T(8,128)(2,1)S(1)}, bf16[128,1024]{1,0:T(8,128)(2,1)S(1)}, u32[]{:S(2)}, u32[]{:S(2)}) collective-permute-start(bf16[128,1024]{1,0:T(8,128)(2,1)S(1)} %get-tuple-element.79), channel_id=1, source_target_pairs={{0,1},{1,0},{2,3},{3,2},{4,5},{5,4},{6,7},{7,6},{8,9},{9,8},{10,11... | collective-permute-start | bytes 786440 | tf_op jit(solution)/shard_map/ppermute | solution.py:385

commit v10 on v9

--- a/solution.py
+++ b/solution.py
@@ -270,12 +270,14 @@
                 both_ref[rows, depth:] = (lower, upper)[k]()
 
         whole = got_refs[0]
+        extra = got_refs[2].shape[0] - tokens if len(got_refs) > 1 else 0
+        pieces = lambda: jnp.concatenate([got_refs[1][...], got_refs[2][:extra, :]])
         halves = lambda: fill(lambda: whole[:tokens, :], lambda: whole[tokens:, :])
         if len(got_refs) == 1:
             halves()
         else:
             pl.when(yc_ref[2] == 1)(halves)
-            pl.when(yc_ref[2] == 0)(lambda: fill(lambda: got_refs[1][...], lambda: got_refs[2][...]))
+            pl.when(yc_ref[2] == 0)(lambda: fill(pieces, lambda: got_refs[2][extra:, :]))
 
     part = jnp.dot(both_ref[:, :depth], first_ref[...], preferred_element_type=F32)
     part = part + jnp.dot(both_ref[:, depth:], second_ref[...], preferred_element_type=F32)
@@ -416,8 +418,9 @@
     inner3 = hop(other0, (1, 2), (2, 1))
     last, inner3, a1, b0 = tie((last, inner3, a1, b0))
     slot3 = jnp.where(inner, middle, last)
-    lower3 = lax.ppermute(last[:tokens], "seq", [(i * 2 + b, i * 2 + 1 - b) for i in (0, 3) for b in range(2)])
-    upper3 = hop(other2[tokens:], (1, 0), (2, 3))
+    cut = tokens - 16
+    lower3 = lax.ppermute(last[:cut], "seq", [(i * 2 + b, i * 2 + 1 - b) for i in (0, 3) for b in range(2)])
+    upper3 = hop(other2[cut:], (1, 0), (2, 3))
     a2 = project(yc, slot2, [other2], w_out)
     rounded = jnp.concatenate([a1[1], a2[1]])
     lower3, upper3, rounded = tie((lower3, upper3, rounded))

time: 127 us -> 128 us (level)
  other arithmetic: 0.81 us -> 2.65 us
    ppermute x7, waiting for transfers between devices: 9.09 us -> 7.55 us  [pair_shards(): lax.ppermute(value, 'seq', [(i * 2 + b, j * 2 + b) for i, j in moves for...]
  transfers between devices with their start and end apart: 23 -> 23, of which waited for: 13 -> 13; matrix products, arithmetic and copies ran while one was open for 3% -> 4% of each run, Pallas kernels for 11% -> 11%
where the time goes in v10:
time: 128 us; the launch traced here: 127 us
  waiting for transfers between devices  48.9 us (38%)
  starting transfers between devices  47.4 us (37%)
  Pallas kernels  18.8 us (15%)
  local copies, waits for them, and re-layouts  8.85 us (7%)
  other arithmetic  2.65 us (2%)
    ppermute x4, waiting for transfers between devices, deliver(): moved = lax.ppermute(value, both, [(i, j) for i, j in pairs if i != j])  20.2 us
    ppermute x7, starting transfers between devices, pair_shards(): lax.ppermute(value, 'seq', [(i * 2 + b, j * 2 + b) for i, j in moves for...  18.1 us
    ppermute x2, waiting for transfers between devices, along(): return lax.ppermute(v, 'seq', pairs)  13.7 us
    pallas_call x4, Pallas kernels, project(): pl.pallas_call(project_kernel, grid_spec=pltpu.PrefetchScalarGridSpec(num...  12.4 us
    ppermute x4, starting transfers between devices, deliver(): moved = lax.ppermute(value, both, [(i, j) for i, j in pairs if i != j])  8.21 us
    ppermute x7, waiting for transfers between devices, pair_shards(): lax.ppermute(value, 'seq', [(i * 2 + b, j * 2 + b) for i, j in moves for...  7.55 us
    ppermute x2, starting transfers between devices, along(): return lax.ppermute(v, 'seq', pairs)  7.43 us
    ppermute x4, starting transfers between devices, pair_shards(): cross = lambda value: lax.ppermute(value, 'grp', sibling)  6.59 us
  transfers between devices with their start and end apart: 23, of which 13 were waited for; matrix products, arithmetic and copies ran while one was open for 4% of the time, Pallas kernels for 11%

profile of v10, /device:TPU:11, one launch (start us, length us, event | category | flops | bytes accessed | tf_op | source)
XLA Modules:
  0.0 126.9 jit_solution(15655757997756002223)
XLA Ops:
  0.0 2.0 %pack.2 = bf16[128,1408]{1,0:T(8,128)(2,1)} custom-call(s32[1]{0:T(128)S(6)} %sub.23.refs_0_, bf16[128,2048]{1,0:T(8,128)(2,1)} %refs_1_.6, bf16[128,256]{1,0:T(8,128)(2,1)} %refs_2_.6, bf16[128,256]{1,0:T(8,128)(2,1)} %refs_3_.4, f32[16,128]{1,0:T(8,128)} %bitcast.10), custom_call_target="tpu_custom_call" | custom-call | flops 1000000 | bytes 1000000 | tf_op jit(solution)/shard_map/pack/pallas_call | solution.py:68
  9.0 2.4 %collective-permute-done.refs_2_ = bf16[128,1408]{1,0:T(8,128)(2,1)S(1)} collective-permute-done((bf16[128,1408]{1,0:T(8,128)(2,1)}, bf16[128,1408]{1,0:T(8,128)(2,1)S(1)}, u32[]{:S(2)}, u32[]{:S(2)}) %collective-permute-start) | collective-permute-done | bytes 360480 | tf_op jit(solution)/shard_map/ppermute | solution.py:366
  12.7 3.2 %collective-permute-start.1 = (bf16[144,1024]{1,0:T(8,128)(2,1)S(1)}, bf16[144,1024]{1,0:T(8,128)(2,1)S(1)}, u32[]{:S(2)}, u32[]{:S(2)}) collective-permute-start(bf16[144,1024]{1,0:T(8,128)(2,1)S(1)} %get-tuple-element.46.send_ref), channel_id=1, source_target_pairs={{0,8},{4,12},{8,16},{12,20},{16,24},{20,28},{1,9},{5,13},{9,17},{1... | collective-permute-start | bytes 884744 | tf_op jit(solution)/shard_map/ppermute | solution.py:364
  16.9 1.3 %collective-permute-start.3 = (bf16[128,1024]{1,0:T(8,128)(2,1)S(1)}, bf16[128,1024]{1,0:T(8,128)(2,1)S(1)}, u32[]{:S(2)}, u32[]{:S(2)}) collective-permute-start(bf16[128,1024]{1,0:T(8,128)(2,1)S(1)} %constant_dynamic-slice_fusion), channel_id=1, source_target_pairs={{0,4},{4,0},{8,12},{12,8},{16,20},{20,16},{24,28},{28,24},{1,5},{5... | collective-permute-start | bytes 786440 | tf_op jit(solution)/shard_map/ppermute | solution.py:372
  19.3 2.3 %collective-permute-done.1.got_ref.refs_4_ = bf16[144,1024]{1,0:T(8,128)(2,1)S(1)} collective-permute-done((bf16[144,1024]{1,0:T(8,128)(2,1)S(1)}, bf16[144,1024]{1,0:T(8,128)(2,1)S(1)}, u32[]{:S(2)}, u32[]{:S(2)}) %collective-permute-start.1) | collective-permute-done | bytes 294944 | tf_op jit(solution)/shard_map/ppermute | solution.py:364
  21.7 4.2 %collective-permute-start.2 = (bf16[128,1024]{1,0:T(8,128)(2,1)S(1)}, bf16[128,1024]{1,0:T(8,128)(2,1)S(1)}, u32[]{:S(2)}, u32[]{:S(2)}) collective-permute-start(bf16[128,1024]{1,0:T(8,128)(2,1)S(1)} %join.1), channel_id=1, source_target_pairs={{0,16},{4,20},{8,24},{12,28},{1,17},{5,21},{9,25},{13,29},{2,18},{... | collective-permute-start | bytes 786440 | tf_op jit(solution)/shard_map/ppermute | solution.py:364
  25.9 11.5 %collective-permute-done.2.refs_5_ = bf16[128,1024]{1,0:T(8,128)(2,1)S(1)} collective-permute-done((bf16[128,1024]{1,0:T(8,128)(2,1)S(1)}, bf16[128,1024]{1,0:T(8,128)(2,1)S(1)}, u32[]{:S(2)}, u32[]{:S(2)}) %collective-permute-start.2) | collective-permute-done | bytes 262176 | tf_op jit(solution)/shard_map/ppermute | solution.py:364
  38.4 5.3 %collective-permute-start.12 = (bf16[256,1024]{1,0:T(8,128)(2,1)S(1)}, bf16[256,1024]{1,0:T(8,128)(2,1)S(1)}, u32[]{:S(2)}, u32[]{:S(2)}) collective-permute-start(bf16[256,1024]{1,0:T(8,128)(2,1)S(1)} %finish.1.own_ref), channel_id=1, source_target_pairs={{8,16},{12,20},{16,8},{20,12},{9,17},{13,21},{17,9},{21,13},{10,18... | collective-permute-start | bytes 1572872 | tf_op jit(solution)/shard_map/ppermute | solution.py:383
  43.7 1.3 %collective-permute-start.6 = (bf16[256,1024]{1,0:T(8,128)(2,1)S(1)}, bf16[256,1024]{1,0:T(8,128)(2,1)S(1)}, u32[]{:S(2)}, u32[]{:S(2)}) collective-permute-start(bf16[256,1024]{1,0:T(8,128)(2,1)S(1)} %finish.1.own_ref), channel_id=1, source_target_pairs={{0,4},{4,0},{8,12},{12,8},{16,20},{20,16},{24,28},{28,24},{1,5},{5... | collective-permute-start | bytes 1572872 | tf_op jit(solution)/shard_map/ppermute | solution.py:386
  45.0 6.4 %collective-permute-done.4.own_ref = bf16[256,1024]{1,0:T(8,128)(2,1)S(1)} collective-permute-done((bf16[256,1024]{1,0:T(8,128)(2,1)S(1)}, bf16[256,1024]{1,0:T(8,128)(2,1)S(1)}, u32[]{:S(2)}, u32[]{:S(2)}) %collective-permute-start.4) | collective-permute-done | bytes 524320 | tf_op jit(solution)/shard_map/ppermute | solution.py:383
  51.4 4.1 %collective-permute-start.5 = (bf16[256,1024]{1,0:T(8,128)(2,1)S(1)}, bf16[256,1024]{1,0:T(8,128)(2,1)}, u32[]{:S(2)}, u32[]{:S(2)}) collective-permute-start(bf16[256,1024]{1,0:T(8,128)(2,1)S(1)} %collective-permute-done.4.own_ref), channel_id=1, source_target_pairs={{8,16},{12,20},{16,8},{20,12},{9,17},{13,21},{17,9},{21,13},{10,18... | collective-permute-start | bytes 1572872 | tf_op jit(solution)/shard_map/ppermute | solution.py:383
  55.5 1.3 %collective-permute-start.13 = (bf16[256,1024]{1,0:T(8,128)(2,1)S(1)}, bf16[256,1024]{1,0:T(8,128)(2,1)S(1)}, u32[]{:S(2)}, u32[]{:S(2)}) collective-permute-start(bf16[256,1024]{1,0:T(8,128)(2,1)S(1)} %collective-permute-done.12), channel_id=1, source_target_pairs={{8,0},{12,4},{16,24},{20,28},{9,1},{13,5},{17,25},{21,29},{10,2},{... | collective-permute-start | bytes 1572872 | tf_op jit(solution)/shard_map/ppermute | solution.py:383
  57.0 1.2 collective-permute-start.9
  58.2 3.2 %collective-permute-start.8 = (bf16[256,1024]{1,0:T(8,128)(2,1)S(1)}, bf16[256,1024]{1,0:T(8,128)(2,1)S(1)}, u32[]{:S(2)}, u32[]{:S(2)}) collective-permute-start(bf16[256,1024]{1,0:T(8,128)(2,1)S(1)} %collective-permute-done.6.refs_0_), channel_id=1, source_target_pairs={{8,16},{12,20},{16,8},{20,12},{9,17},{13,21},{17,9},{21,13},{10,18... | collective-permute-start | bytes 1572872 | tf_op jit(solution)/shard_map/ppermute | solution.py:383
  61.4 2.2 %copy-done = bf16[2048,1024]{1,0:T(8,128)(2,1)S(1)} copy-done((bf16[2048,1024]{1,0:T(8,128)(2,1)S(1)}, bf16[2048,1024]{1,0:T(8,128)(2,1)}, u32[]{:S(2)}) %copy-start) | copy-done | bytes 4194328
  63.6 3.1 %project.4 = (f32[128,1024]{1,0:T(8,128)S(1)}, bf16[128,1024]{1,0:T(8,128)(2,1)S(1)}) custom-call(s32[3]{0:T(128)S(1)} %pad_add_fusion.yc_ref, bf16[256,1024]{1,0:T(8,128)(2,1)S(1)} %finish.1.own_ref, bf16[256,1024]{1,0:T(8,128)(2,1)S(1)} %collective-permute-done.6.refs_0_, bf16[2048,1024]{1,0:T(8,128)(2,1)S(1)} %copy-done, bf16[2048,1024]{1,0:T(8,128)(2,1)S(1)} %copy-done), custom_call_target="tpu_custom_call" | custom-call | flops 1073741824 | bytes 6000000 | tf_op jit(solution)/shard_map/project/pallas_call | solution.py:293
  66.8 1.3 %collective-permute-start.7 = (bf16[256,1024]{1,0:T(8,128)(2,1)}, bf16[256,1024]{1,0:T(8,128)(2,1)S(1)}, u32[]{:S(2)}, u32[]{:S(2)}) collective-permute-start(bf16[256,1024]{1,0:T(8,128)(2,1)} %collective-permute-done.5), channel_id=1, source_target_pairs={{8,0},{12,4},{16,24},{20,28},{9,1},{13,5},{17,25},{21,29},{10,2},{... | collective-permute-start | bytes 1572872 | tf_op jit(solution)/shard_map/ppermute | solution.py:383
  69.3 1.3 %collective-permute-start.14 = (bf16[256,1024]{1,0:T(8,128)(2,1)S(1)}, bf16[256,1024]{1,0:T(8,128)(2,1)S(1)}, u32[]{:S(2)}, u32[]{:S(2)}) collective-permute-start(bf16[256,1024]{1,0:T(8,128)(2,1)S(1)} %broadcast_select_fusion.1.own_ref), channel_id=1, source_target_pairs={{0,4},{4,0},{8,12},{12,8},{16,20},{20,16},{24,28},{28,24},{1,5},{5... | collective-permute-start | bytes 1572872 | tf_op jit(solution)/shard_map/ppermute | solution.py:386
  70.6 3.2 %collective-permute-start.10 = (bf16[128,1024]{1,0:T(8,128)(2,1)S(1)}, bf16[128,1024]{1,0:T(8,128)(2,1)S(1)}, u32[]{:S(2)}, u32[]{:S(2)}) collective-permute-start(bf16[128,1024]{1,0:T(8,128)(2,1)S(1)} %get-tuple-element.62), channel_id=1, source_target_pairs={{0,1},{1,0},{2,3},{3,2},{4,5},{5,4},{6,7},{7,6},{8,9},{9,8},{10,11... | collective-permute-start | bytes 786440 | tf_op jit(solution)/shard_map/ppermute | solution.py:387
  73.8 3.1 %project.5 = (f32[128,1024]{1,0:T(8,128)S(1)}, bf16[128,1024]{1,0:T(8,128)(2,1)S(1)}) custom-call(s32[3]{0:T(128)S(1)} %pad_add_fusion.yc_ref, bf16[256,1024]{1,0:T(8,128)(2,1)S(1)} %collective-permute-done.4.own_ref, bf16[256,1024]{1,0:T(8,128)(2,1)S(1)} %collective-permute-done.9.refs_0_, bf16[2048,1024]{1,0:T(8,128)(2,1)S(1)} %copy-done.1, ...), custom_call_target="tpu_custom_call" | custom-call | flops 1073741824 | bytes 6000000 | tf_op jit(solution)/shard_map/project/pallas_call | solution.py:293
  78.0 1.9 %collective-permute-done.14.refs_0_ = bf16[256,1024]{1,0:T(8,128)(2,1)S(1)} collective-permute-done((bf16[256,1024]{1,0:T(8,128)(2,1)S(1)}, bf16[256,1024]{1,0:T(8,128)(2,1)S(1)}, u32[]{:S(2)}, u32[]{:S(2)}) %collective-permute-start.14) | collective-permute-done | bytes 524320 | tf_op jit(solution)/shard_map/ppermute | solution.py:386
  79.9 2.8 %collective-permute-start.15 = (bf16[144,1024]{1,0:T(8,128)(2,1)S(1)}, bf16[144,1024]{1,0:T(8,128)(2,1)S(1)}, u32[]{:S(2)}, u32[]{:S(2)}) collective-permute-start(bf16[144,1024]{1,0:T(8,128)(2,1)S(1)} %slice.10), channel_id=1, source_target_pairs={{8,0},{12,4},{16,24},{20,28},{9,1},{13,5},{17,25},{21,29},{10,2},{... | collective-permute-start | bytes 884744 | tf_op jit(solution)/shard_map/ppermute | solution.py:383
  83.4 3.1 %project.6 = (f32[128,1024]{1,0:T(8,128)S(1)}, bf16[128,1024]{1,0:T(8,128)(2,1)S(1)}) custom-call(s32[3]{0:T(128)S(1)} %pad_add_fusion.yc_ref, bf16[256,1024]{1,0:T(8,128)(2,1)S(1)} %broadcast_select_fusion.1.own_ref, bf16[256,1024]{1,0:T(8,128)(2,1)S(1)} %collective-permute-done.14.refs_0_, bf16[2048,1024]{1,0:T(8,128)(2,1)S(1)} %copy-done.1, ...), custom_call_target="tpu_custom_call" | custom-call | flops 1073741824 | bytes 6000000 | tf_op jit(solution)/shard_map/project/pallas_call | solution.py:293
  87.5 3.2 %collective-permute-start.16 = (bf16[256,1024]{1,0:T(8,128)(2,1)}, bf16[256,1024]{1,0:T(8,128)(2,1)S(1)}, u32[]{:S(2)}, u32[]{:S(2)}) collective-permute-start(bf16[256,1024]{1,0:T(8,128)(2,1)} %pad_maximum_fusion), channel_id=1, source_target_pairs={{0,1},{1,0},{2,3},{3,2},{4,5},{5,4},{6,7},{7,6},{8,9},{9,8},{10,11... | collective-permute-start | bytes 1572872 | tf_op jit(solution)/shard_map/ppermute | solution.py:387
  90.7 3.1 %project.7 = (f32[128,1024]{1,0:T(8,128)S(1)}, bf16[128,1024]{1,0:T(8,128)(2,1)S(1)}) custom-call(s32[3]{0:T(128)S(1)} %pad_add_fusion.yc_ref, bf16[256,1024]{1,0:T(8,128)(2,1)S(1)} %broadcast_select_fusion.own_ref, bf16[256,1024]{1,0:T(8,128)(2,1)S(1)} %collective-permute-done.8.refs_0_, bf16[112,1024]{1,0:T(8,128)(2,1)S(1)} %collective-permute-done.11.refs_1_, ...), custom_call_target="tpu_custom_call" | custom-call | flops 1073741824 | bytes 6000000 | tf_op jit(solution)/shard_map/project/pallas_call | solution.py:293
  93.9 1.5 %collective-permute-done.17 = bf16[128,1024]{1,0:T(8,128)(2,1)S(1)} collective-permute-done((bf16[128,1024]{1,0:T(8,128)(2,1)S(1)}, bf16[128,1024]{1,0:T(8,128)(2,1)S(1)}, u32[]{:S(2)}, u32[]{:S(2)}) %collective-permute-start.17) | collective-permute-done | bytes 262176 | tf_op jit(solution)/shard_map/ppermute | solution.py:387
  95.7 3.9 %collective-permute-start.20 = (bf16[128,1024]{1,0:T(8,128)(2,1)S(1)}, bf16[128,1024]{1,0:T(8,128)(2,1)S(1)}, u32[]{:S(2)}, u32[]{:S(2)}) collective-permute-start(bf16[128,1024]{1,0:T(8,128)(2,1)S(1)} %get-tuple-element.83), channel_id=1, source_target_pairs={{0,8},{1,12},{2,16},{3,20},{4,9},{5,13},{6,17},{7,21},{8,0},{9,4},... | collective-permute-start | bytes 786440 | tf_op jit(solution)/shard_map/ppermute | solution.py:400
  99.7 3.5 %collective-permute-start.18 = (bf16[128,1024]{1,0:T(8,128)(2,1)S(1)}, bf16[128,1024]{1,0:T(8,128)(2,1)S(1)}, u32[]{:S(2)}, u32[]{:S(2)}) collective-permute-start(bf16[128,1024]{1,0:T(8,128)(2,1)S(1)} %get-tuple-element.81), channel_id=1, source_target_pairs={{1,4},{2,24},{3,28},{4,1},{6,25},{7,29},{9,12},{10,16},{11,20},{12... | collective-permute-start | bytes 786440 | tf_op jit(solution)/shard_map/ppermute | solution.py:400
  104.0 6.1 %collective-permute-done.20 = bf16[128,1024]{1,0:T(8,128)(2,1)S(1)} collective-permute-done((bf16[128,1024]{1,0:T(8,128)(2,1)S(1)}, bf16[128,1024]{1,0:T(8,128)(2,1)S(1)}, u32[]{:S(2)}, u32[]{:S(2)}) %collective-permute-start.20) | collective-permute-done | bytes 262176 | tf_op jit(solution)/shard_map/ppermute | solution.py:400
  110.1 2.1 %collective-permute-done.21 = bf16[128,1024]{1,0:T(8,128)(2,1)S(1)} collective-permute-done((bf16[128,1024]{1,0:T(8,128)(2,1)S(1)}, bf16[128,1024]{1,0:T(8,128)(2,1)S(1)}, u32[]{:S(2)}, u32[]{:S(2)}) %collective-permute-start.21) | collective-permute-done | bytes 262176 | tf_op jit(solution)/shard_map/ppermute | solution.py:400
  112.2 11.7 %collective-permute-done.18 = bf16[128,1024]{1,0:T(8,128)(2,1)S(1)} collective-permute-done((bf16[128,1024]{1,0:T(8,128)(2,1)S(1)}, bf16[128,1024]{1,0:T(8,128)(2,1)S(1)}, u32[]{:S(2)}, u32[]{:S(2)}) %collective-permute-start.18) | collective-permute-done | bytes 262176 | tf_op jit(solution)/shard_map/ppermute | solution.py:400
  124.5 1.5 %collective-permute-done.22.got_ref = bf16[128,1024]{1,0:T(8,128)(2,1)S(1)} collective-permute-done((bf16[128,1024]{1,0:T(8,128)(2,1)S(1)}, bf16[128,1024]{1,0:T(8,128)(2,1)S(1)}, u32[]{:S(2)}, u32[]{:S(2)}) %collective-permute-start.22) | collective-permute-done | bytes 262176 | tf_op jit(solution)/shard_map/ppermute | solution.py:387
  (56 shorter events, 18.0 us)
Async XLA Ops:
  0.0 37.4 %copy-start.3 = (bf16[128,2048]{1,0:T(8,128)(2,1)S(1)}, bf16[128,2048]{1,0:T(8,128)(2,1)}, u32[]{:S(2)}) copy-start(bf16[128,2048]{1,0:T(8,128)(2,1)} %refs_6_.1) | copy-start | bytes 1572868
  2.0 9.5 %collective-permute-start = (bf16[128,1408]{1,0:T(8,128)(2,1)}, bf16[128,1408]{1,0:T(8,128)(2,1)S(1)}, u32[]{:S(2)}, u32[]{:S(2)}) collective-permute-start(bf16[128,1408]{1,0:T(8,128)(2,1)} %pack.2), channel_id=1, source_target_pairs={{0,4},{4,0},{8,12},{12,8},{16,20},{20,16},{24,28},{28,24},{1,5},{5... | collective-permute-start | bytes 1081352 | tf_op jit(solution)/shard_map/ppermute | solution.py:366
  4.6 1.0 copy-start.2
  5.7 0.8 copy-start.4
  6.5 0.8 copy-start.5
  7.4 0.7 copy-start.6
  12.7 8.8 %collective-permute-start.1 = (bf16[144,1024]{1,0:T(8,128)(2,1)S(1)}, bf16[144,1024]{1,0:T(8,128)(2,1)S(1)}, u32[]{:S(2)}, u32[]{:S(2)}) collective-permute-start(bf16[144,1024]{1,0:T(8,128)(2,1)S(1)} %get-tuple-element.46.send_ref), channel_id=1, source_target_pairs={{0,8},{4,12},{8,16},{12,20},{16,24},{20,28},{1,9},{5,13},{9,17},{1... | collective-permute-start | bytes 884744 | tf_op jit(solution)/shard_map/ppermute | solution.py:364
  16.9 9.0 %collective-permute-start.3 = (bf16[128,1024]{1,0:T(8,128)(2,1)S(1)}, bf16[128,1024]{1,0:T(8,128)(2,1)S(1)}, u32[]{:S(2)}, u32[]{:S(2)}) collective-permute-start(bf16[128,1024]{1,0:T(8,128)(2,1)S(1)} %constant_dynamic-slice_fusion), channel_id=1, source_target_pairs={{0,4},{4,0},{8,12},{12,8},{16,20},{20,16},{24,28},{28,24},{1,5},{5... | collective-permute-start | bytes 786440 | tf_op jit(solution)/shard_map/ppermute | solution.py:372
  21.7 15.7 %collective-permute-start.2 = (bf16[128,1024]{1,0:T(8,128)(2,1)S(1)}, bf16[128,1024]{1,0:T(8,128)(2,1)S(1)}, u32[]{:S(2)}, u32[]{:S(2)}) collective-permute-start(bf16[128,1024]{1,0:T(8,128)(2,1)S(1)} %join.1), channel_id=1, source_target_pairs={{0,16},{4,20},{8,24},{12,28},{1,17},{5,21},{9,25},{13,29},{2,18},{... | collective-permute-start | bytes 786440 | tf_op jit(solution)/shard_map/ppermute | solution.py:364
  38.4 13.0 %collective-permute-start.4 = (bf16[256,1024]{1,0:T(8,128)(2,1)S(1)}, bf16[256,1024]{1,0:T(8,128)(2,1)S(1)}, u32[]{:S(2)}, u32[]{:S(2)}) collective-permute-start(bf16[256,1024]{1,0:T(8,128)(2,1)S(1)} %finish.1.own_ref), channel_id=1, source_target_pairs={{0,8},{4,12},{8,0},{12,4},{16,24},{20,28},{24,16},{28,20},{1,9},{5... | collective-permute-start | bytes 1572872 | tf_op jit(solution)/shard_map/ppermute | solution.py:383
  38.4 17.1 %collective-permute-start.12 = (bf16[256,1024]{1,0:T(8,128)(2,1)S(1)}, bf16[256,1024]{1,0:T(8,128)(2,1)S(1)}, u32[]{:S(2)}, u32[]{:S(2)}) collective-permute-start(bf16[256,1024]{1,0:T(8,128)(2,1)S(1)} %finish.1.own_ref), channel_id=1, source_target_pairs={{8,16},{12,20},{16,8},{20,12},{9,17},{13,21},{17,9},{21,13},{10,18... | collective-permute-start | bytes 1572872 | tf_op jit(solution)/shard_map/ppermute | solution.py:383
  43.7 14.5 %collective-permute-start.6 = (bf16[256,1024]{1,0:T(8,128)(2,1)S(1)}, bf16[256,1024]{1,0:T(8,128)(2,1)S(1)}, u32[]{:S(2)}, u32[]{:S(2)}) collective-permute-start(bf16[256,1024]{1,0:T(8,128)(2,1)S(1)} %finish.1.own_ref), channel_id=1, source_target_pairs={{0,4},{4,0},{8,12},{12,8},{16,20},{20,16},{24,28},{28,24},{1,5},{5... | collective-permute-start | bytes 1572872 | tf_op jit(solution)/shard_map/ppermute | solution.py:386
  51.4 15.5 %collective-permute-start.5 = (bf16[256,1024]{1,0:T(8,128)(2,1)S(1)}, bf16[256,1024]{1,0:T(8,128)(2,1)}, u32[]{:S(2)}, u32[]{:S(2)}) collective-permute-start(bf16[256,1024]{1,0:T(8,128)(2,1)S(1)} %collective-permute-done.4.own_ref), channel_id=1, source_target_pairs={{8,16},{12,20},{16,8},{20,12},{9,17},{13,21},{17,9},{21,13},{10,18... | collective-permute-start | bytes 1572872 | tf_op jit(solution)/shard_map/ppermute | solution.py:383
  55.5 12.6 %collective-permute-start.13 = (bf16[256,1024]{1,0:T(8,128)(2,1)S(1)}, bf16[256,1024]{1,0:T(8,128)(2,1)S(1)}, u32[]{:S(2)}, u32[]{:S(2)}) collective-permute-start(bf16[256,1024]{1,0:T(8,128)(2,1)S(1)} %collective-permute-done.12), channel_id=1, source_target_pairs={{8,0},{12,4},{16,24},{20,28},{9,1},{13,5},{17,25},{21,29},{10,2},{... | collective-permute-start | bytes 1572872 | tf_op jit(solution)/shard_map/ppermute | solution.py:383
  57.0 16.8 %collective-permute-start.9 = (bf16[256,1024]{1,0:T(8,128)(2,1)S(1)}, bf16[256,1024]{1,0:T(8,128)(2,1)S(1)}, u32[]{:S(2)}, u32[]{:S(2)}) collective-permute-start(bf16[256,1024]{1,0:T(8,128)(2,1)S(1)} %collective-permute-done.4.own_ref), channel_id=1, source_target_pairs={{0,4},{4,0},{8,12},{12,8},{16,20},{20,16},{24,28},{28,24},{1,5},{5... | collective-permute-start | bytes 1572872 | tf_op jit(solution)/shard_map/ppermute | solution.py:386
  58.2 19.8 %collective-permute-start.8 = (bf16[256,1024]{1,0:T(8,128)(2,1)S(1)}, bf16[256,1024]{1,0:T(8,128)(2,1)S(1)}, u32[]{:S(2)}, u32[]{:S(2)}) collective-permute-start(bf16[256,1024]{1,0:T(8,128)(2,1)S(1)} %collective-permute-done.6.refs_0_), channel_id=1, source_target_pairs={{8,16},{12,20},{16,8},{20,12},{9,17},{13,21},{17,9},{21,13},{10,18... | collective-permute-start | bytes 1572872 | tf_op jit(solution)/shard_map/ppermute | solution.py:383
  61.4 2.2 %copy-start = (bf16[2048,1024]{1,0:T(8,128)(2,1)S(1)}, bf16[2048,1024]{1,0:T(8,128)(2,1)}, u32[]{:S(2)}) copy-start(bf16[2048,1024]{1,0:T(8,128)(2,1)} %refs_4_.1) | copy-start | bytes 12582916
  63.6 10.2 %copy-start.1 = (bf16[2048,1024]{1,0:T(8,128)(2,1)S(1)}, bf16[2048,1024]{1,0:T(8,128)(2,1)}, u32[]{:S(2)}) copy-start(bf16[2048,1024]{1,0:T(8,128)(2,1)} %refs_4_.1) | copy-start | bytes 12582916
  66.8 11.1 %collective-permute-start.7 = (bf16[256,1024]{1,0:T(8,128)(2,1)}, bf16[256,1024]{1,0:T(8,128)(2,1)S(1)}, u32[]{:S(2)}, u32[]{:S(2)}) collective-permute-start(bf16[256,1024]{1,0:T(8,128)(2,1)} %collective-permute-done.5), channel_id=1, source_target_pairs={{8,0},{12,4},{16,24},{20,28},{9,1},{13,5},{17,25},{21,29},{10,2},{... | collective-permute-start | bytes 1572872 | tf_op jit(solution)/shard_map/ppermute | solution.py:383
  69.3 10.6 %collective-permute-start.14 = (bf16[256,1024]{1,0:T(8,128)(2,1)S(1)}, bf16[256,1024]{1,0:T(8,128)(2,1)S(1)}, u32[]{:S(2)}, u32[]{:S(2)}) collective-permute-start(bf16[256,1024]{1,0:T(8,128)(2,1)S(1)} %broadcast_select_fusion.1.own_ref), channel_id=1, source_target_pairs={{0,4},{4,0},{8,12},{12,8},{16,20},{20,16},{24,28},{28,24},{1,5},{5... | collective-permute-start | bytes 1572872 | tf_op jit(solution)/shard_map/ppermute | solution.py:386
  70.6 6.3 %collective-permute-start.10 = (bf16[128,1024]{1,0:T(8,128)(2,1)S(1)}, bf16[128,1024]{1,0:T(8,128)(2,1)S(1)}, u32[]{:S(2)}, u32[]{:S(2)}) collective-permute-start(bf16[128,1024]{1,0:T(8,128)(2,1)S(1)} %get-tuple-element.62), channel_id=1, source_target_pairs={{0,1},{1,0},{2,3},{3,2},{4,5},{5,4},{6,7},{7,6},{8,9},{9,8},{10,11... | collective-permute-start | bytes 786440 | tf_op jit(solution)/shard_map/ppermute | solution.py:387
  79.9 7.6 %collective-permute-start.15 = (bf16[144,1024]{1,0:T(8,128)(2,1)S(1)}, bf16[144,1024]{1,0:T(8,128)(2,1)S(1)}, u32[]{:S(2)}, u32[]{:S(2)}) collective-permute-start(bf16[144,1024]{1,0:T(8,128)(2,1)S(1)} %slice.10), channel_id=1, source_target_pairs={{8,0},{12,4},{16,24},{20,28},{9,1},{13,5},{17,25},{21,29},{10,2},{... | collective-permute-start | bytes 884744 | tf_op jit(solution)/shard_map/ppermute | solution.py:383
  82.7 4.7 %collective-permute-start.11 = (bf16[112,1024]{1,0:T(8,128)(2,1)S(1)}, bf16[112,1024]{1,0:T(8,128)(2,1)S(1)}, u32[]{:S(2)}, u32[]{:S(2)}) collective-permute-start(bf16[112,1024]{1,0:T(8,128)(2,1)S(1)} %slice.8), channel_id=1, source_target_pairs={{0,4},{4,0},{24,28},{28,24},{1,5},{5,1},{25,29},{29,25},{2,6},{6,2... | collective-permute-start | bytes 688136 | tf_op jit(solution)/shard_map/ppermute | solution.py:422
  87.5 8.0 %collective-permute-start.16 = (bf16[256,1024]{1,0:T(8,128)(2,1)}, bf16[256,1024]{1,0:T(8,128)(2,1)S(1)}, u32[]{:S(2)}, u32[]{:S(2)}) collective-permute-start(bf16[256,1024]{1,0:T(8,128)(2,1)} %pad_maximum_fusion), channel_id=1, source_target_pairs={{0,1},{1,0},{2,3},{3,2},{4,5},{5,4},{6,7},{7,6},{8,9},{9,8},{10,11... | collective-permute-start | bytes 1572872 | tf_op jit(solution)/shard_map/ppermute | solution.py:387
  93.8 1.6 %collective-permute-start.17 = (bf16[128,1024]{1,0:T(8,128)(2,1)S(1)}, bf16[128,1024]{1,0:T(8,128)(2,1)S(1)}, u32[]{:S(2)}, u32[]{:S(2)}) collective-permute-start(bf16[128,1024]{1,0:T(8,128)(2,1)S(1)} %get-tuple-element.74), channel_id=1, source_target_pairs={{0,1},{1,0},{2,3},{3,2},{4,5},{5,4},{6,7},{7,6},{8,9},{9,8},{10,11... | collective-permute-start | bytes 786440 | tf_op jit(solution)/shard_map/ppermute | solution.py:387
  95.7 14.4 %collective-permute-start.20 = (bf16[128,1024]{1,0:T(8,128)(2,1)S(1)}, bf16[128,1024]{1,0:T(8,128)(2,1)S(1)}, u32[]{:S(2)}, u32[]{:S(2)}) collective-permute-start(bf16[128,1024]{1,0:T(8,128)(2,1)S(1)} %get-tuple-element.83), channel_id=1, source_target_pairs={{0,8},{1,12},{2,16},{3,20},{4,9},{5,13},{6,17},{7,21},{8,0},{9,4},... | collective-permute-start | bytes 786440 | tf_op jit(solution)/shard_map/ppermute | solution.py:400
  99.6 12.6 %collective-permute-start.21 = (bf16[128,1024]{1,0:T(8,128)(2,1)S(1)}, bf16[128,1024]{1,0:T(8,128)(2,1)S(1)}, u32[]{:S(2)}, u32[]{:S(2)}) collective-permute-start(bf16[128,1024]{1,0:T(8,128)(2,1)S(1)} %get-tuple-element.84), channel_id=1, source_target_pairs={{0,16},{1,20},{2,8},{3,12},{4,17},{5,21},{6,9},{7,13},{8,24},{9,28... | collective-permute-start | bytes 786440 | tf_op jit(solution)/shard_map/ppermute | solution.py:400
  99.7 24.3 %collective-permute-start.18 = (bf16[128,1024]{1,0:T(8,128)(2,1)S(1)}, bf16[128,1024]{1,0:T(8,128)(2,1)S(1)}, u32[]{:S(2)}, u32[]{:S(2)}) collective-permute-start(bf16[128,1024]{1,0:T(8,128)(2,1)S(1)} %get-tuple-element.81), channel_id=1, source_target_pairs={{1,4},{2,24},{3,28},{4,1},{6,25},{7,29},{9,12},{10,16},{11,20},{12... | collective-permute-start | bytes 786440 | tf_op jit(solution)/shard_map/ppermute | solution.py:400
  103.2 21.0 %collective-permute-start.19 = (bf16[128,1024]{1,0:T(8,128)(2,1)S(1)}, bf16[128,1024]{1,0:T(8,128)(2,1)S(1)}, u32[]{:S(2)}, u32[]{:S(2)}) collective-permute-start(bf16[128,1024]{1,0:T(8,128)(2,1)S(1)} %get-tuple-element.82), channel_id=1, source_target_pairs={{0,24},{1,28},{2,0},{3,4},{4,25},{5,29},{6,1},{7,5},{8,16},{9,20},... | collective-permute-start | bytes 786440 | tf_op jit(solution)/shard_map/ppermute | solution.py:400
  124.5 1.6 %collective-permute-start.22 = (bf16[128,1024]{1,0:T(8,128)(2,1)S(1)}, bf16[128,1024]{1,0:T(8,128)(2,1)S(1)}, u32[]{:S(2)}, u32[]{:S(2)}) collective-permute-start(bf16[128,1024]{1,0:T(8,128)(2,1)S(1)} %get-tuple-element.79), channel_id=1, source_target_pairs={{0,1},{1,0},{2,3},{3,2},{4,5},{5,4},{6,7},{7,6},{8,9},{9,8},{10,11... | collective-permute-start | bytes 786440 | tf_op jit(solution)/shard_map/ppermute | solution.py:387
